TPU v7x, 32 devices: a whole 2x2x4 slice. The times are simulated.
32 devices in a mesh: grp: 4 (over z), wide: 8 (over y, x, core).
Axes of the slice: x: 2, y: 2, z: 4, core: 2. Of those that a mesh axis runs over, the one named last changes fastest.
Arguments:
- field: float32 [64, 8, 2048], P('wide', 'grp'), may hold values from -6 to 6
- conduct: float32 [64, 8, 2048], P('wide', 'grp'), may hold values from 0.05 to 0.5
- mode_index: int32 [8, 3], P('grp'), may hold values from 0 to 31
- mode_amp: float32 [8], P('grp'), may hold values from 0 to 0.0625
- mode_phase: float32 [8], P('grp'), may hold values from -3.140625 to 3.140625
- step_index: int32 [1], replicated, may hold values from 0 to 4095
Outputs:
- advanced: float32 [64, 8, 2048], P('wide', 'grp')
All inputs are finite; a program needn't handle non-finite values.
Results may differ from a plain program's by a relative error of at most 0.0003.
Values sent between devices are 32-bit elements; how exact they have to be, the bound alone decides.
No kernel may reach another device: no remote copies, remote signals or barrier semaphores. Data moves between devices by JAX's collectives and lax.ppermute only.
A program may use at most 64 MiB of HBM per device.

v0:
```python
import jax
import jax.numpy as jnp
from jax import lax
from jax.sharding import PartitionSpec as P

time_step = 600.0
implicit_weight = 0.5
two_pi = 6.283185307179586


def padded_2(block, sides, width):
    for axis, dim in sides:
        count = lax.axis_size(axis)
        forward = [(i, i + 1) for i in range(count - 1)]
        backward = [(target, source) for source, target in forward]
        low = lax.ppermute(
            lax.slice_in_dim(block, block.shape[dim] - width, None, axis=dim), axis, forward
        )
        high = lax.ppermute(lax.slice_in_dim(block, 0, width, axis=dim), axis, backward)
        block = jnp.concatenate([low, block, high], axis=dim)
    return block


def boundary_height(
    mode_index, mode_amp, mode_phase, step_index, row_ids, col_ids, row_total, col_total
):
    wave_x = mode_index[:, 0:1]
    wave_y = mode_index[:, 1:2]
    wave_time = mode_index[:, 2]
    moment = step_index[0]
    offset = mode_phase + two_pi / 64.0 * (wave_time * moment % 64).astype(jnp.float32)
    angle_x = two_pi / col_total * (wave_x * col_ids[None, :] % col_total).astype(jnp.float32)
    angle_y = (
        two_pi / row_total * (wave_y * row_ids[None, :] % row_total).astype(jnp.float32)
        + offset[:, None]
    )
    left_cos = jnp.transpose(mode_amp[:, None] * jnp.cos(angle_y))
    left_sin = jnp.transpose(mode_amp[:, None] * jnp.sin(angle_y))
    part_cos = jnp.dot(
        left_cos,
        jnp.cos(angle_x),
        precision=lax.Precision.HIGHEST,
        preferred_element_type=jnp.float32,
    )
    part_sin = jnp.dot(
        left_sin,
        jnp.sin(angle_x),
        precision=lax.Precision.HIGHEST,
        preferred_element_type=jnp.float32,
    )
    return part_cos - part_sin


def face_values(coeff, axis):
    count = coeff.shape[axis]
    before = jnp.concatenate(
        [
            lax.slice_in_dim(coeff, 0, 1, axis=axis),
            lax.slice_in_dim(coeff, 0, count - 1, axis=axis),
        ],
        axis,
    )
    after = jnp.concatenate(
        [
            lax.slice_in_dim(coeff, 1, count, axis=axis),
            lax.slice_in_dim(coeff, count - 1, count, axis=axis),
        ],
        axis,
    )
    return (0.5 * (coeff + before), 0.5 * (coeff + after))


def spread(field, lower_face, upper_face, axis):
    count = field.shape[axis]
    zero_plane = jnp.zeros_like(lax.slice_in_dim(field, 0, 1, axis=axis))
    before = jnp.concatenate([zero_plane, lax.slice_in_dim(field, 0, count - 1, axis=axis)], axis)
    after = jnp.concatenate([lax.slice_in_dim(field, 1, count, axis=axis), zero_plane], axis)
    return upper_face * (after - field) - lower_face * (field - before)


def tridiagonal(lower_face, upper_face, axis):
    count = lower_face.shape[axis]
    weight = implicit_weight * time_step
    zero_plane = jnp.zeros_like(lax.slice_in_dim(lower_face, 0, 1, axis=axis))
    lower = jnp.concatenate(
        [zero_plane, -weight * lax.slice_in_dim(lower_face, 1, count, axis=axis)], axis
    )
    upper = jnp.concatenate(
        [-weight * lax.slice_in_dim(upper_face, 0, count - 1, axis=axis), zero_plane], axis
    )
    diagonal = 1.0 + weight * (lower_face + upper_face)
    return (lower, diagonal, upper)


def shift_forward(values, fill, axis):
    count = values.shape[axis]
    pad_plane = jnp.full_like(lax.slice_in_dim(values, 0, 1, axis=axis), fill)
    return jnp.concatenate([lax.slice_in_dim(values, 1, count, axis=axis), pad_plane], axis)


def shift_backward(values, axis):
    count = values.shape[axis]
    pad_plane = jnp.zeros_like(lax.slice_in_dim(values, 0, 1, axis=axis))
    return jnp.concatenate([pad_plane, lax.slice_in_dim(values, 0, count - 1, axis=axis)], axis)


def every_other(values, start, axis):
    return lax.slice_in_dim(values, start, values.shape[axis], 2, axis)


def cyclic_solve(lower, diagonal, upper, rhs, axis):
    count = rhs.shape[axis]
    if count == 1:
        return rhs / diagonal
    low_even = every_other(lower, 0, axis)
    low_odd = every_other(lower, 1, axis)
    dia_even = every_other(diagonal, 0, axis)
    dia_odd = every_other(diagonal, 1, axis)
    up_even = every_other(upper, 0, axis)
    up_odd = every_other(upper, 1, axis)
    rhs_even = every_other(rhs, 0, axis)
    rhs_odd = every_other(rhs, 1, axis)
    low_next = shift_forward(low_even, 0.0, axis)
    dia_next = shift_forward(dia_even, 1.0, axis)
    up_next = shift_forward(up_even, 0.0, axis)
    rhs_next = shift_forward(rhs_even, 0.0, axis)
    alpha = -low_odd / dia_even
    gamma = -up_odd / dia_next
    reduced = cyclic_solve(
        alpha * low_even,
        dia_odd + alpha * up_even + gamma * low_next,
        gamma * up_next,
        rhs_odd + alpha * rhs_even + gamma * rhs_next,
        axis,
    )
    before = shift_backward(reduced, axis)
    solved_even = (rhs_even - low_even * before - up_even * reduced) / dia_even
    joined = jnp.stack([solved_even, reduced], axis=axis + 1)
    return joined.reshape(rhs.shape)


def moved_lanes(values, stride, fill, upward):
    count = values.shape[-1]
    pad_block = jnp.full(values.shape[:-1] + (stride,), fill, values.dtype)
    if upward:
        return jnp.concatenate([values[..., stride:], pad_block], -1)
    return jnp.concatenate([pad_block, values[..., : count - stride]], -1)


def parallel_reduction(lower, diagonal, upper, rhs):
    count = rhs.shape[-1]
    stride = 1
    while stride < count:
        low_prev = moved_lanes(lower, stride, 0.0, False)
        dia_prev = moved_lanes(diagonal, stride, 1.0, False)
        up_prev = moved_lanes(upper, stride, 0.0, False)
        rhs_prev = moved_lanes(rhs, stride, 0.0, False)
        low_next = moved_lanes(lower, stride, 0.0, True)
        dia_next = moved_lanes(diagonal, stride, 1.0, True)
        up_next = moved_lanes(upper, stride, 0.0, True)
        rhs_next = moved_lanes(rhs, stride, 0.0, True)
        alpha = -lower / dia_prev
        gamma = -upper / dia_next
        diagonal = diagonal + alpha * up_prev + gamma * low_next
        rhs = rhs + alpha * rhs_prev + gamma * rhs_next
        lower = alpha * low_prev
        upper = gamma * up_next
        stride = stride * 2
    return rhs / diagonal


def solve_columns(moved, moved_jac):
    line_count, layer_count, col_count = moved.shape
    flat_rhs = moved.reshape(line_count, layer_count * col_count)
    flat_jac = moved_jac.reshape(line_count, layer_count * col_count)
    y_lower, y_upper = face_values(flat_jac, 0)
    lower, diagonal, upper = tridiagonal(y_lower, y_upper, 0)
    solved = cyclic_solve(lower, diagonal, upper, flat_rhs, 0).reshape(
        line_count, layer_count, col_count
    )
    return lax.all_to_all(solved, "wide", split_axis=0, concat_axis=2, tiled=True)


def on_device(field, conduct, mode_index, mode_amp, mode_phase, step_index):
    row_count, layer_count, col_total = field.shape
    wide_count = lax.axis_size("wide")
    row_total = row_count * wide_count
    layer_total = layer_count * lax.axis_size("grp")
    index_float = mode_index.astype(jnp.float32)
    all_index, all_amp, all_phase = (
        lax.all_gather(index_float, "grp", axis=0, tiled=True),
        lax.all_gather(mode_amp, "grp", axis=0, tiled=True),
        lax.all_gather(mode_phase, "grp", axis=0, tiled=True),
    )
    waves = all_index.astype(jnp.int32)
    layer_ids = lax.axis_index("grp") * layer_count + jnp.arange(layer_count, dtype=jnp.int32)
    zeta = (layer_ids.astype(jnp.float32) + 0.5) / layer_total
    first_row = lax.axis_index("wide") * row_count
    row_ids = jnp.clip(first_row - 1 + jnp.arange(row_count + 2, dtype=jnp.int32), 0, row_total - 1)
    height_rows = boundary_height(
        waves,
        all_amp,
        all_phase,
        step_index,
        row_ids,
        jnp.arange(col_total, dtype=jnp.int32),
        row_total,
        col_total,
    )
    jac_framed = 1.0 + zeta[None, :, None] * height_rows[:, None, :]
    jacobian = jac_framed[1:-1]
    across = conduct * jacobian
    x_lower, x_upper = face_values(across, 2)
    y_lower = 0.5 * (jacobian + jac_framed[:-2])
    y_upper = 0.5 * (jacobian + jac_framed[2:])
    framed = padded_2(field, (("wide", 0),), 1)
    along_y = y_upper * (framed[2:] - field) - y_lower * (field - framed[:-2])
    increment = time_step * (spread(field, x_lower, x_upper, 2) + along_y)
    lower, diagonal, upper = tridiagonal(x_lower, x_upper, 2)
    first = parallel_reduction(lower, diagonal, upper, increment)
    moved, moved_jac = (
        lax.all_to_all(first, "wide", split_axis=2, concat_axis=0, tiled=True),
        lax.all_to_all(jacobian, "wide", split_axis=2, concat_axis=0, tiled=True),
    )
    second = solve_columns(moved, moved_jac)
    return field + second


def solution(mesh):
    return jax.shard_map(
        on_device,
        mesh=mesh,
        in_specs=(
            P("wide", "grp", None),
            P("wide", "grp", None),
            P("grp", None),
            P("grp"),
            P("grp"),
            P(),
        ),
        out_specs=P("wide", "grp", None),
        check_vma=False,
    )
```

profile of v0, /device:TPU:0, one launch (start us, length us, event | category | flops | bytes accessed | tf_op | source)
XLA Modules:
  0.0 83.2 jit_solution(9836907236328708013)
XLA Ops:
  0.0 0.8 fusion.118
  0.8 1.3 %collective-permute-start = (f32[1,2,2048]{2,1,0:T(2,128)S(1)}, f32[1,2,2048]{2,1,0:T(2,128)S(1)}, u32[]{:S(2)}, u32[]{:S(2)}) collective-permute-start(f32[1,2,2048]{2,1,0:T(2,128)S(1)} %get-tuple-element.145), channel_id=1, source_target_pairs={{1,0},{2,1},{3,2},{4,3},{5,4},{6,5},{7,6},{9,8},{10,9},{11,10},{12... | collective-permute-start | bytes 49160 | tf_op jit(solution)/shard_map/ppermute | solution.py:19
  2.1 3.0 %collective-permute-start.1 = (f32[1,2,2048]{2,1,0:T(2,128)S(1)}, f32[1,2,2048]{2,1,0:T(2,128)S(1)}, u32[]{:S(2)}, u32[]{:S(2)}) collective-permute-start(f32[1,2,2048]{2,1,0:T(2,128)S(1)} %get-tuple-element.146), channel_id=1, source_target_pairs={{0,1},{1,2},{2,3},{3,4},{4,5},{5,6},{6,7},{8,9},{9,10},{10,11},{11... | collective-permute-start | bytes 49160 | tf_op jit(solution)/shard_map/ppermute | solution.py:16
  5.1 1.2 %fusion.117 = (f32[8,2,2047]{2,1,0:T(2,128)S(1)}, f32[8,2,2047]{2,1,0:T(2,128)S(1)}) fusion(f32[8,2,2048]{2,1,0:T(2,128)} %param.6), kind=kLoop, calls=%fused_computation.249 | loop fusion | bytes 524032 | tf_op jit(solution)/shard_map/slice | solution.py:77
  6.3 0.7 convert_bitcast_fusion
  7.0 12.6 %all-gather = f32[4,2,3]{2,1,0:T(2,128)S(1)} all-gather(f32[1,2,3]{2,1,0:T(2,128)S(1)} %convert_bitcast_fusion), channel_id=1, replica_groups=mesh['grp'=4,'wide'=8] {'grp'}, dimensions={0}, use_global_device_ids=true | all-gather | bytes 120 | tf_op jit(solution)/shard_map/all_gather | solution.py:191
  20.3 0.2 slice_reduce_fusion.1
  20.5 1.2 %dynamic-slice = u32[1]{0:T(128)} dynamic-slice(u32[32]{0:T(128)} %constant.344, u32[]{:T(128)S(6)} %add.638), dynamic_slice_sizes={1} | dynamic-slice | bytes 12
  22.4 0.9 %dynamic-update-slice.1 = f32[8]{0:T(128)S(1)} dynamic-update-slice(f32[8]{0:T(128)S(1)} %broadcast.340.clone, f32[2]{0:T(128)} %param.10, u32[]{:T(128)} %bitcast) | dynamic-update-slice | bytes 20
  23.2 0.8 %dynamic-update-slice = f32[8]{0:T(128)S(1)} dynamic-update-slice(f32[8]{0:T(128)S(1)} %broadcast.340.clone.1, f32[2]{0:T(128)} %param.9, u32[]{:T(128)} %bitcast) | dynamic-update-slice | bytes 20
  24.1 8.4 %all-reduce.119 = (f32[8]{0:T(128)S(1)}, f32[8]{0:T(128)S(1)}) all-reduce(f32[8]{0:T(128)S(1)} %dynamic-update-slice.1, f32[8]{0:T(128)S(1)} %dynamic-update-slice), channel_id=1, replica_groups=mesh['grp'=4,'wide'=8] {'grp'}, use_global_device_ids=true, to_apply=%add.118 | all-reduce | flops 16 | bytes 128
  32.5 0.6 fusion.15
  33.1 0.6 convolution_subtract_fusion
  33.7 1.0 %copy_multiply_fusion = f32[8,2,2048]{2,0,1:T(8,128)S(1)} fusion(f32[8,2,2048]{2,1,0:T(2,128)} %param.7, f32[10,2,2048]{2,0,1:T(8,128)S(1)} %multiply_add_fusion), kind=kLoop, calls=%fused_computation.28 | loop fusion | flops 32768 | bytes 393216 | tf_op jit(solution)/shard_map/mul | solution.py:212
  35.1 0.1 pad_maximum_fusion.1
  35.2 0.3 fusion.4
  35.6 0.1 slice_multiply_fusion.2
  35.8 0.1 pad_slice_fusion.1
  35.9 0.1 fusion.113
  36.0 0.2 multiply_add_fusion.20
  36.4 0.1 fusion.111
  36.5 0.2 multiply_add_fusion.19
  36.8 0.1 fusion.107
  36.9 0.1 fusion.108
  37.0 0.1 multiply_add_fusion.18
  37.3 0.2 multiply_add_fusion.17
  37.6 0.1 fusion.103
  37.7 0.1 fusion.104
  37.8 0.1 multiply_add_fusion.16
  38.0 0.2 multiply_add_fusion.15
  38.4 0.1 fusion.99
  38.5 0.1 fusion.100
  38.6 0.1 multiply_add_fusion.14
  38.8 0.2 multiply_add_fusion.13
  39.1 0.1 fusion.95
  39.2 0.1 fusion.96
  39.3 0.1 multiply_add_fusion.12
  39.6 0.2 multiply_add_fusion.11
  39.9 0.1 fusion.91
  40.0 0.1 fusion.92
  40.1 0.1 multiply_add_fusion.10
  40.4 0.2 multiply_add_fusion.9
  40.7 0.1 fusion.88
  40.8 0.1 multiply_add_fusion.8
  41.0 0.2 multiply_add_fusion.7
  41.3 0.1 multiply_add_fusion.5
  41.9 1.0 %copy.126 = f32[8,2,2048]{0,1,2:T(2,128)S(1)} copy(f32[8,2,2048]{2,0,1:T(8,128)S(1)} %add_divide_fusion) | data formatting | bytes 262144 | tf_op jit(solution)/shard_map/div | solution.py:169
  42.9 4.0 %reshape.67 = f32[8,1,4096]{2,1,0:T(1,128)} reshape(f32[2048,2,8]{2,1,0:T(2,128)S(1)} %bitcast.55) | data formatting | bytes 262144
  46.9 3.7 %all-to-all-start = ((f32[8,1,4096]{2,1,0:T(1,128)}), f32[8,1,4096]{2,1,0:T(1,128)S(1)}, u32[]{:S(2)}, u32[]{:S(2)}) async-start(f32[8,1,4096]{2,1,0:T(1,128)} %reshape.67), calls=%async_computation | async-start | bytes 262144 | tf_op jit(solution)/shard_map/all_to_all | solution.py:222
  50.7 1.0 %copy.128 = f32[8,2,2048]{0,1,2:T(2,128)S(1)} copy(f32[8,2,2048]{2,0,1:T(8,128)S(1)} %get-tuple-element.49) | data formatting | bytes 262144 | tf_op jit(solution)/shard_map/slice | solution.py:211
  51.7 4.0 %reshape.65 = f32[8,1,4096]{2,1,0:T(1,128)} reshape(f32[2048,2,8]{2,1,0:T(2,128)S(1)} %bitcast.56) | data formatting | bytes 262144
  55.7 0.5 all-to-all-done
  56.2 3.7 %all-to-all-start.1 = ((f32[8,1,4096]{2,1,0:T(1,128)}), f32[8,1,4096]{2,1,0:T(1,128)S(1)}, u32[]{:S(2)}, u32[]{:S(2)}) async-start(f32[8,1,4096]{2,1,0:T(1,128)} %reshape.65), calls=%async_computation.1 | async-start | bytes 262144 | tf_op jit(solution)/shard_map/all_to_all | solution.py:223
  59.9 0.5 broadcast.379
  60.4 1.0 %reduce.6 = f32[8,4096]{1,0:T(8,128)S(1)} reduce(f32[8,1,4096]{2,1,0:T(1,128)S(1)} %all-to-all-done, f32[]{:T(128)} %broadcast.379), dimensions={1}, to_apply=%all_to_all.35.reduce_sub_computation | reduce | bytes 262148 | tf_op jit(solution)/shard_map/all_to_all | solution.py:222
  61.3 3.2 %reshape.68 = f32[2048,2,8]{2,1,0:T(2,128)S(1)} reshape(f32[8,4096]{1,0:T(8,128)S(1)} %reduce.6) | data formatting | bytes 262144
  64.5 0.8 copy.144
  65.4 1.0 %reduce.7 = f32[8,4096]{1,0:T(8,128)S(1)} reduce(f32[8,1,4096]{2,1,0:T(1,128)S(1)} %all-to-all-done.1, f32[]{:T(128)} %broadcast.379), dimensions={1}, to_apply=%all_to_all.38.reduce_sub_computation | reduce | bytes 262148 | tf_op jit(solution)/shard_map/all_to_all | solution.py:223
  66.4 3.2 %reshape.66 = f32[2048,2,8]{2,1,0:T(2,128)S(1)} reshape(f32[8,4096]{1,0:T(8,128)S(1)} %reduce.7) | data formatting | bytes 262144
  69.5 0.8 copy.145
  72.5 0.1 copy.138
  72.6 0.2 reshape_reshape.3
  72.8 9.5 %all_to_all.48 = f32[64,2,256]{2,1,0:T(2,128)S(1)} all-to-all(f32[64,2,256]{2,1,0:T(2,128)S(1)} %reshape_reshape.3), channel_id=1, replica_groups=mesh['grp'=4,'wide'=8] {'wide'}, dimensions={0} | all-to-all | bytes 262144 | tf_op jit(solution)/shard_map/all_to_all | solution.py:181
  82.4 0.8 copy.141
  (148 shorter events, 4.1 us)
Async XLA Ops:
  0.0 35.1 %copy-start = (f32[8,2,2048]{2,1,0:T(2,128)S(1)}, f32[8,2,2048]{2,1,0:T(2,128)}, u32[]{:S(2)}) copy-start(f32[8,2,2048]{2,1,0:T(2,128)} %param.6) | copy-start | bytes 393220
  0.8 34.3 %collective-permute-start = (f32[1,2,2048]{2,1,0:T(2,128)S(1)}, f32[1,2,2048]{2,1,0:T(2,128)S(1)}, u32[]{:S(2)}, u32[]{:S(2)}) collective-permute-start(f32[1,2,2048]{2,1,0:T(2,128)S(1)} %get-tuple-element.145), channel_id=1, source_target_pairs={{1,0},{2,1},{3,2},{4,3},{5,4},{6,5},{7,6},{9,8},{10,9},{11,10},{12... | collective-permute-start | bytes 49160 | tf_op jit(solution)/shard_map/ppermute | solution.py:19
  2.1 33.0 %collective-permute-start.1 = (f32[1,2,2048]{2,1,0:T(2,128)S(1)}, f32[1,2,2048]{2,1,0:T(2,128)S(1)}, u32[]{:S(2)}, u32[]{:S(2)}) collective-permute-start(f32[1,2,2048]{2,1,0:T(2,128)S(1)} %get-tuple-element.146), channel_id=1, source_target_pairs={{0,1},{1,2},{2,3},{3,4},{4,5},{5,6},{6,7},{8,9},{9,10},{10,11},{11... | collective-permute-start | bytes 49160 | tf_op jit(solution)/shard_map/ppermute | solution.py:16
  46.9 9.3 %all-to-all-start = ((f32[8,1,4096]{2,1,0:T(1,128)}), f32[8,1,4096]{2,1,0:T(1,128)S(1)}, u32[]{:S(2)}, u32[]{:S(2)}) async-start(f32[8,1,4096]{2,1,0:T(1,128)} %reshape.67), calls=%async_computation | async-start | bytes 262144 | tf_op jit(solution)/shard_map/all_to_all | solution.py:222
  56.2 9.2 %all-to-all-start.1 = ((f32[8,1,4096]{2,1,0:T(1,128)}), f32[8,1,4096]{2,1,0:T(1,128)S(1)}, u32[]{:S(2)}, u32[]{:S(2)}) async-start(f32[8,1,4096]{2,1,0:T(1,128)} %reshape.65), calls=%async_computation.1 | async-start | bytes 262144 | tf_op jit(solution)/shard_map/all_to_all | solution.py:223
where the time goes:
time: 83.9 us; the launch traced here: 83.2 us
  blocking collectives  30.5 us (36%)
  local copies, waits for them, and re-layouts  28.9 us (34%)
  starting transfers between devices  11.7 us (14%)
  other arithmetic  7.96 us (9%)
  between operations  2.45 us (3%)
  matrix products  1.14 us (1%)
    unnamed x15, local copies, waits for them, and re-layouts  19.1 us
    all_gather x1, blocking collectives, on_device(): lax.all_gather(index_float, 'grp', axis=0, tiled=True)  12.6 us
    all_to_all x1, blocking collectives, solve_columns(): lax.all_to_all(solved, 'wide', split_axis=0, concat_axis=2, tiled=True)  9.53 us
    unnamed x1, blocking collectives  8.37 us
    all_to_all x1, starting transfers between devices, on_device(): lax.all_to_all(first, 'wide', split_axis=2, concat_axis=0, tiled=True)  3.72 us
    all_to_all x1, starting transfers between devices, on_device(): lax.all_to_all(jacobian, 'wide', split_axis=2, concat_axis=0, tiled=True)  3.68 us
    ppermute x1, starting transfers between devices, padded_2(): lax.ppermute(lax.slice_in_dim(block, block.shape[dim] - width, None, axis...  3.03 us
  transfers between devices with their start and end apart: 4, of which 1 were waited for; matrix products, arithmetic and copies ran while one was open for 22% of the time, Pallas kernels for 0%

commit v1 on v0

v1 whole, which is shorter than its diff:
```python
import functools
import math

import jax
import jax.numpy as jnp
from jax import lax
from jax.experimental import pallas as pl
from jax.experimental.pallas import tpu as pltpu
from jax.sharding import PartitionSpec as P

time_step = 600.0
implicit_weight = 0.5
weight = implicit_weight * time_step
LANES = 128
f32 = jnp.float32


def to_lines(block):
    rows, layers, columns = block.shape
    chunks = columns // LANES
    return (
        block.reshape(rows, layers, chunks, LANES)
        .transpose(0, 2, 1, 3)
        .reshape(rows * chunks * layers, LANES)
    )


def from_lines(lines, shape):
    rows, layers, columns = shape
    chunks = columns // LANES
    return (
        lines.reshape(rows, chunks, layers, LANES)
        .transpose(0, 2, 1, 3)
        .reshape(rows, layers, columns)
    )


def turns(wave, index, period):
    product = wave * index
    if period & (period - 1) == 0:
        product = product & (period - 1)
    else:
        product = lax.rem(product, jnp.int32(period))
    return product.astype(f32) * (1.0 / period)


def cos_sin(turn):
    part = turn - jnp.floor(turn + 0.5)
    square = part * part

    def series(first):
        terms = [
            (-1.0) ** n * math.pi ** (2 * n + first) / math.factorial(2 * n + first)
            for n in range(7)
        ]
        total = jnp.full_like(square, terms[-1])
        for term in terms[-2::-1]:
            total = total * square + term
        return total

    half_cos = series(0)
    half_sin = series(1) * part
    return 1.0 - 2.0 * half_sin * half_sin, 2.0 * half_sin * half_cos


def height_lines(modes, first_row, count, row_total, chunks, column_total):
    mode_count = modes.shape[0]
    wave_x = modes[:, 0:1].astype(jnp.int32)
    wave_y = modes[:, 1:2].astype(jnp.int32)
    offset = modes[:, 2:3]
    amp = modes[:, 3:4]
    spot = lax.broadcasted_iota(jnp.int32, (mode_count, count * chunks), 1)
    chunk = spot % chunks
    row = jnp.clip(first_row + spot // chunks, 0, row_total - 1)
    angle = (
        turns(wave_y, row, row_total) + turns(wave_x, chunk * LANES, column_total)
    ) + offset
    left_cos, left_sin = cos_sin(angle)
    lane = lax.broadcasted_iota(jnp.int32, (mode_count, LANES), 1)
    right_cos, right_sin = cos_sin(turns(wave_x, lane, column_total))
    left = jnp.concatenate([amp * left_cos, amp * left_sin], 0)
    right = jnp.concatenate([right_cos, -right_sin], 0)
    return lax.dot_general(
        left,
        right,
        (((0,), (0,)), ((), ())),
        precision=lax.Precision.HIGHEST,
        preferred_element_type=f32,
    )


def inverse(values):
    return pl.reciprocal(values, approx=False)


def from_left(values, stride, lane):
    moved = [pltpu.roll(v, stride, 1) for v in values]
    return [jnp.where(lane < stride, moved[c - 1], moved[c]) for c in range(len(values))]


def from_right(values, stride, lane):
    count = len(values)
    moved = [pltpu.roll(v, LANES - stride, 1) for v in values]
    return [
        jnp.where(lane >= LANES - stride, moved[(c + 1) % count], moved[c]) for c in range(count)
    ]


def solve_chunks(diagonal, link, rhs):
    count = len(rhs)
    if count == 1:
        return [rhs[0] * inverse(diagonal[0])]
    inv = {i: inverse(diagonal[i]) for i in range(0, count, 2)}
    scaled = {i: inv[i] * rhs[i] for i in inv}
    odd_diagonal, odd_link, odd_rhs = [], [], []
    for i in range(1, count, 2):
        d = diagonal[i] - link[i - 1] * (link[i - 1] * inv[i - 1])
        r = rhs[i] + link[i - 1] * scaled[i - 1]
        e = None
        if i + 1 < count:
            by = link[i] * inv[i + 1]
            d = d - link[i] * by
            r = r + link[i] * scaled[i + 1]
            e = by * link[i + 1] if i + 2 < count else None
        odd_diagonal.append(d)
        odd_rhs.append(r)
        odd_link.append(e)
    odd = solve_chunks(odd_diagonal, odd_link, odd_rhs)
    out = [None] * count
    out[1::2] = odd
    for i in range(0, count, 2):
        r = rhs[i]
        if i > 0:
            r = r + link[i - 1] * out[i - 1]
        if i + 1 < count:
            r = r + link[i] * out[i + 1]
        out[i] = r * inv[i]
    return out


def solve_x(diagonal, link, rhs, lane):
    stride = 1
    count = len(rhs)
    while stride < LANES:
        inv = [inverse(d) for d in diagonal]
        t = [q * r for q, r in zip(inv, rhs)]
        w = [q * e for q, e in zip(inv, link)]
        low_d = from_left([e * v for e, v in zip(link, w)], stride, lane)
        low_r = from_left([e * v for e, v in zip(link, t)], stride, lane)
        high_q = from_right(inv, stride, lane)
        high_t = from_right(t, stride, lane)
        high_w = from_right(w, stride, lane)
        diagonal = [
            diagonal[c] - low_d[c] - link[c] * (link[c] * high_q[c]) for c in range(count)
        ]
        rhs = [rhs[c] + low_r[c] + link[c] * high_t[c] for c in range(count)]
        link = [link[c] * high_w[c] for c in range(count)]
        stride *= 2
    return solve_chunks(diagonal, link, rhs)


def pack_kernel(index_ref, amp_ref, phase_ref, step_ref, out_ref):
    count = index_ref.shape[0]
    row = lax.broadcasted_iota(jnp.int32, out_ref.shape, 0)
    lane = lax.broadcasted_iota(jnp.int32, out_ref.shape, 1)
    total = jnp.zeros(out_ref.shape, f32)
    for m in range(count):
        moment = lax.rem(index_ref[m, 2] * step_ref[0], jnp.int32(64)).astype(f32)
        offset = phase_ref[m] * (0.5 / math.pi) + moment * (1.0 / 64.0)
        for place, value in enumerate(
            (index_ref[m, 0].astype(f32), index_ref[m, 1].astype(f32), offset, amp_ref[m])
        ):
            total = jnp.where((row == m) & (lane == place), value, total)
    out_ref[...] = total


def first_kernel(
    sizes, modes_ref, field_ref, low_ref, high_ref, conduct_ref,
    sent_ref, p_ref, u_ref, v_ref, framed, heights, solved,
):
    rows, layers, chunks, row_total, layer_total, column_total = sizes
    width = layers * chunks
    first_row = lax.axis_index("wide") * rows
    first_layer = lax.axis_index("grp") * layers
    zeta = [
        ((first_layer + k).astype(f32) + 0.5) * (1.0 / layer_total) for k in range(layers)
    ]
    framed[0:width] = low_ref[...]
    framed[width : (rows + 1) * width] = field_ref[...]
    framed[(rows + 1) * width : (rows + 2) * width] = high_ref[...]
    heights[...] = height_lines(
        modes_ref[...], first_row - 1, rows + 2, row_total, chunks, column_total
    )
    lane = lax.broadcasted_iota(jnp.int32, (rows, LANES), 1)
    at_start = lane == 0
    at_end = lane == LANES - 1
    half = 0.5 * weight

    for k in range(layers):
        g, f, along = [], [], []
        for c in range(chunks):
            jac_low, jac, jac_high = (
                1.0 + zeta[k] * heights[pl.ds(s * chunks + c, rows, stride=chunks), :]
                for s in range(3)
            )
            place = c * layers + k
            f_low, f_mid, f_high = (
                framed[pl.ds(s * width + place, rows, stride=width), :] for s in range(3)
            )
            g.append(conduct_ref[pl.ds(place, rows, stride=width), :] * jac)
            f.append(f_mid)
            along.append(
                half * (jac + jac_high) * (f_high - f_mid)
                - half * (jac + jac_low) * (f_mid - f_low)
            )
        g_next = from_right(g, 1, lane)
        f_next = from_right(f, 1, lane)
        g_next[-1] = jnp.where(at_end, g[-1], g_next[-1])
        f_next[-1] = jnp.where(at_end, 0.0, f_next[-1])
        face = [half * (a + b) for a, b in zip(g, g_next)]
        flux = [e * (b - a) for e, a, b in zip(face, f, f_next)]
        face_low = from_left(face, 1, lane)
        flux_low = from_left(flux, 1, lane)
        edge = weight * g[0]
        face_low[0] = jnp.where(at_start, edge, face_low[0])
        flux_low[0] = jnp.where(at_start, edge * f[0], flux_low[0])
        diagonal = [1.0 + (a + b) for a, b in zip(face, face_low)]
        rhs = [2.0 * (a - b + y) for a, b, y in zip(flux, flux_low, along)]
        link = face
        link[-1] = jnp.where(at_end, 0.0, link[-1])
        first = solve_x(diagonal, link, rhs, lane)
        for c in range(chunks):
            solved[pl.ds(k * chunks + c, rows, stride=width), :] = first[c]

    jac = [
        jnp.concatenate(
            [1.0 + zeta[k] * heights[j * chunks : (j + 1) * chunks] for k in range(layers)], 0
        )
        for j in range(rows + 2)
    ]
    face = [half * (jac[j] + jac[j + 1]) for j in range(rows + 1)]
    p, u, v = [], [], []
    for j in range(rows):
        r = solved[j * width : (j + 1) * width]
        d = 1.0 + (face[j] + face[j + 1])
        if j == 0:
            inv = inverse(d)
            p.append(r * inv)
            u.append(face[0] * inv)
        else:
            inv = inverse(d - face[j] * v[-1])
            scaled = face[j] * inv
            p.append(r * inv + scaled * p[-1])
            u.append(scaled * u[-1])
        v.append(face[j + 1] * inv)
    for j in range(rows - 2, -1, -1):
        p[j] = p[j] + v[j] * p[j + 1]
        u[j] = u[j] + v[j] * u[j + 1]
        v[j] = v[j] * v[j + 1]
    sent_ref[0:width] = p[0]
    sent_ref[width : 2 * width] = p[-1]
    for j in range(rows):
        p_ref[j * width : (j + 1) * width] = p[j]
        u_ref[j * width : (j + 1) * width] = u[j]
        v_ref[j * width : (j + 1) * width] = v[j]


def matrix_kernel(
    sizes, modes_ref, left_gain_ref, left_link_ref, right_gain_ref, right_link_ref, heights, ends
):
    rows, layers, chunks, row_total, layer_total, column_total = sizes
    width = layers * chunks
    blocks = row_total // rows
    first_layer = lax.axis_index("grp") * layers
    zeta = [
        ((first_layer + k).astype(f32) + 0.5) * (1.0 / layer_total) for k in range(layers)
    ]
    half = 0.5 * weight
    body = height_lines(modes_ref[...], 0, row_total, row_total, chunks, column_total)
    heights[chunks : (row_total + 1) * chunks] = body
    heights[0:chunks] = body[0:chunks]
    heights[(row_total + 1) * chunks : (row_total + 2) * chunks] = body[
        (row_total - 1) * chunks : row_total * chunks
    ]

    def condense(b):
        start = b * (rows * chunks)
        jac = []
        for j in range(rows + 2):
            h = heights[pl.ds(pl.multiple_of(start + j * chunks, 8), chunks), :]
            jac.append(jnp.concatenate([1.0 + z * h for z in zeta], 0))
        face = [half * (jac[j] + jac[j + 1]) for j in range(rows + 1)]
        u, v = [], []
        for j in range(rows):
            d = 1.0 + (face[j] + face[j + 1])
            if j == 0:
                inv = inverse(d)
                u.append(face[0] * inv)
            else:
                inv = inverse(d - face[j] * v[-1])
                u.append(face[j] * inv * u[-1])
            v.append(face[j + 1] * inv)
        u_last, v_last = u[-1], v[-1]
        u_first, v_first = u_last, v_last
        for j in range(rows - 2, -1, -1):
            u_first = u[j] + v[j] * u_first
            v_first = v[j] * v_first
        base = b * (4 * width)
        for n, value in enumerate((u_first, v_first, u_last, v_last)):
            ends[pl.ds(pl.multiple_of(base + n * width, 8), width), :] = value

    group = 4 if blocks % 4 == 0 else 1

    def several(step, carry):
        for n in range(group):
            condense(step * group + n)
        return carry

    lax.fori_loop(0, blocks // group, several, 0)

    def end(b, n):
        return ends[(4 * b + n) * width : (4 * b + n + 1) * width]

    left = jnp.zeros((width, LANES), f32)
    right = jnp.zeros((width, LANES), f32)
    for b in range(blocks):
        u_first, v_first, u_last, v_last = (end(b, n) for n in range(4))
        gain = u_last * inverse(1.0 - u_first * left)
        left_gain_ref[b * width : (b + 1) * width] = gain
        left_link_ref[b * width : (b + 1) * width] = left
        left = v_last + gain * left * v_first
        b = blocks - 1 - b
        u_first, v_first, u_last, v_last = (end(b, n) for n in range(4))
        gain = v_first * inverse(1.0 - v_last * right)
        right_gain_ref[b * width : (b + 1) * width] = gain
        right_link_ref[b * width : (b + 1) * width] = right
        right = u_first + gain * right * u_last


def last_kernel(
    sizes, all_ref, left_gain_ref, left_link_ref, right_gain_ref, right_link_ref,
    p_ref, u_ref, v_ref, field_ref, out_ref,
):
    rows, layers, chunks, row_total, layer_total, column_total = sizes
    width = layers * chunks
    blocks = row_total // rows
    me = lax.axis_index("wide")

    def part(ref, b):
        return ref[b * width : (b + 1) * width]

    left = jnp.zeros((width, LANES), f32)
    right = jnp.zeros((width, LANES), f32)
    for b in range(blocks - 1):
        first, last = part(all_ref, 2 * b), part(all_ref, 2 * b + 1)
        moved = last + part(left_gain_ref, b) * (left + part(left_link_ref, b) * first)
        left = jnp.where(b < me, moved, left)
        b = blocks - 1 - b
        first, last = part(all_ref, 2 * b), part(all_ref, 2 * b + 1)
        moved = first + part(right_gain_ref, b) * (right + part(right_link_ref, b) * last)
        right = jnp.where(b > me, moved, right)

    own = pl.ds(pl.multiple_of(me * width, 8), width)
    left_link, right_link = left_link_ref[own, :], right_link_ref[own, :]
    p_first, u_first, v_first = (part(ref, 0) for ref in (p_ref, u_ref, v_ref))
    p_last, u_last, v_last = (part(ref, rows - 1) for ref in (p_ref, u_ref, v_ref))
    a = 1.0 - left_link * u_first
    b = left_link * v_first
    c = right_link * u_last
    d = 1.0 - right_link * v_last
    y = left + left_link * p_first
    z = right + right_link * p_last
    inv = inverse(a * d - b * c)
    before = (d * y + b * z) * inv
    after = (c * y + a * z) * inv
    for j in range(rows):
        x = part(p_ref, j) + part(u_ref, j) * before + part(v_ref, j) * after
        for k in range(layers):
            spot = pl.ds(j * width + k, chunks, stride=layers)
            out_ref[spot, :] = field_ref[spot, :] + x[k * chunks : (k + 1) * chunks]


def on_device(field, conduct, mode_index, mode_amp, mode_phase, step_index):
    rows, layers, columns = field.shape
    wide_count = lax.axis_size("wide")
    row_total = rows * wide_count
    layer_total = layers * lax.axis_size("grp")
    chunks = columns // LANES
    width = layers * chunks
    sizes = (rows, layers, chunks, row_total, layer_total, columns)
    smem = pl.BlockSpec(memory_space=pltpu.SMEM)

    field_lines = to_lines(field)
    conduct_lines = to_lines(conduct)
    forward = [(i, i + 1) for i in range(wide_count - 1)]
    backward = [(target, source) for source, target in forward]
    low = lax.ppermute(field_lines[(rows - 1) * width :], "wide", forward)
    high = lax.ppermute(field_lines[:width], "wide", backward)

    packed = pl.pallas_call(
        pack_kernel,
        out_shape=jax.ShapeDtypeStruct((mode_index.shape[0], 8), f32),
        in_specs=[smem] * 4,
    )(mode_index, mode_amp, mode_phase, step_index)
    modes = lax.all_gather(packed, "grp", axis=0, tiled=True)

    def lines(count):
        return jax.ShapeDtypeStruct((count * width, LANES), f32)

    sent, p, u, v = pl.pallas_call(
        functools.partial(first_kernel, sizes),
        out_shape=(lines(2), lines(rows), lines(rows), lines(rows)),
        scratch_shapes=[
            pltpu.VMEM(((rows + 2) * width, LANES), f32),
            pltpu.VMEM(((rows + 2) * chunks, LANES), f32),
            pltpu.VMEM((rows * width, LANES), f32),
        ],
        compiler_params=pltpu.CompilerParams(vmem_limit_bytes=16 * 1024 * 1024),
    )(modes, field_lines, low, high, conduct_lines)

    gathered = lax.all_gather(sent, "wide", axis=0, tiled=True)

    scans = pl.pallas_call(
        functools.partial(matrix_kernel, sizes),
        out_shape=(lines(wide_count),) * 4,
        scratch_shapes=[
            pltpu.VMEM(((row_total + 2) * chunks, LANES), f32),
            pltpu.VMEM((4 * wide_count * width, LANES), f32),
        ],
        compiler_params=pltpu.CompilerParams(vmem_limit_bytes=16 * 1024 * 1024),
    )(modes)

    advanced = pl.pallas_call(
        functools.partial(last_kernel, sizes),
        out_shape=lines(rows),
        compiler_params=pltpu.CompilerParams(vmem_limit_bytes=16 * 1024 * 1024),
    )(gathered, *scans, p, u, v, field_lines)
    return from_lines(advanced, field.shape)


def solution(mesh):
    return jax.shard_map(
        on_device,
        mesh=mesh,
        in_specs=(
            P("wide", "grp", None),
            P("wide", "grp", None),
            P("grp", None),
            P("grp"),
            P("grp"),
            P(),
        ),
        out_specs=P("wide", "grp", None),
        check_vma=False,
    )
```

time: 83.9 us -> 39.1 us (0.47)
  local copies, waits for them, and re-layouts: 28.9 us -> 3.23 us
  starting transfers between devices: 11.7 us -> 3.64 us
  other arithmetic: 7.96 us -> 0 us
  Pallas kernels: 0 us -> 6.22 us
  blocking collectives: 30.5 us -> 24.9 us
  between operations: 2.45 us -> 0.72 us
  matrix products: 1.14 us -> 0 us
    unnamed x15 -> x8, local copies, waits for them, and re-layouts: 19.1 us -> 2.49 us
    all_gather x1 -> x2, blocking collectives: 12.6 us -> 24.9 us  [the longest x1 12.9 us: on_device(): gathered = lax.all_gather(sent, 'wide', axis=0, tiled=True)]
    all_to_all x1 -> x0, blocking collectives: 9.53 us -> none  [solve_columns(): lax.all_to_all(solved, 'wide', split_axis=0, concat_axis=2, tiled=True)]
    unnamed x1 -> x0, blocking collectives: 8.37 us -> none
    all_to_all x2 -> x0, starting transfers between devices: 7.4 us -> none  [the longest x1 3.72 us: on_device(): lax.all_to_all(first, 'wide', split_axis=2, concat_axis=0, tiled=True)]
    pallas_call x0 -> x4, Pallas kernels: none -> 6.22 us  [the longest x1 2.59 us: on_device(): pl.pallas_call(functools.partial(first_kernel, sizes), out_shape=(lines(2...]
    slice x110 -> x1, local copies, waits for them, and re-layouts: 6.94 us -> 0.74 us  [on_device(): high = lax.ppermute(field_lines[:width], 'wide', backward)]
    add x28 -> x0, other arithmetic: 3.26 us -> none  [the longest x9 1.63 us: parallel_reduction(): rhs = rhs + alpha * rhs_prev + gamma * rhs_next]
  transfers between devices with their start and end apart: 4 -> 2, of which waited for: 1 -> 0; matrix products, arithmetic and copies ran while one was open for 22% -> 0% of each run, Pallas kernels for 0% -> 7%
where the time goes in v1:
time: 39.1 us; the launch traced here: 38.7 us
  blocking collectives  24.9 us (64%)
  Pallas kernels  6.22 us (16%)
  starting transfers between devices  3.64 us (9%)
  local copies, waits for them, and re-layouts  3.23 us (8%)
  between operations  0.72 us (2%)
    all_gather x1, blocking collectives, on_device(): gathered = lax.all_gather(sent, 'wide', axis=0, tiled=True)  12.9 us
    all_gather x1, blocking collectives, on_device(): modes = lax.all_gather(packed, 'grp', axis=0, tiled=True)  12 us
    pallas_call x1, Pallas kernels, on_device(): pl.pallas_call(functools.partial(first_kernel, sizes), out_shape=(lines(2...  2.59 us
    unnamed x8, local copies, waits for them, and re-layouts  2.49 us
    ppermute x1, starting transfers between devices, on_device(): low = lax.ppermute(field_lines[(rows - 1) * width:], 'wide', forward)  2.35 us
    pallas_call x1, Pallas kernels, on_device(): pl.pallas_call(functools.partial(matrix_kernel, sizes), out_shape=(lines(...  1.58 us
    ppermute x1, starting transfers between devices, on_device(): high = lax.ppermute(field_lines[:width], 'wide', backward)  1.29 us
    pallas_call x1, Pallas kernels, on_device(): pl.pallas_call(pack_kernel, out_shape=jax.ShapeDtypeStruct((mode_index.sh...  1.28 us
  transfers between devices with their start and end apart: 2, of which 0 were waited for; matrix products, arithmetic and copies ran while one was open for 0% of the time, Pallas kernels for 7%

profile of v1, /device:TPU:0, one launch (start us, length us, event | category | flops | bytes accessed | tf_op | source)
XLA Modules:
  0.0 38.7 jit_solution(6194707977860419889)
XLA Ops:
  0.0 0.7 %fusion = (f32[1,16,2,128]{3,2,1,0:T(2,128)S(1)}, f32[1,16,2,128]{3,2,1,0:T(2,128)S(1)}) fusion(f32[8,16,2,128]{3,2,1,0:T(2,128)} %bitcast.19), kind=kLoop, calls=%fused_computation | loop fusion | bytes 65536 | tf_op jit(solution)/shard_map/slice | solution.py:398
  0.7 2.3 %collective-permute-start = (f32[32,128]{1,0:T(8,128)S(1)}, f32[32,128]{1,0:T(8,128)S(1)}, u32[]{:S(2)}, u32[]{:S(2)}) collective-permute-start(f32[32,128]{1,0:T(8,128)S(1)} %bitcast.26), channel_id=1, source_target_pairs={{0,1},{1,2},{2,3},{3,4},{4,5},{5,6},{6,7},{8,9},{9,10},{10,11},{11... | collective-permute-start | bytes 49160 | tf_op jit(solution)/shard_map/ppermute | solution.py:397
  3.1 1.3 %collective-permute-start.1 = (f32[32,128]{1,0:T(8,128)S(1)}, f32[32,128]{1,0:T(8,128)S(1)}, u32[]{:S(2)}, u32[]{:S(2)}) collective-permute-start(f32[32,128]{1,0:T(8,128)S(1)} %bitcast.25), channel_id=1, source_target_pairs={{1,0},{2,1},{3,2},{4,3},{5,4},{6,5},{7,6},{9,8},{10,9},{11,10},{12... | collective-permute-start | bytes 49160 | tf_op jit(solution)/shard_map/ppermute | solution.py:398
  5.0 1.3 %shard_map.64 = f32[2,8]{1,0:T(2,128)} custom-call(s32[2,3]{1,0:T(2,128)} %index_ref.1, f32[2]{0:T(128)} %amp_ref.1, f32[2]{0:T(128)} %phase_ref.1, s32[1]{0:T(128)S(6)} %copy.13.step_ref), custom_call_target="tpu_custom_call" | custom-call | tf_op jit(solution)/shard_map/pallas_call | solution.py:400
  6.3 0.0 copy-start.3
  6.3 0.7 %copy-done.3 = f32[2,8]{1,0:T(2,128)S(1)} copy-done((f32[2,8]{1,0:T(2,128)S(1)}, f32[2,8]{1,0:T(2,128)}, u32[]{:S(2)}) %copy-start.3) | copy-done | bytes 88
  7.0 12.0 %all-gather = f32[4,2,8]{2,1,0:T(2,128)S(1)} all-gather(f32[1,2,8]{2,1,0:T(2,128)S(1)} %bitcast.27), channel_id=1, replica_groups=mesh['grp'=4,'wide'=8] {'grp'}, dimensions={0}, use_global_device_ids=true | all-gather | bytes 320 | tf_op jit(solution)/shard_map/all_gather | solution.py:405
  19.0 1.6 %shard_map.66 = (f32[256,128]{1,0:T(8,128)S(1)}, f32[256,128]{1,0:T(8,128)S(1)}, f32[256,128]{1,0:T(8,128)S(1)}, f32[256,128]{1,0:T(8,128)S(1)}) custom-call(f32[8,8]{1,0:T(8,128)S(1)} %bitcast.23), custom_call_target="tpu_custom_call" | custom-call | tf_op jit(solution)/shard_map/pallas_call | solution.py:423
  20.6 0.0 collective-permute-done.low_ref
  20.6 0.0 collective-permute-done.1.high_ref
  20.6 0.0 copy-start
  20.6 0.9 %copy-done = f32[8,2,2048]{2,1,0:T(2,128)S(1)} copy-done((f32[8,2,2048]{2,1,0:T(2,128)S(1)}, f32[8,2,2048]{2,1,0:T(2,128)}, u32[]{:S(2)}) %copy-start) | copy-done | bytes 131096
  21.5 0.0 copy-start.2
  21.5 0.9 %copy-done.2 = f32[8,2,2048]{2,1,0:T(2,128)S(1)} copy-done((f32[8,2,2048]{2,1,0:T(2,128)S(1)}, f32[8,2,2048]{2,1,0:T(2,128)}, u32[]{:S(2)}) %copy-start.2) | copy-done | bytes 131096
  22.4 2.6 %shard_map.65 = (f32[64,128]{1,0:T(8,128)S(1)}, f32[256,128]{1,0:T(8,128)S(1)}, f32[256,128]{1,0:T(8,128)S(1)}, f32[256,128]{1,0:T(8,128)S(1)}) custom-call(f32[8,8]{1,0:T(8,128)S(1)} %bitcast.24, f32[256,128]{1,0:T(8,128)S(1)} %bitcast.20, f32[32,128]{1,0:T(8,128)S(1)} %collective-permute-done.low_ref, f32[32,128]{1,0:T(8,128)S(1)} %collective-permute-done.1.high_ref, ...), custom_call_target="tpu_custom_call" | custom-call | tf_op jit(solution)/shard_map/pallas_call | solution.py:410
  25.0 0.0 copy-start.1
  25.0 12.9 %all_gather.7.all_ref = f32[512,128]{1,0:T(8,128)S(1)} all-gather(f32[64,128]{1,0:T(8,128)S(1)} %get-tuple-element.13), channel_id=1, replica_groups=mesh['grp'=4,'wide'=8] {'wide'}, dimensions={0}, use_global_device_ids=true | all-gather | bytes 294912 | tf_op jit(solution)/shard_map/all_gather | solution.py:421
  37.9 0.0 copy-done.1
  37.9 0.8 %shard_map.67 = f32[256,128]{1,0:T(8,128)} custom-call(f32[512,128]{1,0:T(8,128)S(1)} %all_gather.7.all_ref, f32[256,128]{1,0:T(8,128)S(1)} %get-tuple-element.14.left_gain_ref, f32[256,128]{1,0:T(8,128)S(1)} %get-tuple-element.15.left_link_ref, f32[256,128]{1,0:T(8,128)S(1)} %get-tuple-element.16.right_gain_ref, ...), custom_call_target="tpu_custom_call" | custom-call | tf_op jit(solution)/shard_map/pallas_call | solution.py:433
Async XLA Ops:
  0.7 19.8 %collective-permute-start = (f32[32,128]{1,0:T(8,128)S(1)}, f32[32,128]{1,0:T(8,128)S(1)}, u32[]{:S(2)}, u32[]{:S(2)}) collective-permute-start(f32[32,128]{1,0:T(8,128)S(1)} %bitcast.26), channel_id=1, source_target_pairs={{0,1},{1,2},{2,3},{3,4},{4,5},{5,6},{6,7},{8,9},{9,10},{10,11},{11... | collective-permute-start | bytes 49160 | tf_op jit(solution)/shard_map/ppermute | solution.py:397
  3.1 17.5 %collective-permute-start.1 = (f32[32,128]{1,0:T(8,128)S(1)}, f32[32,128]{1,0:T(8,128)S(1)}, u32[]{:S(2)}, u32[]{:S(2)}) collective-permute-start(f32[32,128]{1,0:T(8,128)S(1)} %bitcast.25), channel_id=1, source_target_pairs={{1,0},{2,1},{3,2},{4,3},{5,4},{6,5},{7,6},{9,8},{10,9},{11,10},{12... | collective-permute-start | bytes 49160 | tf_op jit(solution)/shard_map/ppermute | solution.py:398
  6.3 0.7 %copy-start.3 = (f32[2,8]{1,0:T(2,128)S(1)}, f32[2,8]{1,0:T(2,128)}, u32[]{:S(2)}) copy-start(f32[2,8]{1,0:T(2,128)} %shard_map.64) | copy-start | bytes 196
  20.6 0.9 %copy-start = (f32[8,2,2048]{2,1,0:T(2,128)S(1)}, f32[8,2,2048]{2,1,0:T(2,128)}, u32[]{:S(2)}) copy-start(f32[8,2,2048]{2,1,0:T(2,128)} %param.6) | copy-start | bytes 393220
  21.5 0.9 %copy-start.2 = (f32[8,2,2048]{2,1,0:T(2,128)S(1)}, f32[8,2,2048]{2,1,0:T(2,128)}, u32[]{:S(2)}) copy-start(f32[8,2,2048]{2,1,0:T(2,128)} %param.7) | copy-start | bytes 393220
  25.0 12.9 %copy-start.1 = (f32[8,2,2048]{2,1,0:T(2,128)S(1)}, f32[8,2,2048]{2,1,0:T(2,128)}, u32[]{:S(2)}) copy-start(f32[8,2,2048]{2,1,0:T(2,128)} %param.6) | copy-start | bytes 393220

commit v2 on v1

--- a/solution.py
+++ b/solution.py
@@ -159,48 +159,134 @@
     return solve_chunks(diagonal, link, rhs)
 
 
-def pack_kernel(index_ref, amp_ref, phase_ref, step_ref, out_ref):
-    count = index_ref.shape[0]
-    row = lax.broadcasted_iota(jnp.int32, out_ref.shape, 0)
-    lane = lax.broadcasted_iota(jnp.int32, out_ref.shape, 1)
-    total = jnp.zeros(out_ref.shape, f32)
+def load_kernel(
+    index_ref, amp_ref, phase_ref, step_ref, field_ref, conduct_ref,
+    packed_ref, field_out, conduct_out, top_ref, bottom_ref,
+    index_in, amp_in, phase_in, step_in, sems,
+):
+    width = top_ref.shape[0]
+    size = field_ref.shape[0]
+    pairs = (
+        (index_ref, index_in),
+        (amp_ref, amp_in),
+        (phase_ref, phase_in),
+        (step_ref, step_in),
+        (field_ref.at[pl.ds(0, width)], top_ref),
+        (field_ref.at[pl.ds(size - width, width)], bottom_ref),
+        (field_ref, field_out),
+        (conduct_ref, conduct_out),
+    )
+    copies = [pltpu.make_async_copy(a, b, sems.at[n]) for n, (a, b) in enumerate(pairs)]
+    for copy in copies:
+        copy.start()
+    for copy in copies[:4]:
+        copy.wait()
+    count = index_in.shape[0]
+    row = lax.broadcasted_iota(jnp.int32, packed_ref.shape, 0)
+    lane = lax.broadcasted_iota(jnp.int32, packed_ref.shape, 1)
+    total = jnp.zeros(packed_ref.shape, f32)
     for m in range(count):
-        moment = lax.rem(index_ref[m, 2] * step_ref[0], jnp.int32(64)).astype(f32)
-        offset = phase_ref[m] * (0.5 / math.pi) + moment * (1.0 / 64.0)
+        moment = lax.rem(index_in[m, 2] * step_in[0], jnp.int32(64)).astype(f32)
+        offset = phase_in[m] * (0.5 / math.pi) + moment * (1.0 / 64.0)
         for place, value in enumerate(
-            (index_ref[m, 0].astype(f32), index_ref[m, 1].astype(f32), offset, amp_ref[m])
+            (index_in[m, 0].astype(f32), index_in[m, 1].astype(f32), offset, amp_in[m])
         ):
             total = jnp.where((row == m) & (lane == place), value, total)
-    out_ref[...] = total
-
-
-def first_kernel(
+    packed_ref[...] = total
+    for copy in copies[4:]:
+        copy.wait()
+
+
+def condense(face):
+    u, v = [], []
+    rows = len(face) - 1
+    for j in range(rows):
+        d = 1.0 + (face[j] + face[j + 1])
+        if j == 0:
+            inv = inverse(d)
+            u.append(face[0] * inv)
+        else:
+            inv = inverse(d - face[j] * v[-1])
+            u.append(face[j] * inv * u[-1])
+        v.append(face[j + 1] * inv)
+    u_first, v_first = u[-1], v[-1]
+    for j in range(rows - 2, -1, -1):
+        u_first = u[j] + v[j] * u_first
+        v_first = v[j] * v_first
+    return u_first, v_first, u[-1], v[-1]
+
+
+def main_kernel(
     sizes, modes_ref, field_ref, low_ref, high_ref, conduct_ref,
-    sent_ref, p_ref, u_ref, v_ref, framed, heights, solved,
+    sent_ref, p_ref, u_ref, v_ref, left_gain_ref, left_link_ref, right_gain_ref, right_link_ref,
+    framed, heights, solved, ends,
 ):
     rows, layers, chunks, row_total, layer_total, column_total = sizes
     width = layers * chunks
-    first_row = lax.axis_index("wide") * rows
+    blocks = row_total // rows
+    me = lax.axis_index("wide")
     first_layer = lax.axis_index("grp") * layers
     zeta = [
         ((first_layer + k).astype(f32) + 0.5) * (1.0 / layer_total) for k in range(layers)
     ]
+    half = 0.5 * weight
     framed[0:width] = low_ref[...]
     framed[width : (rows + 1) * width] = field_ref[...]
     framed[(rows + 1) * width : (rows + 2) * width] = high_ref[...]
-    heights[...] = height_lines(
-        modes_ref[...], first_row - 1, rows + 2, row_total, chunks, column_total
-    )
+    body = height_lines(modes_ref[...], 0, row_total, row_total, chunks, column_total)
+    heights[chunks : (row_total + 1) * chunks] = body
+    heights[0:chunks] = body[0:chunks]
+    heights[(row_total + 1) * chunks : (row_total + 2) * chunks] = body[
+        (row_total - 1) * chunks : row_total * chunks
+    ]
     lane = lax.broadcasted_iota(jnp.int32, (rows, LANES), 1)
     at_start = lane == 0
     at_end = lane == LANES - 1
-    half = 0.5 * weight
-
+
+    def faces(start):
+        jac = []
+        for j in range(rows + 2):
+            h = heights[pl.ds(start + j * chunks, chunks), :]
+            jac.append(jnp.concatenate([1.0 + z * h for z in zeta], 0))
+        return [half * (jac[j] + jac[j + 1]) for j in range(rows + 1)]
+
+    def block_ends(b):
+        start, base = b * (rows * chunks), b * (4 * width)
+        if not isinstance(b, int):
+            start, base = pl.multiple_of(start, 8), pl.multiple_of(base, 8)
+        for n, value in enumerate(condense(faces(start))):
+            ends[pl.ds(base + n * width, width), :] = value
+
+    if blocks <= 8:
+        for b in range(blocks):
+            block_ends(b)
+    else:
+        lax.fori_loop(0, blocks, lambda b, carry: (block_ends(b), carry)[1], 0)
+
+    def end(b, n):
+        return ends[(4 * b + n) * width : (4 * b + n + 1) * width]
+
+    left = jnp.zeros((width, LANES), f32)
+    right = jnp.zeros((width, LANES), f32)
+    for b in range(blocks):
+        u_first, v_first, u_last, v_last = (end(b, n) for n in range(4))
+        gain = u_last * inverse(1.0 - u_first * left)
+        left_gain_ref[b * width : (b + 1) * width] = gain
+        left_link_ref[b * width : (b + 1) * width] = left
+        left = v_last + gain * left * v_first
+        b = blocks - 1 - b
+        u_first, v_first, u_last, v_last = (end(b, n) for n in range(4))
+        gain = v_first * inverse(1.0 - v_last * right)
+        right_gain_ref[b * width : (b + 1) * width] = gain
+        right_link_ref[b * width : (b + 1) * width] = right
+        right = u_first + gain * right * u_last
+
+    own_heights = pl.multiple_of(me * (rows * chunks), 8)
     for k in range(layers):
         g, f, along = [], [], []
         for c in range(chunks):
             jac_low, jac, jac_high = (
-                1.0 + zeta[k] * heights[pl.ds(s * chunks + c, rows, stride=chunks), :]
+                1.0 + zeta[k] * heights[pl.ds(own_heights + s * chunks + c, rows, stride=chunks), :]
                 for s in range(3)
             )
             place = c * layers + k
@@ -232,13 +318,7 @@
         for c in range(chunks):
             solved[pl.ds(k * chunks + c, rows, stride=width), :] = first[c]
 
-    jac = [
-        jnp.concatenate(
-            [1.0 + zeta[k] * heights[j * chunks : (j + 1) * chunks] for k in range(layers)], 0
-        )
-        for j in range(rows + 2)
-    ]
-    face = [half * (jac[j] + jac[j + 1]) for j in range(rows + 1)]
+    face = faces(own_heights)
     p, u, v = [], [], []
     for j in range(rows):
         r = solved[j * width : (j + 1) * width]
@@ -257,88 +337,20 @@
         p[j] = p[j] + v[j] * p[j + 1]
         u[j] = u[j] + v[j] * u[j + 1]
         v[j] = v[j] * v[j + 1]
-    sent_ref[0:width] = p[0]
-    sent_ref[width : 2 * width] = p[-1]
     for j in range(rows):
         p_ref[j * width : (j + 1) * width] = p[j]
         u_ref[j * width : (j + 1) * width] = u[j]
         v_ref[j * width : (j + 1) * width] = v[j]
 
-
-def matrix_kernel(
-    sizes, modes_ref, left_gain_ref, left_link_ref, right_gain_ref, right_link_ref, heights, ends
-):
-    rows, layers, chunks, row_total, layer_total, column_total = sizes
-    width = layers * chunks
-    blocks = row_total // rows
-    first_layer = lax.axis_index("grp") * layers
-    zeta = [
-        ((first_layer + k).astype(f32) + 0.5) * (1.0 / layer_total) for k in range(layers)
-    ]
-    half = 0.5 * weight
-    body = height_lines(modes_ref[...], 0, row_total, row_total, chunks, column_total)
-    heights[chunks : (row_total + 1) * chunks] = body
-    heights[0:chunks] = body[0:chunks]
-    heights[(row_total + 1) * chunks : (row_total + 2) * chunks] = body[
-        (row_total - 1) * chunks : row_total * chunks
-    ]
-
-    def condense(b):
-        start = b * (rows * chunks)
-        jac = []
-        for j in range(rows + 2):
-            h = heights[pl.ds(pl.multiple_of(start + j * chunks, 8), chunks), :]
-            jac.append(jnp.concatenate([1.0 + z * h for z in zeta], 0))
-        face = [half * (jac[j] + jac[j + 1]) for j in range(rows + 1)]
-        u, v = [], []
-        for j in range(rows):
-            d = 1.0 + (face[j] + face[j + 1])
-            if j == 0:
-                inv = inverse(d)
-                u.append(face[0] * inv)
-            else:
-                inv = inverse(d - face[j] * v[-1])
-                u.append(face[j] * inv * u[-1])
-            v.append(face[j + 1] * inv)
-        u_last, v_last = u[-1], v[-1]
-        u_first, v_first = u_last, v_last
-        for j in range(rows - 2, -1, -1):
-            u_first = u[j] + v[j] * u_first
-            v_first = v[j] * v_first
-        base = b * (4 * width)
-        for n, value in enumerate((u_first, v_first, u_last, v_last)):
-            ends[pl.ds(pl.multiple_of(base + n * width, 8), width), :] = value
-
-    group = 4 if blocks % 4 == 0 else 1
-
-    def several(step, carry):
-        for n in range(group):
-            condense(step * group + n)
-        return carry
-
-    lax.fori_loop(0, blocks // group, several, 0)
-
-    def end(b, n):
-        return ends[(4 * b + n) * width : (4 * b + n + 1) * width]
-
-    left = jnp.zeros((width, LANES), f32)
-    right = jnp.zeros((width, LANES), f32)
+    own = pl.ds(pl.multiple_of(me * width, 8), width)
+    upward = p[-1] + left_gain_ref[own, :] * (left_link_ref[own, :] * p[0])
+    downward = p[0] + right_gain_ref[own, :] * (right_link_ref[own, :] * p[-1])
     for b in range(blocks):
-        u_first, v_first, u_last, v_last = (end(b, n) for n in range(4))
-        gain = u_last * inverse(1.0 - u_first * left)
-        left_gain_ref[b * width : (b + 1) * width] = gain
-        left_link_ref[b * width : (b + 1) * width] = left
-        left = v_last + gain * left * v_first
-        b = blocks - 1 - b
-        u_first, v_first, u_last, v_last = (end(b, n) for n in range(4))
-        gain = v_first * inverse(1.0 - v_last * right)
-        right_gain_ref[b * width : (b + 1) * width] = gain
-        right_link_ref[b * width : (b + 1) * width] = right
-        right = u_first + gain * right * u_last
+        sent_ref[b * width : (b + 1) * width] = jnp.where(b > me, upward, downward)
 
 
 def last_kernel(
-    sizes, all_ref, left_gain_ref, left_link_ref, right_gain_ref, right_link_ref,
+    sizes, came_ref, left_gain_ref, left_link_ref, right_gain_ref, right_link_ref,
     p_ref, u_ref, v_ref, field_ref, out_ref,
 ):
     rows, layers, chunks, row_total, layer_total, column_total = sizes
@@ -352,13 +364,9 @@
     left = jnp.zeros((width, LANES), f32)
     right = jnp.zeros((width, LANES), f32)
     for b in range(blocks - 1):
-        first, last = part(all_ref, 2 * b), part(all_ref, 2 * b + 1)
-        moved = last + part(left_gain_ref, b) * (left + part(left_link_ref, b) * first)
-        left = jnp.where(b < me, moved, left)
+        left = jnp.where(b < me, part(came_ref, b) + part(left_gain_ref, b) * left, left)
         b = blocks - 1 - b
-        first, last = part(all_ref, 2 * b), part(all_ref, 2 * b + 1)
-        moved = first + part(right_gain_ref, b) * (right + part(right_link_ref, b) * last)
-        right = jnp.where(b > me, moved, right)
+        right = jnp.where(b > me, part(came_ref, b) + part(right_gain_ref, b) * right, right)
 
     own = pl.ds(pl.multiple_of(me * width, 8), width)
     left_link, right_link = left_link_ref[own, :], right_link_ref[own, :]
@@ -388,53 +396,59 @@
     chunks = columns // LANES
     width = layers * chunks
     sizes = (rows, layers, chunks, row_total, layer_total, columns)
-    smem = pl.BlockSpec(memory_space=pltpu.SMEM)
-
-    field_lines = to_lines(field)
-    conduct_lines = to_lines(conduct)
+    limit = pltpu.CompilerParams(vmem_limit_bytes=16 * 1024 * 1024)
+    anywhere = pl.BlockSpec(memory_space=pl.ANY)
+
+    def lines(count):
+        return jax.ShapeDtypeStruct((count * width, LANES), f32)
+
+    packed, field_lines, conduct_lines, top, bottom = pl.pallas_call(
+        load_kernel,
+        out_shape=(
+            jax.ShapeDtypeStruct((mode_index.shape[0], 8), f32),
+            lines(rows),
+            lines(rows),
+            lines(1),
+            lines(1),
+        ),
+        in_specs=[anywhere] * 6,
+        scratch_shapes=[
+            pltpu.SMEM(mode_index.shape, jnp.int32),
+            pltpu.SMEM(mode_amp.shape, f32),
+            pltpu.SMEM(mode_phase.shape, f32),
+            pltpu.SMEM(step_index.shape, jnp.int32),
+            pltpu.SemaphoreType.DMA((8,)),
+        ],
+        compiler_params=limit,
+    )(mode_index, mode_amp, mode_phase, step_index, to_lines(field), to_lines(conduct))
+
     forward = [(i, i + 1) for i in range(wide_count - 1)]
     backward = [(target, source) for source, target in forward]
-    low = lax.ppermute(field_lines[(rows - 1) * width :], "wide", forward)
-    high = lax.ppermute(field_lines[:width], "wide", backward)
-
-    packed = pl.pallas_call(
-        pack_kernel,
-        out_shape=jax.ShapeDtypeStruct((mode_index.shape[0], 8), f32),
-        in_specs=[smem] * 4,
-    )(mode_index, mode_amp, mode_phase, step_index)
+    low = lax.ppermute(bottom, "wide", forward)
+    high = lax.ppermute(top, "wide", backward)
     modes = lax.all_gather(packed, "grp", axis=0, tiled=True)
 
-    def lines(count):
-        return jax.ShapeDtypeStruct((count * width, LANES), f32)
-
-    sent, p, u, v = pl.pallas_call(
-        functools.partial(first_kernel, sizes),
-        out_shape=(lines(2), lines(rows), lines(rows), lines(rows)),
+    sent, p, u, v, *scans = pl.pallas_call(
+        functools.partial(main_kernel, sizes),
+        out_shape=(lines(wide_count),) + (lines(rows),) * 3 + (lines(wide_count),) * 4,
         scratch_shapes=[
             pltpu.VMEM(((rows + 2) * width, LANES), f32),
-            pltpu.VMEM(((rows + 2) * chunks, LANES), f32),
+            pltpu.VMEM(((row_total + 2) * chunks, LANES), f32),
             pltpu.VMEM((rows * width, LANES), f32),
-        ],
-        compiler_params=pltpu.CompilerParams(vmem_limit_bytes=16 * 1024 * 1024),
-    )(modes, field_lines, low, high, conduct_lines)
-
-    gathered = lax.all_gather(sent, "wide", axis=0, tiled=True)
-
-    scans = pl.pallas_call(
-        functools.partial(matrix_kernel, sizes),
-        out_shape=(lines(wide_count),) * 4,
-        scratch_shapes=[
-            pltpu.VMEM(((row_total + 2) * chunks, LANES), f32),
             pltpu.VMEM((4 * wide_count * width, LANES), f32),
         ],
-        compiler_params=pltpu.CompilerParams(vmem_limit_bytes=16 * 1024 * 1024),
-    )(modes)
+        compiler_params=limit,
+    )(modes, field_lines, low, high, conduct_lines)
+
+    came = lax.all_to_all(
+        sent.reshape(wide_count, width, LANES), "wide", split_axis=0, concat_axis=0
+    ).reshape(wide_count * width, LANES)
 
     advanced = pl.pallas_call(
         functools.partial(last_kernel, sizes),
         out_shape=lines(rows),
-        compiler_params=pltpu.CompilerParams(vmem_limit_bytes=16 * 1024 * 1024),
-    )(gathered, *scans, p, u, v, field_lines)
+        compiler_params=limit,
+    )(came, *scans, p, u, v, field_lines)
     return from_lines(advanced, field.shape)
 
 

time: 39.1 us -> 35.1 us (0.90)
  Pallas kernels: 6.22 us -> 4.45 us
  blocking collectives: 24.9 us -> 23.6 us
  local copies, waits for them, and re-layouts: 3.23 us -> 2.48 us
    all_gather x1 -> x0, blocking collectives: 12.9 us -> none  [on_device(): gathered = lax.all_gather(sent, 'wide', axis=0, tiled=True)]
    all_to_all x0 -> x1, blocking collectives: none -> 11.6 us  [on_device(): lax.all_to_all(sent.reshape(wide_count, width, LANES), 'wide', split_axis...]
    pallas_call x3 -> x2, Pallas kernels: 5.45 us -> 3.72 us  [the longest x1 3.05 us: on_device(): pl.pallas_call(functools.partial(main_kernel, sizes), out_shape=(lines(wi...]
    slice x1 -> x0, local copies, waits for them, and re-layouts: 0.74 us -> none  [on_device(): high = lax.ppermute(field_lines[:width], 'wide', backward)]
    unnamed x8 -> x10, local copies, waits for them, and re-layouts: 2.49 us -> 2.48 us
  transfers between devices with their start and end apart: 2 -> 2, of which waited for: 0 -> 0; matrix products, arithmetic and copies ran while one was open for 0% -> 0% of each run, Pallas kernels for 7% -> 0%
where the time goes in v2:
time: 35.1 us; the launch traced here: 34.9 us
  blocking collectives  23.6 us (67%)
  Pallas kernels  4.45 us (13%)
  starting transfers between devices  3.65 us (10%)
  local copies, waits for them, and re-layouts  2.48 us (7%)
  between operations  0.71 us (2%)
    all_gather x1, blocking collectives, on_device(): modes = lax.all_gather(packed, 'grp', axis=0, tiled=True)  12 us
    all_to_all x1, blocking collectives, on_device(): lax.all_to_all(sent.reshape(wide_count, width, LANES), 'wide', split_axis...  11.6 us
    pallas_call x1, Pallas kernels, on_device(): pl.pallas_call(functools.partial(main_kernel, sizes), out_shape=(lines(wi...  3.05 us
    unnamed x10, local copies, waits for them, and re-layouts  2.48 us
    ppermute x1, starting transfers between devices, on_device(): low = lax.ppermute(bottom, 'wide', forward)  2.36 us
    ppermute x1, starting transfers between devices, on_device(): high = lax.ppermute(top, 'wide', backward)  1.29 us
    pallas_call x1, Pallas kernels, on_device(): pl.pallas_call(functools.partial(last_kernel, sizes), out_shape=lines(row...  0.73 us
  transfers between devices with their start and end apart: 2, of which 0 were waited for; matrix products, arithmetic and copies ran while one was open for 0% of the time, Pallas kernels for 0%

profile of v2, /device:TPU:0, one launch (start us, length us, event | category | flops | bytes accessed | tf_op | source)
XLA Modules:
  0.0 34.9 jit_solution(774542557445493689)
XLA Ops:
  0.7 0.0 copy-start.4
  0.7 0.0 copy-start.2
  0.7 0.0 copy-start.3
  0.7 0.6 %copy-done.4 = f32[2]{0:T(128)S(1)} copy-done((f32[2]{0:T(128)S(1)}, f32[2]{0:T(128)}, u32[]{:S(2)}) %copy-start.4) | copy-done | bytes 32
  1.3 0.0 copy-done.2
  1.3 0.0 copy-done.3
  1.4 0.0 copy-start
  1.4 0.9 %copy-done = f32[8,2,2048]{2,1,0:T(2,128)S(1)} copy-done((f32[8,2,2048]{2,1,0:T(2,128)S(1)}, f32[8,2,2048]{2,1,0:T(2,128)}, u32[]{:S(2)}) %copy-start) | copy-done | bytes 131096
  2.3 0.0 copy-start.1
  2.3 0.9 %copy-done.1 = f32[8,2,2048]{2,1,0:T(2,128)S(1)} copy-done((f32[8,2,2048]{2,1,0:T(2,128)S(1)}, f32[8,2,2048]{2,1,0:T(2,128)}, u32[]{:S(2)}) %copy-start.1) | copy-done | bytes 131096
  3.2 0.7 %shard_map.64 = (f32[2,8]{1,0:T(2,128)S(1)}, f32[256,128]{1,0:T(8,128)S(1)}, f32[256,128]{1,0:T(8,128)S(1)}, f32[32,128]{1,0:T(8,128)S(1)}, f32[32,128]{1,0:T(8,128)S(1)}) custom-call(s32[2,3]{1,0:T(2,128)S(1)} %copy-done.2, f32[2]{0:T(128)S(1)} %copy-done.3, f32[2]{0:T(128)S(1)} %copy-done.4, s32[1]{0:T(128)S(6)} %copy.13.step_ref, ...), custom_call_target="tpu_custom_call" | custom-call | tf_op jit(solution)/shard_map/pallas_call | solution.py:405
  3.8 2.4 %collective-permute-start = (f32[32,128]{1,0:T(8,128)S(1)}, f32[32,128]{1,0:T(8,128)S(1)}, u32[]{:S(2)}, u32[]{:S(2)}) collective-permute-start(f32[32,128]{1,0:T(8,128)S(1)} %get-tuple-element.20), channel_id=1, source_target_pairs={{0,1},{1,2},{2,3},{3,4},{4,5},{5,6},{6,7},{8,9},{9,10},{10,11},{11... | collective-permute-start | bytes 49160 | tf_op jit(solution)/shard_map/ppermute | solution.py:427
  6.2 1.3 %collective-permute-start.1 = (f32[32,128]{1,0:T(8,128)S(1)}, f32[32,128]{1,0:T(8,128)S(1)}, u32[]{:S(2)}, u32[]{:S(2)}) collective-permute-start(f32[32,128]{1,0:T(8,128)S(1)} %get-tuple-element.21), channel_id=1, source_target_pairs={{1,0},{2,1},{3,2},{4,3},{5,4},{6,5},{7,6},{9,8},{10,9},{11,10},{12... | collective-permute-start | bytes 49160 | tf_op jit(solution)/shard_map/ppermute | solution.py:428
  7.5 12.0 %all-gather = f32[4,2,8]{2,1,0:T(2,128)S(1)} all-gather(f32[1,2,8]{2,1,0:T(2,128)S(1)} %bitcast.24), channel_id=1, replica_groups=mesh['grp'=4,'wide'=8] {'grp'}, dimensions={0}, use_global_device_ids=true | all-gather | bytes 320 | tf_op jit(solution)/shard_map/all_gather | solution.py:429
  19.5 0.0 collective-permute-done.low_ref
  19.5 0.0 collective-permute-done.1.high_ref
  19.5 3.1 %shard_map.65 = (f32[256,128]{1,0:T(8,128)S(1)}, f32[256,128]{1,0:T(8,128)S(1)}, f32[256,128]{1,0:T(8,128)S(1)}, f32[256,128]{1,0:T(8,128)S(1)}, f32[256,128]{1,...) custom-call(f32[8,8]{1,0:T(8,128)S(1)} %bitcast.23, ...), custom_call_target="tpu_custom_call" | custom-call | tf_op jit(solution)/shard_map/pallas_call | solution.py:431
  22.6 11.6 %all_to_all.5 = f32[8,32,128]{2,1,0:T(8,128)S(1)} all-to-all(f32[8,32,128]{2,1,0:T(8,128)S(1)} %bitcast.22), channel_id=1, replica_groups=mesh['grp'=4,'wide'=8] {'wide'}, dimensions={0} | all-to-all | bytes 262144 | tf_op jit(solution)/shard_map/all_to_all | solution.py:443
  34.1 0.7 %shard_map.66 = f32[256,128]{1,0:T(8,128)} custom-call(f32[256,128]{1,0:T(8,128)S(1)} %bitcast.19, f32[256,128]{1,0:T(8,128)S(1)} %get-tuple-element.24.left_gain_ref, f32[256,128]{1,0:T(8,128)S(1)} %get-tuple-element.25.left_link_ref, f32[256,128]{1,0:T(8,128)S(1)} %get-tuple-element.26.right_gain_ref, f32[256,128]{1,0:T(8,128)S(1)} %get-tuple-element.27.right_link_ref, ...), custom_call_target="tpu_custom_call" | custom-call | tf_op jit(solution)/shard_map/pallas_call | solution.py:447
Async XLA Ops:
  0.7 0.7 %copy-start.4 = (f32[2]{0:T(128)S(1)}, f32[2]{0:T(128)}, u32[]{:S(2)}) copy-start(f32[2]{0:T(128)} %phase_ref.1) | copy-start | bytes 28
  0.7 0.7 %copy-start.2 = (s32[2,3]{1,0:T(2,128)S(1)}, s32[2,3]{1,0:T(2,128)}, u32[]{:S(2)}) copy-start(s32[2,3]{1,0:T(2,128)} %index_ref.1) | copy-start | bytes 76
  0.7 0.7 %copy-start.3 = (f32[2]{0:T(128)S(1)}, f32[2]{0:T(128)}, u32[]{:S(2)}) copy-start(f32[2]{0:T(128)} %amp_ref.1) | copy-start | bytes 28
  1.4 0.9 %copy-start = (f32[8,2,2048]{2,1,0:T(2,128)S(1)}, f32[8,2,2048]{2,1,0:T(2,128)}, u32[]{:S(2)}) copy-start(f32[8,2,2048]{2,1,0:T(2,128)} %param.6) | copy-start | bytes 393220
  2.3 0.9 %copy-start.1 = (f32[8,2,2048]{2,1,0:T(2,128)S(1)}, f32[8,2,2048]{2,1,0:T(2,128)}, u32[]{:S(2)}) copy-start(f32[8,2,2048]{2,1,0:T(2,128)} %param.7) | copy-start | bytes 393220
  3.8 15.7 %collective-permute-start = (f32[32,128]{1,0:T(8,128)S(1)}, f32[32,128]{1,0:T(8,128)S(1)}, u32[]{:S(2)}, u32[]{:S(2)}) collective-permute-start(f32[32,128]{1,0:T(8,128)S(1)} %get-tuple-element.20), channel_id=1, source_target_pairs={{0,1},{1,2},{2,3},{3,4},{4,5},{5,6},{6,7},{8,9},{9,10},{10,11},{11... | collective-permute-start | bytes 49160 | tf_op jit(solution)/shard_map/ppermute | solution.py:427
  6.2 13.3 %collective-permute-start.1 = (f32[32,128]{1,0:T(8,128)S(1)}, f32[32,128]{1,0:T(8,128)S(1)}, u32[]{:S(2)}, u32[]{:S(2)}) collective-permute-start(f32[32,128]{1,0:T(8,128)S(1)} %get-tuple-element.21), channel_id=1, source_target_pairs={{1,0},{2,1},{3,2},{4,3},{5,4},{6,5},{7,6},{9,8},{10,9},{11,10},{12... | collective-permute-start | bytes 49160 | tf_op jit(solution)/shard_map/ppermute | solution.py:428

commit v3 on v2

--- a/solution.py
+++ b/solution.py
@@ -160,9 +160,9 @@
 
 
 def load_kernel(
-    index_ref, amp_ref, phase_ref, step_ref, field_ref, conduct_ref,
+    step_ref, index_ref, amp_ref, phase_ref, field_ref, conduct_ref,
     packed_ref, field_out, conduct_out, top_ref, bottom_ref,
-    index_in, amp_in, phase_in, step_in, sems,
+    index_in, amp_in, phase_in, sems,
 ):
     width = top_ref.shape[0]
     size = field_ref.shape[0]
@@ -170,7 +170,6 @@
         (index_ref, index_in),
         (amp_ref, amp_in),
         (phase_ref, phase_in),
-        (step_ref, step_in),
         (field_ref.at[pl.ds(0, width)], top_ref),
         (field_ref.at[pl.ds(size - width, width)], bottom_ref),
         (field_ref, field_out),
@@ -179,21 +178,22 @@
     copies = [pltpu.make_async_copy(a, b, sems.at[n]) for n, (a, b) in enumerate(pairs)]
     for copy in copies:
         copy.start()
-    for copy in copies[:4]:
+    for copy in copies[:3]:
         copy.wait()
     count = index_in.shape[0]
-    row = lax.broadcasted_iota(jnp.int32, packed_ref.shape, 0)
-    lane = lax.broadcasted_iota(jnp.int32, packed_ref.shape, 1)
-    total = jnp.zeros(packed_ref.shape, f32)
+    row = lax.broadcasted_iota(jnp.int32, packed_ref.shape[1:], 0)
+    lane = lax.broadcasted_iota(jnp.int32, packed_ref.shape[1:], 1)
+    total = jnp.zeros(packed_ref.shape[1:], f32)
     for m in range(count):
-        moment = lax.rem(index_in[m, 2] * step_in[0], jnp.int32(64)).astype(f32)
+        moment = lax.rem(index_in[m, 2] * step_ref[0], jnp.int32(64)).astype(f32)
         offset = phase_in[m] * (0.5 / math.pi) + moment * (1.0 / 64.0)
         for place, value in enumerate(
             (index_in[m, 0].astype(f32), index_in[m, 1].astype(f32), offset, amp_in[m])
         ):
             total = jnp.where((row == m) & (lane == place), value, total)
-    packed_ref[...] = total
-    for copy in copies[4:]:
+    for n in range(packed_ref.shape[0]):
+        packed_ref[n] = total
+    for copy in copies[3:]:
         copy.wait()
 
 
@@ -217,7 +217,7 @@
 
 
 def main_kernel(
-    sizes, modes_ref, field_ref, low_ref, high_ref, conduct_ref,
+    sizes, modes_ref, field_ref, low_ref, high_ref, late_low_ref, late_high_ref, conduct_ref,
     sent_ref, p_ref, u_ref, v_ref, left_gain_ref, left_link_ref, right_gain_ref, right_link_ref,
     framed, heights, solved, ends,
 ):
@@ -230,9 +230,9 @@
         ((first_layer + k).astype(f32) + 0.5) * (1.0 / layer_total) for k in range(layers)
     ]
     half = 0.5 * weight
-    framed[0:width] = low_ref[...]
+    framed[0:width] = low_ref[...] + late_low_ref[...]
     framed[width : (rows + 1) * width] = field_ref[...]
-    framed[(rows + 1) * width : (rows + 2) * width] = high_ref[...]
+    framed[(rows + 1) * width : (rows + 2) * width] = high_ref[...] + late_high_ref[...]
     body = height_lines(modes_ref[...], 0, row_total, row_total, chunks, column_total)
     heights[chunks : (row_total + 1) * chunks] = body
     heights[0:chunks] = body[0:chunks]
@@ -300,23 +300,17 @@
                 - half * (jac + jac_low) * (f_mid - f_low)
             )
         g_next = from_right(g, 1, lane)
-        f_next = from_right(f, 1, lane)
         g_next[-1] = jnp.where(at_end, g[-1], g_next[-1])
-        f_next[-1] = jnp.where(at_end, 0.0, f_next[-1])
         face = [half * (a + b) for a, b in zip(g, g_next)]
-        flux = [e * (b - a) for e, a, b in zip(face, f, f_next)]
         face_low = from_left(face, 1, lane)
-        flux_low = from_left(flux, 1, lane)
-        edge = weight * g[0]
-        face_low[0] = jnp.where(at_start, edge, face_low[0])
-        flux_low[0] = jnp.where(at_start, edge * f[0], flux_low[0])
+        face_low[0] = jnp.where(at_start, weight * g[0], face_low[0])
         diagonal = [1.0 + (a + b) for a, b in zip(face, face_low)]
-        rhs = [2.0 * (a - b + y) for a, b, y in zip(flux, flux_low, along)]
+        rhs = [2.0 * (a + b) for a, b in zip(f, along)]
         link = face
         link[-1] = jnp.where(at_end, 0.0, link[-1])
-        first = solve_x(diagonal, link, rhs, lane)
+        both = solve_x(diagonal, link, rhs, lane)
         for c in range(chunks):
-            solved[pl.ds(k * chunks + c, rows, stride=width), :] = first[c]
+            solved[pl.ds(k * chunks + c, rows, stride=width), :] = both[c] - 2.0 * f[c]
 
     face = faces(own_heights)
     p, u, v = [], [], []
@@ -392,12 +386,13 @@
     rows, layers, columns = field.shape
     wide_count = lax.axis_size("wide")
     row_total = rows * wide_count
-    layer_total = layers * lax.axis_size("grp")
+    grp_count = lax.axis_size("grp")
+    layer_total = layers * grp_count
     chunks = columns // LANES
     width = layers * chunks
     sizes = (rows, layers, chunks, row_total, layer_total, columns)
     limit = pltpu.CompilerParams(vmem_limit_bytes=16 * 1024 * 1024)
-    anywhere = pl.BlockSpec(memory_space=pl.ANY)
+    hbm = pl.BlockSpec(memory_space=pltpu.HBM)
 
     def lines(count):
         return jax.ShapeDtypeStruct((count * width, LANES), f32)
@@ -405,28 +400,44 @@
     packed, field_lines, conduct_lines, top, bottom = pl.pallas_call(
         load_kernel,
         out_shape=(
-            jax.ShapeDtypeStruct((mode_index.shape[0], 8), f32),
+            jax.ShapeDtypeStruct((grp_count, mode_index.shape[0], 8), f32),
             lines(rows),
             lines(rows),
             lines(1),
             lines(1),
         ),
-        in_specs=[anywhere] * 6,
+        in_specs=[pl.BlockSpec(memory_space=pltpu.SMEM)] + [hbm] * 5,
         scratch_shapes=[
             pltpu.SMEM(mode_index.shape, jnp.int32),
             pltpu.SMEM(mode_amp.shape, f32),
             pltpu.SMEM(mode_phase.shape, f32),
-            pltpu.SMEM(step_index.shape, jnp.int32),
-            pltpu.SemaphoreType.DMA((8,)),
+            pltpu.SemaphoreType.DMA((7,)),
         ],
         compiler_params=limit,
-    )(mode_index, mode_amp, mode_phase, step_index, to_lines(field), to_lines(conduct))
-
-    forward = [(i, i + 1) for i in range(wide_count - 1)]
-    backward = [(target, source) for source, target in forward]
-    low = lax.ppermute(bottom, "wide", forward)
-    high = lax.ppermute(top, "wide", backward)
-    modes = lax.all_gather(packed, "grp", axis=0, tiled=True)
+    )(
+        step_index,
+        *(
+            pltpu.with_memory_space_constraint(a, pltpu.HBM)
+            for a in (mode_index, mode_amp, mode_phase, to_lines(field), to_lines(conduct))
+        ),
+    )
+
+    def neighbour_rows(top, bottom, groups):
+        pairs = [
+            (g * wide_count + i, g * wide_count + i + 1)
+            for g in groups
+            for i in range(wide_count - 1)
+        ]
+        low = lax.ppermute(bottom, ("grp", "wide"), pairs)
+        high = lax.ppermute(top, ("grp", "wide"), [(b, a) for a, b in pairs])
+        return low, high
+
+    early = neighbour_rows(top, bottom, [0])
+    packed, *early = lax.optimization_barrier((packed, *early))
+    modes = lax.all_to_all(packed, "grp", split_axis=0, concat_axis=0)
+    modes, top, bottom = lax.optimization_barrier((modes, top, bottom))
+    late = neighbour_rows(top, bottom, range(1, grp_count))
+    modes = modes.reshape(-1, modes.shape[-1])
 
     sent, p, u, v, *scans = pl.pallas_call(
         functools.partial(main_kernel, sizes),
@@ -438,7 +449,7 @@
             pltpu.VMEM((4 * wide_count * width, LANES), f32),
         ],
         compiler_params=limit,
-    )(modes, field_lines, low, high, conduct_lines)
+    )(modes, field_lines, *early, *late, conduct_lines)
 
     came = lax.all_to_all(
         sent.reshape(wide_count, width, LANES), "wide", split_axis=0, concat_axis=0

time: 35.1 us -> 37.8 us (1.077)
  the two profiles are of different devices: /device:TPU:0 before, /device:TPU:8 now
where the time goes in v3:
time: 37.8 us; the launch traced here: 37.5 us
  blocking collectives  23.6 us (62%)
  starting transfers between devices  5.84 us (15%)
  Pallas kernels  4.88 us (13%)
  waiting for transfers between devices  2.46 us (7%)
  between operations  0.72 us (2%)
    all_to_all x1, blocking collectives, on_device(): lax.all_to_all(sent.reshape(wide_count, width, LANES), 'wide', split_axis...  12 us
    all_to_all x1, blocking collectives, on_device(): modes = lax.all_to_all(packed, 'grp', split_axis=0, concat_axis=0)  11.7 us
    ppermute x2, starting transfers between devices, neighbour_rows(): low = lax.ppermute(bottom, ('grp', 'wide'), pairs)  3.88 us
    pallas_call x1, Pallas kernels, on_device(): pl.pallas_call(functools.partial(main_kernel, sizes), out_shape=(lines(wi...  3.08 us
    ppermute x2, waiting for transfers between devices, neighbour_rows(): high = lax.ppermute(top, ('grp', 'wide'), [(b, a) for a, b in pairs])  2.45 us
    ppermute x2, starting transfers between devices, neighbour_rows(): high = lax.ppermute(top, ('grp', 'wide'), [(b, a) for a, b in pairs])  1.95 us
    pallas_call x1, Pallas kernels, on_device(): pl.pallas_call(load_kernel, out_shape=(jax.ShapeDtypeStruct((grp_count, m...  1.07 us
  transfers between devices with their start and end apart: 4, of which 1 were waited for; matrix products, arithmetic and copies ran while one was open for 0% of the time, Pallas kernels for 0%

profile of v3, /device:TPU:8, one launch (start us, length us, event | category | flops | bytes accessed | tf_op | source)
XLA Modules:
  0.0 37.5 jit_solution(9608382382297360364)
XLA Ops:
  0.7 1.1 %shard_map.64 = (f32[4,2,8]{2,1,0:T(2,128)S(1)}, f32[256,128]{1,0:T(8,128)S(1)}, f32[256,128]{1,0:T(8,128)S(1)}, f32[32,128]{1,0:T(8,128)S(1)}, f32[32,128]{1,0:T(8,128)S(1)}) custom-call(s32[1]{0:T(128)S(6)} %copy.10.step_ref, s32[2,3]{1,0:T(2,128)} %index_ref.1, f32[2]{0:T(128)} %amp_ref.1, f32[2]{0:T(128)} %phase_ref.1, f32[256,128]{1,0:T(8,128)} %bitcast.21, ...), custom_call_target="tpu_custom_call" | custom-call | tf_op jit(solution)/shard_map/pallas_call | solution.py:400
  1.7 0.7 %collective-permute-start = (f32[32,128]{1,0:T(8,128)S(1)}, f32[32,128]{1,0:T(8,128)S(1)}, u32[]{:S(2)}, u32[]{:S(2)}) collective-permute-start(f32[32,128]{1,0:T(8,128)S(1)} %get-tuple-element.32), channel_id=1, source_target_pairs={{0,1},{1,2},{2,3},{3,4},{4,5},{5,6},{6,7}} | collective-permute-start | bytes 49160 | tf_op jit(solution)/shard_map/ppermute | solution.py:431
  2.4 0.7 %collective-permute-start.1 = (f32[32,128]{1,0:T(8,128)S(1)}, f32[32,128]{1,0:T(8,128)S(1)}, u32[]{:S(2)}, u32[]{:S(2)}) collective-permute-start(f32[32,128]{1,0:T(8,128)S(1)} %get-tuple-element.33), channel_id=1, source_target_pairs={{1,0},{2,1},{3,2},{4,3},{5,4},{6,5},{7,6}} | collective-permute-start | bytes 49160 | tf_op jit(solution)/shard_map/ppermute | solution.py:432
  3.1 0.0 collective-permute-done.low_ref
  3.1 0.0 collective-permute-done.1.high_ref
  3.1 11.7 %all_to_all.10 = f32[4,2,8]{2,1,0:T(2,128)S(1)} all-to-all(f32[4,2,8]{2,1,0:T(2,128)S(1)} %get-tuple-element.27), channel_id=1, replica_groups=mesh['grp'=4,'wide'=8] {'grp'}, dimensions={0} | all-to-all | bytes 512 | tf_op jit(solution)/shard_map/all_to_all | solution.py:437
  14.7 3.2 %collective-permute-start.2 = (f32[32,128]{1,0:T(8,128)S(1)}, f32[32,128]{1,0:T(8,128)S(1)}, u32[]{:S(2)}, u32[]{:S(2)}) collective-permute-start(f32[32,128]{1,0:T(8,128)S(1)} %get-tuple-element.32), channel_id=1, source_target_pairs={{8,9},{9,10},{10,11},{11,12},{12,13},{13,14},{14,15},{16,17},{17,1... | collective-permute-start | bytes 49160 | tf_op jit(solution)/shard_map/ppermute | solution.py:431
  18.0 1.3 %collective-permute-start.3 = (f32[32,128]{1,0:T(8,128)S(1)}, f32[32,128]{1,0:T(8,128)S(1)}, u32[]{:S(2)}, u32[]{:S(2)}) collective-permute-start(f32[32,128]{1,0:T(8,128)S(1)} %get-tuple-element.33), channel_id=1, source_target_pairs={{9,8},{10,9},{11,10},{12,11},{13,12},{14,13},{15,14},{17,16},{18,1... | collective-permute-start | bytes 49160 | tf_op jit(solution)/shard_map/ppermute | solution.py:432
  19.3 0.0 collective-permute-done.2.late_low_ref
  19.3 2.4 %collective-permute-done.3.late_high_ref = f32[32,128]{1,0:T(8,128)S(1)} collective-permute-done((f32[32,128]{1,0:T(8,128)S(1)}, f32[32,128]{1,0:T(8,128)S(1)}, u32[]{:S(2)}, u32[]{:S(2)}) %collective-permute-start.3) | collective-permute-done | bytes 16416 | tf_op jit(solution)/shard_map/ppermute | solution.py:432
  21.7 3.1 %shard_map.65 = (f32[256,128]{1,0:T(8,128)S(1)}, f32[256,128]{1,0:T(8,128)S(1)}, f32[256,128]{1,0:T(8,128)S(1)}, f32[256,128]{1,0:T(8,128)S(1)}, f32[256,128]{1,...) custom-call(f32[8,8]{1,0:T(8,128)S(1)} %bitcast.20, ...), custom_call_target="tpu_custom_call" | custom-call | tf_op jit(solution)/shard_map/pallas_call | solution.py:442
  24.8 12.0 %all_to_all.11 = f32[8,32,128]{2,1,0:T(8,128)S(1)} all-to-all(f32[8,32,128]{2,1,0:T(8,128)S(1)} %bitcast.19), channel_id=1, replica_groups=mesh['grp'=4,'wide'=8] {'wide'}, dimensions={0} | all-to-all | bytes 262144 | tf_op jit(solution)/shard_map/all_to_all | solution.py:454
  36.8 0.7 %shard_map.66 = f32[256,128]{1,0:T(8,128)} custom-call(f32[256,128]{1,0:T(8,128)S(1)} %bitcast.18, f32[256,128]{1,0:T(8,128)S(1)} %get-tuple-element.36.left_gain_ref, f32[256,128]{1,0:T(8,128)S(1)} %get-tuple-element.37.left_link_ref, f32[256,128]{1,0:T(8,128)S(1)} %get-tuple-element.38.right_gain_ref, f32[256,128]{1,0:T(8,128)S(1)} %get-tuple-element.39.right_link_ref, ...), custom_call_target="tpu_custom_call" | custom-call | tf_op jit(solution)/shard_map/pallas_call | solution.py:458
Async XLA Ops:
  1.7 1.3 %collective-permute-start = (f32[32,128]{1,0:T(8,128)S(1)}, f32[32,128]{1,0:T(8,128)S(1)}, u32[]{:S(2)}, u32[]{:S(2)}) collective-permute-start(f32[32,128]{1,0:T(8,128)S(1)} %get-tuple-element.32), channel_id=1, source_target_pairs={{0,1},{1,2},{2,3},{3,4},{4,5},{5,6},{6,7}} | collective-permute-start | bytes 49160 | tf_op jit(solution)/shard_map/ppermute | solution.py:431
  2.4 0.7 %collective-permute-start.1 = (f32[32,128]{1,0:T(8,128)S(1)}, f32[32,128]{1,0:T(8,128)S(1)}, u32[]{:S(2)}, u32[]{:S(2)}) collective-permute-start(f32[32,128]{1,0:T(8,128)S(1)} %get-tuple-element.33), channel_id=1, source_target_pairs={{1,0},{2,1},{3,2},{4,3},{5,4},{6,5},{7,6}} | collective-permute-start | bytes 49160 | tf_op jit(solution)/shard_map/ppermute | solution.py:432
  14.7 4.5 %collective-permute-start.2 = (f32[32,128]{1,0:T(8,128)S(1)}, f32[32,128]{1,0:T(8,128)S(1)}, u32[]{:S(2)}, u32[]{:S(2)}) collective-permute-start(f32[32,128]{1,0:T(8,128)S(1)} %get-tuple-element.32), channel_id=1, source_target_pairs={{8,9},{9,10},{10,11},{11,12},{12,13},{13,14},{14,15},{16,17},{17,1... | collective-permute-start | bytes 49160 | tf_op jit(solution)/shard_map/ppermute | solution.py:431
  18.0 3.8 %collective-permute-start.3 = (f32[32,128]{1,0:T(8,128)S(1)}, f32[32,128]{1,0:T(8,128)S(1)}, u32[]{:S(2)}, u32[]{:S(2)}) collective-permute-start(f32[32,128]{1,0:T(8,128)S(1)} %get-tuple-element.33), channel_id=1, source_target_pairs={{9,8},{10,9},{11,10},{12,11},{13,12},{14,13},{15,14},{17,16},{18,1... | collective-permute-start | bytes 49160 | tf_op jit(solution)/shard_map/ppermute | solution.py:432

commit v4 on v3

--- a/solution.py
+++ b/solution.py
@@ -161,17 +161,20 @@
 
 def load_kernel(
     step_ref, index_ref, amp_ref, phase_ref, field_ref, conduct_ref,
-    packed_ref, field_out, conduct_out, top_ref, bottom_ref,
+    packed_ref, field_out, conduct_out, inner_ref, outer_ref,
     index_in, amp_in, phase_in, sems,
 ):
-    width = top_ref.shape[0]
-    size = field_ref.shape[0]
+    width = inner_ref.shape[0]
+    last = field_ref.shape[0] - width
+    odd = lax.rem(lax.axis_index("wide"), 2)
+    inner_rows = pl.ds(pl.multiple_of((1 - odd) * last, 8), width)
+    outer_rows = pl.ds(pl.multiple_of(odd * last, 8), width)
     pairs = (
         (index_ref, index_in),
         (amp_ref, amp_in),
         (phase_ref, phase_in),
-        (field_ref.at[pl.ds(0, width)], top_ref),
-        (field_ref.at[pl.ds(size - width, width)], bottom_ref),
+        (field_ref.at[inner_rows], inner_ref),
+        (field_ref.at[outer_rows], outer_ref),
         (field_ref, field_out),
         (conduct_ref, conduct_out),
     )
@@ -181,9 +184,9 @@
     for copy in copies[:3]:
         copy.wait()
     count = index_in.shape[0]
-    row = lax.broadcasted_iota(jnp.int32, packed_ref.shape[1:], 0)
-    lane = lax.broadcasted_iota(jnp.int32, packed_ref.shape[1:], 1)
-    total = jnp.zeros(packed_ref.shape[1:], f32)
+    row = lax.broadcasted_iota(jnp.int32, packed_ref.shape, 0)
+    lane = lax.broadcasted_iota(jnp.int32, packed_ref.shape, 1)
+    total = jnp.zeros(packed_ref.shape, f32)
     for m in range(count):
         moment = lax.rem(index_in[m, 2] * step_ref[0], jnp.int32(64)).astype(f32)
         offset = phase_in[m] * (0.5 / math.pi) + moment * (1.0 / 64.0)
@@ -191,35 +194,36 @@
             (index_in[m, 0].astype(f32), index_in[m, 1].astype(f32), offset, amp_in[m])
         ):
             total = jnp.where((row == m) & (lane == place), value, total)
-    for n in range(packed_ref.shape[0]):
-        packed_ref[n] = total
+    packed_ref[...] = total
     for copy in copies[3:]:
         copy.wait()
 
 
 def condense(face):
-    u, v = [], []
+    inv, scaled, u, v = [], [], [], []
     rows = len(face) - 1
     for j in range(rows):
         d = 1.0 + (face[j] + face[j + 1])
         if j == 0:
-            inv = inverse(d)
-            u.append(face[0] * inv)
+            inv.append(inverse(d))
+            scaled.append(face[0] * inv[0])
+            u.append(scaled[0])
         else:
-            inv = inverse(d - face[j] * v[-1])
-            u.append(face[j] * inv * u[-1])
-        v.append(face[j + 1] * inv)
-    u_first, v_first = u[-1], v[-1]
+            inv.append(inverse(d - face[j] * v[-1]))
+            scaled.append(face[j] * inv[-1])
+            u.append(scaled[-1] * u[-1])
+        v.append(face[j + 1] * inv[-1])
+    u_all, v_all = list(u), list(v)
     for j in range(rows - 2, -1, -1):
-        u_first = u[j] + v[j] * u_first
-        v_first = v[j] * v_first
-    return u_first, v_first, u[-1], v[-1]
-
-
-def main_kernel(
-    sizes, modes_ref, field_ref, low_ref, high_ref, late_low_ref, late_high_ref, conduct_ref,
-    sent_ref, p_ref, u_ref, v_ref, left_gain_ref, left_link_ref, right_gain_ref, right_link_ref,
-    framed, heights, solved, ends,
+        u_all[j] = u[j] + v[j] * u_all[j + 1]
+        v_all[j] = v[j] * v_all[j + 1]
+    return inv, scaled, v, u_all, v_all
+
+
+def matrix_kernel(
+    sizes, modes_ref,
+    own_heights_ref, inv_ref, scaled_ref, chain_ref, u_ref, v_ref, left_gain_ref, right_gain_ref,
+    joint_ref, heights, ends, links,
 ):
     rows, layers, chunks, row_total, layer_total, column_total = sizes
     width = layers * chunks
@@ -230,18 +234,14 @@
         ((first_layer + k).astype(f32) + 0.5) * (1.0 / layer_total) for k in range(layers)
     ]
     half = 0.5 * weight
-    framed[0:width] = low_ref[...] + late_low_ref[...]
-    framed[width : (rows + 1) * width] = field_ref[...]
-    framed[(rows + 1) * width : (rows + 2) * width] = high_ref[...] + late_high_ref[...]
     body = height_lines(modes_ref[...], 0, row_total, row_total, chunks, column_total)
     heights[chunks : (row_total + 1) * chunks] = body
     heights[0:chunks] = body[0:chunks]
     heights[(row_total + 1) * chunks : (row_total + 2) * chunks] = body[
         (row_total - 1) * chunks : row_total * chunks
     ]
-    lane = lax.broadcasted_iota(jnp.int32, (rows, LANES), 1)
-    at_start = lane == 0
-    at_end = lane == LANES - 1
+    own_start = pl.multiple_of(me * (rows * chunks), 8)
+    own_heights_ref[...] = heights[pl.ds(own_start, (rows + 2) * chunks), :]
 
     def faces(start):
         jac = []
@@ -250,18 +250,29 @@
             jac.append(jnp.concatenate([1.0 + z * h for z in zeta], 0))
         return [half * (jac[j] + jac[j + 1]) for j in range(rows + 1)]
 
-    def block_ends(b):
-        start, base = b * (rows * chunks), b * (4 * width)
-        if not isinstance(b, int):
-            start, base = pl.multiple_of(start, 8), pl.multiple_of(base, 8)
-        for n, value in enumerate(condense(faces(start))):
+    def keep_ends(b, u, v):
+        base = pl.multiple_of(b * (4 * width), 8)
+        for n, value in enumerate((u[0], v[0], u[-1], v[-1])):
             ends[pl.ds(base + n * width, width), :] = value
 
+    inv, scaled, chain, u, v = condense(faces(own_start))
+    for ref, values in (
+        (inv_ref, inv), (scaled_ref, scaled), (chain_ref, chain), (u_ref, u), (v_ref, v)
+    ):
+        for j in range(rows):
+            ref[j * width : (j + 1) * width] = values[j]
+    keep_ends(me, u, v)
+
+    def other_block(n):
+        b = lax.rem(me + 1 + n, blocks)
+        _, _, _, u, v = condense(faces(pl.multiple_of(b * (rows * chunks), 8)))
+        keep_ends(b, u, v)
+
     if blocks <= 8:
-        for b in range(blocks):
-            block_ends(b)
+        for n in range(blocks - 1):
+            other_block(n)
     else:
-        lax.fori_loop(0, blocks, lambda b, carry: (block_ends(b), carry)[1], 0)
+        lax.fori_loop(0, blocks - 1, lambda n, carry: (other_block(n), carry)[1], 0)
 
     def end(b, n):
         return ends[(4 * b + n) * width : (4 * b + n + 1) * width]
@@ -272,21 +283,61 @@
         u_first, v_first, u_last, v_last = (end(b, n) for n in range(4))
         gain = u_last * inverse(1.0 - u_first * left)
         left_gain_ref[b * width : (b + 1) * width] = gain
-        left_link_ref[b * width : (b + 1) * width] = left
+        links[b * width : (b + 1) * width] = left
         left = v_last + gain * left * v_first
         b = blocks - 1 - b
         u_first, v_first, u_last, v_last = (end(b, n) for n in range(4))
         gain = v_first * inverse(1.0 - v_last * right)
         right_gain_ref[b * width : (b + 1) * width] = gain
-        right_link_ref[b * width : (b + 1) * width] = right
+        links[(blocks + b) * width : (blocks + b + 1) * width] = right
         right = u_first + gain * right * u_last
 
-    own_heights = pl.multiple_of(me * (rows * chunks), 8)
+    own = pl.ds(pl.multiple_of(me * width, 8), width)
+    left_link = links[own, :]
+    right_link = links[pl.ds(pl.multiple_of((blocks + me) * width, 8), width), :]
+    a = 1.0 - left_link * u[0]
+    b = left_link * v[0]
+    c = right_link * u[-1]
+    d = 1.0 - right_link * v[-1]
+    inv = inverse(a * d - b * c)
+    joint = (
+        left_gain_ref[own, :] * left_link, right_gain_ref[own, :] * right_link,
+        left_link, right_link, d * inv, b * inv, c * inv, a * inv,
+    )
+    for n, value in enumerate(joint):
+        joint_ref[n * width : (n + 1) * width] = value
+
+
+def first_kernel(
+    sizes, field_ref, inner_ref, outer_ref, late_outer_ref, conduct_ref,
+    heights, inv_ref, scaled_ref, chain_ref, joint_ref,
+    sent_ref, p_ref, framed, solved,
+):
+    rows, layers, chunks, row_total, layer_total, column_total = sizes
+    width = layers * chunks
+    blocks = row_total // rows
+    me = lax.axis_index("wide")
+    odd = lax.rem(me, 2)
+    first_layer = lax.axis_index("grp") * layers
+    zeta = [
+        ((first_layer + k).astype(f32) + 0.5) * (1.0 / layer_total) for k in range(layers)
+    ]
+    half = 0.5 * weight
+    beyond = (rows + 1) * width
+    framed[width:beyond] = field_ref[...]
+    framed[pl.ds(pl.multiple_of((1 - odd) * beyond, 8), width), :] = inner_ref[...]
+    framed[pl.ds(pl.multiple_of(odd * beyond, 8), width), :] = (
+        outer_ref[...] + late_outer_ref[...]
+    )
+    lane = lax.broadcasted_iota(jnp.int32, (rows, LANES), 1)
+    at_start = lane == 0
+    at_end = lane == LANES - 1
+
     for k in range(layers):
         g, f, along = [], [], []
         for c in range(chunks):
             jac_low, jac, jac_high = (
-                1.0 + zeta[k] * heights[pl.ds(own_heights + s * chunks + c, rows, stride=chunks), :]
+                1.0 + zeta[k] * heights[pl.ds(s * chunks + c, rows, stride=chunks), :]
                 for s in range(3)
             )
             place = c * layers + k
@@ -312,40 +363,26 @@
         for c in range(chunks):
             solved[pl.ds(k * chunks + c, rows, stride=width), :] = both[c] - 2.0 * f[c]
 
-    face = faces(own_heights)
-    p, u, v = [], [], []
-    for j in range(rows):
-        r = solved[j * width : (j + 1) * width]
-        d = 1.0 + (face[j] + face[j + 1])
-        if j == 0:
-            inv = inverse(d)
-            p.append(r * inv)
-            u.append(face[0] * inv)
-        else:
-            inv = inverse(d - face[j] * v[-1])
-            scaled = face[j] * inv
-            p.append(r * inv + scaled * p[-1])
-            u.append(scaled * u[-1])
-        v.append(face[j + 1] * inv)
+    def part(ref, j):
+        return ref[j * width : (j + 1) * width]
+
+    p = [part(solved, 0) * part(inv_ref, 0)]
+    for j in range(1, rows):
+        p.append(part(solved, j) * part(inv_ref, j) + part(scaled_ref, j) * p[-1])
     for j in range(rows - 2, -1, -1):
-        p[j] = p[j] + v[j] * p[j + 1]
-        u[j] = u[j] + v[j] * u[j + 1]
-        v[j] = v[j] * v[j + 1]
+        p[j] = p[j] + part(chain_ref, j) * p[j + 1]
     for j in range(rows):
         p_ref[j * width : (j + 1) * width] = p[j]
-        u_ref[j * width : (j + 1) * width] = u[j]
-        v_ref[j * width : (j + 1) * width] = v[j]
-
-    own = pl.ds(pl.multiple_of(me * width, 8), width)
-    upward = p[-1] + left_gain_ref[own, :] * (left_link_ref[own, :] * p[0])
-    downward = p[0] + right_gain_ref[own, :] * (right_link_ref[own, :] * p[-1])
+
+    upward = p[-1] + part(joint_ref, 0) * p[0]
+    downward = p[0] + part(joint_ref, 1) * p[-1]
     for b in range(blocks):
         sent_ref[b * width : (b + 1) * width] = jnp.where(b > me, upward, downward)
 
 
 def last_kernel(
-    sizes, came_ref, left_gain_ref, left_link_ref, right_gain_ref, right_link_ref,
-    p_ref, u_ref, v_ref, field_ref, out_ref,
+    sizes, came_ref, left_gain_ref, right_gain_ref, joint_ref, p_ref, u_ref, v_ref, field_ref,
+    out_ref,
 ):
     rows, layers, chunks, row_total, layer_total, column_total = sizes
     width = layers * chunks
@@ -362,19 +399,10 @@
         b = blocks - 1 - b
         right = jnp.where(b > me, part(came_ref, b) + part(right_gain_ref, b) * right, right)
 
-    own = pl.ds(pl.multiple_of(me * width, 8), width)
-    left_link, right_link = left_link_ref[own, :], right_link_ref[own, :]
-    p_first, u_first, v_first = (part(ref, 0) for ref in (p_ref, u_ref, v_ref))
-    p_last, u_last, v_last = (part(ref, rows - 1) for ref in (p_ref, u_ref, v_ref))
-    a = 1.0 - left_link * u_first
-    b = left_link * v_first
-    c = right_link * u_last
-    d = 1.0 - right_link * v_last
-    y = left + left_link * p_first
-    z = right + right_link * p_last
-    inv = inverse(a * d - b * c)
-    before = (d * y + b * z) * inv
-    after = (c * y + a * z) * inv
+    y = left + part(joint_ref, 2) * part(p_ref, 0)
+    z = right + part(joint_ref, 3) * part(p_ref, rows - 1)
+    before = part(joint_ref, 4) * y + part(joint_ref, 5) * z
+    after = part(joint_ref, 6) * y + part(joint_ref, 7) * z
     for j in range(rows):
         x = part(p_ref, j) + part(u_ref, j) * before + part(v_ref, j) * after
         for k in range(layers):
@@ -397,10 +425,10 @@
     def lines(count):
         return jax.ShapeDtypeStruct((count * width, LANES), f32)
 
-    packed, field_lines, conduct_lines, top, bottom = pl.pallas_call(
+    packed, field_lines, conduct_lines, inner, outer = pl.pallas_call(
         load_kernel,
         out_shape=(
-            jax.ShapeDtypeStruct((grp_count, mode_index.shape[0], 8), f32),
+            jax.ShapeDtypeStruct((mode_index.shape[0], 8), f32),
             lines(rows),
             lines(rows),
             lines(1),
@@ -422,34 +450,45 @@
         ),
     )
 
-    def neighbour_rows(top, bottom, groups):
-        pairs = [
-            (g * wide_count + i, g * wide_count + i + 1)
-            for g in groups
-            for i in range(wide_count - 1)
-        ]
-        low = lax.ppermute(bottom, ("grp", "wide"), pairs)
-        high = lax.ppermute(top, ("grp", "wide"), [(b, a) for a, b in pairs])
-        return low, high
-
-    early = neighbour_rows(top, bottom, [0])
-    packed, *early = lax.optimization_barrier((packed, *early))
-    modes = lax.all_to_all(packed, "grp", split_axis=0, concat_axis=0)
-    modes, top, bottom = lax.optimization_barrier((modes, top, bottom))
-    late = neighbour_rows(top, bottom, range(1, grp_count))
-    modes = modes.reshape(-1, modes.shape[-1])
-
-    sent, p, u, v, *scans = pl.pallas_call(
-        functools.partial(main_kernel, sizes),
-        out_shape=(lines(wide_count),) + (lines(rows),) * 3 + (lines(wide_count),) * 4,
+    def swap(rows_sent, first, groups):
+        pairs = []
+        for g in groups:
+            for i in range(g * wide_count + first, (g + 1) * wide_count - 1, 2):
+                pairs += [(i, i + 1), (i + 1, i)]
+        return lax.ppermute(rows_sent, ("grp", "wide"), pairs)
+
+    inner_came = swap(inner, 0, range(grp_count))
+    outer_came = swap(outer, 1, [0])
+    modes = lax.all_gather(packed, "grp", axis=0, tiled=True)
+    modes, outer = lax.optimization_barrier((modes, outer))
+    late_outer_came = swap(outer, 1, range(1, grp_count))
+
+    own_heights, inv, scaled, chain, u, v, left_gain, right_gain, joint = pl.pallas_call(
+        functools.partial(matrix_kernel, sizes),
+        out_shape=(jax.ShapeDtypeStruct(((rows + 2) * chunks, LANES), f32),)
+        + (lines(rows),) * 5
+        + (lines(wide_count),) * 2
+        + (lines(8),),
+        scratch_shapes=[
+            pltpu.VMEM(((row_total + 2) * chunks, LANES), f32),
+            pltpu.VMEM((4 * wide_count * width, LANES), f32),
+            pltpu.VMEM((2 * wide_count * width, LANES), f32),
+        ],
+        compiler_params=limit,
+    )(modes)
+
+    sent, p = pl.pallas_call(
+        functools.partial(first_kernel, sizes),
+        out_shape=(lines(wide_count), lines(rows)),
         scratch_shapes=[
             pltpu.VMEM(((rows + 2) * width, LANES), f32),
-            pltpu.VMEM(((row_total + 2) * chunks, LANES), f32),
             pltpu.VMEM((rows * width, LANES), f32),
-            pltpu.VMEM((4 * wide_count * width, LANES), f32),
         ],
         compiler_params=limit,
-    )(modes, field_lines, *early, *late, conduct_lines)
+    )(
+        field_lines, inner_came, outer_came, late_outer_came, conduct_lines,
+        own_heights, inv, scaled, chain, joint,
+    )
 
     came = lax.all_to_all(
         sent.reshape(wide_count, width, LANES), "wide", split_axis=0, concat_axis=0
@@ -459,7 +498,7 @@
         functools.partial(last_kernel, sizes),
         out_shape=lines(rows),
         compiler_params=limit,
-    )(came, *scans, p, u, v, field_lines)
+    )(came, left_gain, right_gain, joint, p, u, v, field_lines)
     return from_lines(advanced, field.shape)
 
 

time: 37.8 us -> 32.7 us (0.87)
  the two profiles are of different devices: /device:TPU:8 before, /device:TPU:0 now
where the time goes in v4:
time: 32.7 us; the launch traced here: 32.5 us
  blocking collectives  24.5 us (75%)
  Pallas kernels  5.9 us (18%)
  starting transfers between devices  1.38 us (4%)
  between operations  0.72 us (2%)
    all_gather x1, blocking collectives, on_device(): modes = lax.all_gather(packed, 'grp', axis=0, tiled=True)  12.6 us
    all_to_all x1, blocking collectives, on_device(): lax.all_to_all(sent.reshape(wide_count, width, LANES), 'wide', split_axis...  11.9 us
    pallas_call x1, Pallas kernels, on_device(): pl.pallas_call(functools.partial(first_kernel, sizes), out_shape=(lines(w...  2.54 us
    pallas_call x1, Pallas kernels, on_device(): pl.pallas_call(functools.partial(matrix_kernel, sizes), out_shape=(jax.Sh...  1.57 us
    ppermute x3, starting transfers between devices, swap(): return lax.ppermute(rows_sent, ('grp', 'wide'), pairs)  1.38 us
    pallas_call x1, Pallas kernels, on_device(): pl.pallas_call(load_kernel, out_shape=(jax.ShapeDtypeStruct((mode_index.s...  1.08 us
    pallas_call x1, Pallas kernels, on_device(): pl.pallas_call(functools.partial(last_kernel, sizes), out_shape=lines(row...  0.72 us
  transfers between devices with their start and end apart: 3, of which 0 were waited for; matrix products, arithmetic and copies ran while one was open for 0% of the time, Pallas kernels for 5%

profile of v4, /device:TPU:0, one launch (start us, length us, event | category | flops | bytes accessed | tf_op | source)
XLA Modules:
  0.0 32.5 jit_solution(12761279611940374455)
XLA Ops:
  0.7 1.1 %shard_map.64 = (f32[2,8]{1,0:T(2,128)S(1)}, f32[256,128]{1,0:T(8,128)S(1)}, f32[256,128]{1,0:T(8,128)S(1)}, f32[32,128]{1,0:T(8,128)S(1)}, f32[32,128]{1,0:T(8,128)S(1)}) custom-call(s32[1]{0:T(128)S(6)} %copy.13.step_ref, s32[2,3]{1,0:T(2,128)} %index_ref.1, f32[2]{0:T(128)} %amp_ref.1, f32[2]{0:T(128)} %phase_ref.1, f32[256,128]{1,0:T(8,128)} %bitcast.23, ...), custom_call_target="tpu_custom_call" | custom-call | tf_op jit(solution)/shard_map/pallas_call | solution.py:428
  1.7 12.6 %all-gather = f32[4,2,8]{2,1,0:T(2,128)S(1)} all-gather(f32[1,2,8]{2,1,0:T(2,128)S(1)} %bitcast.22), channel_id=1, replica_groups=mesh['grp'=4,'wide'=8] {'grp'}, dimensions={0}, use_global_device_ids=true | all-gather | bytes 320 | tf_op jit(solution)/shard_map/all_gather | solution.py:462
  14.4 0.7 %collective-permute-start.2 = (f32[32,128]{1,0:T(8,128)S(1)}, f32[32,128]{1,0:T(8,128)S(1)}, u32[]{:S(2)}, u32[]{:S(2)}) collective-permute-start(f32[32,128]{1,0:T(8,128)S(1)} %get-tuple-element.27), channel_id=1, source_target_pairs={{9,10},{10,9},{11,12},{12,11},{13,14},{14,13},{17,18},{18,17},{19,... | collective-permute-start | bytes 49160 | tf_op jit(solution)/shard_map/ppermute | solution.py:458
  15.0 0.1 collective-permute-start
  15.1 0.7 %collective-permute-start.1 = (f32[32,128]{1,0:T(8,128)S(1)}, f32[32,128]{1,0:T(8,128)S(1)}, u32[]{:S(2)}, u32[]{:S(2)}) collective-permute-start(f32[32,128]{1,0:T(8,128)S(1)} %get-tuple-element.27), channel_id=1, source_target_pairs={{1,2},{2,1},{3,4},{4,3},{5,6},{6,5}} | collective-permute-start | bytes 49160 | tf_op jit(solution)/shard_map/ppermute | solution.py:458
  15.8 1.6 %shard_map.65 = (f32[160,128]{1,0:T(8,128)S(1)}, f32[256,128]{1,0:T(8,128)S(1)}, f32[256,128]{1,0:T(8,128)S(1)}, f32[256,128]{1,0:T(8,128)S(1)}, f32[256,128]{1,...) custom-call(f32[8,8]{1,0:T(8,128)S(1)} %bitcast.21), custom_call_target="tpu_custom_call" | custom-call | tf_op jit(solution)/shard_map/pallas_call | solution.py:466
  17.3 0.0 collective-permute-done.2.late_outer_ref
  17.3 0.0 collective-permute-done.inner_ref
  17.4 0.0 collective-permute-done.1.outer_ref
  17.4 2.5 %shard_map.66 = (f32[256,128]{1,0:T(8,128)S(1)}, f32[256,128]{1,0:T(8,128)S(1)}) custom-call(f32[256,128]{1,0:T(8,128)S(1)} %get-tuple-element.23.field_ref, f32[32,128]{1,0:T(8,128)S(1)} %collective-permute-done.inner_ref, f32[32,128]{1,0:T(8,128)S(1)} %collective-permute-done.1.outer_ref, f32[32,128]{1,0:T(8,128)S(1)} %collective-permute-done.2.late_outer_ref, ...), custom_call_target="tpu_custom_call" | custom-call | tf_op jit(solution)/shard_map/pallas_call | solution.py:480
  19.9 11.9 %all_to_all.5 = f32[8,32,128]{2,1,0:T(8,128)S(1)} all-to-all(f32[8,32,128]{2,1,0:T(8,128)S(1)} %bitcast.20), channel_id=1, replica_groups=mesh['grp'=4,'wide'=8] {'wide'}, dimensions={0} | all-to-all | bytes 262144 | tf_op jit(solution)/shard_map/all_to_all | solution.py:493
  31.8 0.7 %shard_map.67 = f32[256,128]{1,0:T(8,128)} custom-call(f32[256,128]{1,0:T(8,128)S(1)} %bitcast.19, f32[256,128]{1,0:T(8,128)S(1)} %get-tuple-element.36.left_gain_ref, f32[256,128]{1,0:T(8,128)S(1)} %get-tuple-element.37.right_gain_ref, f32[256,128]{1,0:T(8,128)S(1)} %get-tuple-element.34.joint_ref, f32[256,128]{1,0:T(8,128)S(1)} %get-tuple-element.38.p_ref, ...), custom_call_target="tpu_custom_call" | custom-call | tf_op jit(solution)/shard_map/pallas_call | solution.py:497
Async XLA Ops:
  14.4 3.0 %collective-permute-start.2 = (f32[32,128]{1,0:T(8,128)S(1)}, f32[32,128]{1,0:T(8,128)S(1)}, u32[]{:S(2)}, u32[]{:S(2)}) collective-permute-start(f32[32,128]{1,0:T(8,128)S(1)} %get-tuple-element.27), channel_id=1, source_target_pairs={{9,10},{10,9},{11,12},{12,11},{13,14},{14,13},{17,18},{18,17},{19,... | collective-permute-start | bytes 49160 | tf_op jit(solution)/shard_map/ppermute | solution.py:458
  15.0 2.3 %collective-permute-start = (f32[32,128]{1,0:T(8,128)S(1)}, f32[32,128]{1,0:T(8,128)S(1)}, u32[]{:S(2)}, u32[]{:S(2)}) collective-permute-start(f32[32,128]{1,0:T(8,128)S(1)} %get-tuple-element.24), channel_id=1, source_target_pairs={{0,1},{1,0},{2,3},{3,2},{4,5},{5,4},{6,7},{7,6},{8,9},{9,8},{10,11... | collective-permute-start | bytes 49160 | tf_op jit(solution)/shard_map/ppermute | solution.py:458
  15.1 2.3 %collective-permute-start.1 = (f32[32,128]{1,0:T(8,128)S(1)}, f32[32,128]{1,0:T(8,128)S(1)}, u32[]{:S(2)}, u32[]{:S(2)}) collective-permute-start(f32[32,128]{1,0:T(8,128)S(1)} %get-tuple-element.27), channel_id=1, source_target_pairs={{1,2},{2,1},{3,4},{4,3},{5,6},{6,5}} | collective-permute-start | bytes 49160 | tf_op jit(solution)/shard_map/ppermute | solution.py:458

commit v5 on v4

--- a/solution.py
+++ b/solution.py
@@ -220,10 +220,10 @@
     return inv, scaled, v, u_all, v_all
 
 
-def matrix_kernel(
-    sizes, modes_ref,
-    own_heights_ref, inv_ref, scaled_ref, chain_ref, u_ref, v_ref, left_gain_ref, right_gain_ref,
-    joint_ref, heights, ends, links,
+def main_kernel(
+    sizes, modes_ref, field_ref, inner_ref, outer_ref, late_outer_ref, conduct_ref,
+    sent_ref, p_ref, u_ref, v_ref, left_gain_ref, right_gain_ref, joint_ref,
+    heights, ends, links, framed, solved,
 ):
     rows, layers, chunks, row_total, layer_total, column_total = sizes
     width = layers * chunks
@@ -241,7 +241,6 @@
         (row_total - 1) * chunks : row_total * chunks
     ]
     own_start = pl.multiple_of(me * (rows * chunks), 8)
-    own_heights_ref[...] = heights[pl.ds(own_start, (rows + 2) * chunks), :]
 
     def faces(start):
         jac = []
@@ -256,11 +255,9 @@
             ends[pl.ds(base + n * width, width), :] = value
 
     inv, scaled, chain, u, v = condense(faces(own_start))
-    for ref, values in (
-        (inv_ref, inv), (scaled_ref, scaled), (chain_ref, chain), (u_ref, u), (v_ref, v)
-    ):
-        for j in range(rows):
-            ref[j * width : (j + 1) * width] = values[j]
+    for j in range(rows):
+        u_ref[j * width : (j + 1) * width] = u[j]
+        v_ref[j * width : (j + 1) * width] = v[j]
     keep_ends(me, u, v)
 
     def other_block(n):
@@ -299,30 +296,15 @@
     b = left_link * v[0]
     c = right_link * u[-1]
     d = 1.0 - right_link * v[-1]
-    inv = inverse(a * d - b * c)
+    by = inverse(a * d - b * c)
     joint = (
         left_gain_ref[own, :] * left_link, right_gain_ref[own, :] * right_link,
-        left_link, right_link, d * inv, b * inv, c * inv, a * inv,
+        left_link, right_link, d * by, b * by, c * by, a * by,
     )
     for n, value in enumerate(joint):
         joint_ref[n * width : (n + 1) * width] = value
 
-
-def first_kernel(
-    sizes, field_ref, inner_ref, outer_ref, late_outer_ref, conduct_ref,
-    heights, inv_ref, scaled_ref, chain_ref, joint_ref,
-    sent_ref, p_ref, framed, solved,
-):
-    rows, layers, chunks, row_total, layer_total, column_total = sizes
-    width = layers * chunks
-    blocks = row_total // rows
-    me = lax.axis_index("wide")
     odd = lax.rem(me, 2)
-    first_layer = lax.axis_index("grp") * layers
-    zeta = [
-        ((first_layer + k).astype(f32) + 0.5) * (1.0 / layer_total) for k in range(layers)
-    ]
-    half = 0.5 * weight
     beyond = (rows + 1) * width
     framed[width:beyond] = field_ref[...]
     framed[pl.ds(pl.multiple_of((1 - odd) * beyond, 8), width), :] = inner_ref[...]
@@ -337,7 +319,7 @@
         g, f, along = [], [], []
         for c in range(chunks):
             jac_low, jac, jac_high = (
-                1.0 + zeta[k] * heights[pl.ds(s * chunks + c, rows, stride=chunks), :]
+                1.0 + zeta[k] * heights[pl.ds(own_start + s * chunks + c, rows, stride=chunks), :]
                 for s in range(3)
             )
             place = c * layers + k
@@ -366,11 +348,11 @@
     def part(ref, j):
         return ref[j * width : (j + 1) * width]
 
-    p = [part(solved, 0) * part(inv_ref, 0)]
+    p = [part(solved, 0) * inv[0]]
     for j in range(1, rows):
-        p.append(part(solved, j) * part(inv_ref, j) + part(scaled_ref, j) * p[-1])
+        p.append(part(solved, j) * inv[j] + scaled[j] * p[-1])
     for j in range(rows - 2, -1, -1):
-        p[j] = p[j] + part(chain_ref, j) * p[j + 1]
+        p[j] = p[j] + chain[j] * p[j + 1]
     for j in range(rows):
         p_ref[j * width : (j + 1) * width] = p[j]
 
@@ -463,32 +445,21 @@
     modes, outer = lax.optimization_barrier((modes, outer))
     late_outer_came = swap(outer, 1, range(1, grp_count))
 
-    own_heights, inv, scaled, chain, u, v, left_gain, right_gain, joint = pl.pallas_call(
-        functools.partial(matrix_kernel, sizes),
-        out_shape=(jax.ShapeDtypeStruct(((rows + 2) * chunks, LANES), f32),)
-        + (lines(rows),) * 5
+    sent, p, u, v, left_gain, right_gain, joint = pl.pallas_call(
+        functools.partial(main_kernel, sizes),
+        out_shape=(lines(wide_count),)
+        + (lines(rows),) * 3
         + (lines(wide_count),) * 2
         + (lines(8),),
         scratch_shapes=[
             pltpu.VMEM(((row_total + 2) * chunks, LANES), f32),
             pltpu.VMEM((4 * wide_count * width, LANES), f32),
             pltpu.VMEM((2 * wide_count * width, LANES), f32),
-        ],
-        compiler_params=limit,
-    )(modes)
-
-    sent, p = pl.pallas_call(
-        functools.partial(first_kernel, sizes),
-        out_shape=(lines(wide_count), lines(rows)),
-        scratch_shapes=[
             pltpu.VMEM(((rows + 2) * width, LANES), f32),
             pltpu.VMEM((rows * width, LANES), f32),
         ],
         compiler_params=limit,
-    )(
-        field_lines, inner_came, outer_came, late_outer_came, conduct_lines,
-        own_heights, inv, scaled, chain, joint,
-    )
+    )(modes, field_lines, inner_came, outer_came, late_outer_came, conduct_lines)
 
     came = lax.all_to_all(
         sent.reshape(wide_count, width, LANES), "wide", split_axis=0, concat_axis=0

time: 32.7 us -> 33.6 us (1.028)
  blocking collectives: 24.5 us -> 25.6 us
  Pallas kernels: 5.9 us -> 5.25 us
  waiting for transfers between devices: 0.01 us -> 0.5 us
    all_to_all x1, blocking collectives: 11.9 us -> 13 us  [on_device(): lax.all_to_all(sent.reshape(wide_count, width, LANES), 'wide', split_axis...]
    pallas_call x2 -> x1, Pallas kernels: 4.1 us -> 3.44 us  [on_device(): pl.pallas_call(functools.partial(main_kernel, sizes), out_shape=(lines(wi...]
    ppermute x3, waiting for transfers between devices: 0.01 us -> 0.5 us  [swap(): return lax.ppermute(rows_sent, ('grp', 'wide'), pairs)]
  transfers between devices with their start and end apart: 3 -> 3, of which waited for: 0 -> 1; matrix products, arithmetic and copies ran while one was open for 0% -> 0% of each run, Pallas kernels for 5% -> 0%
where the time goes in v5:
time: 33.6 us; the launch traced here: 33.4 us
  blocking collectives  25.6 us (76%)
  Pallas kernels  5.25 us (16%)
  starting transfers between devices  1.38 us (4%)
  between operations  0.7 us (2%)
  waiting for transfers between devices  0.5 us (1%)
    all_to_all x1, blocking collectives, on_device(): lax.all_to_all(sent.reshape(wide_count, width, LANES), 'wide', split_axis...  13 us
    all_gather x1, blocking collectives, on_device(): modes = lax.all_gather(packed, 'grp', axis=0, tiled=True)  12.6 us
    pallas_call x1, Pallas kernels, on_device(): pl.pallas_call(functools.partial(main_kernel, sizes), out_shape=(lines(wi...  3.44 us
    ppermute x3, starting transfers between devices, swap(): return lax.ppermute(rows_sent, ('grp', 'wide'), pairs)  1.38 us
    pallas_call x1, Pallas kernels, on_device(): pl.pallas_call(load_kernel, out_shape=(jax.ShapeDtypeStruct((mode_index.s...  1.08 us
    pallas_call x1, Pallas kernels, on_device(): pl.pallas_call(functools.partial(last_kernel, sizes), out_shape=lines(row...  0.73 us
  transfers between devices with their start and end apart: 3, of which 1 were waited for; matrix products, arithmetic and copies ran while one was open for 0% of the time, Pallas kernels for 0%

profile of v5, /device:TPU:0, one launch (start us, length us, event | category | flops | bytes accessed | tf_op | source)
XLA Modules:
  0.0 33.4 jit_solution(12163494984760287077)
XLA Ops:
  0.7 1.1 %shard_map.64 = (f32[2,8]{1,0:T(2,128)S(1)}, f32[256,128]{1,0:T(8,128)S(1)}, f32[256,128]{1,0:T(8,128)S(1)}, f32[32,128]{1,0:T(8,128)S(1)}, f32[32,128]{1,0:T(8,128)S(1)}) custom-call(s32[1]{0:T(128)S(6)} %copy.13.step_ref, s32[2,3]{1,0:T(2,128)} %index_ref.1, f32[2]{0:T(128)} %amp_ref.1, f32[2]{0:T(128)} %phase_ref.1, f32[256,128]{1,0:T(8,128)} %bitcast.23, ...), custom_call_target="tpu_custom_call" | custom-call | tf_op jit(solution)/shard_map/pallas_call | solution.py:410
  1.7 12.6 %all-gather = f32[4,2,8]{2,1,0:T(2,128)S(1)} all-gather(f32[1,2,8]{2,1,0:T(2,128)S(1)} %bitcast.22), channel_id=1, replica_groups=mesh['grp'=4,'wide'=8] {'grp'}, dimensions={0}, use_global_device_ids=true | all-gather | bytes 320 | tf_op jit(solution)/shard_map/all_gather | solution.py:444
  14.4 0.7 %collective-permute-start.2 = (f32[32,128]{1,0:T(8,128)S(1)}, f32[32,128]{1,0:T(8,128)S(1)}, u32[]{:S(2)}, u32[]{:S(2)}) collective-permute-start(f32[32,128]{1,0:T(8,128)S(1)} %get-tuple-element.24), channel_id=1, source_target_pairs={{9,10},{10,9},{11,12},{12,11},{13,14},{14,13},{17,18},{18,17},{19,... | collective-permute-start | bytes 49160 | tf_op jit(solution)/shard_map/ppermute | solution.py:440
  15.0 0.1 collective-permute-start
  15.1 0.7 %collective-permute-start.1 = (f32[32,128]{1,0:T(8,128)S(1)}, f32[32,128]{1,0:T(8,128)S(1)}, u32[]{:S(2)}, u32[]{:S(2)}) collective-permute-start(f32[32,128]{1,0:T(8,128)S(1)} %get-tuple-element.24), channel_id=1, source_target_pairs={{1,2},{2,1},{3,4},{4,3},{5,6},{6,5}} | collective-permute-start | bytes 49160 | tf_op jit(solution)/shard_map/ppermute | solution.py:440
  15.8 0.0 collective-permute-done.2.late_outer_ref
  15.8 0.5 %collective-permute-done.inner_ref = f32[32,128]{1,0:T(8,128)S(1)} collective-permute-done((f32[32,128]{1,0:T(8,128)S(1)}, f32[32,128]{1,0:T(8,128)S(1)}, u32[]{:S(2)}, u32[]{:S(2)}) %collective-permute-start) | collective-permute-done | bytes 16416 | tf_op jit(solution)/shard_map/ppermute | solution.py:440
  16.3 0.0 collective-permute-done.1.outer_ref
  16.3 3.4 %shard_map.65 = (f32[256,128]{1,0:T(8,128)S(1)}, f32[256,128]{1,0:T(8,128)S(1)}, f32[256,128]{1,0:T(8,128)S(1)}, f32[256,128]{1,0:T(8,128)S(1)}, f32[256,128]{1,...) custom-call(f32[8,8]{1,0:T(8,128)S(1)} %bitcast.21, f32[256,128]{1,0:T(8,128)S(1)} %get-tuple-element.22.field_ref, ...), custom_call_target="tpu_custom_call" | custom-call | tf_op jit(solution)/shard_map/pallas_call | solution.py:448
  19.7 13.0 %all_to_all.5 = f32[8,32,128]{2,1,0:T(8,128)S(1)} all-to-all(f32[8,32,128]{2,1,0:T(8,128)S(1)} %bitcast.20), channel_id=1, replica_groups=mesh['grp'=4,'wide'=8] {'wide'}, dimensions={0} | all-to-all | bytes 262144 | tf_op jit(solution)/shard_map/all_to_all | solution.py:464
  32.7 0.7 %shard_map.66 = f32[256,128]{1,0:T(8,128)} custom-call(f32[256,128]{1,0:T(8,128)S(1)} %bitcast.19, f32[256,128]{1,0:T(8,128)S(1)} %get-tuple-element.27.left_gain_ref, f32[256,128]{1,0:T(8,128)S(1)} %get-tuple-element.28.right_gain_ref, f32[256,128]{1,0:T(8,128)S(1)} %get-tuple-element.29.joint_ref, f32[256,128]{1,0:T(8,128)S(1)} %get-tuple-element.30.p_ref, ...), custom_call_target="tpu_custom_call" | custom-call | tf_op jit(solution)/shard_map/pallas_call | solution.py:468
Async XLA Ops:
  14.4 1.4 %collective-permute-start.2 = (f32[32,128]{1,0:T(8,128)S(1)}, f32[32,128]{1,0:T(8,128)S(1)}, u32[]{:S(2)}, u32[]{:S(2)}) collective-permute-start(f32[32,128]{1,0:T(8,128)S(1)} %get-tuple-element.24), channel_id=1, source_target_pairs={{9,10},{10,9},{11,12},{12,11},{13,14},{14,13},{17,18},{18,17},{19,... | collective-permute-start | bytes 49160 | tf_op jit(solution)/shard_map/ppermute | solution.py:440
  15.0 1.2 %collective-permute-start = (f32[32,128]{1,0:T(8,128)S(1)}, f32[32,128]{1,0:T(8,128)S(1)}, u32[]{:S(2)}, u32[]{:S(2)}) collective-permute-start(f32[32,128]{1,0:T(8,128)S(1)} %get-tuple-element.23), channel_id=1, source_target_pairs={{0,1},{1,0},{2,3},{3,2},{4,5},{5,4},{6,7},{7,6},{8,9},{9,8},{10,11... | collective-permute-start | bytes 49160 | tf_op jit(solution)/shard_map/ppermute | solution.py:440
  15.1 1.2 %collective-permute-start.1 = (f32[32,128]{1,0:T(8,128)S(1)}, f32[32,128]{1,0:T(8,128)S(1)}, u32[]{:S(2)}, u32[]{:S(2)}) collective-permute-start(f32[32,128]{1,0:T(8,128)S(1)} %get-tuple-element.24), channel_id=1, source_target_pairs={{1,2},{2,1},{3,4},{4,3},{5,6},{6,5}} | collective-permute-start | bytes 49160 | tf_op jit(solution)/shard_map/ppermute | solution.py:440

commit v6 on v5

--- a/solution.py
+++ b/solution.py
@@ -199,25 +199,37 @@
         copy.wait()
 
 
-def condense(face):
-    inv, scaled, u, v = [], [], [], []
+def block_factors(face):
+    inv, scaled, chain, u = [], [], [], []
     rows = len(face) - 1
+    rest = 1.0 + face[0]
     for j in range(rows):
-        d = 1.0 + (face[j] + face[j + 1])
-        if j == 0:
-            inv.append(inverse(d))
-            scaled.append(face[0] * inv[0])
-            u.append(scaled[0])
-        else:
-            inv.append(inverse(d - face[j] * v[-1]))
-            scaled.append(face[j] * inv[-1])
-            u.append(scaled[-1] * u[-1])
-        v.append(face[j + 1] * inv[-1])
-    u_all, v_all = list(u), list(v)
+        inv.append(inverse(rest + face[j + 1]))
+        scaled.append(face[j] * inv[j])
+        chain.append(face[j + 1] * inv[j])
+        u.append(scaled[j] * u[-1] if j else scaled[j])
+        rest = 1.0 + rest * chain[j]
+    v = list(chain)
     for j in range(rows - 2, -1, -1):
-        u_all[j] = u[j] + v[j] * u_all[j + 1]
-        v_all[j] = v[j] * v_all[j + 1]
-    return inv, scaled, v, u_all, v_all
+        u[j] = u[j] + chain[j] * u[j + 1]
+        v[j] = chain[j] * v[j + 1]
+    return inv, scaled, chain, u, v
+
+
+def block_ends(face):
+    rows = len(face) - 1
+    down = 1.0 + face[0]
+    up = 1.0 + face[rows]
+    v_first = None
+    for j in range(rows):
+        v_last = face[j + 1] * inverse(down + face[j + 1])
+        v_first = v_last if v_first is None else v_first * v_last
+        u_first = face[rows - 1 - j] * inverse(up + face[rows - 1 - j])
+        if j < rows - 1:
+            down = 1.0 + down * v_last
+            up = 1.0 + up * u_first
+    u_last = v_first * (face[0] * inverse(face[rows]))
+    return u_first, v_first, u_last, v_last
 
 
 def main_kernel(
@@ -243,27 +255,27 @@
     own_start = pl.multiple_of(me * (rows * chunks), 8)
 
     def faces(start):
-        jac = []
-        for j in range(rows + 2):
-            h = heights[pl.ds(start + j * chunks, chunks), :]
-            jac.append(jnp.concatenate([1.0 + z * h for z in zeta], 0))
-        return [half * (jac[j] + jac[j + 1]) for j in range(rows + 1)]
-
-    def keep_ends(b, u, v):
+        h = [heights[pl.ds(start + j * chunks, chunks), :] for j in range(rows + 2)]
+        out = []
+        for j in range(rows + 1):
+            both = h[j] + h[j + 1]
+            out.append(jnp.concatenate([weight + (half * z) * both for z in zeta], 0))
+        return out
+
+    def keep_ends(b, values):
         base = pl.multiple_of(b * (4 * width), 8)
-        for n, value in enumerate((u[0], v[0], u[-1], v[-1])):
+        for n, value in enumerate(values):
             ends[pl.ds(base + n * width, width), :] = value
 
-    inv, scaled, chain, u, v = condense(faces(own_start))
+    inv, scaled, chain, u, v = block_factors(faces(own_start))
     for j in range(rows):
         u_ref[j * width : (j + 1) * width] = u[j]
         v_ref[j * width : (j + 1) * width] = v[j]
-    keep_ends(me, u, v)
+    keep_ends(me, (u[0], v[0], u[-1], v[-1]))
 
     def other_block(n):
         b = lax.rem(me + 1 + n, blocks)
-        _, _, _, u, v = condense(faces(pl.multiple_of(b * (rows * chunks), 8)))
-        keep_ends(b, u, v)
+        keep_ends(b, block_ends(faces(pl.multiple_of(b * (rows * chunks), 8))))
 
     if blocks <= 8:
         for n in range(blocks - 1):
@@ -308,9 +320,9 @@
     beyond = (rows + 1) * width
     framed[width:beyond] = field_ref[...]
     framed[pl.ds(pl.multiple_of((1 - odd) * beyond, 8), width), :] = inner_ref[...]
-    framed[pl.ds(pl.multiple_of(odd * beyond, 8), width), :] = (
-        outer_ref[...] + late_outer_ref[...]
-    )
+    outer_rows = jnp.where(first_layer == 0, outer_ref[...], late_outer_ref[...])
+    at_edge = (me == 0) | (me == blocks - 1)
+    framed[pl.ds(pl.multiple_of(odd * beyond, 8), width), :] = jnp.where(at_edge, 0.0, outer_rows)
     lane = lax.broadcasted_iota(jnp.int32, (rows, LANES), 1)
     at_start = lane == 0
     at_end = lane == LANES - 1
@@ -434,13 +446,17 @@
 
     def swap(rows_sent, first, groups):
         pairs = []
-        for g in groups:
-            for i in range(g * wide_count + first, (g + 1) * wide_count - 1, 2):
-                pairs += [(i, i + 1), (i + 1, i)]
+        for g in range(grp_count):
+            for i in range(wide_count):
+                partner = i + 1 if (i - first) % 2 == 0 else i - 1
+                if g not in groups or not 0 <= partner < wide_count:
+                    partner = i
+                pairs.append((g * wide_count + i, g * wide_count + partner))
         return lax.ppermute(rows_sent, ("grp", "wide"), pairs)
 
     inner_came = swap(inner, 0, range(grp_count))
     outer_came = swap(outer, 1, [0])
+    packed, inner_came, outer_came = lax.optimization_barrier((packed, inner_came, outer_came))
     modes = lax.all_gather(packed, "grp", axis=0, tiled=True)
     modes, outer = lax.optimization_barrier((modes, outer))
     late_outer_came = swap(outer, 1, range(1, grp_count))

time: 33.6 us -> 34.2 us (1.018)
  the two profiles are of different devices: /device:TPU:0 before, /device:TPU:8 now
where the time goes in v6:
time: 34.2 us; the launch traced here: 34 us
  blocking collectives  26.2 us (77%)
  Pallas kernels  5.23 us (15%)
  starting transfers between devices  1.38 us (4%)
  between operations  0.7 us (2%)
  waiting for transfers between devices  0.51 us (1%)
    all_to_all x1, blocking collectives, on_device(): lax.all_to_all(sent.reshape(wide_count, width, LANES), 'wide', split_axis...  18 us
    all_gather x1, blocking collectives, on_device(): modes = lax.all_gather(packed, 'grp', axis=0, tiled=True)  8.22 us
    pallas_call x1, Pallas kernels, on_device(): pl.pallas_call(functools.partial(main_kernel, sizes), out_shape=(lines(wi...  3.42 us
    ppermute x3, starting transfers between devices, swap(): return lax.ppermute(rows_sent, ('grp', 'wide'), pairs)  1.38 us
    pallas_call x1, Pallas kernels, on_device(): pl.pallas_call(load_kernel, out_shape=(jax.ShapeDtypeStruct((mode_index.s...  1.08 us
    pallas_call x1, Pallas kernels, on_device(): pl.pallas_call(functools.partial(last_kernel, sizes), out_shape=lines(row...  0.73 us
  transfers between devices with their start and end apart: 3, of which 1 were waited for; matrix products, arithmetic and copies ran while one was open for 0% of the time, Pallas kernels for 0%

profile of v6, /device:TPU:8, one launch (start us, length us, event | category | flops | bytes accessed | tf_op | source)
XLA Modules:
  0.0 34.0 jit_solution(13060784351938329500)
XLA Ops:
  0.7 1.1 %shard_map.64 = (f32[2,8]{1,0:T(2,128)S(1)}, f32[256,128]{1,0:T(8,128)S(1)}, f32[256,128]{1,0:T(8,128)S(1)}, f32[32,128]{1,0:T(8,128)S(1)}, f32[32,128]{1,0:T(8,128)S(1)}) custom-call(s32[1]{0:T(128)S(6)} %copy.13.step_ref, s32[2,3]{1,0:T(2,128)} %index_ref.1, f32[2]{0:T(128)} %amp_ref.1, f32[2]{0:T(128)} %phase_ref.1, f32[256,128]{1,0:T(8,128)} %bitcast.23, ...), custom_call_target="tpu_custom_call" | custom-call | tf_op jit(solution)/shard_map/pallas_call | solution.py:422
  1.7 0.1 collective-permute-start
  1.8 0.7 %collective-permute-start.1 = (f32[32,128]{1,0:T(8,128)S(1)}, f32[32,128]{1,0:T(8,128)S(1)}, u32[]{:S(2)}, u32[]{:S(2)}) collective-permute-start(f32[32,128]{1,0:T(8,128)S(1)} %get-tuple-element.30), channel_id=1, source_target_pairs={{0,0},{1,2},{2,1},{3,4},{4,3},{5,6},{6,5},{7,7},{8,8},{9,9},{10,10... | collective-permute-start | bytes 49160 | tf_op jit(solution)/shard_map/ppermute | solution.py:455
  2.5 0.5 %collective-permute-done.inner_ref = f32[32,128]{1,0:T(8,128)S(1)} collective-permute-done((f32[32,128]{1,0:T(8,128)S(1)}, f32[32,128]{1,0:T(8,128)S(1)}, u32[]{:S(2)}, u32[]{:S(2)}) %collective-permute-start) | collective-permute-done | bytes 16416 | tf_op jit(solution)/shard_map/ppermute | solution.py:455
  3.0 0.0 collective-permute-done.1.outer_ref
  3.0 8.2 %all-gather = f32[4,2,8]{2,1,0:T(2,128)S(1)} all-gather(f32[1,2,8]{2,1,0:T(2,128)S(1)} %bitcast.22), channel_id=1, replica_groups=mesh['grp'=4,'wide'=8] {'grp'}, dimensions={0}, use_global_device_ids=true | all-gather | bytes 320 | tf_op jit(solution)/shard_map/all_gather | solution.py:460
  11.2 0.7 %collective-permute-start.2 = (f32[32,128]{1,0:T(8,128)S(1)}, f32[32,128]{1,0:T(8,128)S(1)}, u32[]{:S(2)}, u32[]{:S(2)}) collective-permute-start(f32[32,128]{1,0:T(8,128)S(1)} %get-tuple-element.30), channel_id=1, source_target_pairs={{0,0},{1,1},{2,2},{3,3},{4,4},{5,5},{6,6},{7,7},{8,8},{9,10},{10,9... | collective-permute-start | bytes 49160 | tf_op jit(solution)/shard_map/ppermute | solution.py:455
  11.9 0.0 collective-permute-done.2.late_outer_ref
  11.9 3.4 %shard_map.65 = (f32[256,128]{1,0:T(8,128)S(1)}, f32[256,128]{1,0:T(8,128)S(1)}, f32[256,128]{1,0:T(8,128)S(1)}, f32[256,128]{1,0:T(8,128)S(1)}, f32[256,128]{1,...) custom-call(f32[8,8]{1,0:T(8,128)S(1)} %bitcast.21, f32[256,128]{1,0:T(8,128)S(1)} %get-tuple-element.27.field_ref, ...), custom_call_target="tpu_custom_call" | custom-call | tf_op jit(solution)/shard_map/pallas_call | solution.py:464
  15.3 18.0 %all_to_all.5 = f32[8,32,128]{2,1,0:T(8,128)S(1)} all-to-all(f32[8,32,128]{2,1,0:T(8,128)S(1)} %bitcast.20), channel_id=1, replica_groups=mesh['grp'=4,'wide'=8] {'wide'}, dimensions={0} | all-to-all | bytes 262144 | tf_op jit(solution)/shard_map/all_to_all | solution.py:480
  33.3 0.7 %shard_map.66 = f32[256,128]{1,0:T(8,128)} custom-call(f32[256,128]{1,0:T(8,128)S(1)} %bitcast.19, f32[256,128]{1,0:T(8,128)S(1)} %get-tuple-element.33.left_gain_ref, f32[256,128]{1,0:T(8,128)S(1)} %get-tuple-element.34.right_gain_ref, f32[256,128]{1,0:T(8,128)S(1)} %get-tuple-element.35.joint_ref, f32[256,128]{1,0:T(8,128)S(1)} %get-tuple-element.36.p_ref, ...), custom_call_target="tpu_custom_call" | custom-call | tf_op jit(solution)/shard_map/pallas_call | solution.py:484
Async XLA Ops:
  1.7 1.2 %collective-permute-start = (f32[32,128]{1,0:T(8,128)S(1)}, f32[32,128]{1,0:T(8,128)S(1)}, u32[]{:S(2)}, u32[]{:S(2)}) collective-permute-start(f32[32,128]{1,0:T(8,128)S(1)} %get-tuple-element.23), channel_id=1, source_target_pairs={{0,1},{1,0},{2,3},{3,2},{4,5},{5,4},{6,7},{7,6},{8,9},{9,8},{10,11... | collective-permute-start | bytes 49160 | tf_op jit(solution)/shard_map/ppermute | solution.py:455
  1.8 1.2 %collective-permute-start.1 = (f32[32,128]{1,0:T(8,128)S(1)}, f32[32,128]{1,0:T(8,128)S(1)}, u32[]{:S(2)}, u32[]{:S(2)}) collective-permute-start(f32[32,128]{1,0:T(8,128)S(1)} %get-tuple-element.30), channel_id=1, source_target_pairs={{0,0},{1,2},{2,1},{3,4},{4,3},{5,6},{6,5},{7,7},{8,8},{9,9},{10,10... | collective-permute-start | bytes 49160 | tf_op jit(solution)/shard_map/ppermute | solution.py:455
  11.2 0.7 %collective-permute-start.2 = (f32[32,128]{1,0:T(8,128)S(1)}, f32[32,128]{1,0:T(8,128)S(1)}, u32[]{:S(2)}, u32[]{:S(2)}) collective-permute-start(f32[32,128]{1,0:T(8,128)S(1)} %get-tuple-element.30), channel_id=1, source_target_pairs={{0,0},{1,1},{2,2},{3,3},{4,4},{5,5},{6,6},{7,7},{8,8},{9,10},{10,9... | collective-permute-start | bytes 49160 | tf_op jit(solution)/shard_map/ppermute | solution.py:455

commit v7 on v6

--- a/solution.py
+++ b/solution.py
@@ -232,10 +232,23 @@
     return u_first, v_first, u_last, v_last
 
 
+def height_kernel(sizes, modes_ref, inner_ref, outer_ref, heights_ref, halo_ref):
+    rows, layers, chunks, row_total, layer_total, column_total = sizes
+    width = layers * chunks
+    body = height_lines(modes_ref[...], 0, row_total, row_total, chunks, column_total)
+    heights_ref[chunks : (row_total + 1) * chunks] = body
+    heights_ref[0:chunks] = body[0:chunks]
+    heights_ref[(row_total + 1) * chunks : (row_total + 2) * chunks] = body[
+        (row_total - 1) * chunks : row_total * chunks
+    ]
+    halo_ref[0:width] = inner_ref[...]
+    halo_ref[width : 2 * width] = outer_ref[...]
+
+
 def main_kernel(
-    sizes, modes_ref, field_ref, inner_ref, outer_ref, late_outer_ref, conduct_ref,
+    sizes, heights, halo_ref, field_ref, late_outer_ref, conduct_ref,
     sent_ref, p_ref, u_ref, v_ref, left_gain_ref, right_gain_ref, joint_ref,
-    heights, ends, links, framed, solved,
+    ends, links, framed, solved,
 ):
     rows, layers, chunks, row_total, layer_total, column_total = sizes
     width = layers * chunks
@@ -246,12 +259,6 @@
         ((first_layer + k).astype(f32) + 0.5) * (1.0 / layer_total) for k in range(layers)
     ]
     half = 0.5 * weight
-    body = height_lines(modes_ref[...], 0, row_total, row_total, chunks, column_total)
-    heights[chunks : (row_total + 1) * chunks] = body
-    heights[0:chunks] = body[0:chunks]
-    heights[(row_total + 1) * chunks : (row_total + 2) * chunks] = body[
-        (row_total - 1) * chunks : row_total * chunks
-    ]
     own_start = pl.multiple_of(me * (rows * chunks), 8)
 
     def faces(start):
@@ -319,8 +326,8 @@
     odd = lax.rem(me, 2)
     beyond = (rows + 1) * width
     framed[width:beyond] = field_ref[...]
-    framed[pl.ds(pl.multiple_of((1 - odd) * beyond, 8), width), :] = inner_ref[...]
-    outer_rows = jnp.where(first_layer == 0, outer_ref[...], late_outer_ref[...])
+    framed[pl.ds(pl.multiple_of((1 - odd) * beyond, 8), width), :] = halo_ref[0:width]
+    outer_rows = jnp.where(first_layer == 0, halo_ref[width : 2 * width], late_outer_ref[...])
     at_edge = (me == 0) | (me == blocks - 1)
     framed[pl.ds(pl.multiple_of(odd * beyond, 8), width), :] = jnp.where(at_edge, 0.0, outer_rows)
     lane = lax.broadcasted_iota(jnp.int32, (rows, LANES), 1)
@@ -456,10 +463,15 @@
 
     inner_came = swap(inner, 0, range(grp_count))
     outer_came = swap(outer, 1, [0])
-    packed, inner_came, outer_came = lax.optimization_barrier((packed, inner_came, outer_came))
     modes = lax.all_gather(packed, "grp", axis=0, tiled=True)
     modes, outer = lax.optimization_barrier((modes, outer))
     late_outer_came = swap(outer, 1, range(1, grp_count))
+
+    heights, halo = pl.pallas_call(
+        functools.partial(height_kernel, sizes),
+        out_shape=(jax.ShapeDtypeStruct(((row_total + 2) * chunks, LANES), f32), lines(2)),
+        compiler_params=limit,
+    )(modes, inner_came, outer_came)
 
     sent, p, u, v, left_gain, right_gain, joint = pl.pallas_call(
         functools.partial(main_kernel, sizes),
@@ -468,14 +480,13 @@
         + (lines(wide_count),) * 2
         + (lines(8),),
         scratch_shapes=[
-            pltpu.VMEM(((row_total + 2) * chunks, LANES), f32),
             pltpu.VMEM((4 * wide_count * width, LANES), f32),
             pltpu.VMEM((2 * wide_count * width, LANES), f32),
             pltpu.VMEM(((rows + 2) * width, LANES), f32),
             pltpu.VMEM((rows * width, LANES), f32),
         ],
         compiler_params=limit,
-    )(modes, field_lines, inner_came, outer_came, late_outer_came, conduct_lines)
+    )(heights, halo, field_lines, late_outer_came, conduct_lines)
 
     came = lax.all_to_all(
         sent.reshape(wide_count, width, LANES), "wide", split_axis=0, concat_axis=0

time: 34.2 us -> 31.2 us (0.912)
  blocking collectives: 26.2 us -> 23.4 us
  waiting for transfers between devices: 0.51 us -> 0.01 us
    all_to_all x1, blocking collectives: 18 us -> 15.1 us  [on_device(): lax.all_to_all(sent.reshape(wide_count, width, LANES), 'wide', split_axis...]
    pallas_call x0 -> x1, Pallas kernels: none -> 0.78 us  [on_device(): pl.pallas_call(functools.partial(height_kernel, sizes), out_shape=(jax.Sh...]
    ppermute x3, waiting for transfers between devices: 0.51 us -> 0.01 us  [swap(): return lax.ppermute(rows_sent, ('grp', 'wide'), pairs)]
    pallas_call x1, Pallas kernels: 3.42 us -> 2.96 us  [on_device(): pl.pallas_call(functools.partial(main_kernel, sizes), out_shape=(lines(wi...]
  transfers between devices with their start and end apart: 3 -> 3, of which waited for: 1 -> 0; matrix products, arithmetic and copies ran while one was open for 0% -> 0% of each run, Pallas kernels for 0% -> 3%
where the time goes in v7:
time: 31.2 us; the launch traced here: 31 us
  blocking collectives  23.4 us (75%)
  Pallas kernels  5.53 us (18%)
  starting transfers between devices  1.38 us (4%)
  between operations  0.72 us (2%)
    all_to_all x1, blocking collectives, on_device(): lax.all_to_all(sent.reshape(wide_count, width, LANES), 'wide', split_axis...  15.1 us
    all_gather x1, blocking collectives, on_device(): modes = lax.all_gather(packed, 'grp', axis=0, tiled=True)  8.23 us
    pallas_call x1, Pallas kernels, on_device(): pl.pallas_call(functools.partial(main_kernel, sizes), out_shape=(lines(wi...  2.96 us
    ppermute x3, starting transfers between devices, swap(): return lax.ppermute(rows_sent, ('grp', 'wide'), pairs)  1.38 us
    pallas_call x1, Pallas kernels, on_device(): pl.pallas_call(load_kernel, out_shape=(jax.ShapeDtypeStruct((mode_index.s...  1.08 us
    pallas_call x1, Pallas kernels, on_device(): pl.pallas_call(functools.partial(height_kernel, sizes), out_shape=(jax.Sh...  0.78 us
    pallas_call x1, Pallas kernels, on_device(): pl.pallas_call(functools.partial(last_kernel, sizes), out_shape=lines(row...  0.72 us
  transfers between devices with their start and end apart: 3, of which 0 were waited for; matrix products, arithmetic and copies ran while one was open for 0% of the time, Pallas kernels for 3%

profile of v7, /device:TPU:8, one launch (start us, length us, event | category | flops | bytes accessed | tf_op | source)
XLA Modules:
  0.0 31.0 jit_solution(14982178753615517730)
XLA Ops:
  0.7 1.1 %shard_map.64 = (f32[2,8]{1,0:T(2,128)S(1)}, f32[256,128]{1,0:T(8,128)S(1)}, f32[256,128]{1,0:T(8,128)S(1)}, f32[32,128]{1,0:T(8,128)S(1)}, f32[32,128]{1,0:T(8,128)S(1)}) custom-call(s32[1]{0:T(128)S(6)} %copy.13.step_ref, s32[2,3]{1,0:T(2,128)} %index_ref.1, f32[2]{0:T(128)} %amp_ref.1, f32[2]{0:T(128)} %phase_ref.1, f32[256,128]{1,0:T(8,128)} %bitcast.23, ...), custom_call_target="tpu_custom_call" | custom-call | tf_op jit(solution)/shard_map/pallas_call | solution.py:429
  1.7 0.1 collective-permute-start
  1.8 0.7 %collective-permute-start.1 = (f32[32,128]{1,0:T(8,128)S(1)}, f32[32,128]{1,0:T(8,128)S(1)}, u32[]{:S(2)}, u32[]{:S(2)}) collective-permute-start(f32[32,128]{1,0:T(8,128)S(1)} %get-tuple-element.28), channel_id=1, source_target_pairs={{0,0},{1,2},{2,1},{3,4},{4,3},{5,6},{6,5},{7,7},{8,8},{9,9},{10,10... | collective-permute-start | bytes 49160 | tf_op jit(solution)/shard_map/ppermute | solution.py:462
  2.5 8.2 %all-gather = f32[4,2,8]{2,1,0:T(2,128)S(1)} all-gather(f32[1,2,8]{2,1,0:T(2,128)S(1)} %bitcast.22), channel_id=1, replica_groups=mesh['grp'=4,'wide'=8] {'grp'}, dimensions={0}, use_global_device_ids=true | all-gather | bytes 320 | tf_op jit(solution)/shard_map/all_gather | solution.py:466
  10.7 0.7 %collective-permute-start.2 = (f32[32,128]{1,0:T(8,128)S(1)}, f32[32,128]{1,0:T(8,128)S(1)}, u32[]{:S(2)}, u32[]{:S(2)}) collective-permute-start(f32[32,128]{1,0:T(8,128)S(1)} %get-tuple-element.28), channel_id=1, source_target_pairs={{0,0},{1,1},{2,2},{3,3},{4,4},{5,5},{6,6},{7,7},{8,8},{9,10},{10,9... | collective-permute-start | bytes 49160 | tf_op jit(solution)/shard_map/ppermute | solution.py:462
  11.4 0.0 collective-permute-done.inner_ref
  11.4 0.0 collective-permute-done.1.outer_ref
  11.4 0.8 %shard_map.65 = (f32[1056,128]{1,0:T(8,128)S(1)}, f32[64,128]{1,0:T(8,128)S(1)}) custom-call(f32[8,8]{1,0:T(8,128)S(1)} %bitcast.21, f32[32,128]{1,0:T(8,128)S(1)} %collective-permute-done.inner_ref, f32[32,128]{1,0:T(8,128)S(1)} %collective-permute-done.1.outer_ref), custom_call_target="tpu_custom_call" | custom-call | tf_op jit(solution)/shard_map/pallas_call | solution.py:470
  12.2 0.0 collective-permute-done.2.late_outer_ref
  12.2 3.0 %shard_map.66 = (f32[256,128]{1,0:T(8,128)S(1)}, f32[256,128]{1,0:T(8,128)S(1)}, f32[256,128]{1,0:T(8,128)S(1)}, f32[256,128]{1,0:T(8,128)S(1)}, f32[256,128]{1,...) custom-call(f32[1056,128]{1,0:T(8,128)S(1)} %get-tuple-element.25.heights, ...), custom_call_target="tpu_custom_call" | custom-call | tf_op jit(solution)/shard_map/pallas_call | solution.py:476
  15.2 15.1 %all_to_all.5 = f32[8,32,128]{2,1,0:T(8,128)S(1)} all-to-all(f32[8,32,128]{2,1,0:T(8,128)S(1)} %bitcast.20), channel_id=1, replica_groups=mesh['grp'=4,'wide'=8] {'wide'}, dimensions={0} | all-to-all | bytes 262144 | tf_op jit(solution)/shard_map/all_to_all | solution.py:491
  30.3 0.7 %shard_map.67 = f32[256,128]{1,0:T(8,128)} custom-call(f32[256,128]{1,0:T(8,128)S(1)} %bitcast.19, f32[256,128]{1,0:T(8,128)S(1)} %get-tuple-element.31.left_gain_ref, f32[256,128]{1,0:T(8,128)S(1)} %get-tuple-element.32.right_gain_ref, f32[256,128]{1,0:T(8,128)S(1)} %get-tuple-element.33.joint_ref, f32[256,128]{1,0:T(8,128)S(1)} %get-tuple-element.34.p_ref, ...), custom_call_target="tpu_custom_call" | custom-call | tf_op jit(solution)/shard_map/pallas_call | solution.py:495
Async XLA Ops:
  1.7 9.6 %collective-permute-start = (f32[32,128]{1,0:T(8,128)S(1)}, f32[32,128]{1,0:T(8,128)S(1)}, u32[]{:S(2)}, u32[]{:S(2)}) collective-permute-start(f32[32,128]{1,0:T(8,128)S(1)} %get-tuple-element.24), channel_id=1, source_target_pairs={{0,1},{1,0},{2,3},{3,2},{4,5},{5,4},{6,7},{7,6},{8,9},{9,8},{10,11... | collective-permute-start | bytes 49160 | tf_op jit(solution)/shard_map/ppermute | solution.py:462
  1.8 9.6 %collective-permute-start.1 = (f32[32,128]{1,0:T(8,128)S(1)}, f32[32,128]{1,0:T(8,128)S(1)}, u32[]{:S(2)}, u32[]{:S(2)}) collective-permute-start(f32[32,128]{1,0:T(8,128)S(1)} %get-tuple-element.28), channel_id=1, source_target_pairs={{0,0},{1,2},{2,1},{3,4},{4,3},{5,6},{6,5},{7,7},{8,8},{9,9},{10,10... | collective-permute-start | bytes 49160 | tf_op jit(solution)/shard_map/ppermute | solution.py:462
  10.7 1.5 %collective-permute-start.2 = (f32[32,128]{1,0:T(8,128)S(1)}, f32[32,128]{1,0:T(8,128)S(1)}, u32[]{:S(2)}, u32[]{:S(2)}) collective-permute-start(f32[32,128]{1,0:T(8,128)S(1)} %get-tuple-element.28), channel_id=1, source_target_pairs={{0,0},{1,1},{2,2},{3,3},{4,4},{5,5},{6,6},{7,7},{8,8},{9,10},{10,9... | collective-permute-start | bytes 49160 | tf_op jit(solution)/shard_map/ppermute | solution.py:462

commit v8 on v7

--- a/solution.py
+++ b/solution.py
@@ -61,6 +61,11 @@
     half_cos = series(0)
     half_sin = series(1) * part
     return 1.0 - 2.0 * half_sin * half_sin, 2.0 * half_sin * half_cos
+
+
+def halves(values):
+    high = values.astype(jnp.bfloat16)
+    return high, (values - high.astype(f32)).astype(jnp.bfloat16)
 
 
 def height_lines(modes, first_row, count, row_total, chunks, column_total):
@@ -80,11 +85,12 @@
     right_cos, right_sin = cos_sin(turns(wave_x, lane, column_total))
     left = jnp.concatenate([amp * left_cos, amp * left_sin], 0)
     right = jnp.concatenate([right_cos, -right_sin], 0)
+    left_high, left_low = halves(left)
+    right_high, right_low = halves(right)
     return lax.dot_general(
-        left,
-        right,
+        jnp.concatenate([left_high, left_high, left_low], 0),
+        jnp.concatenate([right_high, right_low, right_high], 0),
         (((0,), (0,)), ((), ())),
-        precision=lax.Precision.HIGHEST,
         preferred_element_type=f32,
     )
 
@@ -138,8 +144,7 @@
     return out
 
 
-def solve_x(diagonal, link, rhs, lane):
-    stride = 1
+def reduce_lanes(diagonal, link, rhs, lane, stride):
     count = len(rhs)
     while stride < LANES:
         inv = [inverse(d) for d in diagonal]
@@ -157,6 +162,54 @@
         link = [link[c] * high_w[c] for c in range(count)]
         stride *= 2
     return solve_chunks(diagonal, link, rhs)
+
+
+def pack_pair(a, b, odd_lane):
+    even = [jnp.where(odd_lane, pltpu.roll(x, 1, 1), y) for x, y in zip(a, b)]
+    odd = [jnp.where(odd_lane, x, pltpu.roll(y, LANES - 1, 1)) for x, y in zip(a, b)]
+    return even, odd
+
+
+def unpack_pair(even, odd, odd_lane):
+    a = [jnp.where(odd_lane, y, pltpu.roll(x, LANES - 1, 1)) for x, y in zip(even, odd)]
+    b = [jnp.where(odd_lane, pltpu.roll(y, 1, 1), x) for x, y in zip(even, odd)]
+    return a, b
+
+
+def solve_x_pair(g_pair, rhs_pair, lane):
+    odd_lane = (lane & 1) == 1
+    first_cell = lane < 2
+    last_cell = lane >= LANES - 2
+    half = 0.5 * weight
+    g_even, g_odd = pack_pair(*g_pair, odd_lane)
+    r_even, r_odd = pack_pair(*rhs_pair, odd_lane)
+    face = [half * (a + b) for a, b in zip(g_even, g_odd)]
+    after = from_right(g_even, 2, lane)
+    after[-1] = jnp.where(last_cell, g_odd[-1], after[-1])
+    face_after = [half * (a + b) for a, b in zip(g_odd, after)]
+    face_before = from_left(face_after, 2, lane)
+    face_before[0] = jnp.where(first_cell, weight * g_even[0], face_before[0])
+    inv = [inverse(1.0 + (a + b)) for a, b in zip(face_before, face)]
+    d_odd = [1.0 + (a + b) for a, b in zip(face, face_after)]
+    link = list(face_after)
+    link[-1] = jnp.where(last_cell, 0.0, link[-1])
+    link_before = list(face_before)
+    link_before[0] = jnp.where(first_cell, 0.0, link_before[0])
+    t = [q * r for q, r in zip(inv, r_even)]
+    w = [q * e for q, e in zip(inv, face)]
+    next_q = from_right(inv, 2, lane)
+    next_t = from_right(t, 2, lane)
+    next_w = from_right(w, 2, lane)
+    diagonal = [
+        d - e * v - l * (l * q) for d, e, v, l, q in zip(d_odd, face, w, link, next_q)
+    ]
+    rhs = [r + e * v + l * n for r, e, v, l, n in zip(r_odd, face, t, link, next_t)]
+    x_odd = reduce_lanes(diagonal, [l * n for l, n in zip(link, next_w)], rhs, lane, 2)
+    x_before = from_left(x_odd, 2, lane)
+    x_even = [
+        v + q * (l * b) + u * x for v, q, l, b, u, x in zip(t, inv, link_before, x_before, w, x_odd)
+    ]
+    return unpack_pair(x_even, x_odd, odd_lane)
 
 
 def load_kernel(
@@ -331,38 +384,32 @@
     at_edge = (me == 0) | (me == blocks - 1)
     framed[pl.ds(pl.multiple_of(odd * beyond, 8), width), :] = jnp.where(at_edge, 0.0, outer_rows)
     lane = lax.broadcasted_iota(jnp.int32, (rows, LANES), 1)
-    at_start = lane == 0
-    at_end = lane == LANES - 1
-
+    g, f, rhs = [], [], []
     for k in range(layers):
-        g, f, along = [], [], []
+        g.append([])
+        f.append([])
+        rhs.append([])
         for c in range(chunks):
-            jac_low, jac, jac_high = (
-                1.0 + zeta[k] * heights[pl.ds(own_start + s * chunks + c, rows, stride=chunks), :]
+            h_low, h, h_high = (
+                heights[pl.ds(own_start + s * chunks + c, rows, stride=chunks), :]
                 for s in range(3)
             )
             place = c * layers + k
             f_low, f_mid, f_high = (
                 framed[pl.ds(s * width + place, rows, stride=width), :] for s in range(3)
             )
-            g.append(conduct_ref[pl.ds(place, rows, stride=width), :] * jac)
-            f.append(f_mid)
-            along.append(
-                half * (jac + jac_high) * (f_high - f_mid)
-                - half * (jac + jac_low) * (f_mid - f_low)
-            )
-        g_next = from_right(g, 1, lane)
-        g_next[-1] = jnp.where(at_end, g[-1], g_next[-1])
-        face = [half * (a + b) for a, b in zip(g, g_next)]
-        face_low = from_left(face, 1, lane)
-        face_low[0] = jnp.where(at_start, weight * g[0], face_low[0])
-        diagonal = [1.0 + (a + b) for a, b in zip(face, face_low)]
-        rhs = [2.0 * (a + b) for a, b in zip(f, along)]
-        link = face
-        link[-1] = jnp.where(at_end, 0.0, link[-1])
-        both = solve_x(diagonal, link, rhs, lane)
-        for c in range(chunks):
-            solved[pl.ds(k * chunks + c, rows, stride=width), :] = both[c] - 2.0 * f[c]
+            g[k].append(conduct_ref[pl.ds(place, rows, stride=width), :] * (1.0 + zeta[k] * h))
+            f[k].append(f_mid)
+            along = (weight + (half * zeta[k]) * (h + h_high)) * (f_high - f_mid) - (
+                weight + (half * zeta[k]) * (h + h_low)
+            ) * (f_mid - f_low)
+            rhs[k].append(2.0 * (f_mid + along))
+    for k in range(0, layers, 2):
+        both = solve_x_pair(g[k : k + 2], rhs[k : k + 2], lane)
+        for n in range(2):
+            for c in range(chunks):
+                spot = pl.ds((k + n) * chunks + c, rows, stride=width)
+                solved[spot, :] = both[n][c] - 2.0 * f[k + n][c]
 
     def part(ref, j):
         return ref[j * width : (j + 1) * width]

time: 31.2 us -> 30.4 us (0.974)
  Pallas kernels: 5.53 us -> 4.33 us
  blocking collectives: 23.4 us -> 23.8 us
    pallas_call x1, Pallas kernels: 2.96 us -> 2.16 us  [on_device(): pl.pallas_call(functools.partial(main_kernel, sizes), out_shape=(lines(wi...]
    all_to_all x1, blocking collectives: 15.1 us -> 15.5 us  [on_device(): lax.all_to_all(sent.reshape(wide_count, width, LANES), 'wide', split_axis...]
    pallas_call x1, Pallas kernels: 0.78 us -> 0.37 us  [on_device(): pl.pallas_call(functools.partial(height_kernel, sizes), out_shape=(jax.Sh...]
  transfers between devices with their start and end apart: 3 -> 3, of which waited for: 0 -> 0; matrix products, arithmetic and copies ran while one was open for 0% -> 0% of each run, Pallas kernels for 3% -> 1%
where the time goes in v8:
time: 30.4 us; the launch traced here: 30.2 us
  blocking collectives  23.8 us (78%)
  Pallas kernels  4.33 us (14%)
  starting transfers between devices  1.38 us (5%)
  between operations  0.72 us (2%)
    all_to_all x1, blocking collectives, on_device(): lax.all_to_all(sent.reshape(wide_count, width, LANES), 'wide', split_axis...  15.5 us
    all_gather x1, blocking collectives, on_device(): modes = lax.all_gather(packed, 'grp', axis=0, tiled=True)  8.23 us
    pallas_call x1, Pallas kernels, on_device(): pl.pallas_call(functools.partial(main_kernel, sizes), out_shape=(lines(wi...  2.16 us
    ppermute x3, starting transfers between devices, swap(): return lax.ppermute(rows_sent, ('grp', 'wide'), pairs)  1.38 us
    pallas_call x1, Pallas kernels, on_device(): pl.pallas_call(load_kernel, out_shape=(jax.ShapeDtypeStruct((mode_index.s...  1.08 us
    pallas_call x1, Pallas kernels, on_device(): pl.pallas_call(functools.partial(last_kernel, sizes), out_shape=lines(row...  0.72 us
  transfers between devices with their start and end apart: 3, of which 0 were waited for; matrix products, arithmetic and copies ran while one was open for 0% of the time, Pallas kernels for 1%

profile of v8, /device:TPU:8, one launch (start us, length us, event | category | flops | bytes accessed | tf_op | source)
XLA Modules:
  0.0 30.2 jit_solution(1134331359122092440)
XLA Ops:
  0.7 1.1 %shard_map.64 = (f32[2,8]{1,0:T(2,128)S(1)}, f32[256,128]{1,0:T(8,128)S(1)}, f32[256,128]{1,0:T(8,128)S(1)}, f32[32,128]{1,0:T(8,128)S(1)}, f32[32,128]{1,0:T(8,128)S(1)}) custom-call(s32[1]{0:T(128)S(6)} %copy.13.step_ref, s32[2,3]{1,0:T(2,128)} %index_ref.1, f32[2]{0:T(128)} %amp_ref.1, f32[2]{0:T(128)} %phase_ref.1, f32[256,128]{1,0:T(8,128)} %bitcast.23, ...), custom_call_target="tpu_custom_call" | custom-call | tf_op jit(solution)/shard_map/pallas_call | solution.py:476
  1.7 0.1 collective-permute-start
  1.8 0.7 %collective-permute-start.1 = (f32[32,128]{1,0:T(8,128)S(1)}, f32[32,128]{1,0:T(8,128)S(1)}, u32[]{:S(2)}, u32[]{:S(2)}) collective-permute-start(f32[32,128]{1,0:T(8,128)S(1)} %get-tuple-element.28), channel_id=1, source_target_pairs={{0,0},{1,2},{2,1},{3,4},{4,3},{5,6},{6,5},{7,7},{8,8},{9,9},{10,10... | collective-permute-start | bytes 49160 | tf_op jit(solution)/shard_map/ppermute | solution.py:509
  2.5 8.2 %all-gather = f32[4,2,8]{2,1,0:T(2,128)S(1)} all-gather(f32[1,2,8]{2,1,0:T(2,128)S(1)} %bitcast.22), channel_id=1, replica_groups=mesh['grp'=4,'wide'=8] {'grp'}, dimensions={0}, use_global_device_ids=true | all-gather | bytes 320 | tf_op jit(solution)/shard_map/all_gather | solution.py:513
  10.7 0.7 %collective-permute-start.2 = (f32[32,128]{1,0:T(8,128)S(1)}, f32[32,128]{1,0:T(8,128)S(1)}, u32[]{:S(2)}, u32[]{:S(2)}) collective-permute-start(f32[32,128]{1,0:T(8,128)S(1)} %get-tuple-element.28), channel_id=1, source_target_pairs={{0,0},{1,1},{2,2},{3,3},{4,4},{5,5},{6,6},{7,7},{8,8},{9,10},{10,9... | collective-permute-start | bytes 49160 | tf_op jit(solution)/shard_map/ppermute | solution.py:509
  11.4 0.0 collective-permute-done.inner_ref
  11.4 0.0 collective-permute-done.1.outer_ref
  11.4 0.4 %shard_map.65 = (f32[1056,128]{1,0:T(8,128)S(1)}, f32[64,128]{1,0:T(8,128)S(1)}) custom-call(f32[8,8]{1,0:T(8,128)S(1)} %bitcast.21, f32[32,128]{1,0:T(8,128)S(1)} %collective-permute-done.inner_ref, f32[32,128]{1,0:T(8,128)S(1)} %collective-permute-done.1.outer_ref), custom_call_target="tpu_custom_call" | custom-call | tf_op jit(solution)/shard_map/pallas_call | solution.py:517
  11.8 0.0 collective-permute-done.2.late_outer_ref
  11.8 2.2 %shard_map.66 = (f32[256,128]{1,0:T(8,128)S(1)}, f32[256,128]{1,0:T(8,128)S(1)}, f32[256,128]{1,0:T(8,128)S(1)}, f32[256,128]{1,0:T(8,128)S(1)}, f32[256,128]{1,...) custom-call(f32[1056,128]{1,0:T(8,128)S(1)} %get-tuple-element.25.heights, ...), custom_call_target="tpu_custom_call" | custom-call | tf_op jit(solution)/shard_map/pallas_call | solution.py:523
  14.0 15.5 %all_to_all.5 = f32[8,32,128]{2,1,0:T(8,128)S(1)} all-to-all(f32[8,32,128]{2,1,0:T(8,128)S(1)} %bitcast.20), channel_id=1, replica_groups=mesh['grp'=4,'wide'=8] {'wide'}, dimensions={0} | all-to-all | bytes 262144 | tf_op jit(solution)/shard_map/all_to_all | solution.py:538
  29.5 0.7 %shard_map.67 = f32[256,128]{1,0:T(8,128)} custom-call(f32[256,128]{1,0:T(8,128)S(1)} %bitcast.19, f32[256,128]{1,0:T(8,128)S(1)} %get-tuple-element.31.left_gain_ref, f32[256,128]{1,0:T(8,128)S(1)} %get-tuple-element.32.right_gain_ref, f32[256,128]{1,0:T(8,128)S(1)} %get-tuple-element.33.joint_ref, f32[256,128]{1,0:T(8,128)S(1)} %get-tuple-element.34.p_ref, ...), custom_call_target="tpu_custom_call" | custom-call | tf_op jit(solution)/shard_map/pallas_call | solution.py:542
Async XLA Ops:
  1.7 9.6 %collective-permute-start = (f32[32,128]{1,0:T(8,128)S(1)}, f32[32,128]{1,0:T(8,128)S(1)}, u32[]{:S(2)}, u32[]{:S(2)}) collective-permute-start(f32[32,128]{1,0:T(8,128)S(1)} %get-tuple-element.24), channel_id=1, source_target_pairs={{0,1},{1,0},{2,3},{3,2},{4,5},{5,4},{6,7},{7,6},{8,9},{9,8},{10,11... | collective-permute-start | bytes 49160 | tf_op jit(solution)/shard_map/ppermute | solution.py:509
  1.8 9.6 %collective-permute-start.1 = (f32[32,128]{1,0:T(8,128)S(1)}, f32[32,128]{1,0:T(8,128)S(1)}, u32[]{:S(2)}, u32[]{:S(2)}) collective-permute-start(f32[32,128]{1,0:T(8,128)S(1)} %get-tuple-element.28), channel_id=1, source_target_pairs={{0,0},{1,2},{2,1},{3,4},{4,3},{5,6},{6,5},{7,7},{8,8},{9,9},{10,10... | collective-permute-start | bytes 49160 | tf_op jit(solution)/shard_map/ppermute | solution.py:509
  10.7 1.1 %collective-permute-start.2 = (f32[32,128]{1,0:T(8,128)S(1)}, f32[32,128]{1,0:T(8,128)S(1)}, u32[]{:S(2)}, u32[]{:S(2)}) collective-permute-start(f32[32,128]{1,0:T(8,128)S(1)} %get-tuple-element.28), channel_id=1, source_target_pairs={{0,0},{1,1},{2,2},{3,3},{4,4},{5,5},{6,6},{7,7},{8,8},{9,10},{10,9... | collective-permute-start | bytes 49160 | tf_op jit(solution)/shard_map/ppermute | solution.py:509

commit v9 on v8

--- a/solution.py
+++ b/solution.py
@@ -502,9 +502,10 @@
         pairs = []
         for g in range(grp_count):
             for i in range(wide_count):
-                partner = i + 1 if (i - first) % 2 == 0 else i - 1
-                if g not in groups or not 0 <= partner < wide_count:
-                    partner = i
+                shift = first if g in groups else 0
+                partner = i + 1 if (i - shift) % 2 == 0 else i - 1
+                if not 0 <= partner < wide_count:
+                    continue
                 pairs.append((g * wide_count + i, g * wide_count + partner))
         return lax.ppermute(rows_sent, ("grp", "wide"), pairs)
 

time: 30.4 us -> 32.1 us (1.056)
  the two profiles are of different devices: /device:TPU:8 before, /device:TPU:0 now
where the time goes in v9:
time: 32.1 us; the launch traced here: 31.8 us
  blocking collectives  23 us (72%)
  Pallas kernels  4.33 us (13%)
  starting transfers between devices  3.08 us (10%)
  waiting for transfers between devices  0.76 us (2%)
  between operations  0.7 us (2%)
    all_gather x1, blocking collectives, on_device(): modes = lax.all_gather(packed, 'grp', axis=0, tiled=True)  13.9 us
    all_to_all x1, blocking collectives, on_device(): lax.all_to_all(sent.reshape(wide_count, width, LANES), 'wide', split_axis...  9.05 us
    ppermute x3, starting transfers between devices, swap(): return lax.ppermute(rows_sent, ('grp', 'wide'), pairs)  3.08 us
    pallas_call x1, Pallas kernels, on_device(): pl.pallas_call(functools.partial(main_kernel, sizes), out_shape=(lines(wi...  2.16 us
    pallas_call x1, Pallas kernels, on_device(): pl.pallas_call(load_kernel, out_shape=(jax.ShapeDtypeStruct((mode_index.s...  1.08 us
    ppermute x3, waiting for transfers between devices, swap(): return lax.ppermute(rows_sent, ('grp', 'wide'), pairs)  0.76 us
    pallas_call x1, Pallas kernels, on_device(): pl.pallas_call(functools.partial(last_kernel, sizes), out_shape=lines(row...  0.72 us
  transfers between devices with their start and end apart: 3, of which 1 were waited for; matrix products, arithmetic and copies ran while one was open for 0% of the time, Pallas kernels for 1%

profile of v9, /device:TPU:0, one launch (start us, length us, event | category | flops | bytes accessed | tf_op | source)
XLA Modules:
  0.0 31.8 jit_solution(5217617480055798901)
XLA Ops:
  0.7 1.1 %shard_map.64 = (f32[2,8]{1,0:T(2,128)S(1)}, f32[256,128]{1,0:T(8,128)S(1)}, f32[256,128]{1,0:T(8,128)S(1)}, f32[32,128]{1,0:T(8,128)S(1)}, f32[32,128]{1,0:T(8,128)S(1)}) custom-call(s32[1]{0:T(128)S(6)} %copy.13.step_ref, s32[2,3]{1,0:T(2,128)} %index_ref.1, f32[2]{0:T(128)} %amp_ref.1, f32[2]{0:T(128)} %phase_ref.1, f32[256,128]{1,0:T(8,128)} %bitcast.23, ...), custom_call_target="tpu_custom_call" | custom-call | tf_op jit(solution)/shard_map/pallas_call | solution.py:476
  1.7 0.5 %collective-permute-start = (f32[32,128]{1,0:T(8,128)S(1)}, f32[32,128]{1,0:T(8,128)S(1)}, u32[]{:S(2)}, u32[]{:S(2)}) collective-permute-start(f32[32,128]{1,0:T(8,128)S(1)} %get-tuple-element.24), channel_id=1, source_target_pairs={{0,1},{1,0},{2,3},{3,2},{4,5},{5,4},{6,7},{7,6},{8,9},{9,8},{10,11... | collective-permute-start | bytes 49160 | tf_op jit(solution)/shard_map/ppermute | solution.py:510
  2.3 0.7 %collective-permute-start.1 = (f32[32,128]{1,0:T(8,128)S(1)}, f32[32,128]{1,0:T(8,128)S(1)}, u32[]{:S(2)}, u32[]{:S(2)}) collective-permute-start(f32[32,128]{1,0:T(8,128)S(1)} %get-tuple-element.28), channel_id=1, source_target_pairs={{1,2},{2,1},{3,4},{4,3},{5,6},{6,5},{8,9},{9,8},{10,11},{11,10},{1... | collective-permute-start | bytes 49160 | tf_op jit(solution)/shard_map/ppermute | solution.py:510
  2.9 13.9 %all-gather = f32[4,2,8]{2,1,0:T(2,128)S(1)} all-gather(f32[1,2,8]{2,1,0:T(2,128)S(1)} %bitcast.22), channel_id=1, replica_groups=mesh['grp'=4,'wide'=8] {'grp'}, dimensions={0}, use_global_device_ids=true | all-gather | bytes 320 | tf_op jit(solution)/shard_map/all_gather | solution.py:514
  16.8 1.9 %collective-permute-start.2 = (f32[32,128]{1,0:T(8,128)S(1)}, f32[32,128]{1,0:T(8,128)S(1)}, u32[]{:S(2)}, u32[]{:S(2)}) collective-permute-start(f32[32,128]{1,0:T(8,128)S(1)} %get-tuple-element.28), channel_id=1, source_target_pairs={{0,1},{1,0},{2,3},{3,2},{4,5},{5,4},{6,7},{7,6},{9,10},{10,9},{11,... | collective-permute-start | bytes 49160 | tf_op jit(solution)/shard_map/ppermute | solution.py:510
  18.7 0.0 collective-permute-done.inner_ref
  18.8 0.0 collective-permute-done.1.outer_ref
  18.8 0.4 %shard_map.65 = (f32[1056,128]{1,0:T(8,128)S(1)}, f32[64,128]{1,0:T(8,128)S(1)}) custom-call(f32[8,8]{1,0:T(8,128)S(1)} %bitcast.21, f32[32,128]{1,0:T(8,128)S(1)} %collective-permute-done.inner_ref, f32[32,128]{1,0:T(8,128)S(1)} %collective-permute-done.1.outer_ref), custom_call_target="tpu_custom_call" | custom-call | tf_op jit(solution)/shard_map/pallas_call | solution.py:518
  19.1 0.8 %collective-permute-done.2.late_outer_ref = f32[32,128]{1,0:T(8,128)S(1)} collective-permute-done((f32[32,128]{1,0:T(8,128)S(1)}, f32[32,128]{1,0:T(8,128)S(1)}, u32[]{:S(2)}, u32[]{:S(2)}) %collective-permute-start.2) | collective-permute-done | bytes 16416 | tf_op jit(solution)/shard_map/ppermute | solution.py:510
  19.9 2.2 %shard_map.66 = (f32[256,128]{1,0:T(8,128)S(1)}, f32[256,128]{1,0:T(8,128)S(1)}, f32[256,128]{1,0:T(8,128)S(1)}, f32[256,128]{1,0:T(8,128)S(1)}, f32[256,128]{1,...) custom-call(f32[1056,128]{1,0:T(8,128)S(1)} %get-tuple-element.25.heights, ...), custom_call_target="tpu_custom_call" | custom-call | tf_op jit(solution)/shard_map/pallas_call | solution.py:524
  22.1 9.0 %all_to_all.5 = f32[8,32,128]{2,1,0:T(8,128)S(1)} all-to-all(f32[8,32,128]{2,1,0:T(8,128)S(1)} %bitcast.20), channel_id=1, replica_groups=mesh['grp'=4,'wide'=8] {'wide'}, dimensions={0} | all-to-all | bytes 262144 | tf_op jit(solution)/shard_map/all_to_all | solution.py:539
  31.1 0.7 %shard_map.67 = f32[256,128]{1,0:T(8,128)} custom-call(f32[256,128]{1,0:T(8,128)S(1)} %bitcast.19, f32[256,128]{1,0:T(8,128)S(1)} %get-tuple-element.31.left_gain_ref, f32[256,128]{1,0:T(8,128)S(1)} %get-tuple-element.32.right_gain_ref, f32[256,128]{1,0:T(8,128)S(1)} %get-tuple-element.33.joint_ref, f32[256,128]{1,0:T(8,128)S(1)} %get-tuple-element.34.p_ref, ...), custom_call_target="tpu_custom_call" | custom-call | tf_op jit(solution)/shard_map/pallas_call | solution.py:543
Async XLA Ops:
  1.7 17.0 %collective-permute-start = (f32[32,128]{1,0:T(8,128)S(1)}, f32[32,128]{1,0:T(8,128)S(1)}, u32[]{:S(2)}, u32[]{:S(2)}) collective-permute-start(f32[32,128]{1,0:T(8,128)S(1)} %get-tuple-element.24), channel_id=1, source_target_pairs={{0,1},{1,0},{2,3},{3,2},{4,5},{5,4},{6,7},{7,6},{8,9},{9,8},{10,11... | collective-permute-start | bytes 49160 | tf_op jit(solution)/shard_map/ppermute | solution.py:510
  2.3 16.5 %collective-permute-start.1 = (f32[32,128]{1,0:T(8,128)S(1)}, f32[32,128]{1,0:T(8,128)S(1)}, u32[]{:S(2)}, u32[]{:S(2)}) collective-permute-start(f32[32,128]{1,0:T(8,128)S(1)} %get-tuple-element.28), channel_id=1, source_target_pairs={{1,2},{2,1},{3,4},{4,3},{5,6},{6,5},{8,9},{9,8},{10,11},{11,10},{1... | collective-permute-start | bytes 49160 | tf_op jit(solution)/shard_map/ppermute | solution.py:510
  16.8 3.1 %collective-permute-start.2 = (f32[32,128]{1,0:T(8,128)S(1)}, f32[32,128]{1,0:T(8,128)S(1)}, u32[]{:S(2)}, u32[]{:S(2)}) collective-permute-start(f32[32,128]{1,0:T(8,128)S(1)} %get-tuple-element.28), channel_id=1, source_target_pairs={{0,1},{1,0},{2,3},{3,2},{4,5},{5,4},{6,7},{7,6},{9,10},{10,9},{11,... | collective-permute-start | bytes 49160 | tf_op jit(solution)/shard_map/ppermute | solution.py:510

commit v10 on v8

--- a/solution.py
+++ b/solution.py
@@ -285,7 +285,7 @@
     return u_first, v_first, u_last, v_last
 
 
-def height_kernel(sizes, modes_ref, inner_ref, outer_ref, heights_ref, halo_ref):
+def height_kernel(sizes, modes_ref, heights_ref):
     rows, layers, chunks, row_total, layer_total, column_total = sizes
     width = layers * chunks
     body = height_lines(modes_ref[...], 0, row_total, row_total, chunks, column_total)
@@ -294,12 +294,10 @@
     heights_ref[(row_total + 1) * chunks : (row_total + 2) * chunks] = body[
         (row_total - 1) * chunks : row_total * chunks
     ]
-    halo_ref[0:width] = inner_ref[...]
-    halo_ref[width : 2 * width] = outer_ref[...]
 
 
 def main_kernel(
-    sizes, heights, halo_ref, field_ref, late_outer_ref, conduct_ref,
+    sizes, heights, inner_ref, early_ref, late_ref, field_ref, conduct_ref,
     sent_ref, p_ref, u_ref, v_ref, left_gain_ref, right_gain_ref, joint_ref,
     ends, links, framed, solved,
 ):
@@ -379,8 +377,9 @@
     odd = lax.rem(me, 2)
     beyond = (rows + 1) * width
     framed[width:beyond] = field_ref[...]
-    framed[pl.ds(pl.multiple_of((1 - odd) * beyond, 8), width), :] = halo_ref[0:width]
-    outer_rows = jnp.where(first_layer == 0, halo_ref[width : 2 * width], late_outer_ref[...])
+    framed[pl.ds(pl.multiple_of((1 - odd) * beyond, 8), width), :] = inner_ref[...]
+    other = pl.ds(pl.multiple_of(odd * width, 8), width)
+    outer_rows = jnp.where(first_layer == 0, early_ref[other, :], late_ref[other, :])
     at_edge = (me == 0) | (me == blocks - 1)
     framed[pl.ds(pl.multiple_of(odd * beyond, 8), width), :] = jnp.where(at_edge, 0.0, outer_rows)
     lane = lax.broadcasted_iota(jnp.int32, (rows, LANES), 1)
@@ -498,27 +497,28 @@
         ),
     )
 
-    def swap(rows_sent, first, groups):
-        pairs = []
-        for g in range(grp_count):
-            for i in range(wide_count):
-                partner = i + 1 if (i - first) % 2 == 0 else i - 1
-                if g not in groups or not 0 <= partner < wide_count:
-                    partner = i
-                pairs.append((g * wide_count + i, g * wide_count + partner))
-        return lax.ppermute(rows_sent, ("grp", "wide"), pairs)
-
-    inner_came = swap(inner, 0, range(grp_count))
-    outer_came = swap(outer, 1, [0])
+    swaps = [(i, i ^ 1) for i in range(wide_count)]
+    inner_came = lax.ppermute(inner, "wide", swaps)
+    pairs = [[0, wide_count - 1]] + [[i, i + 1] for i in range(1, wide_count - 1, 2)]
+
+    def gather_rows(rows_sent):
+        return lax.all_gather(rows_sent, "wide", axis_index_groups=pairs, axis=0, tiled=True)
+
+    def no_rows(rows_sent):
+        return jnp.zeros((2 * width, LANES), f32)
+
+    in_first = lax.axis_index("grp") == 0
+    early = lax.cond(in_first, gather_rows, no_rows, outer)
+    packed, early = lax.optimization_barrier((packed, early))
     modes = lax.all_gather(packed, "grp", axis=0, tiled=True)
     modes, outer = lax.optimization_barrier((modes, outer))
-    late_outer_came = swap(outer, 1, range(1, grp_count))
-
-    heights, halo = pl.pallas_call(
+    late = lax.cond(in_first, no_rows, gather_rows, outer)
+
+    heights = pl.pallas_call(
         functools.partial(height_kernel, sizes),
-        out_shape=(jax.ShapeDtypeStruct(((row_total + 2) * chunks, LANES), f32), lines(2)),
+        out_shape=jax.ShapeDtypeStruct(((row_total + 2) * chunks, LANES), f32),
         compiler_params=limit,
-    )(modes, inner_came, outer_came)
+    )(modes)
 
     sent, p, u, v, left_gain, right_gain, joint = pl.pallas_call(
         functools.partial(main_kernel, sizes),
@@ -533,7 +533,7 @@
             pltpu.VMEM((rows * width, LANES), f32),
         ],
         compiler_params=limit,
-    )(heights, halo, field_lines, late_outer_came, conduct_lines)
+    )(heights, inner_came, early, late, field_lines, conduct_lines)
 
     came = lax.all_to_all(
         sent.reshape(wide_count, width, LANES), "wide", split_axis=0, concat_axis=0

time: 30.4 us -> 30.9 us (1.016)
  blocking collectives: 23.8 us -> 25.6 us
  starting transfers between devices: 1.38 us -> 0.07 us
    all_to_all x1, blocking collectives: 15.5 us -> 8.23 us  [on_device(): lax.all_to_all(sent.reshape(wide_count, width, LANES), 'wide', split_axis...]
    all_gather x0 -> x1, blocking collectives: none -> 4.74 us  [gather_rows(): lax.all_gather(rows_sent, 'wide', axis_index_groups=pairs, axis=0, tiled=...]
    all_gather x1, blocking collectives: 8.23 us -> 12.6 us  [on_device(): modes = lax.all_gather(packed, 'grp', axis=0, tiled=True)]
    ppermute x3 -> x1, starting transfers between devices: 1.38 us -> 0.07 us  [on_device(): inner_came = lax.ppermute(inner, 'wide', swaps)]
  transfers between devices with their start and end apart: 3 -> 1, of which waited for: 0 -> 0; matrix products, arithmetic and copies ran while one was open for 0% -> 0% of each run, Pallas kernels for 1% -> 1%
where the time goes in v10:
time: 30.9 us; the launch traced here: 30.7 us
  blocking collectives  25.6 us (83%)
  Pallas kernels  4.33 us (14%)
  between operations  0.7 us (2%)
    all_gather x1, blocking collectives, on_device(): modes = lax.all_gather(packed, 'grp', axis=0, tiled=True)  12.6 us
    all_to_all x1, blocking collectives, on_device(): lax.all_to_all(sent.reshape(wide_count, width, LANES), 'wide', split_axis...  8.23 us
    all_gather x1, blocking collectives, gather_rows(): lax.all_gather(rows_sent, 'wide', axis_index_groups=pairs, axis=0, tiled=...  4.74 us
    pallas_call x1, Pallas kernels, on_device(): pl.pallas_call(functools.partial(main_kernel, sizes), out_shape=(lines(wi...  2.16 us
    pallas_call x1, Pallas kernels, on_device(): pl.pallas_call(load_kernel, out_shape=(jax.ShapeDtypeStruct((mode_index.s...  1.08 us
    pallas_call x1, Pallas kernels, on_device(): pl.pallas_call(functools.partial(last_kernel, sizes), out_shape=lines(row...  0.72 us
  transfers between devices with their start and end apart: 1, of which 0 were waited for; matrix products, arithmetic and copies ran while one was open for 0% of the time, Pallas kernels for 1%

profile of v10, /device:TPU:8, one launch (start us, length us, event | category | flops | bytes accessed | tf_op | source)
XLA Modules:
  0.0 30.7 jit_solution(16553604889152185490)
XLA Ops:
  0.7 1.1 %shard_map.64 = (f32[2,8]{1,0:T(2,128)S(1)}, f32[256,128]{1,0:T(8,128)S(1)}, f32[256,128]{1,0:T(8,128)S(1)}, f32[32,128]{1,0:T(8,128)S(1)}, f32[32,128]{1,0:T(8,128)S(1)}) custom-call(s32[1]{0:T(128)S(6)} %copy.17.step_ref, s32[2,3]{1,0:T(2,128)} %index_ref.1, f32[2]{0:T(128)} %amp_ref.1, f32[2]{0:T(128)} %phase_ref.1, f32[256,128]{1,0:T(8,128)} %bitcast.23, ...), custom_call_target="tpu_custom_call" | custom-call | tf_op jit(solution)/shard_map/pallas_call | solution.py:475
  1.7 0.1 collective-permute-start
  1.9 12.6 %all-gather = f32[4,2,8]{2,1,0:T(2,128)S(1)} all-gather(f32[1,2,8]{2,1,0:T(2,128)S(1)} %bitcast.22), channel_id=1, replica_groups=mesh['grp'=4,'wide'=8] {'grp'}, dimensions={0}, use_global_device_ids=true | all-gather | bytes 320 | tf_op jit(solution)/shard_map/all_gather | solution.py:513
  14.5 0.4 %shard_map.65.heights = f32[1056,128]{1,0:T(8,128)S(1)} custom-call(f32[8,8]{1,0:T(8,128)S(1)} %bitcast.21), custom_call_target="tpu_custom_call" | custom-call | tf_op jit(solution)/shard_map/pallas_call | solution.py:517
  14.8 4.8 %conditional.3 = (f32[64,128]{1,0:T(8,128)S(1)}) conditional(s32[]{:T(128)} %convert_element_type.4, f32[32,128]{1,0:T(8,128)S(1)} %get-tuple-element.35, () %tuple.22), branch_computations={%region_2.0_spmd, %region_3.0_spmd} | conditional | bytes 49160 | solution.py:515
  14.8 4.7 %all_gather.7 = f32[64,128]{1,0:T(8,128)S(1)} all-gather(f32[32,128]{1,0:T(8,128)S(1)} %param.2), channel_id=1, replica_groups={{0,7},{1,2},{3,4},{5,6},{8,15},{9,10},{11,12},{13,14},{16,23},{17,18},{..., dimensions={0}, use_global_device_ids=true | all-gather | bytes 49152 | tf_op jit(solution)/shard_map/cond/branch_0_fun/all_gather | solution.py:505
  19.6 0.0 collective-permute-done.inner_ref
  19.6 2.2 %shard_map.66 = (f32[256,128]{1,0:T(8,128)S(1)}, f32[256,128]{1,0:T(8,128)S(1)}, f32[256,128]{1,0:T(8,128)S(1)}, f32[256,128]{1,0:T(8,128)S(1)}, f32[256,128]{1,...) custom-call(f32[1056,128]{1,0:T(8,128)S(1)} %shard_map.65.heights, ...), custom_call_target="tpu_custom_call" | custom-call | tf_op jit(solution)/shard_map/pallas_call | solution.py:523
  21.8 8.2 %all_to_all.5 = f32[8,32,128]{2,1,0:T(8,128)S(1)} all-to-all(f32[8,32,128]{2,1,0:T(8,128)S(1)} %bitcast.20), channel_id=1, replica_groups=mesh['grp'=4,'wide'=8] {'wide'}, dimensions={0} | all-to-all | bytes 262144 | tf_op jit(solution)/shard_map/all_to_all | solution.py:538
  30.0 0.7 %shard_map.67 = f32[256,128]{1,0:T(8,128)} custom-call(f32[256,128]{1,0:T(8,128)S(1)} %bitcast.19, f32[256,128]{1,0:T(8,128)S(1)} %get-tuple-element.39.left_gain_ref, f32[256,128]{1,0:T(8,128)S(1)} %get-tuple-element.40.right_gain_ref, f32[256,128]{1,0:T(8,128)S(1)} %get-tuple-element.41.joint_ref, f32[256,128]{1,0:T(8,128)S(1)} %get-tuple-element.42.p_ref, ...), custom_call_target="tpu_custom_call" | custom-call | tf_op jit(solution)/shard_map/pallas_call | solution.py:542
  (2 shorter events, 0.0 us)
Async XLA Ops:
  1.7 17.9 %collective-permute-start = (f32[32,128]{1,0:T(8,128)S(1)}, f32[32,128]{1,0:T(8,128)S(1)}, u32[]{:S(2)}, u32[]{:S(2)}) collective-permute-start(f32[32,128]{1,0:T(8,128)S(1)} %get-tuple-element.33), channel_id=1, source_target_pairs={{0,1},{1,0},{2,3},{3,2},{4,5},{5,4},{6,7},{7,6},{8,9},{9,8},{10,11... | collective-permute-start | bytes 49160 | tf_op jit(solution)/shard_map/ppermute | solution.py:501

commit v11 on v10

--- a/solution.py
+++ b/solution.py
@@ -285,19 +285,25 @@
     return u_first, v_first, u_last, v_last
 
 
-def height_kernel(sizes, modes_ref, heights_ref):
+def height_kernel(
+    sizes, modes_ref, modes_came_ref, inner_ref, outer_ref, heights_ref, halo_ref
+):
     rows, layers, chunks, row_total, layer_total, column_total = sizes
     width = layers * chunks
-    body = height_lines(modes_ref[...], 0, row_total, row_total, chunks, column_total)
+    odd = lax.rem(lax.axis_index("wide"), 2) == 1
+    modes = jnp.where(odd, modes_ref[...], modes_came_ref[...])
+    body = height_lines(modes, 0, row_total, row_total, chunks, column_total)
     heights_ref[chunks : (row_total + 1) * chunks] = body
     heights_ref[0:chunks] = body[0:chunks]
     heights_ref[(row_total + 1) * chunks : (row_total + 2) * chunks] = body[
         (row_total - 1) * chunks : row_total * chunks
     ]
+    halo_ref[0:width] = inner_ref[...]
+    halo_ref[width : 2 * width] = outer_ref[...]
 
 
 def main_kernel(
-    sizes, heights, inner_ref, early_ref, late_ref, field_ref, conduct_ref,
+    sizes, heights, halo_ref, late_ref, field_ref, conduct_ref,
     sent_ref, p_ref, u_ref, v_ref, left_gain_ref, right_gain_ref, joint_ref,
     ends, links, framed, solved,
 ):
@@ -377,9 +383,11 @@
     odd = lax.rem(me, 2)
     beyond = (rows + 1) * width
     framed[width:beyond] = field_ref[...]
-    framed[pl.ds(pl.multiple_of((1 - odd) * beyond, 8), width), :] = inner_ref[...]
+    framed[pl.ds(pl.multiple_of((1 - odd) * beyond, 8), width), :] = halo_ref[0:width]
     other = pl.ds(pl.multiple_of(odd * width, 8), width)
-    outer_rows = jnp.where(first_layer == 0, early_ref[other, :], late_ref[other, :])
+    outer_rows = jnp.where(
+        first_layer == 0, halo_ref[width : 2 * width], late_ref[other, :]
+    )
     at_edge = (me == 0) | (me == blocks - 1)
     framed[pl.ds(pl.multiple_of(odd * beyond, 8), width), :] = jnp.where(at_edge, 0.0, outer_rows)
     lane = lax.broadcasted_iota(jnp.int32, (rows, LANES), 1)
@@ -500,25 +508,32 @@
     swaps = [(i, i ^ 1) for i in range(wide_count)]
     inner_came = lax.ppermute(inner, "wide", swaps)
     pairs = [[0, wide_count - 1]] + [[i, i + 1] for i in range(1, wide_count - 1, 2)]
+    early_came = lax.ppermute(
+        outer, ("grp", "wide"), [pair for a, b in pairs[1:] for pair in ((a, b), (b, a))]
+    )
+
+    odd = lax.axis_index("wide") % 2 == 1
+    mode_shape = (grp_count * packed.shape[0], packed.shape[1])
+
+    def gather_modes(own):
+        return lax.all_gather(own, "grp", axis=0, tiled=True)
+
+    modes = lax.cond(odd, gather_modes, lambda own: jnp.zeros(mode_shape, f32), packed)
+    modes_came = lax.ppermute(modes, "wide", swaps)
+    modes, modes_came, outer = lax.optimization_barrier((modes, modes_came, outer))
 
     def gather_rows(rows_sent):
         return lax.all_gather(rows_sent, "wide", axis_index_groups=pairs, axis=0, tiled=True)
 
-    def no_rows(rows_sent):
-        return jnp.zeros((2 * width, LANES), f32)
-
-    in_first = lax.axis_index("grp") == 0
-    early = lax.cond(in_first, gather_rows, no_rows, outer)
-    packed, early = lax.optimization_barrier((packed, early))
-    modes = lax.all_gather(packed, "grp", axis=0, tiled=True)
-    modes, outer = lax.optimization_barrier((modes, outer))
-    late = lax.cond(in_first, no_rows, gather_rows, outer)
-
-    heights = pl.pallas_call(
+    late_came = lax.cond(
+        lax.axis_index("grp") == 0, lambda own: jnp.zeros((2 * width, LANES), f32), gather_rows, outer
+    )
+
+    heights, halo = pl.pallas_call(
         functools.partial(height_kernel, sizes),
-        out_shape=jax.ShapeDtypeStruct(((row_total + 2) * chunks, LANES), f32),
+        out_shape=(jax.ShapeDtypeStruct(((row_total + 2) * chunks, LANES), f32), lines(2)),
         compiler_params=limit,
-    )(modes)
+    )(modes, modes_came, inner_came, early_came)
 
     sent, p, u, v, left_gain, right_gain, joint = pl.pallas_call(
         functools.partial(main_kernel, sizes),
@@ -533,7 +548,7 @@
             pltpu.VMEM((rows * width, LANES), f32),
         ],
         compiler_params=limit,
-    )(heights, inner_came, early, late, field_lines, conduct_lines)
+    )(heights, halo, late_came, field_lines, conduct_lines)
 
     came = lax.all_to_all(
         sent.reshape(wide_count, width, LANES), "wide", split_axis=0, concat_axis=0

time: 30.9 us -> 29.3 us (0.948)
  blocking collectives: 25.6 us -> 13.1 us
  starting transfers between devices: 0.07 us -> 9.56 us
  waiting for transfers between devices: 0.01 us -> 0.83 us
  Pallas kernels: 4.33 us -> 4.95 us
    all_gather x1 -> x0, blocking collectives: 12.6 us -> none  [on_device(): modes = lax.all_gather(packed, 'grp', axis=0, tiled=True)]
    ppermute x0 -> x2, starting transfers between devices: none -> 9.49 us  [the longest x1 8.83 us: on_device(): modes_came = lax.ppermute(modes, 'wide', swaps)]
    ppermute x0 -> x2, waiting for transfers between devices: none -> 0.83 us  [the longest x1 0.82 us: on_device(): modes_came = lax.ppermute(modes, 'wide', swaps)]
    pallas_call x1, Pallas kernels: 1.08 us -> 1.68 us  [on_device(): pl.pallas_call(load_kernel, out_shape=(jax.ShapeDtypeStruct((mode_index.s...]
  transfers between devices with their start and end apart: 1 -> 3, of which waited for: 0 -> 1; matrix products, arithmetic and copies ran while one was open for 0% -> 0% of each run, Pallas kernels for 1% -> 0%
where the time goes in v11:
time: 29.3 us; the launch traced here: 29.1 us
  blocking collectives  13.1 us (45%)
  starting transfers between devices  9.56 us (33%)
  Pallas kernels  4.95 us (17%)
  waiting for transfers between devices  0.83 us (3%)
  between operations  0.72 us (2%)
    ppermute x1, starting transfers between devices, on_device(): modes_came = lax.ppermute(modes, 'wide', swaps)  8.83 us
    all_to_all x1, blocking collectives, on_device(): lax.all_to_all(sent.reshape(wide_count, width, LANES), 'wide', split_axis...  8.12 us
    all_gather x1, blocking collectives, gather_rows(): lax.all_gather(rows_sent, 'wide', axis_index_groups=pairs, axis=0, tiled=...  4.94 us
    pallas_call x1, Pallas kernels, on_device(): pl.pallas_call(functools.partial(main_kernel, sizes), out_shape=(lines(wi...  2.17 us
    pallas_call x1, Pallas kernels, on_device(): pl.pallas_call(load_kernel, out_shape=(jax.ShapeDtypeStruct((mode_index.s...  1.68 us
    ppermute x1, waiting for transfers between devices, on_device(): modes_came = lax.ppermute(modes, 'wide', swaps)  0.82 us
    pallas_call x1, Pallas kernels, on_device(): pl.pallas_call(functools.partial(last_kernel, sizes), out_shape=lines(row...  0.72 us
    ppermute x1, starting transfers between devices, on_device(): lax.ppermute(outer, ('grp', 'wide'), [pair for a, b in pairs[1:] for pair...  0.66 us
  transfers between devices with their start and end apart: 3, of which 1 were waited for; matrix products, arithmetic and copies ran while one was open for 0% of the time, Pallas kernels for 0%

profile of v11, /device:TPU:8, one launch (start us, length us, event | category | flops | bytes accessed | tf_op | source)
XLA Modules:
  0.0 29.1 jit_solution(6187447635031298385)
XLA Ops:
  0.7 1.7 %shard_map.64 = (f32[2,8]{1,0:T(2,128)S(1)}, f32[256,128]{1,0:T(8,128)S(1)}, f32[256,128]{1,0:T(8,128)S(1)}, f32[32,128]{1,0:T(8,128)S(1)}, f32[32,128]{1,0:T(8,128)}) custom-call(s32[1]{0:T(128)S(6)} %copy.17.step_ref, s32[2,3]{1,0:T(2,128)} %index_ref.1, f32[2]{0:T(128)} %amp_ref.1, f32[2]{0:T(128)} %phase_ref.1, f32[256,128]{1,0:T(8,128)} %bitcast.21, ...), custom_call_target="tpu_custom_call" | custom-call | tf_op jit(solution)/shard_map/pallas_call | solution.py:483
  2.3 0.1 collective-permute-start.1
  2.4 0.7 %collective-permute-start.2 = (f32[32,128]{1,0:T(8,128)}, f32[32,128]{1,0:T(8,128)S(1)}, u32[]{:S(2)}, u32[]{:S(2)}) collective-permute-start(f32[32,128]{1,0:T(8,128)} %get-tuple-element.37), channel_id=1, source_target_pairs={{1,2},{2,1},{3,4},{4,3},{5,6},{6,5}} | collective-permute-start | bytes 49160 | tf_op jit(solution)/shard_map/ppermute | solution.py:511
  3.1 8.8 %collective-permute-start = (f32[8,8]{1,0:T(8,128)S(1)}, f32[8,8]{1,0:T(8,128)S(1)}, u32[]{:S(2)}, u32[]{:S(2)}) collective-permute-start(f32[8,8]{1,0:T(8,128)S(1)} %get-tuple-element.47.modes_ref), channel_id=1, source_target_pairs={{0,1},{1,0},{2,3},{3,2},{4,5},{5,4},{6,7},{7,6},{8,9},{9,8},{10,11... | collective-permute-start | bytes 776 | tf_op jit(solution)/shard_map/ppermute | solution.py:522
  12.0 0.8 %collective-permute-done.modes_came_ref = f32[8,8]{1,0:T(8,128)S(1)} collective-permute-done((f32[8,8]{1,0:T(8,128)S(1)}, f32[8,8]{1,0:T(8,128)S(1)}, u32[]{:S(2)}, u32[]{:S(2)}) %collective-permute-start) | collective-permute-done | bytes 288 | tf_op jit(solution)/shard_map/ppermute | solution.py:522
  12.8 4.9 %conditional.3 = (f32[64,128]{1,0:T(8,128)S(1)}) conditional(s32[]{:T(128)} %convert_element_type.7, f32[32,128]{1,0:T(8,128)} %get-tuple-element.37, () %tuple.20), branch_computations={%region_2.3_spmd, %region_3.4_spmd} | conditional | bytes 49160 | solution.py:528
  12.8 4.9 %all_gather.5 = f32[64,128]{1,0:T(8,128)S(1)} all-gather(f32[32,128]{1,0:T(8,128)} %param.2), channel_id=1, replica_groups={{0,7},{1,2},{3,4},{5,6},{8,15},{9,10},{11,12},{13,14},{16,23},{17,18},{..., dimensions={0}, use_global_device_ids=true | all-gather | bytes 49152 | tf_op jit(solution)/shard_map/cond/branch_0_fun/all_gather | solution.py:526
  17.7 0.0 collective-permute-done.1.inner_ref
  17.7 0.0 collective-permute-done.2.outer_ref
  17.7 0.4 %shard_map.65 = (f32[1056,128]{1,0:T(8,128)S(1)}, f32[64,128]{1,0:T(8,128)S(1)}) custom-call(f32[8,8]{1,0:T(8,128)S(1)} %get-tuple-element.47.modes_ref, f32[8,8]{1,0:T(8,128)S(1)} %collective-permute-done.modes_came_ref, f32[32,128]{1,0:T(8,128)S(1)} %collective-permute-done.1.inner_ref, f32[32,128]{1,0:T(8,128)S(1)} %collective-permute-done.2.outer_ref), custom_call_target="tpu_custom_call" | custom-call | tf_op jit(solution)/shard_map/pallas_call | solution.py:532
  18.1 2.2 %shard_map.66 = (f32[256,128]{1,0:T(8,128)S(1)}, f32[256,128]{1,0:T(8,128)S(1)}, f32[256,128]{1,0:T(8,128)S(1)}, f32[256,128]{1,0:T(8,128)S(1)}, f32[256,128]{1,...) custom-call(f32[1056,128]{1,0:T(8,128)S(1)} %get-tuple-element.35.heights, ...), custom_call_target="tpu_custom_call" | custom-call | tf_op jit(solution)/shard_map/pallas_call | solution.py:538
  20.3 8.1 %all_to_all.5 = f32[8,32,128]{2,1,0:T(8,128)S(1)} all-to-all(f32[8,32,128]{2,1,0:T(8,128)S(1)} %bitcast.20), channel_id=1, replica_groups=mesh['grp'=4,'wide'=8] {'wide'}, dimensions={0} | all-to-all | bytes 262144 | tf_op jit(solution)/shard_map/all_to_all | solution.py:553
  28.4 0.7 %shard_map.67 = f32[256,128]{1,0:T(8,128)} custom-call(f32[256,128]{1,0:T(8,128)S(1)} %bitcast.19, f32[256,128]{1,0:T(8,128)S(1)} %get-tuple-element.41.left_gain_ref, f32[256,128]{1,0:T(8,128)S(1)} %get-tuple-element.42.right_gain_ref, f32[256,128]{1,0:T(8,128)S(1)} %get-tuple-element.43.joint_ref, f32[256,128]{1,0:T(8,128)S(1)} %get-tuple-element.44.p_ref, ...), custom_call_target="tpu_custom_call" | custom-call | tf_op jit(solution)/shard_map/pallas_call | solution.py:557
  (2 shorter events, 0.0 us)
Async XLA Ops:
  2.3 15.4 %collective-permute-start.1 = (f32[32,128]{1,0:T(8,128)S(1)}, f32[32,128]{1,0:T(8,128)S(1)}, u32[]{:S(2)}, u32[]{:S(2)}) collective-permute-start(f32[32,128]{1,0:T(8,128)S(1)} %get-tuple-element.34), channel_id=1, source_target_pairs={{0,1},{1,0},{2,3},{3,2},{4,5},{5,4},{6,7},{7,6},{8,9},{9,8},{10,11... | collective-permute-start | bytes 49160 | tf_op jit(solution)/shard_map/ppermute | solution.py:509
  2.4 15.3 %collective-permute-start.2 = (f32[32,128]{1,0:T(8,128)}, f32[32,128]{1,0:T(8,128)S(1)}, u32[]{:S(2)}, u32[]{:S(2)}) collective-permute-start(f32[32,128]{1,0:T(8,128)} %get-tuple-element.37), channel_id=1, source_target_pairs={{1,2},{2,1},{3,4},{4,3},{5,6},{6,5}} | collective-permute-start | bytes 49160 | tf_op jit(solution)/shard_map/ppermute | solution.py:511
  3.1 9.7 %collective-permute-start = (f32[8,8]{1,0:T(8,128)S(1)}, f32[8,8]{1,0:T(8,128)S(1)}, u32[]{:S(2)}, u32[]{:S(2)}) collective-permute-start(f32[8,8]{1,0:T(8,128)S(1)} %get-tuple-element.47.modes_ref), channel_id=1, source_target_pairs={{0,1},{1,0},{2,3},{3,2},{4,5},{5,4},{6,7},{7,6},{8,9},{9,8},{10,11... | collective-permute-start | bytes 776 | tf_op jit(solution)/shard_map/ppermute | solution.py:522

commit v12 on v10

--- a/solution.py
+++ b/solution.py
@@ -214,10 +214,10 @@
 
 def load_kernel(
     step_ref, index_ref, amp_ref, phase_ref, field_ref, conduct_ref,
-    packed_ref, field_out, conduct_out, inner_ref, outer_ref,
+    packed_ref, field_out, conduct_out, both_ref, outer_ref,
     index_in, amp_in, phase_in, sems,
 ):
-    width = inner_ref.shape[0]
+    width = outer_ref.shape[0]
     last = field_ref.shape[0] - width
     odd = lax.rem(lax.axis_index("wide"), 2)
     inner_rows = pl.ds(pl.multiple_of((1 - odd) * last, 8), width)
@@ -226,7 +226,8 @@
         (index_ref, index_in),
         (amp_ref, amp_in),
         (phase_ref, phase_in),
-        (field_ref.at[inner_rows], inner_ref),
+        (field_ref.at[inner_rows], both_ref.at[pl.ds(0, width)]),
+        (field_ref.at[outer_rows], both_ref.at[pl.ds(width, width)]),
         (field_ref.at[outer_rows], outer_ref),
         (field_ref, field_out),
         (conduct_ref, conduct_out),
@@ -285,19 +286,19 @@
     return u_first, v_first, u_last, v_last
 
 
-def height_kernel(sizes, modes_ref, heights_ref):
+def height_kernel(sizes, modes_ref, modes_came_ref, heights_ref):
     rows, layers, chunks, row_total, layer_total, column_total = sizes
-    width = layers * chunks
-    body = height_lines(modes_ref[...], 0, row_total, row_total, chunks, column_total)
+    odd = lax.rem(lax.axis_index("wide"), 2) == 1
+    modes = jnp.where(odd, modes_ref[...], modes_came_ref[...])
+    body = height_lines(modes, 0, row_total, row_total, chunks, column_total)
     heights_ref[chunks : (row_total + 1) * chunks] = body
     heights_ref[0:chunks] = body[0:chunks]
     heights_ref[(row_total + 1) * chunks : (row_total + 2) * chunks] = body[
         (row_total - 1) * chunks : row_total * chunks
     ]
 
-
 def main_kernel(
-    sizes, heights, inner_ref, early_ref, late_ref, field_ref, conduct_ref,
+    sizes, heights, both_ref, below_ref, above_ref, field_ref, conduct_ref,
     sent_ref, p_ref, u_ref, v_ref, left_gain_ref, right_gain_ref, joint_ref,
     ends, links, framed, solved,
 ):
@@ -377,9 +378,8 @@
     odd = lax.rem(me, 2)
     beyond = (rows + 1) * width
     framed[width:beyond] = field_ref[...]
-    framed[pl.ds(pl.multiple_of((1 - odd) * beyond, 8), width), :] = inner_ref[...]
-    other = pl.ds(pl.multiple_of(odd * width, 8), width)
-    outer_rows = jnp.where(first_layer == 0, early_ref[other, :], late_ref[other, :])
+    framed[pl.ds(pl.multiple_of((1 - odd) * beyond, 8), width), :] = both_ref[0:width]
+    outer_rows = jnp.where(odd == 1, above_ref[...], below_ref[...])
     at_edge = (me == 0) | (me == blocks - 1)
     framed[pl.ds(pl.multiple_of(odd * beyond, 8), width), :] = jnp.where(at_edge, 0.0, outer_rows)
     lane = lax.broadcasted_iota(jnp.int32, (rows, LANES), 1)
@@ -472,13 +472,13 @@
     def lines(count):
         return jax.ShapeDtypeStruct((count * width, LANES), f32)
 
-    packed, field_lines, conduct_lines, inner, outer = pl.pallas_call(
+    packed, field_lines, conduct_lines, both, outer = pl.pallas_call(
         load_kernel,
         out_shape=(
             jax.ShapeDtypeStruct((mode_index.shape[0], 8), f32),
             lines(rows),
             lines(rows),
-            lines(1),
+            lines(2),
             lines(1),
         ),
         in_specs=[pl.BlockSpec(memory_space=pltpu.SMEM)] + [hbm] * 5,
@@ -486,7 +486,7 @@
             pltpu.SMEM(mode_index.shape, jnp.int32),
             pltpu.SMEM(mode_amp.shape, f32),
             pltpu.SMEM(mode_phase.shape, f32),
-            pltpu.SemaphoreType.DMA((7,)),
+            pltpu.SemaphoreType.DMA((8,)),
         ],
         compiler_params=limit,
     )(
@@ -497,28 +497,43 @@
         ),
     )
 
+    place = lax.axis_index("wide")
+    odd = place % 2 == 1
     swaps = [(i, i ^ 1) for i in range(wide_count)]
-    inner_came = lax.ppermute(inner, "wide", swaps)
-    pairs = [[0, wide_count - 1]] + [[i, i + 1] for i in range(1, wide_count - 1, 2)]
-
-    def gather_rows(rows_sent):
-        return lax.all_gather(rows_sent, "wide", axis_index_groups=pairs, axis=0, tiled=True)
-
-    def no_rows(rows_sent):
-        return jnp.zeros((2 * width, LANES), f32)
-
-    in_first = lax.axis_index("grp") == 0
-    early = lax.cond(in_first, gather_rows, no_rows, outer)
-    packed, early = lax.optimization_barrier((packed, early))
-    modes = lax.all_gather(packed, "grp", axis=0, tiled=True)
-    modes, outer = lax.optimization_barrier((modes, outer))
-    late = lax.cond(in_first, no_rows, gather_rows, outer)
+    cores = [list(range(n, wide_count, 2)) for n in range(2)]
+    both_came = lax.ppermute(both, "wide", swaps)
+
+    def gather_modes(own):
+        return lax.all_gather(own, "grp", axis=0, tiled=True)
+
+    def no_modes(own):
+        return jnp.zeros((grp_count * own.shape[0], own.shape[1]), f32)
+
+    modes = lax.cond(odd, gather_modes, no_modes, packed)
+    modes, outer, both_came = lax.optimization_barrier((modes, outer, both_came))
+
+    def gather_rows(own, came):
+        rows_sent = jnp.concatenate([own, came[width:]], 0)
+        rows_all = lax.all_gather(rows_sent, "wide", axis_index_groups=cores, axis=0)
+        chip = place // 2
+        below = lax.dynamic_index_in_dim(rows_all, jnp.maximum(chip - 1, 0), 0, False)
+        above = lax.dynamic_index_in_dim(
+            rows_all, jnp.minimum(chip + 1, wide_count // 2 - 1), 0, False
+        )
+        return below[width:], above[:width]
+
+    def no_rows(own, came):
+        return jnp.zeros_like(own), jnp.zeros_like(own)
+
+    below, above = lax.cond(odd, no_rows, gather_rows, outer, both_came)
+    above_came = lax.ppermute(above, "wide", swaps)
+    modes_came = lax.ppermute(modes, "wide", swaps)
 
     heights = pl.pallas_call(
         functools.partial(height_kernel, sizes),
         out_shape=jax.ShapeDtypeStruct(((row_total + 2) * chunks, LANES), f32),
         compiler_params=limit,
-    )(modes)
+    )(modes, modes_came)
 
     sent, p, u, v, left_gain, right_gain, joint = pl.pallas_call(
         functools.partial(main_kernel, sizes),
@@ -533,7 +548,7 @@
             pltpu.VMEM((rows * width, LANES), f32),
         ],
         compiler_params=limit,
-    )(heights, inner_came, early, late, field_lines, conduct_lines)
+    )(heights, both_came, below, above_came, field_lines, conduct_lines)
 
     came = lax.all_to_all(
         sent.reshape(wide_count, width, LANES), "wide", split_axis=0, concat_axis=0

time: 30.9 us -> 26.7 us (0.86)
  the two profiles are of different devices: /device:TPU:8 before, /device:TPU:0 now
where the time goes in v12:
time: 26.7 us; the launch traced here: 26.5 us
  blocking collectives  18.6 us (70%)
  Pallas kernels  4.36 us (16%)
  waiting for transfers between devices  1.68 us (6%)
  starting transfers between devices  1.09 us (4%)
  between operations  0.7 us (3%)
    all_gather x1, blocking collectives, gather_rows(): lax.all_gather(rows_sent, 'wide', axis_index_groups=cores, axis=0)  9.8 us
    all_to_all x1, blocking collectives, on_device(): lax.all_to_all(sent.reshape(wide_count, width, LANES), 'wide', split_axis...  8.84 us
    pallas_call x1, Pallas kernels, on_device(): pl.pallas_call(functools.partial(main_kernel, sizes), out_shape=(lines(wi...  2.16 us
    pallas_call x1, Pallas kernels, on_device(): pl.pallas_call(load_kernel, out_shape=(jax.ShapeDtypeStruct((mode_index.s...  1.11 us
    ppermute x1, waiting for transfers between devices, on_device(): both_came = lax.ppermute(both, 'wide', swaps)  0.86 us
    ppermute x1, waiting for transfers between devices, on_device(): modes_came = lax.ppermute(modes, 'wide', swaps)  0.82 us
    pallas_call x1, Pallas kernels, on_device(): pl.pallas_call(functools.partial(last_kernel, sizes), out_shape=lines(row...  0.72 us
  transfers between devices with their start and end apart: 3, of which 2 were waited for; matrix products, arithmetic and copies ran while one was open for 0% of the time, Pallas kernels for 1%

profile of v12, /device:TPU:0, one launch (start us, length us, event | category | flops | bytes accessed | tf_op | source)
XLA Modules:
  0.0 26.5 jit_solution(14173542233768365610)
XLA Ops:
  0.7 1.1 %shard_map.64 = (f32[2,8]{1,0:T(2,128)S(1)}, f32[256,128]{1,0:T(8,128)S(1)}, f32[256,128]{1,0:T(8,128)S(1)}, f32[64,128]{1,0:T(8,128)S(1)}, f32[32,128]{1,0:T(8,128)S(1)}) custom-call(s32[1]{0:T(128)S(6)} %copy.19.step_ref, s32[2,3]{1,0:T(2,128)} %index_ref.1, f32[2]{0:T(128)} %amp_ref.1, f32[2]{0:T(128)} %phase_ref.1, f32[256,128]{1,0:T(8,128)} %bitcast.27, ...), custom_call_target="tpu_custom_call" | custom-call | tf_op jit(solution)/shard_map/pallas_call | solution.py:475
  1.8 0.5 %collective-permute-start = (f32[64,128]{1,0:T(8,128)S(1)}, f32[64,128]{1,0:T(8,128)S(1)}, u32[]{:S(2)}, u32[]{:S(2)}) collective-permute-start(f32[64,128]{1,0:T(8,128)S(1)} %get-tuple-element.37), channel_id=1, source_target_pairs={{0,1},{1,0},{2,3},{3,2},{4,5},{5,4},{6,7},{7,6},{8,9},{9,8},{10,11... | collective-permute-start | bytes 98312 | tf_op jit(solution)/shard_map/ppermute | solution.py:504
  2.3 0.9 %collective-permute-done.both_ref = f32[64,128]{1,0:T(8,128)S(1)} collective-permute-done((f32[64,128]{1,0:T(8,128)S(1)}, f32[64,128]{1,0:T(8,128)S(1)}, u32[]{:S(2)}, u32[]{:S(2)}) %collective-permute-start) | collective-permute-done | bytes 32800 | tf_op jit(solution)/shard_map/ppermute | solution.py:504
  3.1 9.8 %conditional.3 = (f32[32,128]{1,0:T(8,128)S(1)}, f32[32,128]{1,0:T(8,128)S(1)}) conditional(s32[]{:T(128)} %convert_element_type.4, (f32[64,128]{1,0:T(8,128)S(1)}, f32[32,128]{1,0:T(8,128)S(1)}, s32[]{:T(128)}) %tuple.22, () %tuple.23), branch_computations={%region_2.3_spmd, %region_3.4_spmd} | conditional | flops 8215 | bytes 327952 | solution.py:528
  3.2 9.8 %all-gather = f32[256,128]{1,0:T(8,128)S(1)} all-gather(f32[64,128]{1,0:T(8,128)S(1)} %pad_maximum_fusion), channel_id=2, replica_groups={{0,2,4,6},{1,3,5,7},{8,10,12,14},{9,11,13,15},{16,18,20,22},{17,19,21,2..., dimensions={0}, use_global_device_ids=true | all-gather | bytes 163840 | tf_op jit(solution)/shard_map/cond/branch_0_fun/all_gather | solution.py:517
  13.0 0.1 collective-permute-start.2
  13.1 0.5 %collective-permute-start.1 = (f32[8,8]{1,0:T(8,128)S(1)}, f32[8,8]{1,0:T(8,128)S(1)}, u32[]{:S(2)}, u32[]{:S(2)}) collective-permute-start(f32[8,8]{1,0:T(8,128)S(1)} %get-tuple-element.58.modes_ref), channel_id=1, source_target_pairs={{0,1},{1,0},{2,3},{3,2},{4,5},{5,4},{6,7},{7,6},{8,9},{9,8},{10,11... | collective-permute-start | bytes 776 | tf_op jit(solution)/shard_map/ppermute | solution.py:530
  13.5 0.8 %collective-permute-done.1.modes_came_ref = f32[8,8]{1,0:T(8,128)S(1)} collective-permute-done((f32[8,8]{1,0:T(8,128)S(1)}, f32[8,8]{1,0:T(8,128)S(1)}, u32[]{:S(2)}, u32[]{:S(2)}) %collective-permute-start.1) | collective-permute-done | bytes 288 | tf_op jit(solution)/shard_map/ppermute | solution.py:530
  14.4 0.4 %shard_map.65.heights = f32[1056,128]{1,0:T(8,128)S(1)} custom-call(f32[8,8]{1,0:T(8,128)S(1)} %get-tuple-element.58.modes_ref, f32[8,8]{1,0:T(8,128)S(1)} %collective-permute-done.1.modes_came_ref), custom_call_target="tpu_custom_call" | custom-call | tf_op jit(solution)/shard_map/pallas_call | solution.py:532
  14.8 0.0 collective-permute-done.2.above_ref
  14.8 2.2 %shard_map.66 = (f32[256,128]{1,0:T(8,128)S(1)}, f32[256,128]{1,0:T(8,128)S(1)}, f32[256,128]{1,0:T(8,128)S(1)}, f32[256,128]{1,0:T(8,128)S(1)}, f32[256,128]{1,...) custom-call(f32[1056,128]{1,0:T(8,128)S(1)} %shard_map.65.heights, ...), custom_call_target="tpu_custom_call" | custom-call | tf_op jit(solution)/shard_map/pallas_call | solution.py:538
  16.9 8.8 %all_to_all.5 = f32[8,32,128]{2,1,0:T(8,128)S(1)} all-to-all(f32[8,32,128]{2,1,0:T(8,128)S(1)} %bitcast.25), channel_id=1, replica_groups=mesh['grp'=4,'wide'=8] {'wide'}, dimensions={0} | all-to-all | bytes 262144 | tf_op jit(solution)/shard_map/all_to_all | solution.py:553
  25.8 0.7 %shard_map.67 = f32[256,128]{1,0:T(8,128)} custom-call(f32[256,128]{1,0:T(8,128)S(1)} %bitcast.24, f32[256,128]{1,0:T(8,128)S(1)} %get-tuple-element.46.left_gain_ref, f32[256,128]{1,0:T(8,128)S(1)} %get-tuple-element.47.right_gain_ref, f32[256,128]{1,0:T(8,128)S(1)} %get-tuple-element.48.joint_ref, f32[256,128]{1,0:T(8,128)S(1)} %get-tuple-element.49.p_ref, ...), custom_call_target="tpu_custom_call" | custom-call | tf_op jit(solution)/shard_map/pallas_call | solution.py:557
  (5 shorter events, 0.0 us)
Async XLA Ops:
  1.8 1.4 %collective-permute-start = (f32[64,128]{1,0:T(8,128)S(1)}, f32[64,128]{1,0:T(8,128)S(1)}, u32[]{:S(2)}, u32[]{:S(2)}) collective-permute-start(f32[64,128]{1,0:T(8,128)S(1)} %get-tuple-element.37), channel_id=1, source_target_pairs={{0,1},{1,0},{2,3},{3,2},{4,5},{5,4},{6,7},{7,6},{8,9},{9,8},{10,11... | collective-permute-start | bytes 98312 | tf_op jit(solution)/shard_map/ppermute | solution.py:504
  13.0 1.8 %collective-permute-start.2 = (f32[32,128]{1,0:T(8,128)S(1)}, f32[32,128]{1,0:T(8,128)S(1)}, u32[]{:S(2)}, u32[]{:S(2)}) collective-permute-start(f32[32,128]{1,0:T(8,128)S(1)} %get-tuple-element.42), channel_id=1, source_target_pairs={{0,1},{1,0},{2,3},{3,2},{4,5},{5,4},{6,7},{7,6},{8,9},{9,8},{10,11... | collective-permute-start | bytes 49160 | tf_op jit(solution)/shard_map/ppermute | solution.py:529
  13.1 1.3 %collective-permute-start.1 = (f32[8,8]{1,0:T(8,128)S(1)}, f32[8,8]{1,0:T(8,128)S(1)}, u32[]{:S(2)}, u32[]{:S(2)}) collective-permute-start(f32[8,8]{1,0:T(8,128)S(1)} %get-tuple-element.58.modes_ref), channel_id=1, source_target_pairs={{0,1},{1,0},{2,3},{3,2},{4,5},{5,4},{6,7},{7,6},{8,9},{9,8},{10,11... | collective-permute-start | bytes 776 | tf_op jit(solution)/shard_map/ppermute | solution.py:530

commit v13 on v12

--- a/solution.py
+++ b/solution.py
@@ -270,37 +270,26 @@
     return inv, scaled, chain, u, v
 
 
-def block_ends(face):
-    rows = len(face) - 1
-    down = 1.0 + face[0]
-    up = 1.0 + face[rows]
+def block_ends(faces):
+    rows = len(faces[0]) - 1
+    down = [1.0 + face[0] for face in faces]
+    up = [1.0 + face[rows] for face in faces]
     v_first = None
     for j in range(rows):
-        v_last = face[j + 1] * inverse(down + face[j + 1])
-        v_first = v_last if v_first is None else v_first * v_last
-        u_first = face[rows - 1 - j] * inverse(up + face[rows - 1 - j])
+        v_last = [f[j + 1] * inverse(d + f[j + 1]) for f, d in zip(faces, down)]
+        u_first = [f[rows - 1 - j] * inverse(d + f[rows - 1 - j]) for f, d in zip(faces, up)]
+        v_first = [a * b for a, b in zip(v_first, v_last)] if j else v_last
         if j < rows - 1:
-            down = 1.0 + down * v_last
-            up = 1.0 + up * u_first
-    u_last = v_first * (face[0] * inverse(face[rows]))
-    return u_first, v_first, u_last, v_last
-
-
-def height_kernel(sizes, modes_ref, modes_came_ref, heights_ref):
-    rows, layers, chunks, row_total, layer_total, column_total = sizes
-    odd = lax.rem(lax.axis_index("wide"), 2) == 1
-    modes = jnp.where(odd, modes_ref[...], modes_came_ref[...])
-    body = height_lines(modes, 0, row_total, row_total, chunks, column_total)
-    heights_ref[chunks : (row_total + 1) * chunks] = body
-    heights_ref[0:chunks] = body[0:chunks]
-    heights_ref[(row_total + 1) * chunks : (row_total + 2) * chunks] = body[
-        (row_total - 1) * chunks : row_total * chunks
-    ]
+            down = [1.0 + d * v for d, v in zip(down, v_last)]
+            up = [1.0 + d * u for d, u in zip(up, u_first)]
+    u_last = [v * (f[0] * inverse(f[rows])) for f, v in zip(faces, v_first)]
+    return list(zip(u_first, v_first, u_last, v_last))
+
 
 def main_kernel(
-    sizes, heights, both_ref, below_ref, above_ref, field_ref, conduct_ref,
+    sizes, modes_ref, modes_came_ref, both_ref, below_ref, above_ref, field_ref, conduct_ref,
     sent_ref, p_ref, u_ref, v_ref, left_gain_ref, right_gain_ref, joint_ref,
-    ends, links, framed, solved,
+    heights, ends, links, framed, solved,
 ):
     rows, layers, chunks, row_total, layer_total, column_total = sizes
     width = layers * chunks
@@ -311,6 +300,14 @@
         ((first_layer + k).astype(f32) + 0.5) * (1.0 / layer_total) for k in range(layers)
     ]
     half = 0.5 * weight
+    odd = lax.rem(me, 2)
+    modes = jnp.where(odd == 1, modes_ref[...], modes_came_ref[...])
+    body = height_lines(modes, 0, row_total, row_total, chunks, column_total)
+    heights[chunks : (row_total + 1) * chunks] = body
+    heights[0:chunks] = body[0:chunks]
+    heights[(row_total + 1) * chunks : (row_total + 2) * chunks] = body[
+        (row_total - 1) * chunks : row_total * chunks
+    ]
     own_start = pl.multiple_of(me * (rows * chunks), 8)
 
     def faces(start):
@@ -332,15 +329,18 @@
         v_ref[j * width : (j + 1) * width] = v[j]
     keep_ends(me, (u[0], v[0], u[-1], v[-1]))
 
-    def other_block(n):
-        b = lax.rem(me + 1 + n, blocks)
-        keep_ends(b, block_ends(faces(pl.multiple_of(b * (rows * chunks), 8))))
-
+    def other_blocks(first, count):
+        spots = [lax.rem(me + 1 + first + n, blocks) for n in range(count)]
+        starts = [pl.multiple_of(b * (rows * chunks), 8) for b in spots]
+        for b, values in zip(spots, block_ends([faces(start) for start in starts])):
+            keep_ends(b, values)
+
+    group = 4
     if blocks <= 8:
-        for n in range(blocks - 1):
-            other_block(n)
+        for first in range(0, blocks - 1, group):
+            other_blocks(first, min(group, blocks - 1 - first))
     else:
-        lax.fori_loop(0, blocks - 1, lambda n, carry: (other_block(n), carry)[1], 0)
+        lax.fori_loop(0, blocks - 1, lambda n, carry: (other_blocks(n, 1), carry)[1], 0)
 
     def end(b, n):
         return ends[(4 * b + n) * width : (4 * b + n + 1) * width]
@@ -375,7 +375,6 @@
     for n, value in enumerate(joint):
         joint_ref[n * width : (n + 1) * width] = value
 
-    odd = lax.rem(me, 2)
     beyond = (rows + 1) * width
     framed[width:beyond] = field_ref[...]
     framed[pl.ds(pl.multiple_of((1 - odd) * beyond, 8), width), :] = both_ref[0:width]
@@ -429,7 +428,7 @@
 
 def last_kernel(
     sizes, came_ref, left_gain_ref, right_gain_ref, joint_ref, p_ref, u_ref, v_ref, field_ref,
-    out_ref,
+    out_ref, done, sems,
 ):
     rows, layers, chunks, row_total, layer_total, column_total = sizes
     width = layers * chunks
@@ -450,11 +449,18 @@
     z = right + part(joint_ref, 3) * part(p_ref, rows - 1)
     before = part(joint_ref, 4) * y + part(joint_ref, 5) * z
     after = part(joint_ref, 6) * y + part(joint_ref, 7) * z
+    copies = []
     for j in range(rows):
         x = part(p_ref, j) + part(u_ref, j) * before + part(v_ref, j) * after
         for k in range(layers):
             spot = pl.ds(j * width + k, chunks, stride=layers)
-            out_ref[spot, :] = field_ref[spot, :] + x[k * chunks : (k + 1) * chunks]
+            done[spot, :] = field_ref[spot, :] + x[k * chunks : (k + 1) * chunks]
+        if j % 2 == 1:
+            slab = pl.ds((j - 1) * width, 2 * width)
+            copies.append(pltpu.make_async_copy(done.at[slab], out_ref.at[slab], sems.at[j // 2]))
+            copies[-1].start()
+    for copy in copies:
+        copy.wait()
 
 
 def on_device(field, conduct, mode_index, mode_amp, mode_phase, step_index):
@@ -529,12 +535,6 @@
     above_came = lax.ppermute(above, "wide", swaps)
     modes_came = lax.ppermute(modes, "wide", swaps)
 
-    heights = pl.pallas_call(
-        functools.partial(height_kernel, sizes),
-        out_shape=jax.ShapeDtypeStruct(((row_total + 2) * chunks, LANES), f32),
-        compiler_params=limit,
-    )(modes, modes_came)
-
     sent, p, u, v, left_gain, right_gain, joint = pl.pallas_call(
         functools.partial(main_kernel, sizes),
         out_shape=(lines(wide_count),)
@@ -542,13 +542,14 @@
         + (lines(wide_count),) * 2
         + (lines(8),),
         scratch_shapes=[
+            pltpu.VMEM(((row_total + 2) * chunks, LANES), f32),
             pltpu.VMEM((4 * wide_count * width, LANES), f32),
             pltpu.VMEM((2 * wide_count * width, LANES), f32),
             pltpu.VMEM(((rows + 2) * width, LANES), f32),
             pltpu.VMEM((rows * width, LANES), f32),
         ],
         compiler_params=limit,
-    )(heights, both_came, below, above_came, field_lines, conduct_lines)
+    )(modes, modes_came, both_came, below, above_came, field_lines, conduct_lines)
 
     came = lax.all_to_all(
         sent.reshape(wide_count, width, LANES), "wide", split_axis=0, concat_axis=0
@@ -557,6 +558,11 @@
     advanced = pl.pallas_call(
         functools.partial(last_kernel, sizes),
         out_shape=lines(rows),
+        out_specs=hbm,
+        scratch_shapes=[
+            pltpu.VMEM((rows * width, LANES), f32),
+            pltpu.SemaphoreType.DMA((rows // 2,)),
+        ],
         compiler_params=limit,
     )(came, left_gain, right_gain, joint, p, u, v, field_lines)
     return from_lines(advanced, field.shape)

time: 26.7 us -> 26.9 us (level)
    pallas_call x1, Pallas kernels: 2.16 us -> 2.68 us  [on_device(): pl.pallas_call(functools.partial(main_kernel, sizes), out_shape=(lines(wi...]
    pallas_call x1 -> x0, Pallas kernels: 0.37 us -> none  [on_device(): pl.pallas_call(functools.partial(height_kernel, sizes), out_shape=jax.Sha...]
  transfers between devices with their start and end apart: 3 -> 3, of which waited for: 2 -> 2; matrix products, arithmetic and copies ran while one was open for 0% -> 0% of each run, Pallas kernels for 1% -> 0%
where the time goes in v13:
time: 26.9 us; the launch traced here: 26.7 us
  blocking collectives  18.6 us (69%)
  Pallas kernels  4.54 us (17%)
  waiting for transfers between devices  1.68 us (6%)
  starting transfers between devices  1.09 us (4%)
  between operations  0.69 us (3%)
    all_gather x1, blocking collectives, gather_rows(): lax.all_gather(rows_sent, 'wide', axis_index_groups=cores, axis=0)  9.8 us
    all_to_all x1, blocking collectives, on_device(): lax.all_to_all(sent.reshape(wide_count, width, LANES), 'wide', split_axis...  8.85 us
    pallas_call x1, Pallas kernels, on_device(): pl.pallas_call(functools.partial(main_kernel, sizes), out_shape=(lines(wi...  2.68 us
    pallas_call x1, Pallas kernels, on_device(): pl.pallas_call(load_kernel, out_shape=(jax.ShapeDtypeStruct((mode_index.s...  1.11 us
    ppermute x1, waiting for transfers between devices, on_device(): both_came = lax.ppermute(both, 'wide', swaps)  0.86 us
    ppermute x1, waiting for transfers between devices, on_device(): modes_came = lax.ppermute(modes, 'wide', swaps)  0.82 us
    pallas_call x1, Pallas kernels, on_device(): pl.pallas_call(functools.partial(last_kernel, sizes), out_shape=lines(row...  0.75 us
  transfers between devices with their start and end apart: 3, of which 2 were waited for; matrix products, arithmetic and copies ran while one was open for 0% of the time, Pallas kernels for 0%

profile of v13, /device:TPU:0, one launch (start us, length us, event | category | flops | bytes accessed | tf_op | source)
XLA Modules:
  0.0 26.7 jit_solution(17291420895133570056)
XLA Ops:
  0.7 1.1 %shard_map.64 = (f32[2,8]{1,0:T(2,128)S(1)}, f32[256,128]{1,0:T(8,128)S(1)}, f32[256,128]{1,0:T(8,128)S(1)}, f32[64,128]{1,0:T(8,128)S(1)}, f32[32,128]{1,0:T(8,128)S(1)}) custom-call(s32[1]{0:T(128)S(6)} %copy.19.step_ref, s32[2,3]{1,0:T(2,128)} %index_ref.1, f32[2]{0:T(128)} %amp_ref.1, f32[2]{0:T(128)} %phase_ref.1, f32[256,128]{1,0:T(8,128)} %bitcast.27, ...), custom_call_target="tpu_custom_call" | custom-call | tf_op jit(solution)/shard_map/pallas_call | solution.py:481
  1.8 0.5 %collective-permute-start = (f32[64,128]{1,0:T(8,128)S(1)}, f32[64,128]{1,0:T(8,128)S(1)}, u32[]{:S(2)}, u32[]{:S(2)}) collective-permute-start(f32[64,128]{1,0:T(8,128)S(1)} %get-tuple-element.37), channel_id=1, source_target_pairs={{0,1},{1,0},{2,3},{3,2},{4,5},{5,4},{6,7},{7,6},{8,9},{9,8},{10,11... | collective-permute-start | bytes 98312 | tf_op jit(solution)/shard_map/ppermute | solution.py:510
  2.3 0.9 %collective-permute-done.both_ref = f32[64,128]{1,0:T(8,128)S(1)} collective-permute-done((f32[64,128]{1,0:T(8,128)S(1)}, f32[64,128]{1,0:T(8,128)S(1)}, u32[]{:S(2)}, u32[]{:S(2)}) %collective-permute-start) | collective-permute-done | bytes 32800 | tf_op jit(solution)/shard_map/ppermute | solution.py:510
  3.1 9.8 %conditional.3 = (f32[32,128]{1,0:T(8,128)S(1)}, f32[32,128]{1,0:T(8,128)S(1)}) conditional(s32[]{:T(128)} %convert_element_type.4, (f32[64,128]{1,0:T(8,128)S(1)}, f32[32,128]{1,0:T(8,128)S(1)}, s32[]{:T(128)}) %tuple.22, () %tuple.23), branch_computations={%region_2.3_spmd, %region_3.4_spmd} | conditional | flops 8215 | bytes 327952 | solution.py:534
  3.2 9.8 %all-gather = f32[256,128]{1,0:T(8,128)S(1)} all-gather(f32[64,128]{1,0:T(8,128)S(1)} %pad_maximum_fusion), channel_id=2, replica_groups={{0,2,4,6},{1,3,5,7},{8,10,12,14},{9,11,13,15},{16,18,20,22},{17,19,21,2..., dimensions={0}, use_global_device_ids=true | all-gather | bytes 163840 | tf_op jit(solution)/shard_map/cond/branch_0_fun/all_gather | solution.py:523
  13.0 0.1 collective-permute-start.2
  13.1 0.5 %collective-permute-start.1 = (f32[8,8]{1,0:T(8,128)S(1)}, f32[8,8]{1,0:T(8,128)S(1)}, u32[]{:S(2)}, u32[]{:S(2)}) collective-permute-start(f32[8,8]{1,0:T(8,128)S(1)} %get-tuple-element.58.modes_ref), channel_id=1, source_target_pairs={{0,1},{1,0},{2,3},{3,2},{4,5},{5,4},{6,7},{7,6},{8,9},{9,8},{10,11... | collective-permute-start | bytes 776 | tf_op jit(solution)/shard_map/ppermute | solution.py:536
  13.5 0.8 %collective-permute-done.1.modes_came_ref = f32[8,8]{1,0:T(8,128)S(1)} collective-permute-done((f32[8,8]{1,0:T(8,128)S(1)}, f32[8,8]{1,0:T(8,128)S(1)}, u32[]{:S(2)}, u32[]{:S(2)}) %collective-permute-start.1) | collective-permute-done | bytes 288 | tf_op jit(solution)/shard_map/ppermute | solution.py:536
  14.4 0.0 collective-permute-done.2.above_ref
  14.4 2.7 %shard_map.65 = (f32[256,128]{1,0:T(8,128)S(1)}, f32[256,128]{1,0:T(8,128)S(1)}, f32[256,128]{1,0:T(8,128)S(1)}, f32[256,128]{1,0:T(8,128)S(1)}, f32[256,128]{1,...) custom-call(f32[8,8]{1,0:T(8,128)S(1)} %get-tuple-element.58.modes_ref, ...), custom_call_target="tpu_custom_call" | custom-call | tf_op jit(solution)/shard_map/pallas_call | solution.py:538
  17.1 8.8 %all_to_all.5 = f32[8,32,128]{2,1,0:T(8,128)S(1)} all-to-all(f32[8,32,128]{2,1,0:T(8,128)S(1)} %bitcast.25), channel_id=1, replica_groups=mesh['grp'=4,'wide'=8] {'wide'}, dimensions={0} | all-to-all | bytes 262144 | tf_op jit(solution)/shard_map/all_to_all | solution.py:554
  25.9 0.7 %shard_map.66 = f32[256,128]{1,0:T(8,128)} custom-call(f32[256,128]{1,0:T(8,128)S(1)} %bitcast.24, f32[256,128]{1,0:T(8,128)S(1)} %get-tuple-element.46.left_gain_ref, f32[256,128]{1,0:T(8,128)S(1)} %get-tuple-element.47.right_gain_ref, f32[256,128]{1,0:T(8,128)S(1)} %get-tuple-element.48.joint_ref, f32[256,128]{1,0:T(8,128)S(1)} %get-tuple-element.49.p_ref, ...), custom_call_target="tpu_custom_call" | custom-call | tf_op jit(solution)/shard_map/pallas_call | solution.py:558
  (5 shorter events, 0.0 us)
Async XLA Ops:
  1.8 1.4 %collective-permute-start = (f32[64,128]{1,0:T(8,128)S(1)}, f32[64,128]{1,0:T(8,128)S(1)}, u32[]{:S(2)}, u32[]{:S(2)}) collective-permute-start(f32[64,128]{1,0:T(8,128)S(1)} %get-tuple-element.37), channel_id=1, source_target_pairs={{0,1},{1,0},{2,3},{3,2},{4,5},{5,4},{6,7},{7,6},{8,9},{9,8},{10,11... | collective-permute-start | bytes 98312 | tf_op jit(solution)/shard_map/ppermute | solution.py:510
  13.0 1.4 %collective-permute-start.2 = (f32[32,128]{1,0:T(8,128)S(1)}, f32[32,128]{1,0:T(8,128)S(1)}, u32[]{:S(2)}, u32[]{:S(2)}) collective-permute-start(f32[32,128]{1,0:T(8,128)S(1)} %get-tuple-element.42), channel_id=1, source_target_pairs={{0,1},{1,0},{2,3},{3,2},{4,5},{5,4},{6,7},{7,6},{8,9},{9,8},{10,11... | collective-permute-start | bytes 49160 | tf_op jit(solution)/shard_map/ppermute | solution.py:535
  13.1 1.3 %collective-permute-start.1 = (f32[8,8]{1,0:T(8,128)S(1)}, f32[8,8]{1,0:T(8,128)S(1)}, u32[]{:S(2)}, u32[]{:S(2)}) collective-permute-start(f32[8,8]{1,0:T(8,128)S(1)} %get-tuple-element.58.modes_ref), channel_id=1, source_target_pairs={{0,1},{1,0},{2,3},{3,2},{4,5},{5,4},{6,7},{7,6},{8,9},{9,8},{10,11... | collective-permute-start | bytes 776 | tf_op jit(solution)/shard_map/ppermute | solution.py:536

commit v14 on v12

--- a/solution.py
+++ b/solution.py
@@ -300,7 +300,7 @@
 def main_kernel(
     sizes, heights, both_ref, below_ref, above_ref, field_ref, conduct_ref,
     sent_ref, p_ref, u_ref, v_ref, left_gain_ref, right_gain_ref, joint_ref,
-    ends, links, framed, solved,
+    ends, links, halo, solved,
 ):
     rows, layers, chunks, row_total, layer_total, column_total = sizes
     width = layers * chunks
@@ -375,32 +375,42 @@
     for n, value in enumerate(joint):
         joint_ref[n * width : (n + 1) * width] = value
 
-    odd = lax.rem(me, 2)
-    beyond = (rows + 1) * width
-    framed[width:beyond] = field_ref[...]
-    framed[pl.ds(pl.multiple_of((1 - odd) * beyond, 8), width), :] = both_ref[0:width]
-    outer_rows = jnp.where(odd == 1, above_ref[...], below_ref[...])
-    at_edge = (me == 0) | (me == blocks - 1)
-    framed[pl.ds(pl.multiple_of(odd * beyond, 8), width), :] = jnp.where(at_edge, 0.0, outer_rows)
+    odd = lax.rem(me, 2) == 1
+    inner = both_ref[0:width]
+    below = jnp.where(odd, inner, below_ref[...])
+    above = jnp.where(odd, above_ref[...], inner)
+    halo[0:width] = jnp.where(me == 0, 0.0, below)
+    halo[width : 2 * width] = jnp.where(me == blocks - 1, 0.0, above)
     lane = lax.broadcasted_iota(jnp.int32, (rows, LANES), 1)
-    g, f, rhs = [], [], []
-    for k in range(layers):
-        g.append([])
-        f.append([])
-        rhs.append([])
-        for c in range(chunks):
-            h_low, h, h_high = (
-                heights[pl.ds(own_start + s * chunks + c, rows, stride=chunks), :]
-                for s in range(3)
-            )
+    row = lax.broadcasted_iota(jnp.int32, (rows, LANES), 0)
+
+    def neighbours(values, low, high):
+        return (
+            jnp.where(row == 0, low, pltpu.roll(values, 1, 0)),
+            jnp.where(row == rows - 1, high, pltpu.roll(values, rows - 1, 0)),
+        )
+
+    g = [[] for _ in range(layers)]
+    f = [[] for _ in range(layers)]
+    rhs = [[] for _ in range(layers)]
+    for c in range(chunks):
+        h = heights[pl.ds(own_start + chunks + c, rows, stride=chunks), :]
+        h_low, h_high = neighbours(
+            h,
+            heights[pl.ds(own_start + c, 1), :],
+            heights[pl.ds(own_start + (rows + 1) * chunks + c, 1), :],
+        )
+        low_sum, high_sum = h + h_low, h + h_high
+        for k in range(layers):
             place = c * layers + k
-            f_low, f_mid, f_high = (
-                framed[pl.ds(s * width + place, rows, stride=width), :] for s in range(3)
+            f_mid = field_ref[pl.ds(place, rows, stride=width), :]
+            f_low, f_high = neighbours(
+                f_mid, halo[pl.ds(place, 1), :], halo[pl.ds(width + place, 1), :]
             )
             g[k].append(conduct_ref[pl.ds(place, rows, stride=width), :] * (1.0 + zeta[k] * h))
             f[k].append(f_mid)
-            along = (weight + (half * zeta[k]) * (h + h_high)) * (f_high - f_mid) - (
-                weight + (half * zeta[k]) * (h + h_low)
+            along = (weight + (half * zeta[k]) * high_sum) * (f_high - f_mid) - (
+                weight + (half * zeta[k]) * low_sum
             ) * (f_mid - f_low)
             rhs[k].append(2.0 * (f_mid + along))
     for k in range(0, layers, 2):
@@ -544,7 +554,7 @@
         scratch_shapes=[
             pltpu.VMEM((4 * wide_count * width, LANES), f32),
             pltpu.VMEM((2 * wide_count * width, LANES), f32),
-            pltpu.VMEM(((rows + 2) * width, LANES), f32),
+            pltpu.VMEM((2 * width, LANES), f32),
             pltpu.VMEM((rows * width, LANES), f32),
         ],
         compiler_params=limit,

time: 26.7 us -> 26.5 us (level)
  no operation moved by 1% of the time
where the time goes in v14:
time: 26.5 us; the launch traced here: 26.3 us
  blocking collectives  18.6 us (70%)
  Pallas kernels  4.2 us (16%)
  waiting for transfers between devices  1.68 us (6%)
  starting transfers between devices  1.09 us (4%)
  between operations  0.7 us (3%)
    all_gather x1, blocking collectives, gather_rows(): lax.all_gather(rows_sent, 'wide', axis_index_groups=cores, axis=0)  9.8 us
    all_to_all x1, blocking collectives, on_device(): lax.all_to_all(sent.reshape(wide_count, width, LANES), 'wide', split_axis...  8.84 us
    pallas_call x1, Pallas kernels, on_device(): pl.pallas_call(functools.partial(main_kernel, sizes), out_shape=(lines(wi...  2 us
    pallas_call x1, Pallas kernels, on_device(): pl.pallas_call(load_kernel, out_shape=(jax.ShapeDtypeStruct((mode_index.s...  1.11 us
    ppermute x1, waiting for transfers between devices, on_device(): both_came = lax.ppermute(both, 'wide', swaps)  0.86 us
    ppermute x1, waiting for transfers between devices, on_device(): modes_came = lax.ppermute(modes, 'wide', swaps)  0.82 us
    pallas_call x1, Pallas kernels, on_device(): pl.pallas_call(functools.partial(last_kernel, sizes), out_shape=lines(row...  0.72 us
  transfers between devices with their start and end apart: 3, of which 2 were waited for; matrix products, arithmetic and copies ran while one was open for 0% of the time, Pallas kernels for 1%

profile of v14, /device:TPU:0, one launch (start us, length us, event | category | flops | bytes accessed | tf_op | source)
XLA Modules:
  0.0 26.3 jit_solution(2919910362852172099)
XLA Ops:
  0.7 1.1 %shard_map.64 = (f32[2,8]{1,0:T(2,128)S(1)}, f32[256,128]{1,0:T(8,128)S(1)}, f32[256,128]{1,0:T(8,128)S(1)}, f32[64,128]{1,0:T(8,128)S(1)}, f32[32,128]{1,0:T(8,128)S(1)}) custom-call(s32[1]{0:T(128)S(6)} %copy.19.step_ref, s32[2,3]{1,0:T(2,128)} %index_ref.1, f32[2]{0:T(128)} %amp_ref.1, f32[2]{0:T(128)} %phase_ref.1, f32[256,128]{1,0:T(8,128)} %bitcast.27, ...), custom_call_target="tpu_custom_call" | custom-call | tf_op jit(solution)/shard_map/pallas_call | solution.py:485
  1.8 0.5 %collective-permute-start = (f32[64,128]{1,0:T(8,128)S(1)}, f32[64,128]{1,0:T(8,128)S(1)}, u32[]{:S(2)}, u32[]{:S(2)}) collective-permute-start(f32[64,128]{1,0:T(8,128)S(1)} %get-tuple-element.37), channel_id=1, source_target_pairs={{0,1},{1,0},{2,3},{3,2},{4,5},{5,4},{6,7},{7,6},{8,9},{9,8},{10,11... | collective-permute-start | bytes 98312 | tf_op jit(solution)/shard_map/ppermute | solution.py:514
  2.3 0.9 %collective-permute-done.both_ref = f32[64,128]{1,0:T(8,128)S(1)} collective-permute-done((f32[64,128]{1,0:T(8,128)S(1)}, f32[64,128]{1,0:T(8,128)S(1)}, u32[]{:S(2)}, u32[]{:S(2)}) %collective-permute-start) | collective-permute-done | bytes 32800 | tf_op jit(solution)/shard_map/ppermute | solution.py:514
  3.1 9.8 %conditional.3 = (f32[32,128]{1,0:T(8,128)S(1)}, f32[32,128]{1,0:T(8,128)S(1)}) conditional(s32[]{:T(128)} %convert_element_type.4, (f32[64,128]{1,0:T(8,128)S(1)}, f32[32,128]{1,0:T(8,128)S(1)}, s32[]{:T(128)}) %tuple.22, () %tuple.23), branch_computations={%region_2.3_spmd, %region_3.4_spmd} | conditional | flops 8215 | bytes 327952 | solution.py:538
  3.2 9.8 %all-gather = f32[256,128]{1,0:T(8,128)S(1)} all-gather(f32[64,128]{1,0:T(8,128)S(1)} %pad_maximum_fusion), channel_id=2, replica_groups={{0,2,4,6},{1,3,5,7},{8,10,12,14},{9,11,13,15},{16,18,20,22},{17,19,21,2..., dimensions={0}, use_global_device_ids=true | all-gather | bytes 163840 | tf_op jit(solution)/shard_map/cond/branch_0_fun/all_gather | solution.py:527
  13.0 0.1 collective-permute-start.2
  13.1 0.5 %collective-permute-start.1 = (f32[8,8]{1,0:T(8,128)S(1)}, f32[8,8]{1,0:T(8,128)S(1)}, u32[]{:S(2)}, u32[]{:S(2)}) collective-permute-start(f32[8,8]{1,0:T(8,128)S(1)} %get-tuple-element.58.modes_ref), channel_id=1, source_target_pairs={{0,1},{1,0},{2,3},{3,2},{4,5},{5,4},{6,7},{7,6},{8,9},{9,8},{10,11... | collective-permute-start | bytes 776 | tf_op jit(solution)/shard_map/ppermute | solution.py:540
  13.5 0.8 %collective-permute-done.1.modes_came_ref = f32[8,8]{1,0:T(8,128)S(1)} collective-permute-done((f32[8,8]{1,0:T(8,128)S(1)}, f32[8,8]{1,0:T(8,128)S(1)}, u32[]{:S(2)}, u32[]{:S(2)}) %collective-permute-start.1) | collective-permute-done | bytes 288 | tf_op jit(solution)/shard_map/ppermute | solution.py:540
  14.4 0.4 %shard_map.65.heights = f32[1056,128]{1,0:T(8,128)S(1)} custom-call(f32[8,8]{1,0:T(8,128)S(1)} %get-tuple-element.58.modes_ref, f32[8,8]{1,0:T(8,128)S(1)} %collective-permute-done.1.modes_came_ref), custom_call_target="tpu_custom_call" | custom-call | tf_op jit(solution)/shard_map/pallas_call | solution.py:542
  14.8 0.0 collective-permute-done.2.above_ref
  14.8 2.0 %shard_map.66 = (f32[256,128]{1,0:T(8,128)S(1)}, f32[256,128]{1,0:T(8,128)S(1)}, f32[256,128]{1,0:T(8,128)S(1)}, f32[256,128]{1,0:T(8,128)S(1)}, f32[256,128]{1,...) custom-call(f32[1056,128]{1,0:T(8,128)S(1)} %shard_map.65.heights, ...), custom_call_target="tpu_custom_call" | custom-call | tf_op jit(solution)/shard_map/pallas_call | solution.py:548
  16.8 8.8 %all_to_all.5 = f32[8,32,128]{2,1,0:T(8,128)S(1)} all-to-all(f32[8,32,128]{2,1,0:T(8,128)S(1)} %bitcast.25), channel_id=1, replica_groups=mesh['grp'=4,'wide'=8] {'wide'}, dimensions={0} | all-to-all | bytes 262144 | tf_op jit(solution)/shard_map/all_to_all | solution.py:563
  25.6 0.7 %shard_map.67 = f32[256,128]{1,0:T(8,128)} custom-call(f32[256,128]{1,0:T(8,128)S(1)} %bitcast.24, f32[256,128]{1,0:T(8,128)S(1)} %get-tuple-element.46.left_gain_ref, f32[256,128]{1,0:T(8,128)S(1)} %get-tuple-element.47.right_gain_ref, f32[256,128]{1,0:T(8,128)S(1)} %get-tuple-element.48.joint_ref, f32[256,128]{1,0:T(8,128)S(1)} %get-tuple-element.49.p_ref, ...), custom_call_target="tpu_custom_call" | custom-call | tf_op jit(solution)/shard_map/pallas_call | solution.py:567
  (5 shorter events, 0.0 us)
Async XLA Ops:
  1.8 1.4 %collective-permute-start = (f32[64,128]{1,0:T(8,128)S(1)}, f32[64,128]{1,0:T(8,128)S(1)}, u32[]{:S(2)}, u32[]{:S(2)}) collective-permute-start(f32[64,128]{1,0:T(8,128)S(1)} %get-tuple-element.37), channel_id=1, source_target_pairs={{0,1},{1,0},{2,3},{3,2},{4,5},{5,4},{6,7},{7,6},{8,9},{9,8},{10,11... | collective-permute-start | bytes 98312 | tf_op jit(solution)/shard_map/ppermute | solution.py:514
  13.0 1.8 %collective-permute-start.2 = (f32[32,128]{1,0:T(8,128)S(1)}, f32[32,128]{1,0:T(8,128)S(1)}, u32[]{:S(2)}, u32[]{:S(2)}) collective-permute-start(f32[32,128]{1,0:T(8,128)S(1)} %get-tuple-element.42), channel_id=1, source_target_pairs={{0,1},{1,0},{2,3},{3,2},{4,5},{5,4},{6,7},{7,6},{8,9},{9,8},{10,11... | collective-permute-start | bytes 49160 | tf_op jit(solution)/shard_map/ppermute | solution.py:539
  13.1 1.3 %collective-permute-start.1 = (f32[8,8]{1,0:T(8,128)S(1)}, f32[8,8]{1,0:T(8,128)S(1)}, u32[]{:S(2)}, u32[]{:S(2)}) collective-permute-start(f32[8,8]{1,0:T(8,128)S(1)} %get-tuple-element.58.modes_ref), channel_id=1, source_target_pairs={{0,1},{1,0},{2,3},{3,2},{4,5},{5,4},{6,7},{7,6},{8,9},{9,8},{10,11... | collective-permute-start | bytes 776 | tf_op jit(solution)/shard_map/ppermute | solution.py:540

commit v15 on v14

--- a/solution.py
+++ b/solution.py
@@ -212,9 +212,9 @@
     return unpack_pair(x_even, x_odd, odd_lane)
 
 
-def load_kernel(
-    step_ref, index_ref, amp_ref, phase_ref, field_ref, conduct_ref,
-    packed_ref, field_out, conduct_out, both_ref, outer_ref,
+def pack_kernel(
+    step_ref, index_ref, amp_ref, phase_ref, field_ref,
+    packed_ref, both_ref, outer_ref,
     index_in, amp_in, phase_in, sems,
 ):
     width = outer_ref.shape[0]
@@ -229,8 +229,6 @@
         (field_ref.at[inner_rows], both_ref.at[pl.ds(0, width)]),
         (field_ref.at[outer_rows], both_ref.at[pl.ds(width, width)]),
         (field_ref.at[outer_rows], outer_ref),
-        (field_ref, field_out),
-        (conduct_ref, conduct_out),
     )
     copies = [pltpu.make_async_copy(a, b, sems.at[n]) for n, (a, b) in enumerate(pairs)]
     for copy in copies:
@@ -253,6 +251,22 @@
         copy.wait()
 
 
+def load_kernel(sizes, field_ref, conduct_ref, field_out, turned_ref, conduct_in, sems):
+    rows, layers, chunks, row_total, layer_total, column_total = sizes
+    width = layers * chunks
+    copies = (
+        pltpu.make_async_copy(field_ref, field_out, sems.at[0]),
+        pltpu.make_async_copy(conduct_ref, conduct_in, sems.at[1]),
+    )
+    for copy in copies:
+        copy.start()
+    for n, (copy, ref) in enumerate(zip(copies, (field_out, conduct_in))):
+        copy.wait()
+        for place in range(width):
+            spot = (n * width + place) * rows
+            turned_ref[spot : spot + rows] = ref[pl.ds(place, rows, stride=width), :]
+
+
 def block_factors(face):
     inv, scaled, chain, u = [], [], [], []
     rows = len(face) - 1
@@ -286,10 +300,10 @@
     return u_first, v_first, u_last, v_last
 
 
-def height_kernel(sizes, modes_ref, modes_came_ref, heights_ref):
+def height_kernel(sizes, handed_ref, came_ref, heights_ref):
     rows, layers, chunks, row_total, layer_total, column_total = sizes
     odd = lax.rem(lax.axis_index("wide"), 2) == 1
-    modes = jnp.where(odd, modes_ref[...], modes_came_ref[...])
+    modes = jnp.where(odd, handed_ref[layers * chunks :], came_ref[layers * chunks :])
     body = height_lines(modes, 0, row_total, row_total, chunks, column_total)
     heights_ref[chunks : (row_total + 1) * chunks] = body
     heights_ref[0:chunks] = body[0:chunks]
@@ -298,7 +312,7 @@
     ]
 
 def main_kernel(
-    sizes, heights, both_ref, below_ref, above_ref, field_ref, conduct_ref,
+    sizes, heights, both_ref, below_ref, came_ref, turned_ref,
     sent_ref, p_ref, u_ref, v_ref, left_gain_ref, right_gain_ref, joint_ref,
     ends, links, halo, solved,
 ):
@@ -378,7 +392,7 @@
     odd = lax.rem(me, 2) == 1
     inner = both_ref[0:width]
     below = jnp.where(odd, inner, below_ref[...])
-    above = jnp.where(odd, above_ref[...], inner)
+    above = jnp.where(odd, came_ref[0:width], inner)
     halo[0:width] = jnp.where(me == 0, 0.0, below)
     halo[width : 2 * width] = jnp.where(me == blocks - 1, 0.0, above)
     lane = lax.broadcasted_iota(jnp.int32, (rows, LANES), 1)
@@ -403,11 +417,13 @@
         low_sum, high_sum = h + h_low, h + h_high
         for k in range(layers):
             place = c * layers + k
-            f_mid = field_ref[pl.ds(place, rows, stride=width), :]
+            f_mid = turned_ref[place * rows : (place + 1) * rows]
             f_low, f_high = neighbours(
                 f_mid, halo[pl.ds(place, 1), :], halo[pl.ds(width + place, 1), :]
             )
-            g[k].append(conduct_ref[pl.ds(place, rows, stride=width), :] * (1.0 + zeta[k] * h))
+            g[k].append(
+                turned_ref[(width + place) * rows : (width + place + 1) * rows] * (1.0 + zeta[k] * h)
+            )
             f[k].append(f_mid)
             along = (weight + (half * zeta[k]) * high_sum) * (f_high - f_mid) - (
                 weight + (half * zeta[k]) * low_sum
@@ -482,30 +498,29 @@
     def lines(count):
         return jax.ShapeDtypeStruct((count * width, LANES), f32)
 
-    packed, field_lines, conduct_lines, both, outer = pl.pallas_call(
-        load_kernel,
-        out_shape=(
-            jax.ShapeDtypeStruct((mode_index.shape[0], 8), f32),
-            lines(rows),
-            lines(rows),
-            lines(2),
-            lines(1),
-        ),
-        in_specs=[pl.BlockSpec(memory_space=pltpu.SMEM)] + [hbm] * 5,
-        scratch_shapes=[
-            pltpu.SMEM(mode_index.shape, jnp.int32),
-            pltpu.SMEM(mode_amp.shape, f32),
-            pltpu.SMEM(mode_phase.shape, f32),
-            pltpu.SemaphoreType.DMA((8,)),
-        ],
-        compiler_params=limit,
-    )(
+    step_index, mode_index, mode_amp, mode_phase, field_lines, conduct_lines = (
         step_index,
         *(
             pltpu.with_memory_space_constraint(a, pltpu.HBM)
             for a in (mode_index, mode_amp, mode_phase, to_lines(field), to_lines(conduct))
         ),
     )
+    packed, both, outer = pl.pallas_call(
+        pack_kernel,
+        out_shape=(
+            jax.ShapeDtypeStruct((mode_index.shape[0], LANES), f32),
+            lines(2),
+            lines(1),
+        ),
+        in_specs=[pl.BlockSpec(memory_space=pltpu.SMEM)] + [hbm] * 4,
+        scratch_shapes=[
+            pltpu.SMEM(mode_index.shape, jnp.int32),
+            pltpu.SMEM(mode_amp.shape, f32),
+            pltpu.SMEM(mode_phase.shape, f32),
+            pltpu.SemaphoreType.DMA((6,)),
+        ],
+        compiler_params=limit,
+    )(step_index, mode_index, mode_amp, mode_phase, field_lines)
 
     place = lax.axis_index("wide")
     odd = place % 2 == 1
@@ -536,14 +551,29 @@
         return jnp.zeros_like(own), jnp.zeros_like(own)
 
     below, above = lax.cond(odd, no_rows, gather_rows, outer, both_came)
-    above_came = lax.ppermute(above, "wide", swaps)
-    modes_came = lax.ppermute(modes, "wide", swaps)
-
+    handed = jnp.concatenate([above, modes], 0)
+    came = lax.ppermute(handed, "wide", swaps)
+    handed, field, conduct = lax.optimization_barrier((handed, field, conduct))
+    field_lines, turned = pl.pallas_call(
+        functools.partial(load_kernel, sizes),
+        out_shape=(lines(rows), lines(2 * rows)),
+        in_specs=[hbm] * 2,
+        scratch_shapes=[
+            pltpu.VMEM((rows * width, LANES), f32),
+            pltpu.SemaphoreType.DMA((2,)),
+        ],
+        compiler_params=limit,
+    )(
+        *(
+            pltpu.with_memory_space_constraint(to_lines(a), pltpu.HBM)
+            for a in (field, conduct)
+        )
+    )
     heights = pl.pallas_call(
         functools.partial(height_kernel, sizes),
         out_shape=jax.ShapeDtypeStruct(((row_total + 2) * chunks, LANES), f32),
         compiler_params=limit,
-    )(modes, modes_came)
+    )(handed, came)
 
     sent, p, u, v, left_gain, right_gain, joint = pl.pallas_call(
         functools.partial(main_kernel, sizes),
@@ -558,7 +588,7 @@
             pltpu.VMEM((rows * width, LANES), f32),
         ],
         compiler_params=limit,
-    )(heights, both_came, below, above_came, field_lines, conduct_lines)
+    )(heights, both_came, below, came, turned)
 
     came = lax.all_to_all(
         sent.reshape(wide_count, width, LANES), "wide", split_axis=0, concat_axis=0

time: 26.5 us -> 26.3 us (level)
  Pallas kernels: 4.2 us -> 4.99 us
  waiting for transfers between devices: 1.68 us -> 0.94 us
  starting transfers between devices: 1.09 us -> 0.59 us
    pallas_call x1 -> x2, Pallas kernels: 1.11 us -> 1.95 us  [the longest x1 1.09 us: on_device(): pl.pallas_call(functools.partial(load_kernel, sizes), out_shape=(lines(ro...]
    ppermute x2 -> x1, waiting for transfers between devices: 0.83 us -> 0.08 us  [on_device(): came = lax.ppermute(handed, 'wide', swaps)]
    ppermute x2 -> x1, starting transfers between devices: 0.57 us -> 0.07 us  [on_device(): came = lax.ppermute(handed, 'wide', swaps)]
  transfers between devices with their start and end apart: 3 -> 2, of which waited for: 2 -> 2; matrix products, arithmetic and copies ran while one was open for 0% -> 0% of each run, Pallas kernels for 1% -> 4%
where the time goes in v15:
time: 26.3 us; the launch traced here: 26 us
  blocking collectives  18.7 us (71%)
  Pallas kernels  4.99 us (19%)
  waiting for transfers between devices  0.94 us (4%)
  between operations  0.71 us (3%)
  starting transfers between devices  0.59 us (2%)
    all_gather x1, blocking collectives, gather_rows(): lax.all_gather(rows_sent, 'wide', axis_index_groups=cores, axis=0)  9.8 us
    all_to_all x1, blocking collectives, on_device(): lax.all_to_all(sent.reshape(wide_count, width, LANES), 'wide', split_axis...  8.93 us
    pallas_call x1, Pallas kernels, on_device(): pl.pallas_call(functools.partial(main_kernel, sizes), out_shape=(lines(wi...  1.94 us
    pallas_call x1, Pallas kernels, on_device(): pl.pallas_call(functools.partial(load_kernel, sizes), out_shape=(lines(ro...  1.09 us
    pallas_call x1, Pallas kernels, on_device(): pl.pallas_call(pack_kernel, out_shape=(jax.ShapeDtypeStruct((mode_index.s...  0.86 us
    ppermute x1, waiting for transfers between devices, on_device(): both_came = lax.ppermute(both, 'wide', swaps)  0.86 us
    pallas_call x1, Pallas kernels, on_device(): pl.pallas_call(functools.partial(last_kernel, sizes), out_shape=lines(row...  0.73 us
  transfers between devices with their start and end apart: 2, of which 2 were waited for; matrix products, arithmetic and copies ran while one was open for 0% of the time, Pallas kernels for 4%

profile of v15, /device:TPU:0, one launch (start us, length us, event | category | flops | bytes accessed | tf_op | source)
XLA Modules:
  0.0 26.0 jit_solution(2786425592974904853)
XLA Ops:
  0.7 0.9 %shard_map.64 = (f32[2,128]{1,0:T(2,128)S(1)}, f32[64,128]{1,0:T(8,128)S(1)}, f32[32,128]{1,0:T(8,128)S(1)}) custom-call(s32[1]{0:T(128)S(6)} %copy.22.step_ref, s32[2,3]{1,0:T(2,128)} %index_ref.1, f32[2]{0:T(128)} %amp_ref.1, f32[2]{0:T(128)} %phase_ref.1, f32[256,128]{1,0:T(8,128)} %bitcast.31), custom_call_target="tpu_custom_call" | custom-call | tf_op jit(solution)/shard_map/pallas_call | solution.py:508
  1.5 0.5 %collective-permute-start = (f32[64,128]{1,0:T(8,128)S(1)}, f32[64,128]{1,0:T(8,128)S(1)}, u32[]{:S(2)}, u32[]{:S(2)}) collective-permute-start(f32[64,128]{1,0:T(8,128)S(1)} %get-tuple-element.40), channel_id=1, source_target_pairs={{0,1},{1,0},{2,3},{3,2},{4,5},{5,4},{6,7},{7,6},{8,9},{9,8},{10,11... | collective-permute-start | bytes 98312 | tf_op jit(solution)/shard_map/ppermute | solution.py:529
  2.0 0.9 %collective-permute-done.both_ref = f32[64,128]{1,0:T(8,128)S(1)} collective-permute-done((f32[64,128]{1,0:T(8,128)S(1)}, f32[64,128]{1,0:T(8,128)S(1)}, u32[]{:S(2)}, u32[]{:S(2)}) %collective-permute-start) | collective-permute-done | bytes 32800 | tf_op jit(solution)/shard_map/ppermute | solution.py:529
  2.9 9.8 %conditional.3 = (f32[32,128]{1,0:T(8,128)S(1)}, f32[32,128]{1,0:T(8,128)S(1)}) conditional(s32[]{:T(128)} %convert_element_type.4, (f32[64,128]{1,0:T(8,128)S(1)}, f32[32,128]{1,0:T(8,128)S(1)}, s32[]{:T(128)}) %tuple.23, () %tuple.24), branch_computations={%region_2.3_spmd, %region_3.4_spmd} | conditional | flops 8215 | bytes 327952 | solution.py:553
  2.9 9.8 %all-gather = f32[256,128]{1,0:T(8,128)S(1)} all-gather(f32[64,128]{1,0:T(8,128)S(1)} %pad_maximum_fusion), channel_id=2, replica_groups={{0,2,4,6},{1,3,5,7},{8,10,12,14},{9,11,13,15},{16,18,20,22},{17,19,21,2..., dimensions={0}, use_global_device_ids=true | all-gather | bytes 163840 | tf_op jit(solution)/shard_map/cond/branch_0_fun/all_gather | solution.py:542
  12.7 0.1 collective-permute-start.1
  12.8 1.1 %shard_map.66 = (f32[256,128]{1,0:T(8,128)S(1)}, f32[512,128]{1,0:T(8,128)S(1)}) custom-call(f32[256,128]{1,0:T(8,128)} %bitcast.32, f32[256,128]{1,0:T(8,128)} %bitcast.34), custom_call_target="tpu_custom_call" | custom-call | tf_op jit(solution)/shard_map/pallas_call | solution.py:557
  13.9 0.1 collective-permute-done.1.came_ref
  14.0 0.4 %shard_map.65.heights = f32[1056,128]{1,0:T(8,128)S(1)} custom-call(f32[40,128]{1,0:T(8,128)S(1)} %constant_dynamic-update-slice_fusion.handed_ref, f32[40,128]{1,0:T(8,128)S(1)} %collective-permute-done.1.came_ref), custom_call_target="tpu_custom_call" | custom-call | tf_op jit(solution)/shard_map/pallas_call | solution.py:572
  14.4 1.9 %shard_map.67 = (f32[256,128]{1,0:T(8,128)S(1)}, f32[256,128]{1,0:T(8,128)S(1)}, f32[256,128]{1,0:T(8,128)S(1)}, f32[256,128]{1,0:T(8,128)S(1)}, f32[256,128]{1,...) custom-call(f32[1056,128]{1,0:T(8,128)S(1)} %shard_map.65.heights, ...), custom_call_target="tpu_custom_call" | custom-call | tf_op jit(solution)/shard_map/pallas_call | solution.py:578
  16.3 8.9 %all_to_all.5 = f32[8,32,128]{2,1,0:T(8,128)S(1)} all-to-all(f32[8,32,128]{2,1,0:T(8,128)S(1)} %bitcast.30), channel_id=1, replica_groups=mesh['grp'=4,'wide'=8] {'wide'}, dimensions={0} | all-to-all | bytes 262144 | tf_op jit(solution)/shard_map/all_to_all | solution.py:593
  25.3 0.7 %shard_map.68 = f32[256,128]{1,0:T(8,128)} custom-call(f32[256,128]{1,0:T(8,128)S(1)} %bitcast.29, f32[256,128]{1,0:T(8,128)S(1)} %get-tuple-element.51.left_gain_ref, f32[256,128]{1,0:T(8,128)S(1)} %get-tuple-element.52.right_gain_ref, f32[256,128]{1,0:T(8,128)S(1)} %get-tuple-element.53.joint_ref, f32[256,128]{1,0:T(8,128)S(1)} %get-tuple-element.54.p_ref, ...), custom_call_target="tpu_custom_call" | custom-call | tf_op jit(solution)/shard_map/pallas_call | solution.py:597
  (7 shorter events, 0.0 us)
Async XLA Ops:
  1.5 1.4 %collective-permute-start = (f32[64,128]{1,0:T(8,128)S(1)}, f32[64,128]{1,0:T(8,128)S(1)}, u32[]{:S(2)}, u32[]{:S(2)}) collective-permute-start(f32[64,128]{1,0:T(8,128)S(1)} %get-tuple-element.40), channel_id=1, source_target_pairs={{0,1},{1,0},{2,3},{3,2},{4,5},{5,4},{6,7},{7,6},{8,9},{9,8},{10,11... | collective-permute-start | bytes 98312 | tf_op jit(solution)/shard_map/ppermute | solution.py:529
  12.7 1.3 %collective-permute-start.1 = (f32[40,128]{1,0:T(8,128)S(1)}, f32[40,128]{1,0:T(8,128)S(1)}, u32[]{:S(2)}, u32[]{:S(2)}) collective-permute-start(f32[40,128]{1,0:T(8,128)S(1)} %constant_dynamic-update-slice_fusion.handed_ref), channel_id=1, source_target_pairs={{0,1},{1,0},{2,3},{3,2},{4,5},{5,4},{6,7},{7,6},{8,9},{9,8},{10,11... | collective-permute-start | bytes 61448 | tf_op jit(solution)/shard_map/ppermute | solution.py:555

commit v16 on v15

--- a/solution.py
+++ b/solution.py
@@ -286,18 +286,16 @@
 
 def block_ends(face):
     rows = len(face) - 1
-    down = 1.0 + face[0]
-    up = 1.0 + face[rows]
-    v_first = None
+    rest = 1.0 + face[0]
+    chain = None
     for j in range(rows):
-        v_last = face[j + 1] * inverse(down + face[j + 1])
-        v_first = v_last if v_first is None else v_first * v_last
-        u_first = face[rows - 1 - j] * inverse(up + face[rows - 1 - j])
+        inv = inverse(rest + face[j + 1])
+        v_last = face[j + 1] * inv
+        corner = corner + chain * (chain * inv) if j else inv
+        chain = chain * v_last if j else v_last
         if j < rows - 1:
-            down = 1.0 + down * v_last
-            up = 1.0 + up * u_first
-    u_last = v_first * (face[0] * inverse(face[rows]))
-    return u_first, v_first, u_last, v_last
+            rest = 1.0 + rest * v_last
+    return face[0] * corner, chain, chain * (face[0] * inverse(face[rows])), v_last
 
 
 def height_kernel(sizes, handed_ref, came_ref, heights_ref):
@@ -326,68 +324,6 @@
     ]
     half = 0.5 * weight
     own_start = pl.multiple_of(me * (rows * chunks), 8)
-
-    def faces(start):
-        h = [heights[pl.ds(start + j * chunks, chunks), :] for j in range(rows + 2)]
-        out = []
-        for j in range(rows + 1):
-            both = h[j] + h[j + 1]
-            out.append(jnp.concatenate([weight + (half * z) * both for z in zeta], 0))
-        return out
-
-    def keep_ends(b, values):
-        base = pl.multiple_of(b * (4 * width), 8)
-        for n, value in enumerate(values):
-            ends[pl.ds(base + n * width, width), :] = value
-
-    inv, scaled, chain, u, v = block_factors(faces(own_start))
-    for j in range(rows):
-        u_ref[j * width : (j + 1) * width] = u[j]
-        v_ref[j * width : (j + 1) * width] = v[j]
-    keep_ends(me, (u[0], v[0], u[-1], v[-1]))
-
-    def other_block(n):
-        b = lax.rem(me + 1 + n, blocks)
-        keep_ends(b, block_ends(faces(pl.multiple_of(b * (rows * chunks), 8))))
-
-    if blocks <= 8:
-        for n in range(blocks - 1):
-            other_block(n)
-    else:
-        lax.fori_loop(0, blocks - 1, lambda n, carry: (other_block(n), carry)[1], 0)
-
-    def end(b, n):
-        return ends[(4 * b + n) * width : (4 * b + n + 1) * width]
-
-    left = jnp.zeros((width, LANES), f32)
-    right = jnp.zeros((width, LANES), f32)
-    for b in range(blocks):
-        u_first, v_first, u_last, v_last = (end(b, n) for n in range(4))
-        gain = u_last * inverse(1.0 - u_first * left)
-        left_gain_ref[b * width : (b + 1) * width] = gain
-        links[b * width : (b + 1) * width] = left
-        left = v_last + gain * left * v_first
-        b = blocks - 1 - b
-        u_first, v_first, u_last, v_last = (end(b, n) for n in range(4))
-        gain = v_first * inverse(1.0 - v_last * right)
-        right_gain_ref[b * width : (b + 1) * width] = gain
-        links[(blocks + b) * width : (blocks + b + 1) * width] = right
-        right = u_first + gain * right * u_last
-
-    own = pl.ds(pl.multiple_of(me * width, 8), width)
-    left_link = links[own, :]
-    right_link = links[pl.ds(pl.multiple_of((blocks + me) * width, 8), width), :]
-    a = 1.0 - left_link * u[0]
-    b = left_link * v[0]
-    c = right_link * u[-1]
-    d = 1.0 - right_link * v[-1]
-    by = inverse(a * d - b * c)
-    joint = (
-        left_gain_ref[own, :] * left_link, right_gain_ref[own, :] * right_link,
-        left_link, right_link, d * by, b * by, c * by, a * by,
-    )
-    for n, value in enumerate(joint):
-        joint_ref[n * width : (n + 1) * width] = value
 
     odd = lax.rem(me, 2) == 1
     inner = both_ref[0:width]
@@ -436,6 +372,68 @@
                 spot = pl.ds((k + n) * chunks + c, rows, stride=width)
                 solved[spot, :] = both[n][c] - 2.0 * f[k + n][c]
 
+    def faces(start):
+        h = [heights[pl.ds(start + j * chunks, chunks), :] for j in range(rows + 2)]
+        out = []
+        for j in range(rows + 1):
+            both = h[j] + h[j + 1]
+            out.append(jnp.concatenate([weight + (half * z) * both for z in zeta], 0))
+        return out
+
+    def keep_ends(b, values):
+        base = pl.multiple_of(b * (4 * width), 8)
+        for n, value in enumerate(values):
+            ends[pl.ds(base + n * width, width), :] = value
+
+    inv, scaled, chain, u, v = block_factors(faces(own_start))
+    for j in range(rows):
+        u_ref[j * width : (j + 1) * width] = u[j]
+        v_ref[j * width : (j + 1) * width] = v[j]
+    keep_ends(me, (u[0], v[0], u[-1], v[-1]))
+
+    def other_block(n):
+        b = lax.rem(me + 1 + n, blocks)
+        keep_ends(b, block_ends(faces(pl.multiple_of(b * (rows * chunks), 8))))
+
+    if blocks <= 8:
+        for n in range(blocks - 1):
+            other_block(n)
+    else:
+        lax.fori_loop(0, blocks - 1, lambda n, carry: (other_block(n), carry)[1], 0)
+
+    def end(b, n):
+        return ends[(4 * b + n) * width : (4 * b + n + 1) * width]
+
+    left = jnp.zeros((width, LANES), f32)
+    right = jnp.zeros((width, LANES), f32)
+    for b in range(blocks):
+        u_first, v_first, u_last, v_last = (end(b, n) for n in range(4))
+        gain = u_last * inverse(1.0 - u_first * left)
+        left_gain_ref[b * width : (b + 1) * width] = gain
+        links[b * width : (b + 1) * width] = left
+        left = v_last + gain * left * v_first
+        b = blocks - 1 - b
+        u_first, v_first, u_last, v_last = (end(b, n) for n in range(4))
+        gain = v_first * inverse(1.0 - v_last * right)
+        right_gain_ref[b * width : (b + 1) * width] = gain
+        links[(blocks + b) * width : (blocks + b + 1) * width] = right
+        right = u_first + gain * right * u_last
+
+    own = pl.ds(pl.multiple_of(me * width, 8), width)
+    left_link = links[own, :]
+    right_link = links[pl.ds(pl.multiple_of((blocks + me) * width, 8), width), :]
+    a = 1.0 - left_link * u[0]
+    b = left_link * v[0]
+    c = right_link * u[-1]
+    d = 1.0 - right_link * v[-1]
+    by = inverse(a * d - b * c)
+    joint = (
+        left_gain_ref[own, :] * left_link, right_gain_ref[own, :] * right_link,
+        left_link, right_link, d * by, b * by, c * by, a * by,
+    )
+    for n, value in enumerate(joint):
+        joint_ref[n * width : (n + 1) * width] = value
+
     def part(ref, j):
         return ref[j * width : (j + 1) * width]
 

time: 26.3 us -> 26.3 us (level)
  no operation moved by 1% of the time
where the time goes in v16:
time: 26.3 us; the launch traced here: 26 us
  blocking collectives  18.7 us (71%)
  Pallas kernels  5 us (19%)
  waiting for transfers between devices  0.94 us (4%)
  between operations  0.71 us (3%)
  starting transfers between devices  0.59 us (2%)
    all_gather x1, blocking collectives, gather_rows(): lax.all_gather(rows_sent, 'wide', axis_index_groups=cores, axis=0)  9.8 us
    all_to_all x1, blocking collectives, on_device(): lax.all_to_all(sent.reshape(wide_count, width, LANES), 'wide', split_axis...  8.93 us
    pallas_call x1, Pallas kernels, on_device(): pl.pallas_call(functools.partial(main_kernel, sizes), out_shape=(lines(wi...  1.95 us
    pallas_call x1, Pallas kernels, on_device(): pl.pallas_call(functools.partial(load_kernel, sizes), out_shape=(lines(ro...  1.09 us
    pallas_call x1, Pallas kernels, on_device(): pl.pallas_call(pack_kernel, out_shape=(jax.ShapeDtypeStruct((mode_index.s...  0.86 us
    ppermute x1, waiting for transfers between devices, on_device(): both_came = lax.ppermute(both, 'wide', swaps)  0.86 us
    pallas_call x1, Pallas kernels, on_device(): pl.pallas_call(functools.partial(last_kernel, sizes), out_shape=lines(row...  0.73 us
  transfers between devices with their start and end apart: 2, of which 2 were waited for; matrix products, arithmetic and copies ran while one was open for 0% of the time, Pallas kernels for 4%

profile of v16, /device:TPU:0, one launch (start us, length us, event | category | flops | bytes accessed | tf_op | source)
XLA Modules:
  0.0 26.0 jit_solution(13397992011134050559)
XLA Ops:
  0.7 0.9 %shard_map.64 = (f32[2,128]{1,0:T(2,128)S(1)}, f32[64,128]{1,0:T(8,128)S(1)}, f32[32,128]{1,0:T(8,128)S(1)}) custom-call(s32[1]{0:T(128)S(6)} %copy.22.step_ref, s32[2,3]{1,0:T(2,128)} %index_ref.1, f32[2]{0:T(128)} %amp_ref.1, f32[2]{0:T(128)} %phase_ref.1, f32[256,128]{1,0:T(8,128)} %bitcast.31), custom_call_target="tpu_custom_call" | custom-call | tf_op jit(solution)/shard_map/pallas_call | solution.py:506
  1.5 0.5 %collective-permute-start = (f32[64,128]{1,0:T(8,128)S(1)}, f32[64,128]{1,0:T(8,128)S(1)}, u32[]{:S(2)}, u32[]{:S(2)}) collective-permute-start(f32[64,128]{1,0:T(8,128)S(1)} %get-tuple-element.40), channel_id=1, source_target_pairs={{0,1},{1,0},{2,3},{3,2},{4,5},{5,4},{6,7},{7,6},{8,9},{9,8},{10,11... | collective-permute-start | bytes 98312 | tf_op jit(solution)/shard_map/ppermute | solution.py:527
  2.0 0.9 %collective-permute-done.both_ref = f32[64,128]{1,0:T(8,128)S(1)} collective-permute-done((f32[64,128]{1,0:T(8,128)S(1)}, f32[64,128]{1,0:T(8,128)S(1)}, u32[]{:S(2)}, u32[]{:S(2)}) %collective-permute-start) | collective-permute-done | bytes 32800 | tf_op jit(solution)/shard_map/ppermute | solution.py:527
  2.9 9.8 %conditional.3 = (f32[32,128]{1,0:T(8,128)S(1)}, f32[32,128]{1,0:T(8,128)S(1)}) conditional(s32[]{:T(128)} %convert_element_type.4, (f32[64,128]{1,0:T(8,128)S(1)}, f32[32,128]{1,0:T(8,128)S(1)}, s32[]{:T(128)}) %tuple.23, () %tuple.24), branch_computations={%region_2.3_spmd, %region_3.4_spmd} | conditional | flops 8215 | bytes 327952 | solution.py:551
  2.9 9.8 %all-gather = f32[256,128]{1,0:T(8,128)S(1)} all-gather(f32[64,128]{1,0:T(8,128)S(1)} %pad_maximum_fusion), channel_id=2, replica_groups={{0,2,4,6},{1,3,5,7},{8,10,12,14},{9,11,13,15},{16,18,20,22},{17,19,21,2..., dimensions={0}, use_global_device_ids=true | all-gather | bytes 163840 | tf_op jit(solution)/shard_map/cond/branch_0_fun/all_gather | solution.py:540
  12.7 0.1 collective-permute-start.1
  12.8 1.1 %shard_map.66 = (f32[256,128]{1,0:T(8,128)S(1)}, f32[512,128]{1,0:T(8,128)S(1)}) custom-call(f32[256,128]{1,0:T(8,128)} %bitcast.32, f32[256,128]{1,0:T(8,128)} %bitcast.34), custom_call_target="tpu_custom_call" | custom-call | tf_op jit(solution)/shard_map/pallas_call | solution.py:555
  13.9 0.1 collective-permute-done.1.came_ref
  14.0 0.4 %shard_map.65.heights = f32[1056,128]{1,0:T(8,128)S(1)} custom-call(f32[40,128]{1,0:T(8,128)S(1)} %constant_dynamic-update-slice_fusion.handed_ref, f32[40,128]{1,0:T(8,128)S(1)} %collective-permute-done.1.came_ref), custom_call_target="tpu_custom_call" | custom-call | tf_op jit(solution)/shard_map/pallas_call | solution.py:570
  14.4 1.9 %shard_map.67 = (f32[256,128]{1,0:T(8,128)S(1)}, f32[256,128]{1,0:T(8,128)S(1)}, f32[256,128]{1,0:T(8,128)S(1)}, f32[256,128]{1,0:T(8,128)S(1)}, f32[256,128]{1,...) custom-call(f32[1056,128]{1,0:T(8,128)S(1)} %shard_map.65.heights, ...), custom_call_target="tpu_custom_call" | custom-call | tf_op jit(solution)/shard_map/pallas_call | solution.py:576
  16.3 8.9 %all_to_all.5 = f32[8,32,128]{2,1,0:T(8,128)S(1)} all-to-all(f32[8,32,128]{2,1,0:T(8,128)S(1)} %bitcast.30), channel_id=1, replica_groups=mesh['grp'=4,'wide'=8] {'wide'}, dimensions={0} | all-to-all | bytes 262144 | tf_op jit(solution)/shard_map/all_to_all | solution.py:591
  25.3 0.7 %shard_map.68 = f32[256,128]{1,0:T(8,128)} custom-call(f32[256,128]{1,0:T(8,128)S(1)} %bitcast.29, f32[256,128]{1,0:T(8,128)S(1)} %get-tuple-element.51.left_gain_ref, f32[256,128]{1,0:T(8,128)S(1)} %get-tuple-element.52.right_gain_ref, f32[256,128]{1,0:T(8,128)S(1)} %get-tuple-element.53.joint_ref, f32[256,128]{1,0:T(8,128)S(1)} %get-tuple-element.54.p_ref, ...), custom_call_target="tpu_custom_call" | custom-call | tf_op jit(solution)/shard_map/pallas_call | solution.py:595
  (7 shorter events, 0.0 us)
Async XLA Ops:
  1.5 1.4 %collective-permute-start = (f32[64,128]{1,0:T(8,128)S(1)}, f32[64,128]{1,0:T(8,128)S(1)}, u32[]{:S(2)}, u32[]{:S(2)}) collective-permute-start(f32[64,128]{1,0:T(8,128)S(1)} %get-tuple-element.40), channel_id=1, source_target_pairs={{0,1},{1,0},{2,3},{3,2},{4,5},{5,4},{6,7},{7,6},{8,9},{9,8},{10,11... | collective-permute-start | bytes 98312 | tf_op jit(solution)/shard_map/ppermute | solution.py:527
  12.7 1.3 %collective-permute-start.1 = (f32[40,128]{1,0:T(8,128)S(1)}, f32[40,128]{1,0:T(8,128)S(1)}, u32[]{:S(2)}, u32[]{:S(2)}) collective-permute-start(f32[40,128]{1,0:T(8,128)S(1)} %constant_dynamic-update-slice_fusion.handed_ref), channel_id=1, source_target_pairs={{0,1},{1,0},{2,3},{3,2},{4,5},{5,4},{6,7},{7,6},{8,9},{9,8},{10,11... | collective-permute-start | bytes 61448 | tf_op jit(solution)/shard_map/ppermute | solution.py:553

commit v17 on v15

--- a/solution.py
+++ b/solution.py
@@ -112,7 +112,7 @@
     ]
 
 
-def solve_chunks(diagonal, link, rhs):
+def solve_chunks(diagonal, link, rhs, tick):
     count = len(rhs)
     if count == 1:
         return [rhs[0] * inverse(diagonal[0])]
@@ -131,7 +131,9 @@
         odd_diagonal.append(d)
         odd_rhs.append(r)
         odd_link.append(e)
-    odd = solve_chunks(odd_diagonal, odd_link, odd_rhs)
+    tick()
+    odd = solve_chunks(odd_diagonal, odd_link, odd_rhs, tick)
+    tick()
     out = [None] * count
     out[1::2] = odd
     for i in range(0, count, 2):
@@ -144,24 +146,27 @@
     return out
 
 
-def reduce_lanes(diagonal, link, rhs, lane, stride):
+def reduce_lanes(diagonal, link, rhs, lane, stride, tick):
     count = len(rhs)
     while stride < LANES:
         inv = [inverse(d) for d in diagonal]
         t = [q * r for q, r in zip(inv, rhs)]
         w = [q * e for q, e in zip(inv, link)]
+        tick()
         low_d = from_left([e * v for e, v in zip(link, w)], stride, lane)
         low_r = from_left([e * v for e, v in zip(link, t)], stride, lane)
         high_q = from_right(inv, stride, lane)
         high_t = from_right(t, stride, lane)
         high_w = from_right(w, stride, lane)
+        tick()
         diagonal = [
             diagonal[c] - low_d[c] - link[c] * (link[c] * high_q[c]) for c in range(count)
         ]
         rhs = [rhs[c] + low_r[c] + link[c] * high_t[c] for c in range(count)]
         link = [link[c] * high_w[c] for c in range(count)]
         stride *= 2
-    return solve_chunks(diagonal, link, rhs)
+        tick()
+    return solve_chunks(diagonal, link, rhs, tick)
 
 
 def pack_pair(a, b, odd_lane):
@@ -176,7 +181,7 @@
     return a, b
 
 
-def solve_x_pair(g_pair, rhs_pair, lane):
+def solve_x_pair(g_pair, rhs_pair, lane, tick):
     odd_lane = (lane & 1) == 1
     first_cell = lane < 2
     last_cell = lane >= LANES - 2
@@ -195,16 +200,18 @@
     link[-1] = jnp.where(last_cell, 0.0, link[-1])
     link_before = list(face_before)
     link_before[0] = jnp.where(first_cell, 0.0, link_before[0])
+    tick()
     t = [q * r for q, r in zip(inv, r_even)]
     w = [q * e for q, e in zip(inv, face)]
     next_q = from_right(inv, 2, lane)
     next_t = from_right(t, 2, lane)
     next_w = from_right(w, 2, lane)
+    tick()
     diagonal = [
         d - e * v - l * (l * q) for d, e, v, l, q in zip(d_odd, face, w, link, next_q)
     ]
     rhs = [r + e * v + l * n for r, e, v, l, n in zip(r_odd, face, t, link, next_t)]
-    x_odd = reduce_lanes(diagonal, [l * n for l, n in zip(link, next_w)], rhs, lane, 2)
+    x_odd = reduce_lanes(diagonal, [l * n for l, n in zip(link, next_w)], rhs, lane, 2, tick)
     x_before = from_left(x_odd, 2, lane)
     x_even = [
         v + q * (l * b) + u * x for v, q, l, b, u, x in zip(t, inv, link_before, x_before, w, x_odd)
@@ -277,6 +284,7 @@
         chain.append(face[j + 1] * inv[j])
         u.append(scaled[j] * u[-1] if j else scaled[j])
         rest = 1.0 + rest * chain[j]
+        yield
     v = list(chain)
     for j in range(rows - 2, -1, -1):
         u[j] = u[j] + chain[j] * u[j + 1]
@@ -284,20 +292,22 @@
     return inv, scaled, chain, u, v
 
 
-def block_ends(face):
-    rows = len(face) - 1
-    down = 1.0 + face[0]
-    up = 1.0 + face[rows]
-    v_first = None
+def block_ends(face, rows):
+    rest = [1.0 + f for f in face(0)]
+    chain, corner = None, None
     for j in range(rows):
-        v_last = face[j + 1] * inverse(down + face[j + 1])
-        v_first = v_last if v_first is None else v_first * v_last
-        u_first = face[rows - 1 - j] * inverse(up + face[rows - 1 - j])
+        after = face(j + 1)
+        inv = [inverse(r + f) for r, f in zip(rest, after)]
+        v_last = [f * q for f, q in zip(after, inv)]
+        corner = [a + b * (b * q) for a, b, q in zip(corner, chain, inv)] if j else inv
+        chain = [b * v for b, v in zip(chain, v_last)] if j else v_last
         if j < rows - 1:
-            down = 1.0 + down * v_last
-            up = 1.0 + up * u_first
-    u_last = v_first * (face[0] * inverse(face[rows]))
-    return u_first, v_first, u_last, v_last
+            rest = [1.0 + r * v for r, v in zip(rest, v_last)]
+        yield
+    return [
+        (f * a, b, b * (f * inverse(g)), v)
+        for f, g, a, b, v in zip(face(0), after, corner, chain, v_last)
+    ]
 
 
 def height_kernel(sizes, handed_ref, came_ref, heights_ref):
@@ -327,67 +337,80 @@
     half = 0.5 * weight
     own_start = pl.multiple_of(me * (rows * chunks), 8)
 
-    def faces(start):
-        h = [heights[pl.ds(start + j * chunks, chunks), :] for j in range(rows + 2)]
-        out = []
-        for j in range(rows + 1):
-            both = h[j] + h[j + 1]
-            out.append(jnp.concatenate([weight + (half * z) * both for z in zeta], 0))
-        return out
+    def face(start, j):
+        both = heights[pl.ds(start + j * chunks, 2 * chunks), :]
+        both = both[:chunks] + both[chunks:]
+        return jnp.concatenate([weight + (half * z) * both for z in zeta], 0)
 
     def keep_ends(b, values):
         base = pl.multiple_of(b * (4 * width), 8)
         for n, value in enumerate(values):
             ends[pl.ds(base + n * width, width), :] = value
 
-    inv, scaled, chain, u, v = block_factors(faces(own_start))
-    for j in range(rows):
-        u_ref[j * width : (j + 1) * width] = u[j]
-        v_ref[j * width : (j + 1) * width] = v[j]
-    keep_ends(me, (u[0], v[0], u[-1], v[-1]))
-
-    def other_block(n):
-        b = lax.rem(me + 1 + n, blocks)
-        keep_ends(b, block_ends(faces(pl.multiple_of(b * (rows * chunks), 8))))
-
-    if blocks <= 8:
-        for n in range(blocks - 1):
-            other_block(n)
-    else:
-        lax.fori_loop(0, blocks - 1, lambda n, carry: (other_block(n), carry)[1], 0)
+    factors = []
+
+    def other_blocks(first, count):
+        spots = [lax.rem(me + 1 + first + n, blocks) for n in range(count)]
+        starts = [pl.multiple_of(b * (rows * chunks), 8) for b in spots]
+        values = yield from block_ends(lambda j: [face(start, j) for start in starts], rows)
+        for b, ends_of_one in zip(spots, values):
+            keep_ends(b, ends_of_one)
 
     def end(b, n):
         return ends[(4 * b + n) * width : (4 * b + n + 1) * width]
 
-    left = jnp.zeros((width, LANES), f32)
-    right = jnp.zeros((width, LANES), f32)
-    for b in range(blocks):
-        u_first, v_first, u_last, v_last = (end(b, n) for n in range(4))
-        gain = u_last * inverse(1.0 - u_first * left)
-        left_gain_ref[b * width : (b + 1) * width] = gain
-        links[b * width : (b + 1) * width] = left
-        left = v_last + gain * left * v_first
-        b = blocks - 1 - b
-        u_first, v_first, u_last, v_last = (end(b, n) for n in range(4))
-        gain = v_first * inverse(1.0 - v_last * right)
-        right_gain_ref[b * width : (b + 1) * width] = gain
-        links[(blocks + b) * width : (blocks + b + 1) * width] = right
-        right = u_first + gain * right * u_last
-
-    own = pl.ds(pl.multiple_of(me * width, 8), width)
-    left_link = links[own, :]
-    right_link = links[pl.ds(pl.multiple_of((blocks + me) * width, 8), width), :]
-    a = 1.0 - left_link * u[0]
-    b = left_link * v[0]
-    c = right_link * u[-1]
-    d = 1.0 - right_link * v[-1]
-    by = inverse(a * d - b * c)
-    joint = (
-        left_gain_ref[own, :] * left_link, right_gain_ref[own, :] * right_link,
-        left_link, right_link, d * by, b * by, c * by, a * by,
-    )
-    for n, value in enumerate(joint):
-        joint_ref[n * width : (n + 1) * width] = value
+    def scan_steps(group):
+        for first in range(0, blocks - 1, group) if group else ():
+            yield from other_blocks(first, min(group, blocks - 1 - first))
+        inv, scaled, chain, u, v = yield from block_factors([face(own_start, j) for j in range(rows + 1)])
+        factors.extend((inv, scaled, chain))
+        for j in range(rows):
+            u_ref[j * width : (j + 1) * width] = u[j]
+            v_ref[j * width : (j + 1) * width] = v[j]
+        keep_ends(me, (u[0], v[0], u[-1], v[-1]))
+        left = jnp.zeros((width, LANES), f32)
+        right = jnp.zeros((width, LANES), f32)
+        for b in range(blocks):
+            u_first, v_first, u_last, v_last = (end(b, n) for n in range(4))
+            gain = u_last * inverse(1.0 - u_first * left)
+            left_gain_ref[b * width : (b + 1) * width] = gain
+            links[b * width : (b + 1) * width] = left
+            left = v_last + gain * left * v_first
+            b = blocks - 1 - b
+            u_first, v_first, u_last, v_last = (end(b, n) for n in range(4))
+            gain = v_first * inverse(1.0 - v_last * right)
+            right_gain_ref[b * width : (b + 1) * width] = gain
+            links[(blocks + b) * width : (blocks + b + 1) * width] = right
+            right = u_first + gain * right * u_last
+            yield
+        own = pl.ds(pl.multiple_of(me * width, 8), width)
+        left_link = links[own, :]
+        right_link = links[pl.ds(pl.multiple_of((blocks + me) * width, 8), width), :]
+        a = 1.0 - left_link * u[0]
+        b = left_link * v[0]
+        c = right_link * u[-1]
+        d = 1.0 - right_link * v[-1]
+        by = inverse(a * d - b * c)
+        joint = (
+            left_gain_ref[own, :] * left_link, right_gain_ref[own, :] * right_link,
+            left_link, right_link, d * by, b * by, c * by, a * by,
+        )
+        for n, value in enumerate(joint):
+            joint_ref[n * width : (n + 1) * width] = value
+
+    if blocks <= 8:
+        steps = scan_steps(4)
+    else:
+        def one_block(n, carry):
+            for _ in other_blocks(n, 1):
+                pass
+            return carry
+
+        lax.fori_loop(0, blocks - 1, one_block, 0)
+        steps = scan_steps(0)
+
+    def tick():
+        next(steps, None)
 
     odd = lax.rem(me, 2) == 1
     inner = both_ref[0:width]
@@ -430,11 +453,15 @@
             ) * (f_mid - f_low)
             rhs[k].append(2.0 * (f_mid + along))
     for k in range(0, layers, 2):
-        both = solve_x_pair(g[k : k + 2], rhs[k : k + 2], lane)
+        both = solve_x_pair(g[k : k + 2], rhs[k : k + 2], lane, tick)
         for n in range(2):
             for c in range(chunks):
                 spot = pl.ds((k + n) * chunks + c, rows, stride=width)
                 solved[spot, :] = both[n][c] - 2.0 * f[k + n][c]
+
+    for _ in steps:
+        pass
+    inv, scaled, chain = factors
 
     def part(ref, j):
         return ref[j * width : (j + 1) * width]

time: 26.3 us -> 26.3 us (level)
  no operation moved by 1% of the time
where the time goes in v17:
time: 26.3 us; the launch traced here: 26 us
  blocking collectives  18.7 us (71%)
  Pallas kernels  4.99 us (19%)
  waiting for transfers between devices  0.94 us (4%)
  between operations  0.71 us (3%)
  starting transfers between devices  0.59 us (2%)
    all_gather x1, blocking collectives, gather_rows(): lax.all_gather(rows_sent, 'wide', axis_index_groups=cores, axis=0)  9.8 us
    all_to_all x1, blocking collectives, on_device(): lax.all_to_all(sent.reshape(wide_count, width, LANES), 'wide', split_axis...  8.93 us
    pallas_call x1, Pallas kernels, on_device(): pl.pallas_call(functools.partial(main_kernel, sizes), out_shape=(lines(wi...  1.93 us
    pallas_call x1, Pallas kernels, on_device(): pl.pallas_call(functools.partial(load_kernel, sizes), out_shape=(lines(ro...  1.09 us
    pallas_call x1, Pallas kernels, on_device(): pl.pallas_call(pack_kernel, out_shape=(jax.ShapeDtypeStruct((mode_index.s...  0.86 us
    ppermute x1, waiting for transfers between devices, on_device(): both_came = lax.ppermute(both, 'wide', swaps)  0.86 us
    pallas_call x1, Pallas kernels, on_device(): pl.pallas_call(functools.partial(last_kernel, sizes), out_shape=lines(row...  0.73 us
  transfers between devices with their start and end apart: 2, of which 2 were waited for; matrix products, arithmetic and copies ran while one was open for 0% of the time, Pallas kernels for 4%

profile of v17, /device:TPU:0, one launch (start us, length us, event | category | flops | bytes accessed | tf_op | source)
XLA Modules:
  0.0 26.0 jit_solution(2501388334992201422)
XLA Ops:
  0.7 0.9 %shard_map.64 = (f32[2,128]{1,0:T(2,128)S(1)}, f32[64,128]{1,0:T(8,128)S(1)}, f32[32,128]{1,0:T(8,128)S(1)}) custom-call(s32[1]{0:T(128)S(6)} %copy.22.step_ref, s32[2,3]{1,0:T(2,128)} %index_ref.1, f32[2]{0:T(128)} %amp_ref.1, f32[2]{0:T(128)} %phase_ref.1, f32[256,128]{1,0:T(8,128)} %bitcast.31), custom_call_target="tpu_custom_call" | custom-call | tf_op jit(solution)/shard_map/pallas_call | solution.py:535
  1.5 0.5 %collective-permute-start = (f32[64,128]{1,0:T(8,128)S(1)}, f32[64,128]{1,0:T(8,128)S(1)}, u32[]{:S(2)}, u32[]{:S(2)}) collective-permute-start(f32[64,128]{1,0:T(8,128)S(1)} %get-tuple-element.40), channel_id=1, source_target_pairs={{0,1},{1,0},{2,3},{3,2},{4,5},{5,4},{6,7},{7,6},{8,9},{9,8},{10,11... | collective-permute-start | bytes 98312 | tf_op jit(solution)/shard_map/ppermute | solution.py:556
  2.0 0.9 %collective-permute-done.both_ref = f32[64,128]{1,0:T(8,128)S(1)} collective-permute-done((f32[64,128]{1,0:T(8,128)S(1)}, f32[64,128]{1,0:T(8,128)S(1)}, u32[]{:S(2)}, u32[]{:S(2)}) %collective-permute-start) | collective-permute-done | bytes 32800 | tf_op jit(solution)/shard_map/ppermute | solution.py:556
  2.9 9.8 %conditional.3 = (f32[32,128]{1,0:T(8,128)S(1)}, f32[32,128]{1,0:T(8,128)S(1)}) conditional(s32[]{:T(128)} %convert_element_type.4, (f32[64,128]{1,0:T(8,128)S(1)}, f32[32,128]{1,0:T(8,128)S(1)}, s32[]{:T(128)}) %tuple.23, () %tuple.24), branch_computations={%region_2.3_spmd, %region_3.4_spmd} | conditional | flops 8215 | bytes 327952 | solution.py:580
  2.9 9.8 %all-gather = f32[256,128]{1,0:T(8,128)S(1)} all-gather(f32[64,128]{1,0:T(8,128)S(1)} %pad_maximum_fusion), channel_id=2, replica_groups={{0,2,4,6},{1,3,5,7},{8,10,12,14},{9,11,13,15},{16,18,20,22},{17,19,21,2..., dimensions={0}, use_global_device_ids=true | all-gather | bytes 163840 | tf_op jit(solution)/shard_map/cond/branch_0_fun/all_gather | solution.py:569
  12.7 0.1 collective-permute-start.1
  12.8 1.1 %shard_map.66 = (f32[256,128]{1,0:T(8,128)S(1)}, f32[512,128]{1,0:T(8,128)S(1)}) custom-call(f32[256,128]{1,0:T(8,128)} %bitcast.32, f32[256,128]{1,0:T(8,128)} %bitcast.34), custom_call_target="tpu_custom_call" | custom-call | tf_op jit(solution)/shard_map/pallas_call | solution.py:584
  13.9 0.1 collective-permute-done.1.came_ref
  14.0 0.4 %shard_map.65.heights = f32[1056,128]{1,0:T(8,128)S(1)} custom-call(f32[40,128]{1,0:T(8,128)S(1)} %constant_dynamic-update-slice_fusion.handed_ref, f32[40,128]{1,0:T(8,128)S(1)} %collective-permute-done.1.came_ref), custom_call_target="tpu_custom_call" | custom-call | tf_op jit(solution)/shard_map/pallas_call | solution.py:599
  14.4 1.9 %shard_map.67 = (f32[256,128]{1,0:T(8,128)S(1)}, f32[256,128]{1,0:T(8,128)S(1)}, f32[256,128]{1,0:T(8,128)S(1)}, f32[256,128]{1,0:T(8,128)S(1)}, f32[256,128]{1,...) custom-call(f32[1056,128]{1,0:T(8,128)S(1)} %shard_map.65.heights, ...), custom_call_target="tpu_custom_call" | custom-call | tf_op jit(solution)/shard_map/pallas_call | solution.py:605
  16.3 8.9 %all_to_all.5 = f32[8,32,128]{2,1,0:T(8,128)S(1)} all-to-all(f32[8,32,128]{2,1,0:T(8,128)S(1)} %bitcast.30), channel_id=1, replica_groups=mesh['grp'=4,'wide'=8] {'wide'}, dimensions={0} | all-to-all | bytes 262144 | tf_op jit(solution)/shard_map/all_to_all | solution.py:620
  25.3 0.7 %shard_map.68 = f32[256,128]{1,0:T(8,128)} custom-call(f32[256,128]{1,0:T(8,128)S(1)} %bitcast.29, f32[256,128]{1,0:T(8,128)S(1)} %get-tuple-element.51.left_gain_ref, f32[256,128]{1,0:T(8,128)S(1)} %get-tuple-element.52.right_gain_ref, f32[256,128]{1,0:T(8,128)S(1)} %get-tuple-element.53.joint_ref, f32[256,128]{1,0:T(8,128)S(1)} %get-tuple-element.54.p_ref, ...), custom_call_target="tpu_custom_call" | custom-call | tf_op jit(solution)/shard_map/pallas_call | solution.py:624
  (7 shorter events, 0.0 us)
Async XLA Ops:
  1.5 1.4 %collective-permute-start = (f32[64,128]{1,0:T(8,128)S(1)}, f32[64,128]{1,0:T(8,128)S(1)}, u32[]{:S(2)}, u32[]{:S(2)}) collective-permute-start(f32[64,128]{1,0:T(8,128)S(1)} %get-tuple-element.40), channel_id=1, source_target_pairs={{0,1},{1,0},{2,3},{3,2},{4,5},{5,4},{6,7},{7,6},{8,9},{9,8},{10,11... | collective-permute-start | bytes 98312 | tf_op jit(solution)/shard_map/ppermute | solution.py:556
  12.7 1.3 %collective-permute-start.1 = (f32[40,128]{1,0:T(8,128)S(1)}, f32[40,128]{1,0:T(8,128)S(1)}, u32[]{:S(2)}, u32[]{:S(2)}) collective-permute-start(f32[40,128]{1,0:T(8,128)S(1)} %constant_dynamic-update-slice_fusion.handed_ref), channel_id=1, source_target_pairs={{0,1},{1,0},{2,3},{3,2},{4,5},{5,4},{6,7},{7,6},{8,9},{9,8},{10,11... | collective-permute-start | bytes 61448 | tf_op jit(solution)/shard_map/ppermute | solution.py:582

commit v18 on v15

--- a/solution.py
+++ b/solution.py
@@ -312,7 +312,7 @@
     ]
 
 def main_kernel(
-    sizes, heights, both_ref, below_ref, came_ref, turned_ref,
+    sizes, heights, inner_ref, below_ref, late_ref, came_ref, turned_ref,
     sent_ref, p_ref, u_ref, v_ref, left_gain_ref, right_gain_ref, joint_ref,
     ends, links, halo, solved,
 ):
@@ -390,9 +390,13 @@
         joint_ref[n * width : (n + 1) * width] = value
 
     odd = lax.rem(me, 2) == 1
-    inner = both_ref[0:width]
-    below = jnp.where(odd, inner, below_ref[...])
-    above = jnp.where(odd, came_ref[0:width], inner)
+    in_first = first_layer == 0
+    other = pl.ds(pl.multiple_of(lax.rem(me, 2) * width, 8), width)
+    came = came_ref[0:width]
+    inner = jnp.where(in_first, inner_ref[...], came)
+    outer = jnp.where(in_first, jnp.where(odd, came, below_ref[...]), late_ref[other, :])
+    below = jnp.where(odd, inner, outer)
+    above = jnp.where(odd, outer, inner)
     halo[0:width] = jnp.where(me == 0, 0.0, below)
     halo[width : 2 * width] = jnp.where(me == blocks - 1, 0.0, above)
     lane = lax.broadcasted_iota(jnp.int32, (rows, LANES), 1)
@@ -524,18 +528,10 @@
 
     place = lax.axis_index("wide")
     odd = place % 2 == 1
+    in_first = lax.axis_index("grp") == 0
     swaps = [(i, i ^ 1) for i in range(wide_count)]
     cores = [list(range(n, wide_count, 2)) for n in range(2)]
-    both_came = lax.ppermute(both, "wide", swaps)
-
-    def gather_modes(own):
-        return lax.all_gather(own, "grp", axis=0, tiled=True)
-
-    def no_modes(own):
-        return jnp.zeros((grp_count * own.shape[0], own.shape[1]), f32)
-
-    modes = lax.cond(odd, gather_modes, no_modes, packed)
-    modes, outer, both_came = lax.optimization_barrier((modes, outer, both_came))
+    pairs = [[0, wide_count - 1]] + [[i, i + 1] for i in range(1, wide_count - 1, 2)]
 
     def gather_rows(own, came):
         rows_sent = jnp.concatenate([own, came[width:]], 0)
@@ -550,8 +546,24 @@
     def no_rows(own, came):
         return jnp.zeros_like(own), jnp.zeros_like(own)
 
-    below, above = lax.cond(odd, no_rows, gather_rows, outer, both_came)
-    handed = jnp.concatenate([above, modes], 0)
+    def early_rows(own, mine):
+        came = lax.ppermute(mine, "wide", swaps)
+        return (came[:width],) + lax.cond(odd, no_rows, gather_rows, own, came)
+
+    def no_early_rows(own, mine):
+        return jnp.zeros_like(own), jnp.zeros_like(own), mine[:width]
+
+    inner_came, below, to_other = lax.cond(in_first, early_rows, no_early_rows, outer, both)
+    packed, to_other = lax.optimization_barrier((packed, to_other))
+
+    def gather_modes(own):
+        return lax.all_gather(own, "grp", axis=0, tiled=True)
+
+    def no_modes(own):
+        return jnp.zeros((grp_count * own.shape[0], own.shape[1]), f32)
+
+    modes = lax.cond(odd, gather_modes, no_modes, packed)
+    handed = jnp.concatenate([to_other, modes], 0)
     came = lax.ppermute(handed, "wide", swaps)
     handed, field, conduct = lax.optimization_barrier((handed, field, conduct))
     field_lines, turned = pl.pallas_call(
@@ -569,6 +581,15 @@
             for a in (field, conduct)
         )
     )
+    field_lines, turned, outer = lax.optimization_barrier((field_lines, turned, outer))
+
+    def gather_pairs(rows_sent):
+        return lax.all_gather(rows_sent, "wide", axis_index_groups=pairs, axis=0, tiled=True)
+
+    def no_pairs(rows_sent):
+        return jnp.zeros((2 * width, LANES), f32)
+
+    late = lax.cond(in_first, no_pairs, gather_pairs, outer)
     heights = pl.pallas_call(
         functools.partial(height_kernel, sizes),
         out_shape=jax.ShapeDtypeStruct(((row_total + 2) * chunks, LANES), f32),
@@ -588,7 +609,7 @@
             pltpu.VMEM((rows * width, LANES), f32),
         ],
         compiler_params=limit,
-    )(heights, both_came, below, came, turned)
+    )(heights, inner_came, below, late, came, turned)
 
     came = lax.all_to_all(
         sent.reshape(wide_count, width, LANES), "wide", split_axis=0, concat_axis=0

time: 26.3 us -> 29.8 us (1.13)
  the two profiles are of different devices: /device:TPU:0 before, /device:TPU:8 now
where the time goes in v18:
time: 29.8 us; the launch traced here: 29.3 us
  blocking collectives  14.6 us (49%)
  starting transfers between devices  6.26 us (21%)
  Pallas kernels  5.88 us (20%)
  local copies, waits for them, and re-layouts  1.21 us (4%)
  other arithmetic  0.72 us (2%)
  between operations  0.68 us (2%)
    all_to_all x1, blocking collectives, on_device(): lax.all_to_all(sent.reshape(wide_count, width, LANES), 'wide', split_axis...  9.23 us
    ppermute x1, starting transfers between devices, on_device(): came = lax.ppermute(handed, 'wide', swaps)  6.26 us
    all_gather x1, blocking collectives, gather_pairs(): lax.all_gather(rows_sent, 'wide', axis_index_groups=pairs, axis=0, tiled=...  5.33 us
    pallas_call x1, Pallas kernels, on_device(): pl.pallas_call(functools.partial(main_kernel, sizes), out_shape=(lines(wi...  2.84 us
    pallas_call x1, Pallas kernels, on_device(): pl.pallas_call(functools.partial(load_kernel, sizes), out_shape=(lines(ro...  1.08 us
    pallas_call x1, Pallas kernels, on_device(): pl.pallas_call(pack_kernel, out_shape=(jax.ShapeDtypeStruct((mode_index.s...  0.86 us
    pallas_call x1, Pallas kernels, on_device(): pl.pallas_call(functools.partial(last_kernel, sizes), out_shape=lines(row...  0.73 us
    concatenate x1, other arithmetic, on_device(): handed = jnp.concatenate([to_other, modes], 0)  0.72 us
  transfers between devices with their start and end apart: 1, of which 0 were waited for; matrix products, arithmetic and copies ran while one was open for 0% of the time, Pallas kernels for 4%

profile of v18, /device:TPU:8, one launch (start us, length us, event | category | flops | bytes accessed | tf_op | source)
XLA Modules:
  0.0 29.3 jit_solution(748279827291103788)
XLA Ops:
  0.7 0.9 %shard_map.64 = (f32[2,128]{1,0:T(2,128)S(1)}, f32[64,128]{1,0:T(8,128)S(1)}, f32[32,128]{1,0:T(8,128)S(1)}) custom-call(s32[1]{0:T(128)S(6)} %copy.29.step_ref, s32[2,3]{1,0:T(2,128)} %index_ref.1, f32[2]{0:T(128)} %amp_ref.1, f32[2]{0:T(128)} %phase_ref.1, f32[256,128]{1,0:T(8,128)} %bitcast.31), custom_call_target="tpu_custom_call" | custom-call | tf_op jit(solution)/shard_map/pallas_call | solution.py:512
  1.5 1.2 %conditional.4 = (f32[32,128]{1,0:T(8,128)S(1)}, f32[32,128]{1,0:T(8,128)}, f32[32,128]{1,0:T(8,128)}) conditional(s32[]{:T(128)} %convert_element_type.10, f32[64,128]{1,0:T(8,128)S(1)} %get-tuple-element.61, (f32[64,128]{1,0:T(8,128)S(1)}, pred[]{:T(512)}, f32[32,128]{1,0:T(8,128)S(1)}, s32[]{:T(128)}) %tuple.36), branch_computations={%region_0.1_spmd, %region_1.4_spmd} | conditional | flops 8216 | bytes 491885 | solution.py:556
  1.5 0.6 %slice.14 = f32[32,128]{1,0:T(8,128)} slice(f32[64,128]{1,0:T(8,128)S(1)} %param), slice={[0:32], [0:128]} | slice | bytes 32768 | tf_op jit(solution)/shard_map/cond/branch_0_fun/slice | solution.py:554
  2.1 0.6 %broadcast.10.clone = f32[32,128]{1,0:T(8,128)} broadcast(f32[]{:T(128)} %constant.44.clone), dimensions={} | broadcast | bytes 16388 | tf_op jit(solution)/shard_map/broadcast.1
  2.7 0.7 %pad_maximum_fusion.1.handed_ref = f32[40,128]{1,0:T(8,128)S(1)} fusion(f32[8,128]{1,0:T(8,128)S(1)} %get-tuple-element.95, f32[32,128]{1,0:T(8,128)} %get-tuple-element.64), kind=kLoop, calls=%fused_computation.3 | loop fusion | flops 5120 | bytes 40960 | tf_op jit(solution)/shard_map/concatenate | solution.py:566
  3.5 6.3 %collective-permute-start.1 = (f32[40,128]{1,0:T(8,128)S(1)}, f32[40,128]{1,0:T(8,128)S(1)}, u32[]{:S(2)}, u32[]{:S(2)}) collective-permute-start(f32[40,128]{1,0:T(8,128)S(1)} %pad_maximum_fusion.1.handed_ref), channel_id=1, source_target_pairs={{0,1},{1,0},{2,3},{3,2},{4,5},{5,4},{6,7},{7,6},{8,9},{9,8},{10,11... | collective-permute-start | bytes 61448 | tf_op jit(solution)/shard_map/ppermute | solution.py:567
  9.7 1.1 %shard_map.66 = (f32[256,128]{1,0:T(8,128)S(1)}, f32[512,128]{1,0:T(8,128)S(1)}) custom-call(f32[256,128]{1,0:T(8,128)} %bitcast.32, f32[256,128]{1,0:T(8,128)} %bitcast.34), custom_call_target="tpu_custom_call" | custom-call | tf_op jit(solution)/shard_map/pallas_call | solution.py:569
  10.8 5.3 %conditional.6 = (f32[64,128]{1,0:T(8,128)S(1)}) conditional(s32[]{:T(128)} %convert_element_type.10, f32[32,128]{1,0:T(8,128)S(1)} %get-tuple-element.73, () %tuple.41), branch_computations={%region_6.7_spmd, %region_7.8_spmd} | conditional | bytes 49160 | solution.py:592
  10.8 5.3 %all_gather.11 = f32[64,128]{1,0:T(8,128)S(1)} all-gather(f32[32,128]{1,0:T(8,128)S(1)} %param.6), channel_id=1, replica_groups={{0,7},{1,2},{3,4},{5,6},{8,15},{9,10},{11,12},{13,14},{16,23},{17,18},{..., dimensions={0}, use_global_device_ids=true | all-gather | bytes 49152 | tf_op jit(solution)/shard_map/cond/branch_0_fun/all_gather | solution.py:587
  16.2 0.0 collective-permute-done.1.came_ref
  16.2 0.4 %shard_map.65.heights = f32[1056,128]{1,0:T(8,128)S(1)} custom-call(f32[40,128]{1,0:T(8,128)S(1)} %pad_maximum_fusion.1.handed_ref, f32[40,128]{1,0:T(8,128)S(1)} %collective-permute-done.1.came_ref), custom_call_target="tpu_custom_call" | custom-call | tf_op jit(solution)/shard_map/pallas_call | solution.py:593
  16.5 2.8 %shard_map.67 = (f32[256,128]{1,0:T(8,128)S(1)}, f32[256,128]{1,0:T(8,128)S(1)}, f32[256,128]{1,0:T(8,128)S(1)}, f32[256,128]{1,0:T(8,128)S(1)}, f32[256,128]{1,...) custom-call(f32[1056,128]{1,0:T(8,128)S(1)} %shard_map.65.heights, ...), custom_call_target="tpu_custom_call" | custom-call | tf_op jit(solution)/shard_map/pallas_call | solution.py:599
  19.4 9.2 %all_to_all.5 = f32[8,32,128]{2,1,0:T(8,128)S(1)} all-to-all(f32[8,32,128]{2,1,0:T(8,128)S(1)} %bitcast.30), channel_id=1, replica_groups=mesh['grp'=4,'wide'=8] {'wide'}, dimensions={0} | all-to-all | bytes 262144 | tf_op jit(solution)/shard_map/all_to_all | solution.py:614
  28.6 0.7 %shard_map.68 = f32[256,128]{1,0:T(8,128)} custom-call(f32[256,128]{1,0:T(8,128)S(1)} %bitcast.29, f32[256,128]{1,0:T(8,128)S(1)} %get-tuple-element.76.left_gain_ref, f32[256,128]{1,0:T(8,128)S(1)} %get-tuple-element.77.right_gain_ref, f32[256,128]{1,0:T(8,128)S(1)} %get-tuple-element.78.joint_ref, f32[256,128]{1,0:T(8,128)S(1)} %get-tuple-element.79.p_ref, ...), custom_call_target="tpu_custom_call" | custom-call | tf_op jit(solution)/shard_map/pallas_call | solution.py:618
  (3 shorter events, 0.0 us)
Async XLA Ops:
  3.5 12.7 %collective-permute-start.1 = (f32[40,128]{1,0:T(8,128)S(1)}, f32[40,128]{1,0:T(8,128)S(1)}, u32[]{:S(2)}, u32[]{:S(2)}) collective-permute-start(f32[40,128]{1,0:T(8,128)S(1)} %pad_maximum_fusion.1.handed_ref), channel_id=1, source_target_pairs={{0,1},{1,0},{2,3},{3,2},{4,5},{5,4},{6,7},{7,6},{8,9},{9,8},{10,11... | collective-permute-start | bytes 61448 | tf_op jit(solution)/shard_map/ppermute | solution.py:567

commit v19 on v18

--- a/solution.py
+++ b/solution.py
@@ -214,7 +214,7 @@
 
 def pack_kernel(
     step_ref, index_ref, amp_ref, phase_ref, field_ref,
-    packed_ref, both_ref, outer_ref,
+    packed_ref, both_ref, inner_ref, outer_ref, late_ref,
     index_in, amp_in, phase_in, sems,
 ):
     width = outer_ref.shape[0]
@@ -228,7 +228,9 @@
         (phase_ref, phase_in),
         (field_ref.at[inner_rows], both_ref.at[pl.ds(0, width)]),
         (field_ref.at[outer_rows], both_ref.at[pl.ds(width, width)]),
+        (field_ref.at[inner_rows], inner_ref),
         (field_ref.at[outer_rows], outer_ref),
+        (field_ref.at[outer_rows], late_ref),
     )
     copies = [pltpu.make_async_copy(a, b, sems.at[n]) for n, (a, b) in enumerate(pairs)]
     for copy in copies:
@@ -312,7 +314,7 @@
     ]
 
 def main_kernel(
-    sizes, heights, inner_ref, below_ref, late_ref, came_ref, turned_ref,
+    sizes, heights, rows_ref, came_ref, turned_ref,
     sent_ref, p_ref, u_ref, v_ref, left_gain_ref, right_gain_ref, joint_ref,
     ends, links, halo, solved,
 ):
@@ -393,8 +395,10 @@
     in_first = first_layer == 0
     other = pl.ds(pl.multiple_of(lax.rem(me, 2) * width, 8), width)
     came = came_ref[0:width]
-    inner = jnp.where(in_first, inner_ref[...], came)
-    outer = jnp.where(in_first, jnp.where(odd, came, below_ref[...]), late_ref[other, :])
+    inner = jnp.where(in_first, rows_ref[0:width], came)
+    outer = jnp.where(
+        in_first, jnp.where(odd, came, rows_ref[width : 2 * width]), rows_ref[other, :]
+    )
     below = jnp.where(odd, inner, outer)
     above = jnp.where(odd, outer, inner)
     halo[0:width] = jnp.where(me == 0, 0.0, below)
@@ -509,11 +513,13 @@
             for a in (mode_index, mode_amp, mode_phase, to_lines(field), to_lines(conduct))
         ),
     )
-    packed, both, outer = pl.pallas_call(
+    packed, both, inner, outer, outer_late = pl.pallas_call(
         pack_kernel,
         out_shape=(
             jax.ShapeDtypeStruct((mode_index.shape[0], LANES), f32),
             lines(2),
+            lines(1),
+            lines(1),
             lines(1),
         ),
         in_specs=[pl.BlockSpec(memory_space=pltpu.SMEM)] + [hbm] * 4,
@@ -521,7 +527,7 @@
             pltpu.SMEM(mode_index.shape, jnp.int32),
             pltpu.SMEM(mode_amp.shape, f32),
             pltpu.SMEM(mode_phase.shape, f32),
-            pltpu.SemaphoreType.DMA((6,)),
+            pltpu.SemaphoreType.DMA((8,)),
         ],
         compiler_params=limit,
     )(step_index, mode_index, mode_amp, mode_phase, field_lines)
@@ -543,27 +549,32 @@
         )
         return below[width:], above[:width]
 
-    def no_rows(own, came):
-        return jnp.zeros_like(own), jnp.zeros_like(own)
-
-    def early_rows(own, mine):
-        came = lax.ppermute(mine, "wide", swaps)
-        return (came[:width],) + lax.cond(odd, no_rows, gather_rows, own, came)
-
-    def no_early_rows(own, mine):
-        return jnp.zeros_like(own), jnp.zeros_like(own), mine[:width]
-
-    inner_came, below, to_other = lax.cond(in_first, early_rows, no_early_rows, outer, both)
-    packed, to_other = lax.optimization_barrier((packed, to_other))
-
-    def gather_modes(own):
-        return lax.all_gather(own, "grp", axis=0, tiled=True)
-
-    def no_modes(own):
-        return jnp.zeros((grp_count * own.shape[0], own.shape[1]), f32)
-
-    modes = lax.cond(odd, gather_modes, no_modes, packed)
-    handed = jnp.concatenate([to_other, modes], 0)
+    mode_shape = (grp_count * packed.shape[0], LANES)
+
+    def gather_modes(own, outer_own, inner_own, both_other):
+        modes = lax.all_gather(own, "grp", axis=0, tiled=True)
+        return jnp.concatenate([inner_own, modes], 0), jnp.zeros_like(outer_own)
+
+    def early_rows(own, outer_own, inner_own, both_other):
+        below, above = gather_rows(outer_own, both_other)
+        return jnp.concatenate([above, jnp.zeros(mode_shape, f32)], 0), below
+
+    def no_early_rows(own, outer_own, inner_own, both_other):
+        return (
+            jnp.concatenate([inner_own, jnp.zeros(mode_shape, f32)], 0),
+            jnp.zeros_like(outer_own),
+        )
+
+    def even_core(*operands):
+        return lax.cond(in_first, early_rows, no_early_rows, *operands)
+
+    both_came = lax.cond(
+        in_first,
+        lambda mine: lax.ppermute(mine, "wide", swaps),
+        lambda mine: jnp.zeros_like(mine),
+        both,
+    )
+    handed, below = lax.cond(odd, gather_modes, even_core, packed, outer, inner, both_came)
     came = lax.ppermute(handed, "wide", swaps)
     handed, field, conduct = lax.optimization_barrier((handed, field, conduct))
     field_lines, turned = pl.pallas_call(
@@ -581,15 +592,15 @@
             for a in (field, conduct)
         )
     )
-    field_lines, turned, outer = lax.optimization_barrier((field_lines, turned, outer))
-
-    def gather_pairs(rows_sent):
+    field_lines, turned, outer_late = lax.optimization_barrier((field_lines, turned, outer_late))
+
+    def gather_pairs(rows_sent, both_other, below):
         return lax.all_gather(rows_sent, "wide", axis_index_groups=pairs, axis=0, tiled=True)
 
-    def no_pairs(rows_sent):
-        return jnp.zeros((2 * width, LANES), f32)
-
-    late = lax.cond(in_first, no_pairs, gather_pairs, outer)
+    def pass_rows(rows_sent, both_other, below):
+        return jnp.concatenate([both_other[:width], below], 0)
+
+    rows_came = lax.cond(in_first, pass_rows, gather_pairs, outer_late, both_came, below)
     heights = pl.pallas_call(
         functools.partial(height_kernel, sizes),
         out_shape=jax.ShapeDtypeStruct(((row_total + 2) * chunks, LANES), f32),
@@ -609,7 +620,7 @@
             pltpu.VMEM((rows * width, LANES), f32),
         ],
         compiler_params=limit,
-    )(heights, inner_came, below, late, came, turned)
+    )(heights, rows_came, came, turned)
 
     came = lax.all_to_all(
         sent.reshape(wide_count, width, LANES), "wide", split_axis=0, concat_axis=0

time: 29.8 us -> 27.3 us (0.916)
  the two profiles are of different devices: /device:TPU:8 before, /device:TPU:0 now
where the time goes in v19:
time: 27.3 us; the launch traced here: 26.8 us
  blocking collectives  18 us (66%)
  Pallas kernels  5.05 us (18%)
  local copies, waits for them, and re-layouts  1.45 us (5%)
  waiting for transfers between devices  0.99 us (4%)
  between operations  0.7 us (3%)
  starting transfers between devices  0.59 us (2%)
    all_gather x1, blocking collectives, gather_rows(): lax.all_gather(rows_sent, 'wide', axis_index_groups=cores, axis=0)  9.8 us
    all_to_all x1, blocking collectives, on_device(): lax.all_to_all(sent.reshape(wide_count, width, LANES), 'wide', split_axis...  8.19 us
    pallas_call x1, Pallas kernels, on_device(): pl.pallas_call(functools.partial(main_kernel, sizes), out_shape=(lines(wi...  1.95 us
    pallas_call x1, Pallas kernels, on_device(): pl.pallas_call(functools.partial(load_kernel, sizes), out_shape=(lines(ro...  1.09 us
    ppermute x1, waiting for transfers between devices, on_device(): lax.ppermute(mine, 'wide', swaps)  0.99 us
    pallas_call x1, Pallas kernels, on_device(): pl.pallas_call(pack_kernel, out_shape=(jax.ShapeDtypeStruct((mode_index.s...  0.91 us
    pallas_call x1, Pallas kernels, on_device(): pl.pallas_call(functools.partial(last_kernel, sizes), out_shape=lines(row...  0.73 us
    slice x1, local copies, waits for them, and re-layouts, pass_rows(): return jnp.concatenate([both_other[:width], below], 0)  0.72 us
  transfers between devices with their start and end apart: 2, of which 1 were waited for; matrix products, arithmetic and copies ran while one was open for 3% of the time, Pallas kernels for 4%

profile of v19, /device:TPU:0, one launch (start us, length us, event | category | flops | bytes accessed | tf_op | source)
XLA Modules:
  0.0 26.8 jit_solution(17675105564191934068)
XLA Ops:
  0.7 0.9 %shard_map.64 = (f32[2,128]{1,0:T(2,128)S(1)}, f32[64,128]{1,0:T(8,128)S(1)}, f32[32,128]{1,0:T(8,128)S(1)}, f32[32,128]{1,0:T(8,128)S(1)}, f32[32,128]{1,0:T(8,128)S(1)}) custom-call(s32[1]{0:T(128)S(6)} %copy.27.step_ref, s32[2,3]{1,0:T(2,128)} %index_ref.1, f32[2]{0:T(128)} %amp_ref.1, f32[2]{0:T(128)} %phase_ref.1, f32[256,128]{1,0:T(8,128)} %bitcast.31), custom_call_target="tpu_custom_call" | custom-call | tf_op jit(solution)/shard_map/pallas_call | solution.py:516
  1.6 1.5 %conditional.4 = (f32[64,128]{1,0:T(8,128)}) conditional(s32[]{:T(128)} %convert_element_type.11, () %tuple.34, f32[64,128]{1,0:T(8,128)S(1)} %get-tuple-element.73), branch_computations={%region_0.1_spmd, %region_1.2_spmd} | conditional | bytes 131120 | solution.py:571
  1.6 0.5 %collective-permute-start = (f32[64,128]{1,0:T(8,128)S(1)}, f32[64,128]{1,0:T(8,128)}, u32[]{:S(2)}, u32[]{:S(2)}) collective-permute-start(f32[64,128]{1,0:T(8,128)S(1)} %param.1), channel_id=1, source_target_pairs={{0,1},{1,0},{2,3},{3,2},{4,5},{5,4},{6,7},{7,6},{8,9},{9,8},{10,11... | collective-permute-start | bytes 98312 | tf_op jit(solution)/shard_map/cond/branch_1_fun/ppermute | solution.py:573
  2.1 1.0 %collective-permute-done = f32[64,128]{1,0:T(8,128)} collective-permute-done((f32[64,128]{1,0:T(8,128)S(1)}, f32[64,128]{1,0:T(8,128)}, u32[]{:S(2)}, u32[]{:S(2)}) %collective-permute-start) | collective-permute-done | bytes 32800 | tf_op jit(solution)/shard_map/cond/branch_1_fun/ppermute | solution.py:573
  3.1 10.5 %conditional.5 = ((f32[40,128]{1,0:T(8,128)S(1)}, f32[32,128]{1,0:T(8,128)S(1)})) conditional(s32[]{:T(128)} %convert_element_type.10, (pred[]{:T(512)}, f32[32,128]{1,0:T(8,128)S(1)}, f32[64,128]{1,0:T(8,128)}, f32[32,128]{1,0:T(8,128)S(1)}, s32[]{:T(128)}) %tuple.35, (f32[2,128]{1,0:T(2,128)S(1)}, f32[32,128]{1,0:T(8,128)S(1)}) %tuple.36), branch_computations={%region_2.5_spmd, %region_5.6_spmd} | conditional | flops 8216 | bytes 364857 | solution.py:577
  3.1 10.5 %conditional = (f32[40,128]{1,0:T(8,128)S(1)}, f32[32,128]{1,0:T(8,128)S(1)}) conditional(s32[]{:T(128)} %convert_element_type.2, f32[32,128]{1,0:T(8,128)S(1)} %get-tuple-element.42, (f32[64,128]{1,0:T(8,128)}, f32[32,128]{1,0:T(8,128)S(1)}, s32[]{:T(128)}) %tuple.26), branch_computations={%region_3.3_spmd, %region_4.4_spmd} | conditional | flops 8215 | bytes 364820 | solution.py:569
  3.1 0.7 %slice.12 = f32[32,128]{1,0:T(8,128)S(1)} slice(f32[64,128]{1,0:T(8,128)} %get-tuple-element.39), slice={[32:64], [0:128]} | slice | bytes 32768 | tf_op jit(solution)/shard_map/cond/branch_0_fun/cond/branch_1_fun/slice | solution.py:543
  3.8 9.8 %all-gather = f32[256,128]{1,0:T(8,128)S(1)} all-gather(f32[64,128]{1,0:T(8,128)S(1)} %pad_maximum_fusion), channel_id=2, replica_groups={{0,2,4,6},{1,3,5,7},{8,10,12,14},{9,11,13,15},{16,18,20,22},{17,19,21,2..., dimensions={0}, use_global_device_ids=true | all-gather | bytes 163840 | tf_op jit(solution)/shard_map/cond/branch_0_fun/cond/branch_1_fun/all_gather | solution.py:544
  13.7 0.1 collective-permute-start.1
  13.7 1.1 %shard_map.66 = (f32[256,128]{1,0:T(8,128)S(1)}, f32[512,128]{1,0:T(8,128)S(1)}) custom-call(f32[256,128]{1,0:T(8,128)} %bitcast.32, f32[256,128]{1,0:T(8,128)} %bitcast.34), custom_call_target="tpu_custom_call" | custom-call | tf_op jit(solution)/shard_map/pallas_call | solution.py:580
  14.8 0.7 %conditional.6 = (f32[64,128]{1,0:T(8,128)S(1)}) conditional(s32[]{:T(128)} %convert_element_type.11, f32[32,128]{1,0:T(8,128)S(1)} %get-tuple-element.83, (f32[64,128]{1,0:T(8,128)}, f32[32,128]{1,0:T(8,128)S(1)}) %tuple.39), branch_computations={%region_6.7_spmd, %region_7.8_spmd} | conditional | flops 8192 | bytes 98312 | solution.py:603
  14.9 0.7 %slice.17 = f32[32,128]{1,0:T(8,128)S(1)} slice(f32[64,128]{1,0:T(8,128)} %get-tuple-element.48), slice={[0:32], [0:128]} | slice | bytes 32768 | tf_op jit(solution)/shard_map/cond/branch_1_fun/slice | solution.py:601
  15.6 0.0 collective-permute-done.1.came_ref
  15.6 0.4 %shard_map.65.heights = f32[1056,128]{1,0:T(8,128)S(1)} custom-call(f32[40,128]{1,0:T(8,128)S(1)} %get-tuple-element.77.handed_ref, f32[40,128]{1,0:T(8,128)S(1)} %collective-permute-done.1.came_ref), custom_call_target="tpu_custom_call" | custom-call | tf_op jit(solution)/shard_map/pallas_call | solution.py:604
  16.0 1.9 %shard_map.67 = (f32[256,128]{1,0:T(8,128)S(1)}, f32[256,128]{1,0:T(8,128)S(1)}, f32[256,128]{1,0:T(8,128)S(1)}, f32[256,128]{1,0:T(8,128)S(1)}, f32[256,128]{1,...) custom-call(f32[1056,128]{1,0:T(8,128)S(1)} %shard_map.65.heights, ...), custom_call_target="tpu_custom_call" | custom-call | tf_op jit(solution)/shard_map/pallas_call | solution.py:610
  17.9 8.2 %all_to_all.5 = f32[8,32,128]{2,1,0:T(8,128)S(1)} all-to-all(f32[8,32,128]{2,1,0:T(8,128)S(1)} %bitcast.30), channel_id=1, replica_groups=mesh['grp'=4,'wide'=8] {'wide'}, dimensions={0} | all-to-all | bytes 262144 | tf_op jit(solution)/shard_map/all_to_all | solution.py:625
  26.1 0.7 %shard_map.68 = f32[256,128]{1,0:T(8,128)} custom-call(f32[256,128]{1,0:T(8,128)S(1)} %bitcast.29, f32[256,128]{1,0:T(8,128)S(1)} %get-tuple-element.87.left_gain_ref, f32[256,128]{1,0:T(8,128)S(1)} %get-tuple-element.88.right_gain_ref, f32[256,128]{1,0:T(8,128)S(1)} %get-tuple-element.89.joint_ref, f32[256,128]{1,0:T(8,128)S(1)} %get-tuple-element.90.p_ref, ...), custom_call_target="tpu_custom_call" | custom-call | tf_op jit(solution)/shard_map/pallas_call | solution.py:629
  (4 shorter events, 0.0 us)
Async XLA Ops:
  1.6 1.5 %collective-permute-start = (f32[64,128]{1,0:T(8,128)S(1)}, f32[64,128]{1,0:T(8,128)}, u32[]{:S(2)}, u32[]{:S(2)}) collective-permute-start(f32[64,128]{1,0:T(8,128)S(1)} %param.1), channel_id=1, source_target_pairs={{0,1},{1,0},{2,3},{3,2},{4,5},{5,4},{6,7},{7,6},{8,9},{9,8},{10,11... | collective-permute-start | bytes 98312 | tf_op jit(solution)/shard_map/cond/branch_1_fun/ppermute | solution.py:573
  13.7 1.9 %collective-permute-start.1 = (f32[40,128]{1,0:T(8,128)S(1)}, f32[40,128]{1,0:T(8,128)S(1)}, u32[]{:S(2)}, u32[]{:S(2)}) collective-permute-start(f32[40,128]{1,0:T(8,128)S(1)} %get-tuple-element.77.handed_ref), channel_id=1, source_target_pairs={{0,1},{1,0},{2,3},{3,2},{4,5},{5,4},{6,7},{7,6},{8,9},{9,8},{10,11... | collective-permute-start | bytes 61448 | tf_op jit(solution)/shard_map/ppermute | solution.py:578

commit v20 on v15

--- a/solution.py
+++ b/solution.py
@@ -147,19 +147,16 @@
 def reduce_lanes(diagonal, link, rhs, lane, stride):
     count = len(rhs)
     while stride < LANES:
+        high_r = from_right(rhs, stride, lane)
+        high_e = from_right(link, stride, lane)
         inv = [inverse(d) for d in diagonal]
-        t = [q * r for q, r in zip(inv, rhs)]
         w = [q * e for q, e in zip(inv, link)]
         low_d = from_left([e * v for e, v in zip(link, w)], stride, lane)
-        low_r = from_left([e * v for e, v in zip(link, t)], stride, lane)
-        high_q = from_right(inv, stride, lane)
-        high_t = from_right(t, stride, lane)
-        high_w = from_right(w, stride, lane)
-        diagonal = [
-            diagonal[c] - low_d[c] - link[c] * (link[c] * high_q[c]) for c in range(count)
-        ]
-        rhs = [rhs[c] + low_r[c] + link[c] * high_t[c] for c in range(count)]
-        link = [link[c] * high_w[c] for c in range(count)]
+        low_r = from_left([r * v for r, v in zip(rhs, w)], stride, lane)
+        by = [e * q for e, q in zip(link, from_right(inv, stride, lane))]
+        diagonal = [diagonal[c] - low_d[c] - link[c] * by[c] for c in range(count)]
+        rhs = [rhs[c] + low_r[c] + by[c] * high_r[c] for c in range(count)]
+        link = [by[c] * high_e[c] for c in range(count)]
         stride *= 2
     return solve_chunks(diagonal, link, rhs)
 
@@ -284,22 +281,6 @@
     return inv, scaled, chain, u, v
 
 
-def block_ends(face):
-    rows = len(face) - 1
-    down = 1.0 + face[0]
-    up = 1.0 + face[rows]
-    v_first = None
-    for j in range(rows):
-        v_last = face[j + 1] * inverse(down + face[j + 1])
-        v_first = v_last if v_first is None else v_first * v_last
-        u_first = face[rows - 1 - j] * inverse(up + face[rows - 1 - j])
-        if j < rows - 1:
-            down = 1.0 + down * v_last
-            up = 1.0 + up * u_first
-    u_last = v_first * (face[0] * inverse(face[rows]))
-    return u_first, v_first, u_last, v_last
-
-
 def height_kernel(sizes, handed_ref, came_ref, heights_ref):
     rows, layers, chunks, row_total, layer_total, column_total = sizes
     odd = lax.rem(lax.axis_index("wide"), 2) == 1
@@ -313,8 +294,8 @@
 
 def main_kernel(
     sizes, heights, both_ref, below_ref, came_ref, turned_ref,
-    sent_ref, p_ref, u_ref, v_ref, left_gain_ref, right_gain_ref, joint_ref,
-    ends, links, halo, solved,
+    sent_ref, p_ref, u_ref, v_ref, gain_ref, joint_ref,
+    halo, solved,
 ):
     rows, layers, chunks, row_total, layer_total, column_total = sizes
     width = layers * chunks
@@ -327,63 +308,58 @@
     half = 0.5 * weight
     own_start = pl.multiple_of(me * (rows * chunks), 8)
 
-    def faces(start):
-        h = [heights[pl.ds(start + j * chunks, chunks), :] for j in range(rows + 2)]
-        out = []
-        for j in range(rows + 1):
-            both = h[j] + h[j + 1]
-            out.append(jnp.concatenate([weight + (half * z) * both for z in zeta], 0))
-        return out
-
-    def keep_ends(b, values):
-        base = pl.multiple_of(b * (4 * width), 8)
-        for n, value in enumerate(values):
-            ends[pl.ds(base + n * width, width), :] = value
-
-    inv, scaled, chain, u, v = block_factors(faces(own_start))
+    def face(low, high):
+        both = heights[pl.ds(low, chunks), :] + heights[pl.ds(high, chunks), :]
+        return jnp.concatenate([weight + (half * z) * both for z in zeta], 0)
+
+    def aligned(index):
+        return pl.multiple_of(index, 8)
+
+    inv, scaled, chain, u, v = block_factors(
+        [face(own_start + j * chunks, own_start + (j + 1) * chunks) for j in range(rows + 1)]
+    )
     for j in range(rows):
         u_ref[j * width : (j + 1) * width] = u[j]
         v_ref[j * width : (j + 1) * width] = v[j]
-    keep_ends(me, (u[0], v[0], u[-1], v[-1]))
-
-    def other_block(n):
-        b = lax.rem(me + 1 + n, blocks)
-        keep_ends(b, block_ends(faces(pl.multiple_of(b * (rows * chunks), 8))))
-
+
+    def one_block(n, carry):
+        rest, link, left_link = carry
+        upward = n < me
+        b = jnp.where(upward, n, blocks - 1 - (n - me))
+        start = b * (rows * chunks) + jnp.where(upward, 0, (rows + 1) * chunks)
+        step = jnp.where(upward, chunks, -chunks)
+        places = [aligned(start + j * step) for j in range(rows + 2)]
+        first = face(places[0], places[1])
+        anew = (n == 0) | (n == me)
+        left_link = jnp.where(n == me, link, left_link)
+        rest = jnp.where(anew, 1.0 + first, rest)
+        for j in range(rows):
+            after = face(places[j + 1], places[j + 2])
+            link = after * inverse(rest + after)
+            through = through * link if j else link
+            rest = 1.0 + rest * link
+        gain_ref[pl.ds(aligned(b * width), width), :] = through * (first * inverse(after))
+        return rest, link, left_link
+
+    gain_ref[pl.ds(aligned(me * width), width), :] = u[-1]
+    nothing = 0.0 * u[0]
+    carry = (nothing, nothing, nothing)
     if blocks <= 8:
         for n in range(blocks - 1):
-            other_block(n)
+            carry = one_block(n, carry)
     else:
-        lax.fori_loop(0, blocks - 1, lambda n, carry: (other_block(n), carry)[1], 0)
-
-    def end(b, n):
-        return ends[(4 * b + n) * width : (4 * b + n + 1) * width]
-
-    left = jnp.zeros((width, LANES), f32)
-    right = jnp.zeros((width, LANES), f32)
-    for b in range(blocks):
-        u_first, v_first, u_last, v_last = (end(b, n) for n in range(4))
-        gain = u_last * inverse(1.0 - u_first * left)
-        left_gain_ref[b * width : (b + 1) * width] = gain
-        links[b * width : (b + 1) * width] = left
-        left = v_last + gain * left * v_first
-        b = blocks - 1 - b
-        u_first, v_first, u_last, v_last = (end(b, n) for n in range(4))
-        gain = v_first * inverse(1.0 - v_last * right)
-        right_gain_ref[b * width : (b + 1) * width] = gain
-        links[(blocks + b) * width : (blocks + b + 1) * width] = right
-        right = u_first + gain * right * u_last
-
-    own = pl.ds(pl.multiple_of(me * width, 8), width)
-    left_link = links[own, :]
-    right_link = links[pl.ds(pl.multiple_of((blocks + me) * width, 8), width), :]
+        carry = lax.fori_loop(0, blocks - 1, one_block, carry)
+    _, link, left_link = carry
+    left_link = jnp.where(me == blocks - 1, link, left_link)
+    right_link = jnp.where(me == blocks - 1, 0.0, link)
+
     a = 1.0 - left_link * u[0]
     b = left_link * v[0]
     c = right_link * u[-1]
     d = 1.0 - right_link * v[-1]
     by = inverse(a * d - b * c)
     joint = (
-        left_gain_ref[own, :] * left_link, right_gain_ref[own, :] * right_link,
+        u[-1] * inverse(a) * left_link, v[0] * inverse(d) * right_link,
         left_link, right_link, d * by, b * by, c * by, a * by,
     )
     for n, value in enumerate(joint):
@@ -454,7 +430,7 @@
 
 
 def last_kernel(
-    sizes, came_ref, left_gain_ref, right_gain_ref, joint_ref, p_ref, u_ref, v_ref, field_ref,
+    sizes, came_ref, gain_ref, joint_ref, p_ref, u_ref, v_ref, field_ref,
     out_ref,
 ):
     rows, layers, chunks, row_total, layer_total, column_total = sizes
@@ -468,9 +444,9 @@
     left = jnp.zeros((width, LANES), f32)
     right = jnp.zeros((width, LANES), f32)
     for b in range(blocks - 1):
-        left = jnp.where(b < me, part(came_ref, b) + part(left_gain_ref, b) * left, left)
+        left = jnp.where(b < me, part(came_ref, b) + part(gain_ref, b) * left, left)
         b = blocks - 1 - b
-        right = jnp.where(b > me, part(came_ref, b) + part(right_gain_ref, b) * right, right)
+        right = jnp.where(b > me, part(came_ref, b) + part(gain_ref, b) * right, right)
 
     y = left + part(joint_ref, 2) * part(p_ref, 0)
     z = right + part(joint_ref, 3) * part(p_ref, rows - 1)
@@ -575,15 +551,12 @@
         compiler_params=limit,
     )(handed, came)
 
-    sent, p, u, v, left_gain, right_gain, joint = pl.pallas_call(
+    sent, p, u, v, gain, joint = pl.pallas_call(
         functools.partial(main_kernel, sizes),
         out_shape=(lines(wide_count),)
         + (lines(rows),) * 3
-        + (lines(wide_count),) * 2
-        + (lines(8),),
+        + (lines(wide_count), lines(8)),
         scratch_shapes=[
-            pltpu.VMEM((4 * wide_count * width, LANES), f32),
-            pltpu.VMEM((2 * wide_count * width, LANES), f32),
             pltpu.VMEM((2 * width, LANES), f32),
             pltpu.VMEM((rows * width, LANES), f32),
         ],
@@ -598,7 +571,7 @@
         functools.partial(last_kernel, sizes),
         out_shape=lines(rows),
         compiler_params=limit,
-    )(came, left_gain, right_gain, joint, p, u, v, field_lines)
+    )(came, gain, joint, p, u, v, field_lines)
     return from_lines(advanced, field.shape)
 
 

time: 26.3 us -> 26.1 us (level)
  no operation moved by 1% of the time
where the time goes in v20:
time: 26.1 us; the launch traced here: 25.8 us
  blocking collectives  18.7 us (72%)
  Pallas kernels  4.82 us (18%)
  waiting for transfers between devices  0.94 us (4%)
  between operations  0.71 us (3%)
  starting transfers between devices  0.59 us (2%)
    all_gather x1, blocking collectives, gather_rows(): lax.all_gather(rows_sent, 'wide', axis_index_groups=cores, axis=0)  9.8 us
    all_to_all x1, blocking collectives, on_device(): lax.all_to_all(sent.reshape(wide_count, width, LANES), 'wide', split_axis...  8.93 us
    pallas_call x1, Pallas kernels, on_device(): pl.pallas_call(functools.partial(main_kernel, sizes), out_shape=(lines(wi...  1.77 us
    pallas_call x1, Pallas kernels, on_device(): pl.pallas_call(functools.partial(load_kernel, sizes), out_shape=(lines(ro...  1.09 us
    pallas_call x1, Pallas kernels, on_device(): pl.pallas_call(pack_kernel, out_shape=(jax.ShapeDtypeStruct((mode_index.s...  0.86 us
    ppermute x1, waiting for transfers between devices, on_device(): both_came = lax.ppermute(both, 'wide', swaps)  0.86 us
    pallas_call x1, Pallas kernels, on_device(): pl.pallas_call(functools.partial(last_kernel, sizes), out_shape=lines(row...  0.73 us
  transfers between devices with their start and end apart: 2, of which 2 were waited for; matrix products, arithmetic and copies ran while one was open for 0% of the time, Pallas kernels for 4%

profile of v20, /device:TPU:0, one launch (start us, length us, event | category | flops | bytes accessed | tf_op | source)
XLA Modules:
  0.0 25.8 jit_solution(3828478826093745300)
XLA Ops:
  0.7 0.9 %shard_map.64 = (f32[2,128]{1,0:T(2,128)S(1)}, f32[64,128]{1,0:T(8,128)S(1)}, f32[32,128]{1,0:T(8,128)S(1)}) custom-call(s32[1]{0:T(128)S(6)} %copy.22.step_ref, s32[2,3]{1,0:T(2,128)} %index_ref.1, f32[2]{0:T(128)} %amp_ref.1, f32[2]{0:T(128)} %phase_ref.1, f32[256,128]{1,0:T(8,128)} %bitcast.31), custom_call_target="tpu_custom_call" | custom-call | tf_op jit(solution)/shard_map/pallas_call | solution.py:484
  1.5 0.5 %collective-permute-start = (f32[64,128]{1,0:T(8,128)S(1)}, f32[64,128]{1,0:T(8,128)S(1)}, u32[]{:S(2)}, u32[]{:S(2)}) collective-permute-start(f32[64,128]{1,0:T(8,128)S(1)} %get-tuple-element.39), channel_id=1, source_target_pairs={{0,1},{1,0},{2,3},{3,2},{4,5},{5,4},{6,7},{7,6},{8,9},{9,8},{10,11... | collective-permute-start | bytes 98312 | tf_op jit(solution)/shard_map/ppermute | solution.py:505
  2.0 0.9 %collective-permute-done.both_ref = f32[64,128]{1,0:T(8,128)S(1)} collective-permute-done((f32[64,128]{1,0:T(8,128)S(1)}, f32[64,128]{1,0:T(8,128)S(1)}, u32[]{:S(2)}, u32[]{:S(2)}) %collective-permute-start) | collective-permute-done | bytes 32800 | tf_op jit(solution)/shard_map/ppermute | solution.py:505
  2.9 9.8 %conditional.3 = (f32[32,128]{1,0:T(8,128)S(1)}, f32[32,128]{1,0:T(8,128)S(1)}) conditional(s32[]{:T(128)} %convert_element_type.4, (f32[64,128]{1,0:T(8,128)S(1)}, f32[32,128]{1,0:T(8,128)S(1)}, s32[]{:T(128)}) %tuple.23, () %tuple.24), branch_computations={%region_2.3_spmd, %region_3.4_spmd} | conditional | flops 8215 | bytes 327952 | solution.py:529
  2.9 9.8 %all-gather = f32[256,128]{1,0:T(8,128)S(1)} all-gather(f32[64,128]{1,0:T(8,128)S(1)} %pad_maximum_fusion), channel_id=2, replica_groups={{0,2,4,6},{1,3,5,7},{8,10,12,14},{9,11,13,15},{16,18,20,22},{17,19,21,2..., dimensions={0}, use_global_device_ids=true | all-gather | bytes 163840 | tf_op jit(solution)/shard_map/cond/branch_0_fun/all_gather | solution.py:518
  12.7 0.1 collective-permute-start.1
  12.8 1.1 %shard_map.66 = (f32[256,128]{1,0:T(8,128)S(1)}, f32[512,128]{1,0:T(8,128)S(1)}) custom-call(f32[256,128]{1,0:T(8,128)} %bitcast.32, f32[256,128]{1,0:T(8,128)} %bitcast.34), custom_call_target="tpu_custom_call" | custom-call | tf_op jit(solution)/shard_map/pallas_call | solution.py:533
  13.9 0.1 collective-permute-done.1.came_ref
  14.0 0.4 %shard_map.65.heights = f32[1056,128]{1,0:T(8,128)S(1)} custom-call(f32[40,128]{1,0:T(8,128)S(1)} %constant_dynamic-update-slice_fusion.handed_ref, f32[40,128]{1,0:T(8,128)S(1)} %collective-permute-done.1.came_ref), custom_call_target="tpu_custom_call" | custom-call | tf_op jit(solution)/shard_map/pallas_call | solution.py:548
  14.4 1.8 %shard_map.67 = (f32[256,128]{1,0:T(8,128)S(1)}, f32[256,128]{1,0:T(8,128)S(1)}, f32[256,128]{1,0:T(8,128)S(1)}, f32[256,128]{1,0:T(8,128)S(1)}, f32[256,128]{1,0:T(8,128)S(1)}, /*index=5*/f32[256,128]{1,0:T(8,128)S(1)}) custom-call(f32[1056,128]{1,0:T(8,128)S(1)} %shard_map.65.heights, f32[64,128]{1,0:T(8,128)S(1)} %collective-permute-done.both_ref, ...), custom_call_target="tpu_custom_call" | custom-call | tf_op jit(solution)/shard_map/pallas_call | solution.py:554
  16.2 8.9 %all_to_all.5 = f32[8,32,128]{2,1,0:T(8,128)S(1)} all-to-all(f32[8,32,128]{2,1,0:T(8,128)S(1)} %bitcast.30), channel_id=1, replica_groups=mesh['grp'=4,'wide'=8] {'wide'}, dimensions={0} | all-to-all | bytes 262144 | tf_op jit(solution)/shard_map/all_to_all | solution.py:566
  25.1 0.7 %shard_map.68 = f32[256,128]{1,0:T(8,128)} custom-call(f32[256,128]{1,0:T(8,128)S(1)} %bitcast.29, f32[256,128]{1,0:T(8,128)S(1)} %get-tuple-element.50.gain_ref, f32[256,128]{1,0:T(8,128)S(1)} %get-tuple-element.51.joint_ref, f32[256,128]{1,0:T(8,128)S(1)} %get-tuple-element.52.p_ref, f32[256,128]{1,0:T(8,128)S(1)} %get-tuple-element.53.u_ref, ...), custom_call_target="tpu_custom_call" | custom-call | tf_op jit(solution)/shard_map/pallas_call | solution.py:570
  (7 shorter events, 0.0 us)
Async XLA Ops:
  1.5 1.4 %collective-permute-start = (f32[64,128]{1,0:T(8,128)S(1)}, f32[64,128]{1,0:T(8,128)S(1)}, u32[]{:S(2)}, u32[]{:S(2)}) collective-permute-start(f32[64,128]{1,0:T(8,128)S(1)} %get-tuple-element.39), channel_id=1, source_target_pairs={{0,1},{1,0},{2,3},{3,2},{4,5},{5,4},{6,7},{7,6},{8,9},{9,8},{10,11... | collective-permute-start | bytes 98312 | tf_op jit(solution)/shard_map/ppermute | solution.py:505
  12.7 1.3 %collective-permute-start.1 = (f32[40,128]{1,0:T(8,128)S(1)}, f32[40,128]{1,0:T(8,128)S(1)}, u32[]{:S(2)}, u32[]{:S(2)}) collective-permute-start(f32[40,128]{1,0:T(8,128)S(1)} %constant_dynamic-update-slice_fusion.handed_ref), channel_id=1, source_target_pairs={{0,1},{1,0},{2,3},{3,2},{4,5},{5,4},{6,7},{7,6},{8,9},{9,8},{10,11... | collective-permute-start | bytes 61448 | tf_op jit(solution)/shard_map/ppermute | solution.py:531

commit v21 on v20

--- a/solution.py
+++ b/solution.py
@@ -315,7 +315,7 @@
     def aligned(index):
         return pl.multiple_of(index, 8)
 
-    inv, scaled, chain, u, v = block_factors(
+    own_inv, scaled, chain, u, v = block_factors(
         [face(own_start + j * chunks, own_start + (j + 1) * chunks) for j in range(rows + 1)]
     )
     for j in range(rows):
@@ -323,7 +323,7 @@
         v_ref[j * width : (j + 1) * width] = v[j]
 
     def one_block(n, carry):
-        rest, link, left_link = carry
+        passed, link, left_link = carry
         upward = n < me
         b = jnp.where(upward, n, blocks - 1 - (n - me))
         start = b * (rows * chunks) + jnp.where(upward, 0, (rows + 1) * chunks)
@@ -332,14 +332,15 @@
         first = face(places[0], places[1])
         anew = (n == 0) | (n == me)
         left_link = jnp.where(n == me, link, left_link)
-        rest = jnp.where(anew, 1.0 + first, rest)
+        passed = jnp.where(anew, first, passed)
         for j in range(rows):
             after = face(places[j + 1], places[j + 2])
-            link = after * inverse(rest + after)
+            inv = inverse(passed + (1.0 + after))
+            link = after * inv
             through = through * link if j else link
-            rest = 1.0 + rest * link
+            passed = ((1.0 + passed) * after) * inv
         gain_ref[pl.ds(aligned(b * width), width), :] = through * (first * inverse(after))
-        return rest, link, left_link
+        return passed, link, left_link
 
     gain_ref[pl.ds(aligned(me * width), width), :] = u[-1]
     nothing = 0.0 * u[0]
@@ -415,9 +416,9 @@
     def part(ref, j):
         return ref[j * width : (j + 1) * width]
 
-    p = [part(solved, 0) * inv[0]]
+    p = [part(solved, 0) * own_inv[0]]
     for j in range(1, rows):
-        p.append(part(solved, j) * inv[j] + scaled[j] * p[-1])
+        p.append(part(solved, j) * own_inv[j] + scaled[j] * p[-1])
     for j in range(rows - 2, -1, -1):
         p[j] = p[j] + chain[j] * p[j + 1]
     for j in range(rows):

time: 26.1 us -> 26.2 us (level)
  no operation moved by 1% of the time
where the time goes in v21:
time: 26.2 us; the launch traced here: 25.9 us
  blocking collectives  18.7 us (71%)
  Pallas kernels  4.88 us (19%)
  waiting for transfers between devices  0.94 us (4%)
  between operations  0.71 us (3%)
  starting transfers between devices  0.59 us (2%)
    all_gather x1, blocking collectives, gather_rows(): lax.all_gather(rows_sent, 'wide', axis_index_groups=cores, axis=0)  9.8 us
    all_to_all x1, blocking collectives, on_device(): lax.all_to_all(sent.reshape(wide_count, width, LANES), 'wide', split_axis...  8.93 us
    pallas_call x1, Pallas kernels, on_device(): pl.pallas_call(functools.partial(main_kernel, sizes), out_shape=(lines(wi...  1.84 us
    pallas_call x1, Pallas kernels, on_device(): pl.pallas_call(functools.partial(load_kernel, sizes), out_shape=(lines(ro...  1.09 us
    pallas_call x1, Pallas kernels, on_device(): pl.pallas_call(pack_kernel, out_shape=(jax.ShapeDtypeStruct((mode_index.s...  0.86 us
    ppermute x1, waiting for transfers between devices, on_device(): both_came = lax.ppermute(both, 'wide', swaps)  0.86 us
    pallas_call x1, Pallas kernels, on_device(): pl.pallas_call(functools.partial(last_kernel, sizes), out_shape=lines(row...  0.73 us
  transfers between devices with their start and end apart: 2, of which 2 were waited for; matrix products, arithmetic and copies ran while one was open for 0% of the time, Pallas kernels for 4%

profile of v21, /device:TPU:0, one launch (start us, length us, event | category | flops | bytes accessed | tf_op | source)
XLA Modules:
  0.0 25.9 jit_solution(9382233003218823751)
XLA Ops:
  0.7 0.9 %shard_map.64 = (f32[2,128]{1,0:T(2,128)S(1)}, f32[64,128]{1,0:T(8,128)S(1)}, f32[32,128]{1,0:T(8,128)S(1)}) custom-call(s32[1]{0:T(128)S(6)} %copy.22.step_ref, s32[2,3]{1,0:T(2,128)} %index_ref.1, f32[2]{0:T(128)} %amp_ref.1, f32[2]{0:T(128)} %phase_ref.1, f32[256,128]{1,0:T(8,128)} %bitcast.31), custom_call_target="tpu_custom_call" | custom-call | tf_op jit(solution)/shard_map/pallas_call | solution.py:485
  1.5 0.5 %collective-permute-start = (f32[64,128]{1,0:T(8,128)S(1)}, f32[64,128]{1,0:T(8,128)S(1)}, u32[]{:S(2)}, u32[]{:S(2)}) collective-permute-start(f32[64,128]{1,0:T(8,128)S(1)} %get-tuple-element.39), channel_id=1, source_target_pairs={{0,1},{1,0},{2,3},{3,2},{4,5},{5,4},{6,7},{7,6},{8,9},{9,8},{10,11... | collective-permute-start | bytes 98312 | tf_op jit(solution)/shard_map/ppermute | solution.py:506
  2.0 0.9 %collective-permute-done.both_ref = f32[64,128]{1,0:T(8,128)S(1)} collective-permute-done((f32[64,128]{1,0:T(8,128)S(1)}, f32[64,128]{1,0:T(8,128)S(1)}, u32[]{:S(2)}, u32[]{:S(2)}) %collective-permute-start) | collective-permute-done | bytes 32800 | tf_op jit(solution)/shard_map/ppermute | solution.py:506
  2.9 9.8 %conditional.3 = (f32[32,128]{1,0:T(8,128)S(1)}, f32[32,128]{1,0:T(8,128)S(1)}) conditional(s32[]{:T(128)} %convert_element_type.4, (f32[64,128]{1,0:T(8,128)S(1)}, f32[32,128]{1,0:T(8,128)S(1)}, s32[]{:T(128)}) %tuple.23, () %tuple.24), branch_computations={%region_2.3_spmd, %region_3.4_spmd} | conditional | flops 8215 | bytes 327952 | solution.py:530
  2.9 9.8 %all-gather = f32[256,128]{1,0:T(8,128)S(1)} all-gather(f32[64,128]{1,0:T(8,128)S(1)} %pad_maximum_fusion), channel_id=2, replica_groups={{0,2,4,6},{1,3,5,7},{8,10,12,14},{9,11,13,15},{16,18,20,22},{17,19,21,2..., dimensions={0}, use_global_device_ids=true | all-gather | bytes 163840 | tf_op jit(solution)/shard_map/cond/branch_0_fun/all_gather | solution.py:519
  12.7 0.1 collective-permute-start.1
  12.8 1.1 %shard_map.66 = (f32[256,128]{1,0:T(8,128)S(1)}, f32[512,128]{1,0:T(8,128)S(1)}) custom-call(f32[256,128]{1,0:T(8,128)} %bitcast.32, f32[256,128]{1,0:T(8,128)} %bitcast.34), custom_call_target="tpu_custom_call" | custom-call | tf_op jit(solution)/shard_map/pallas_call | solution.py:534
  13.9 0.1 collective-permute-done.1.came_ref
  14.0 0.4 %shard_map.65.heights = f32[1056,128]{1,0:T(8,128)S(1)} custom-call(f32[40,128]{1,0:T(8,128)S(1)} %constant_dynamic-update-slice_fusion.handed_ref, f32[40,128]{1,0:T(8,128)S(1)} %collective-permute-done.1.came_ref), custom_call_target="tpu_custom_call" | custom-call | tf_op jit(solution)/shard_map/pallas_call | solution.py:549
  14.4 1.8 %shard_map.67 = (f32[256,128]{1,0:T(8,128)S(1)}, f32[256,128]{1,0:T(8,128)S(1)}, f32[256,128]{1,0:T(8,128)S(1)}, f32[256,128]{1,0:T(8,128)S(1)}, f32[256,128]{1,0:T(8,128)S(1)}, /*index=5*/f32[256,128]{1,0:T(8,128)S(1)}) custom-call(f32[1056,128]{1,0:T(8,128)S(1)} %shard_map.65.heights, f32[64,128]{1,0:T(8,128)S(1)} %collective-permute-done.both_ref, ...), custom_call_target="tpu_custom_call" | custom-call | tf_op jit(solution)/shard_map/pallas_call | solution.py:555
  16.2 8.9 %all_to_all.5 = f32[8,32,128]{2,1,0:T(8,128)S(1)} all-to-all(f32[8,32,128]{2,1,0:T(8,128)S(1)} %bitcast.30), channel_id=1, replica_groups=mesh['grp'=4,'wide'=8] {'wide'}, dimensions={0} | all-to-all | bytes 262144 | tf_op jit(solution)/shard_map/all_to_all | solution.py:567
  25.2 0.7 %shard_map.68 = f32[256,128]{1,0:T(8,128)} custom-call(f32[256,128]{1,0:T(8,128)S(1)} %bitcast.29, f32[256,128]{1,0:T(8,128)S(1)} %get-tuple-element.50.gain_ref, f32[256,128]{1,0:T(8,128)S(1)} %get-tuple-element.51.joint_ref, f32[256,128]{1,0:T(8,128)S(1)} %get-tuple-element.52.p_ref, f32[256,128]{1,0:T(8,128)S(1)} %get-tuple-element.53.u_ref, ...), custom_call_target="tpu_custom_call" | custom-call | tf_op jit(solution)/shard_map/pallas_call | solution.py:571
  (7 shorter events, 0.0 us)
Async XLA Ops:
  1.5 1.4 %collective-permute-start = (f32[64,128]{1,0:T(8,128)S(1)}, f32[64,128]{1,0:T(8,128)S(1)}, u32[]{:S(2)}, u32[]{:S(2)}) collective-permute-start(f32[64,128]{1,0:T(8,128)S(1)} %get-tuple-element.39), channel_id=1, source_target_pairs={{0,1},{1,0},{2,3},{3,2},{4,5},{5,4},{6,7},{7,6},{8,9},{9,8},{10,11... | collective-permute-start | bytes 98312 | tf_op jit(solution)/shard_map/ppermute | solution.py:506
  12.7 1.3 %collective-permute-start.1 = (f32[40,128]{1,0:T(8,128)S(1)}, f32[40,128]{1,0:T(8,128)S(1)}, u32[]{:S(2)}, u32[]{:S(2)}) collective-permute-start(f32[40,128]{1,0:T(8,128)S(1)} %constant_dynamic-update-slice_fusion.handed_ref), channel_id=1, source_target_pairs={{0,1},{1,0},{2,3},{3,2},{4,5},{5,4},{6,7},{7,6},{8,9},{9,8},{10,11... | collective-permute-start | bytes 61448 | tf_op jit(solution)/shard_map/ppermute | solution.py:532

commit v22 on v20

--- a/solution.py
+++ b/solution.py
@@ -209,42 +209,58 @@
     return unpack_pair(x_even, x_odd, odd_lane)
 
 
-def pack_kernel(
-    step_ref, index_ref, amp_ref, phase_ref, field_ref,
-    packed_ref, both_ref, outer_ref,
-    index_in, amp_in, phase_in, sems,
-):
+def row_copies(field_ref, both_ref, outer_ref, sems):
     width = outer_ref.shape[0]
     last = field_ref.shape[0] - width
     odd = lax.rem(lax.axis_index("wide"), 2)
     inner_rows = pl.ds(pl.multiple_of((1 - odd) * last, 8), width)
     outer_rows = pl.ds(pl.multiple_of(odd * last, 8), width)
     pairs = (
-        (index_ref, index_in),
-        (amp_ref, amp_in),
-        (phase_ref, phase_in),
         (field_ref.at[inner_rows], both_ref.at[pl.ds(0, width)]),
         (field_ref.at[outer_rows], both_ref.at[pl.ds(width, width)]),
         (field_ref.at[outer_rows], outer_ref),
     )
-    copies = [pltpu.make_async_copy(a, b, sems.at[n]) for n, (a, b) in enumerate(pairs)]
+    return [pltpu.make_async_copy(a, b, sems.at[n]) for n, (a, b) in enumerate(pairs)]
+
+
+def row_kernel(field_ref, packed_ref, both_ref, outer_ref, row_sems):
+    copies = row_copies(field_ref, both_ref, outer_ref, row_sems)
     for copy in copies:
         copy.start()
-    for copy in copies[:3]:
+    packed_ref[...] = jnp.zeros(packed_ref.shape, f32)
+    for copy in copies:
+        copy.wait()
+
+
+def pack_kernel(
+    field_ref, step_ref, index_ref, amp_ref, phase_ref,
+    packed_ref, both_ref, outer_ref,
+    row_sems, step_in, index_in, amp_in, phase_in, mode_sems,
+):
+    pairs = (
+        (step_ref, step_in), (index_ref, index_in), (amp_ref, amp_in), (phase_ref, phase_in)
+    )
+    mode_copies = [
+        pltpu.make_async_copy(a, b, mode_sems.at[n]) for n, (a, b) in enumerate(pairs)
+    ]
+    copies = row_copies(field_ref, both_ref, outer_ref, row_sems)
+    for copy in mode_copies + copies:
+        copy.start()
+    for copy in mode_copies:
         copy.wait()
     count = index_in.shape[0]
     row = lax.broadcasted_iota(jnp.int32, packed_ref.shape, 0)
     lane = lax.broadcasted_iota(jnp.int32, packed_ref.shape, 1)
     total = jnp.zeros(packed_ref.shape, f32)
     for m in range(count):
-        moment = lax.rem(index_in[m, 2] * step_ref[0], jnp.int32(64)).astype(f32)
+        moment = lax.rem(index_in[m, 2] * step_in[0], jnp.int32(64)).astype(f32)
         offset = phase_in[m] * (0.5 / math.pi) + moment * (1.0 / 64.0)
         for place, value in enumerate(
             (index_in[m, 0].astype(f32), index_in[m, 1].astype(f32), offset, amp_in[m])
         ):
             total = jnp.where((row == m) & (lane == place), value, total)
     packed_ref[...] = total
-    for copy in copies[3:]:
+    for copy in copies:
         copy.wait()
 
 
@@ -474,32 +490,40 @@
     def lines(count):
         return jax.ShapeDtypeStruct((count * width, LANES), f32)
 
-    step_index, mode_index, mode_amp, mode_phase, field_lines, conduct_lines = (
-        step_index,
-        *(
-            pltpu.with_memory_space_constraint(a, pltpu.HBM)
-            for a in (mode_index, mode_amp, mode_phase, to_lines(field), to_lines(conduct))
-        ),
-    )
-    packed, both, outer = pl.pallas_call(
-        pack_kernel,
-        out_shape=(
-            jax.ShapeDtypeStruct((mode_index.shape[0], LANES), f32),
-            lines(2),
-            lines(1),
-        ),
-        in_specs=[pl.BlockSpec(memory_space=pltpu.SMEM)] + [hbm] * 4,
-        scratch_shapes=[
-            pltpu.SMEM(mode_index.shape, jnp.int32),
-            pltpu.SMEM(mode_amp.shape, f32),
-            pltpu.SMEM(mode_phase.shape, f32),
-            pltpu.SemaphoreType.DMA((6,)),
-        ],
-        compiler_params=limit,
-    )(step_index, mode_index, mode_amp, mode_phase, field_lines)
-
     place = lax.axis_index("wide")
     odd = place % 2 == 1
+    first_shapes = (
+        jax.ShapeDtypeStruct((mode_index.shape[0], LANES), f32),
+        lines(2),
+        lines(1),
+    )
+    row_sems = pltpu.SemaphoreType.DMA((3,))
+
+    def pack_modes_and_rows(field_lines, *mode_arrays):
+        return pl.pallas_call(
+            pack_kernel,
+            out_shape=first_shapes,
+            in_specs=[hbm] * 5,
+            scratch_shapes=[row_sems]
+            + [pltpu.SMEM(a.shape, a.dtype) for a in mode_arrays]
+            + [pltpu.SemaphoreType.DMA((4,))],
+            compiler_params=limit,
+        )(*(pltpu.with_memory_space_constraint(a, pltpu.HBM) for a in (field_lines, *mode_arrays)))
+
+    def pack_rows(field_lines, *mode_arrays):
+        return pl.pallas_call(
+            row_kernel,
+            out_shape=first_shapes,
+            in_specs=[hbm],
+            scratch_shapes=[row_sems],
+            compiler_params=limit,
+        )(pltpu.with_memory_space_constraint(field_lines, pltpu.HBM))
+
+    packed, both, outer = lax.cond(
+        odd, pack_modes_and_rows, pack_rows,
+        to_lines(field), step_index, mode_index, mode_amp, mode_phase,
+    )
+
     swaps = [(i, i ^ 1) for i in range(wide_count)]
     cores = [list(range(n, wide_count, 2)) for n in range(2)]
     both_came = lax.ppermute(both, "wide", swaps)

time: 26.1 us -> 25.5 us (0.977)
  starting transfers between devices: 0.59 us -> 1.27 us
  between operations: 0.71 us -> 0.06 us
  blocking collectives: 18.7 us -> 18.1 us
    ppermute x1, starting transfers between devices: 0.52 us -> 1.2 us  [on_device(): both_came = lax.ppermute(both, 'wide', swaps)]
    all_gather x1, blocking collectives: 9.8 us -> 9.29 us  [gather_rows(): lax.all_gather(rows_sent, 'wide', axis_index_groups=cores, axis=0)]
where the time goes in v22:
time: 25.5 us; the launch traced here: 25.2 us
  blocking collectives  18.1 us (71%)
  Pallas kernels  4.77 us (19%)
  starting transfers between devices  1.27 us (5%)
  waiting for transfers between devices  0.94 us (4%)
    all_gather x1, blocking collectives, gather_rows(): lax.all_gather(rows_sent, 'wide', axis_index_groups=cores, axis=0)  9.29 us
    all_to_all x1, blocking collectives, on_device(): lax.all_to_all(sent.reshape(wide_count, width, LANES), 'wide', split_axis...  8.82 us
    pallas_call x1, Pallas kernels, on_device(): pl.pallas_call(functools.partial(main_kernel, sizes), out_shape=(lines(wi...  1.77 us
    ppermute x1, starting transfers between devices, on_device(): both_came = lax.ppermute(both, 'wide', swaps)  1.2 us
    pallas_call x1, Pallas kernels, on_device(): pl.pallas_call(functools.partial(load_kernel, sizes), out_shape=(lines(ro...  1.09 us
    ppermute x1, waiting for transfers between devices, on_device(): both_came = lax.ppermute(both, 'wide', swaps)  0.86 us
    pallas_call x1, Pallas kernels, pack_rows(): pl.pallas_call(row_kernel, out_shape=first_shapes, in_specs=[hbm], scratc...  0.82 us
    pallas_call x1, Pallas kernels, on_device(): pl.pallas_call(functools.partial(last_kernel, sizes), out_shape=lines(row...  0.73 us
  transfers between devices with their start and end apart: 2, of which 2 were waited for; matrix products, arithmetic and copies ran while one was open for 0% of the time, Pallas kernels for 4%

profile of v22, /device:TPU:0, one launch (start us, length us, event | category | flops | bytes accessed | tf_op | source)
XLA Modules:
  0.0 25.2 jit_solution(7510892033657189673)
XLA Ops:
  0.0 0.8 %conditional.3 = (f32[64,128]{1,0:T(8,128)S(1)}, f32[32,128]{1,0:T(8,128)S(1)}, f32[2,128]{1,0:T(2,128)S(1)}) conditional(s32[]{:T(128)} %convert_element_type.2, f32[256,128]{1,0:T(8,128)} %bitcast.31, (f32[256,128]{1,0:T(8,128)}, s32[1]{0:T(128)}, s32[2,3]{1,0:T(2,128)}, f32[2]{0:T(128)}, f32[2]{0:T(128)}) %tuple.46), branch_computations={%region_0.1_spmd, %region_1.2_spmd} | conditional | bytes 24 | solution.py:522
  0.0 0.8 %branch_0_fun.1 = (f32[2,128]{1,0:T(2,128)S(1)}, f32[64,128]{1,0:T(8,128)S(1)}, f32[32,128]{1,0:T(8,128)S(1)}) custom-call(f32[256,128]{1,0:T(8,128)} %field_ref), custom_call_target="tpu_custom_call" | custom-call | tf_op jit(solution)/shard_map/cond/branch_0_fun/pallas_call | solution.py:514
  0.8 1.2 %collective-permute-start = (f32[64,128]{1,0:T(8,128)S(1)}, f32[64,128]{1,0:T(8,128)S(1)}, u32[]{:S(2)}, u32[]{:S(2)}) collective-permute-start(f32[64,128]{1,0:T(8,128)S(1)} %get-tuple-element.68), channel_id=1, source_target_pairs={{0,1},{1,0},{2,3},{3,2},{4,5},{5,4},{6,7},{7,6},{8,9},{9,8},{10,11... | collective-permute-start | bytes 98312 | tf_op jit(solution)/shard_map/ppermute | solution.py:529
  2.0 0.9 %collective-permute-done.both_ref = f32[64,128]{1,0:T(8,128)S(1)} collective-permute-done((f32[64,128]{1,0:T(8,128)S(1)}, f32[64,128]{1,0:T(8,128)S(1)}, u32[]{:S(2)}, u32[]{:S(2)}) %collective-permute-start) | collective-permute-done | bytes 32800 | tf_op jit(solution)/shard_map/ppermute | solution.py:529
  2.9 9.3 %conditional.5 = (f32[32,128]{1,0:T(8,128)S(1)}, f32[32,128]{1,0:T(8,128)S(1)}) conditional(s32[]{:T(128)} %convert_element_type.2, (f32[64,128]{1,0:T(8,128)S(1)}, f32[32,128]{1,0:T(8,128)S(1)}, s32[]{:T(128)}) %tuple.36, () %tuple.37), branch_computations={%region_4.5_spmd, %region_5.6_spmd} | conditional | flops 8215 | bytes 327952 | solution.py:553
  2.9 9.3 %all-gather = f32[256,128]{1,0:T(8,128)S(1)} all-gather(f32[64,128]{1,0:T(8,128)S(1)} %pad_maximum_fusion), channel_id=2, replica_groups={{0,2,4,6},{1,3,5,7},{8,10,12,14},{9,11,13,15},{16,18,20,22},{17,19,21,2..., dimensions={0}, use_global_device_ids=true | all-gather | bytes 163840 | tf_op jit(solution)/shard_map/cond/branch_0_fun/all_gather | solution.py:542
  12.2 0.1 collective-permute-start.1
  12.3 1.1 %shard_map.69 = (f32[256,128]{1,0:T(8,128)S(1)}, f32[512,128]{1,0:T(8,128)S(1)}) custom-call(f32[256,128]{1,0:T(8,128)} %bitcast.33, f32[256,128]{1,0:T(8,128)} %bitcast.35), custom_call_target="tpu_custom_call" | custom-call | tf_op jit(solution)/shard_map/pallas_call | solution.py:557
  13.4 0.1 collective-permute-done.1.came_ref
  13.5 0.4 %shard_map.68.heights = f32[1056,128]{1,0:T(8,128)S(1)} custom-call(f32[40,128]{1,0:T(8,128)S(1)} %constant_dynamic-update-slice_fusion.handed_ref, f32[40,128]{1,0:T(8,128)S(1)} %collective-permute-done.1.came_ref), custom_call_target="tpu_custom_call" | custom-call | tf_op jit(solution)/shard_map/pallas_call | solution.py:572
  13.9 1.8 %shard_map.70 = (f32[256,128]{1,0:T(8,128)S(1)}, f32[256,128]{1,0:T(8,128)S(1)}, f32[256,128]{1,0:T(8,128)S(1)}, f32[256,128]{1,0:T(8,128)S(1)}, f32[256,128]{1,0:T(8,128)S(1)}, /*index=5*/f32[256,128]{1,0:T(8,128)S(1)}) custom-call(f32[1056,128]{1,0:T(8,128)S(1)} %shard_map.68.heights, f32[64,128]{1,0:T(8,128)S(1)} %collective-permute-done.both_ref, ...), custom_call_target="tpu_custom_call" | custom-call | tf_op jit(solution)/shard_map/pallas_call | solution.py:578
  15.6 8.8 %all_to_all.5 = f32[8,32,128]{2,1,0:T(8,128)S(1)} all-to-all(f32[8,32,128]{2,1,0:T(8,128)S(1)} %bitcast.30), channel_id=1, replica_groups=mesh['grp'=4,'wide'=8] {'wide'}, dimensions={0} | all-to-all | bytes 262144 | tf_op jit(solution)/shard_map/all_to_all | solution.py:590
  24.5 0.7 %shard_map.71 = f32[256,128]{1,0:T(8,128)} custom-call(f32[256,128]{1,0:T(8,128)S(1)} %bitcast.29, f32[256,128]{1,0:T(8,128)S(1)} %get-tuple-element.79.gain_ref, f32[256,128]{1,0:T(8,128)S(1)} %get-tuple-element.80.joint_ref, f32[256,128]{1,0:T(8,128)S(1)} %get-tuple-element.81.p_ref, f32[256,128]{1,0:T(8,128)S(1)} %get-tuple-element.82.u_ref, ...), custom_call_target="tpu_custom_call" | custom-call | tf_op jit(solution)/shard_map/pallas_call | solution.py:594
  (7 shorter events, 0.0 us)
Async XLA Ops:
  0.8 2.1 %collective-permute-start = (f32[64,128]{1,0:T(8,128)S(1)}, f32[64,128]{1,0:T(8,128)S(1)}, u32[]{:S(2)}, u32[]{:S(2)}) collective-permute-start(f32[64,128]{1,0:T(8,128)S(1)} %get-tuple-element.68), channel_id=1, source_target_pairs={{0,1},{1,0},{2,3},{3,2},{4,5},{5,4},{6,7},{7,6},{8,9},{9,8},{10,11... | collective-permute-start | bytes 98312 | tf_op jit(solution)/shard_map/ppermute | solution.py:529
  12.2 1.3 %collective-permute-start.1 = (f32[40,128]{1,0:T(8,128)S(1)}, f32[40,128]{1,0:T(8,128)S(1)}, u32[]{:S(2)}, u32[]{:S(2)}) collective-permute-start(f32[40,128]{1,0:T(8,128)S(1)} %constant_dynamic-update-slice_fusion.handed_ref), channel_id=1, source_target_pairs={{0,1},{1,0},{2,3},{3,2},{4,5},{5,4},{6,7},{7,6},{8,9},{9,8},{10,11... | collective-permute-start | bytes 61448 | tf_op jit(solution)/shard_map/ppermute | solution.py:555

commit v23 on v20

--- a/solution.py
+++ b/solution.py
@@ -68,12 +68,13 @@
     return high, (values - high.astype(f32)).astype(jnp.bfloat16)
 
 
-def height_lines(modes, first_row, count, row_total, chunks, column_total):
+def height_lines(modes, step, first_row, count, row_total, chunks, column_total):
     mode_count = modes.shape[0]
     wave_x = modes[:, 0:1].astype(jnp.int32)
     wave_y = modes[:, 1:2].astype(jnp.int32)
-    offset = modes[:, 2:3]
-    amp = modes[:, 3:4]
+    moment = modes[:, 2:3] * step * (1.0 / 64.0)
+    offset = modes[:, 3:4] * (0.5 / math.pi) + (moment - jnp.floor(moment))
+    amp = modes[:, 4:5]
     spot = lax.broadcasted_iota(jnp.int32, (mode_count, count * chunks), 1)
     chunk = spot % chunks
     row = jnp.clip(first_row + spot // chunks, 0, row_total - 1)
@@ -210,42 +211,49 @@
 
 
 def pack_kernel(
-    step_ref, index_ref, amp_ref, phase_ref, field_ref,
-    packed_ref, both_ref, outer_ref,
+    field_ref, index_ref, amp_ref, phase_ref,
+    packed_ref, both_ref,
     index_in, amp_in, phase_in, sems,
 ):
-    width = outer_ref.shape[0]
+    width = both_ref.shape[0] // 2
     last = field_ref.shape[0] - width
-    odd = lax.rem(lax.axis_index("wide"), 2)
-    inner_rows = pl.ds(pl.multiple_of((1 - odd) * last, 8), width)
-    outer_rows = pl.ds(pl.multiple_of(odd * last, 8), width)
     pairs = (
         (index_ref, index_in),
         (amp_ref, amp_in),
         (phase_ref, phase_in),
-        (field_ref.at[inner_rows], both_ref.at[pl.ds(0, width)]),
-        (field_ref.at[outer_rows], both_ref.at[pl.ds(width, width)]),
-        (field_ref.at[outer_rows], outer_ref),
+        (field_ref.at[pl.ds(0, width)], both_ref.at[pl.ds(0, width)]),
+        (field_ref.at[pl.ds(last, width)], both_ref.at[pl.ds(width, width)]),
     )
     copies = [pltpu.make_async_copy(a, b, sems.at[n]) for n, (a, b) in enumerate(pairs)]
     for copy in copies:
         copy.start()
     for copy in copies[:3]:
         copy.wait()
-    count = index_in.shape[0]
     row = lax.broadcasted_iota(jnp.int32, packed_ref.shape, 0)
     lane = lax.broadcasted_iota(jnp.int32, packed_ref.shape, 1)
     total = jnp.zeros(packed_ref.shape, f32)
-    for m in range(count):
-        moment = lax.rem(index_in[m, 2] * step_ref[0], jnp.int32(64)).astype(f32)
-        offset = phase_in[m] * (0.5 / math.pi) + moment * (1.0 / 64.0)
-        for place, value in enumerate(
-            (index_in[m, 0].astype(f32), index_in[m, 1].astype(f32), offset, amp_in[m])
-        ):
+    for m in range(index_in.shape[0]):
+        waves = [index_in[m, n].astype(f32) for n in range(3)]
+        for place, value in enumerate((*waves, phase_in[m], amp_in[m])):
             total = jnp.where((row == m) & (lane == place), value, total)
     packed_ref[...] = total
     for copy in copies[3:]:
         copy.wait()
+
+
+def row_kernel(field_ref, step_ref, table_ref, inner_ref, outer_ref, step_in, sems):
+    width = inner_ref.shape[0]
+    pairs = (
+        (step_ref, step_in),
+        (field_ref.at[pl.ds(field_ref.shape[0] - width, width)], inner_ref),
+        (field_ref.at[pl.ds(0, width)], outer_ref),
+    )
+    copies = [pltpu.make_async_copy(a, b, sems.at[n]) for n, (a, b) in enumerate(pairs)]
+    for copy in copies:
+        copy.start()
+    for copy in copies:
+        copy.wait()
+    table_ref[...] = jnp.full(table_ref.shape, step_in[0].astype(f32), f32)
 
 
 def load_kernel(sizes, field_ref, conduct_ref, field_out, turned_ref, conduct_in, sems):
@@ -284,8 +292,11 @@
 def height_kernel(sizes, handed_ref, came_ref, heights_ref):
     rows, layers, chunks, row_total, layer_total, column_total = sizes
     odd = lax.rem(lax.axis_index("wide"), 2) == 1
-    modes = jnp.where(odd, handed_ref[layers * chunks :], came_ref[layers * chunks :])
-    body = height_lines(modes, 0, row_total, row_total, chunks, column_total)
+    first = 2 * layers * chunks
+    own, other = handed_ref[first:], came_ref[first:]
+    modes = jnp.where(odd, own, other)
+    step = jnp.where(odd, other, own)[:, 0:1]
+    body = height_lines(modes, step, 0, row_total, row_total, chunks, column_total)
     heights_ref[chunks : (row_total + 1) * chunks] = body
     heights_ref[0:chunks] = body[0:chunks]
     heights_ref[(row_total + 1) * chunks : (row_total + 2) * chunks] = body[
@@ -366,9 +377,8 @@
         joint_ref[n * width : (n + 1) * width] = value
 
     odd = lax.rem(me, 2) == 1
-    inner = both_ref[0:width]
-    below = jnp.where(odd, inner, below_ref[...])
-    above = jnp.where(odd, came_ref[0:width], inner)
+    below = jnp.where(odd, came_ref[width : 2 * width], below_ref[...])
+    above = jnp.where(odd, came_ref[0:width], both_ref[0:width])
     halo[0:width] = jnp.where(me == 0, 0.0, below)
     halo[width : 2 * width] = jnp.where(me == blocks - 1, 0.0, above)
     lane = lax.broadcasted_iota(jnp.int32, (rows, LANES), 1)
@@ -474,44 +484,52 @@
     def lines(count):
         return jax.ShapeDtypeStruct((count * width, LANES), f32)
 
-    step_index, mode_index, mode_amp, mode_phase, field_lines, conduct_lines = (
-        step_index,
-        *(
-            pltpu.with_memory_space_constraint(a, pltpu.HBM)
-            for a in (mode_index, mode_amp, mode_phase, to_lines(field), to_lines(conduct))
-        ),
-    )
-    packed, both, outer = pl.pallas_call(
-        pack_kernel,
-        out_shape=(
-            jax.ShapeDtypeStruct((mode_index.shape[0], LANES), f32),
-            lines(2),
-            lines(1),
-        ),
-        in_specs=[pl.BlockSpec(memory_space=pltpu.SMEM)] + [hbm] * 4,
-        scratch_shapes=[
-            pltpu.SMEM(mode_index.shape, jnp.int32),
-            pltpu.SMEM(mode_amp.shape, f32),
-            pltpu.SMEM(mode_phase.shape, f32),
-            pltpu.SemaphoreType.DMA((6,)),
-        ],
-        compiler_params=limit,
-    )(step_index, mode_index, mode_amp, mode_phase, field_lines)
-
     place = lax.axis_index("wide")
     odd = place % 2 == 1
     swaps = [(i, i ^ 1) for i in range(wide_count)]
     cores = [list(range(n, wide_count, 2)) for n in range(2)]
+    table_shape = (grp_count * mode_index.shape[0], LANES)
+    packed_shape = (mode_index.shape[0], LANES)
+    in_hbm = lambda arrays: [pltpu.with_memory_space_constraint(a, pltpu.HBM) for a in arrays]
+
+    def pack_modes(*arrays):
+        return pl.pallas_call(
+            pack_kernel,
+            out_shape=(jax.ShapeDtypeStruct(packed_shape, f32), lines(2)),
+            in_specs=[hbm] * 4,
+            scratch_shapes=[pltpu.SMEM(a.shape, a.dtype) for a in arrays[1:]]
+            + [pltpu.SemaphoreType.DMA((5,))],
+            compiler_params=limit,
+        )(*in_hbm(arrays))
+
+    def pack_nothing(*arrays):
+        return jnp.zeros(packed_shape, f32), jnp.zeros((2 * width, LANES), f32)
+
+    packed, both = lax.cond(
+        odd, pack_modes, pack_nothing, to_lines(field), mode_index, mode_amp, mode_phase
+    )
     both_came = lax.ppermute(both, "wide", swaps)
 
-    def gather_modes(own):
-        return lax.all_gather(own, "grp", axis=0, tiled=True)
-
-    def no_modes(own):
-        return jnp.zeros((grp_count * own.shape[0], own.shape[1]), f32)
-
-    modes = lax.cond(odd, gather_modes, no_modes, packed)
-    modes, outer, both_came = lax.optimization_barrier((modes, outer, both_came))
+    def gather_modes(own, *arrays):
+        empty = jnp.zeros((width, LANES), f32)
+        return lax.all_gather(own, "grp", axis=0, tiled=True), empty, empty
+
+    def load_rows(own, *arrays):
+        return pl.pallas_call(
+            row_kernel,
+            out_shape=(jax.ShapeDtypeStruct(table_shape, f32), lines(1), lines(1)),
+            in_specs=[hbm] * 2,
+            scratch_shapes=[
+                pltpu.SMEM(step_index.shape, step_index.dtype),
+                pltpu.SemaphoreType.DMA((3,)),
+            ],
+            compiler_params=limit,
+        )(*in_hbm(arrays))
+
+    table, inner, outer = lax.cond(
+        odd, gather_modes, load_rows, packed, to_lines(field), step_index
+    )
+    table, inner, outer, both_came = lax.optimization_barrier((table, inner, outer, both_came))
 
     def gather_rows(own, came):
         rows_sent = jnp.concatenate([own, came[width:]], 0)
@@ -527,7 +545,7 @@
         return jnp.zeros_like(own), jnp.zeros_like(own)
 
     below, above = lax.cond(odd, no_rows, gather_rows, outer, both_came)
-    handed = jnp.concatenate([above, modes], 0)
+    handed = jnp.concatenate([above, inner, table], 0)
     came = lax.ppermute(handed, "wide", swaps)
     handed, field, conduct = lax.optimization_barrier((handed, field, conduct))
     field_lines, turned = pl.pallas_call(

time: 26.1 us -> 25 us (0.958)
  blocking collectives: 18.7 us -> 17.5 us
  waiting for transfers between devices: 0.94 us -> 0.11 us
  starting transfers between devices: 0.59 us -> 1.37 us
  Pallas kernels: 4.82 us -> 5.5 us
  between operations: 0.71 us -> 0.07 us
    ppermute x1, waiting for transfers between devices: 0.86 us -> 0.01 us  [on_device(): both_came = lax.ppermute(both, 'wide', swaps)]
    ppermute x1, starting transfers between devices: 0.52 us -> 1.3 us  [on_device(): both_came = lax.ppermute(both, 'wide', swaps)]
    all_to_all x1, blocking collectives: 8.93 us -> 8.2 us  [on_device(): lax.all_to_all(sent.reshape(wide_count, width, LANES), 'wide', split_axis...]
    pallas_call x1, Pallas kernels: 0.86 us -> 1.41 us  [load_rows(): pl.pallas_call(row_kernel, out_shape=(jax.ShapeDtypeStruct(table_shape, f...]
    all_gather x1, blocking collectives: 9.8 us -> 9.3 us  [gather_rows(): lax.all_gather(rows_sent, 'wide', axis_index_groups=cores, axis=0)]
  transfers between devices with their start and end apart: 2 -> 2, of which waited for: 2 -> 1; matrix products, arithmetic and copies ran while one was open for 0% -> 0% of each run, Pallas kernels for 4% -> 10%
where the time goes in v23:
time: 25 us; the launch traced here: 24.6 us
  blocking collectives  17.5 us (70%)
  Pallas kernels  5.5 us (22%)
  starting transfers between devices  1.37 us (5%)
    all_gather x1, blocking collectives, gather_rows(): lax.all_gather(rows_sent, 'wide', axis_index_groups=cores, axis=0)  9.3 us
    all_to_all x1, blocking collectives, on_device(): lax.all_to_all(sent.reshape(wide_count, width, LANES), 'wide', split_axis...  8.2 us
    pallas_call x1, Pallas kernels, on_device(): pl.pallas_call(functools.partial(main_kernel, sizes), out_shape=(lines(wi...  1.77 us
    pallas_call x1, Pallas kernels, load_rows(): pl.pallas_call(row_kernel, out_shape=(jax.ShapeDtypeStruct(table_shape, f...  1.41 us
    ppermute x1, starting transfers between devices, on_device(): both_came = lax.ppermute(both, 'wide', swaps)  1.3 us
    pallas_call x1, Pallas kernels, on_device(): pl.pallas_call(functools.partial(load_kernel, sizes), out_shape=(lines(ro...  1.09 us
    pallas_call x1, Pallas kernels, on_device(): pl.pallas_call(functools.partial(last_kernel, sizes), out_shape=lines(row...  0.73 us
    pallas_call x1, Pallas kernels, on_device(): pl.pallas_call(functools.partial(height_kernel, sizes), out_shape=jax.Sha...  0.51 us
  transfers between devices with their start and end apart: 2, of which 1 were waited for; matrix products, arithmetic and copies ran while one was open for 0% of the time, Pallas kernels for 10%

profile of v23, /device:TPU:0, one launch (start us, length us, event | category | flops | bytes accessed | tf_op | source)
XLA Modules:
  0.0 24.6 jit_solution(6856659837999030543)
XLA Ops:
  0.0 1.3 %collective-permute-start = (f32[64,128]{1,0:T(8,128)S(1)}, f32[64,128]{1,0:T(8,128)S(1)}, u32[]{:S(2)}, u32[]{:S(2)}) collective-permute-start(f32[64,128]{1,0:T(8,128)S(1)} %get-tuple-element.64), channel_id=1, source_target_pairs={{0,1},{1,0},{2,3},{3,2},{4,5},{5,4},{6,7},{7,6},{8,9},{9,8},{10,11... | collective-permute-start | bytes 98312 | tf_op jit(solution)/shard_map/ppermute | solution.py:511
  1.3 1.4 %conditional.4 = ((f32[8,128]{1,0:T(8,128)S(1)}, f32[32,128]{1,0:T(8,128)S(1)}, f32[32,128]{1,0:T(8,128)S(1)})) conditional(s32[]{:T(128)} %convert_element_type.2, (f32[256,128]{1,0:T(8,128)}, s32[1]{0:T(128)}) %tuple.51, f32[2,128]{1,0:T(2,128)S(1)} %get-tuple-element.60), branch_computations={%region_2.3_spmd, %region_3.4_spmd} | conditional | bytes 37928 | solution.py:529
  1.3 1.4 %branch_0_fun.1 = (f32[8,128]{1,0:T(8,128)S(1)}, f32[32,128]{1,0:T(8,128)S(1)}, f32[32,128]{1,0:T(8,128)S(1)}) custom-call(f32[256,128]{1,0:T(8,128)} %get-tuple-element.33.field_ref, s32[1]{0:T(128)} %get-tuple-element.89.step_ref), custom_call_target="tpu_custom_call" | custom-call | tf_op jit(solution)/shard_map/cond/branch_0_fun/pallas_call | solution.py:518
  2.7 0.0 collective-permute-done.both_ref
  2.7 9.4 %conditional.5 = (f32[32,128]{1,0:T(8,128)S(1)}, f32[32,128]{1,0:T(8,128)S(1)}) conditional(s32[]{:T(128)} %convert_element_type.2, (f32[64,128]{1,0:T(8,128)S(1)}, f32[32,128]{1,0:T(8,128)S(1)}, s32[]{:T(128)}) %tuple.38, () %tuple.39), branch_computations={%region_4.5_spmd, %region_5.6_spmd} | conditional | flops 8215 | bytes 327952 | solution.py:547
  2.8 9.3 %all-gather = f32[256,128]{1,0:T(8,128)S(1)} all-gather(f32[64,128]{1,0:T(8,128)S(1)} %pad_maximum_fusion), channel_id=2, replica_groups={{0,2,4,6},{1,3,5,7},{8,10,12,14},{9,11,13,15},{16,18,20,22},{17,19,21,2..., dimensions={0}, use_global_device_ids=true | all-gather | bytes 163840 | tf_op jit(solution)/shard_map/cond/branch_0_fun/all_gather | solution.py:536
  12.2 0.1 collective-permute-start.1
  12.2 1.1 %shard_map.69 = (f32[256,128]{1,0:T(8,128)S(1)}, f32[512,128]{1,0:T(8,128)S(1)}) custom-call(f32[256,128]{1,0:T(8,128)} %bitcast.33, f32[256,128]{1,0:T(8,128)} %bitcast.35), custom_call_target="tpu_custom_call" | custom-call | tf_op jit(solution)/shard_map/pallas_call | solution.py:551
  13.3 0.1 collective-permute-done.1.came_ref
  13.4 0.5 %shard_map.68.heights = f32[1056,128]{1,0:T(8,128)S(1)} custom-call(f32[72,128]{1,0:T(8,128)S(1)} %constant_dynamic-update-slice_fusion.handed_ref, f32[72,128]{1,0:T(8,128)S(1)} %collective-permute-done.1.came_ref), custom_call_target="tpu_custom_call" | custom-call | tf_op jit(solution)/shard_map/pallas_call | solution.py:566
  13.9 1.8 %shard_map.70 = (f32[256,128]{1,0:T(8,128)S(1)}, f32[256,128]{1,0:T(8,128)S(1)}, f32[256,128]{1,0:T(8,128)S(1)}, f32[256,128]{1,0:T(8,128)S(1)}, f32[256,128]{1,0:T(8,128)S(1)}, /*index=5*/f32[256,128]{1,0:T(8,128)S(1)}) custom-call(f32[1056,128]{1,0:T(8,128)S(1)} %shard_map.68.heights, f32[64,128]{1,0:T(8,128)S(1)} %collective-permute-done.both_ref, ...), custom_call_target="tpu_custom_call" | custom-call | tf_op jit(solution)/shard_map/pallas_call | solution.py:572
  15.7 8.2 %all_to_all.5 = f32[8,32,128]{2,1,0:T(8,128)S(1)} all-to-all(f32[8,32,128]{2,1,0:T(8,128)S(1)} %bitcast.30), channel_id=1, replica_groups=mesh['grp'=4,'wide'=8] {'wide'}, dimensions={0} | all-to-all | bytes 262144 | tf_op jit(solution)/shard_map/all_to_all | solution.py:584
  23.9 0.7 %shard_map.71 = f32[256,128]{1,0:T(8,128)} custom-call(f32[256,128]{1,0:T(8,128)S(1)} %bitcast.29, f32[256,128]{1,0:T(8,128)S(1)} %get-tuple-element.76.gain_ref, f32[256,128]{1,0:T(8,128)S(1)} %get-tuple-element.77.joint_ref, f32[256,128]{1,0:T(8,128)S(1)} %get-tuple-element.78.p_ref, f32[256,128]{1,0:T(8,128)S(1)} %get-tuple-element.79.u_ref, ...), custom_call_target="tpu_custom_call" | custom-call | tf_op jit(solution)/shard_map/pallas_call | solution.py:588
  (9 shorter events, 0.0 us)
Async XLA Ops:
  0.0 2.7 %collective-permute-start = (f32[64,128]{1,0:T(8,128)S(1)}, f32[64,128]{1,0:T(8,128)S(1)}, u32[]{:S(2)}, u32[]{:S(2)}) collective-permute-start(f32[64,128]{1,0:T(8,128)S(1)} %get-tuple-element.64), channel_id=1, source_target_pairs={{0,1},{1,0},{2,3},{3,2},{4,5},{5,4},{6,7},{7,6},{8,9},{9,8},{10,11... | collective-permute-start | bytes 98312 | tf_op jit(solution)/shard_map/ppermute | solution.py:511
  12.2 1.3 %collective-permute-start.1 = (f32[72,128]{1,0:T(8,128)S(1)}, f32[72,128]{1,0:T(8,128)S(1)}, u32[]{:S(2)}, u32[]{:S(2)}) collective-permute-start(f32[72,128]{1,0:T(8,128)S(1)} %constant_dynamic-update-slice_fusion.handed_ref), channel_id=1, source_target_pairs={{0,1},{1,0},{2,3},{3,2},{4,5},{5,4},{6,7},{7,6},{8,9},{9,8},{10,11... | collective-permute-start | bytes 110600 | tf_op jit(solution)/shard_map/ppermute | solution.py:549

commit v24 on v23

--- a/solution.py
+++ b/solution.py
@@ -72,8 +72,9 @@
     mode_count = modes.shape[0]
     wave_x = modes[:, 0:1].astype(jnp.int32)
     wave_y = modes[:, 1:2].astype(jnp.int32)
-    moment = modes[:, 2:3] * step * (1.0 / 64.0)
+    moment = modes[:, 2:3] * (step * (1.0 / 64.0))
     offset = modes[:, 3:4] * (0.5 / math.pi) + (moment - jnp.floor(moment))
+    offset = jnp.concatenate([offset] * (count * chunks // LANES), 1)
     amp = modes[:, 4:5]
     spot = lax.broadcasted_iota(jnp.int32, (mode_count, count * chunks), 1)
     chunk = spot % chunks
@@ -253,7 +254,8 @@
         copy.start()
     for copy in copies:
         copy.wait()
-    table_ref[...] = jnp.full(table_ref.shape, step_in[0].astype(f32), f32)
+    step = step_in[...].astype(f32).reshape(1, 1)
+    table_ref[...] = jnp.broadcast_to(step, table_ref.shape)
 
 
 def load_kernel(sizes, field_ref, conduct_ref, field_out, turned_ref, conduct_in, sems):
@@ -295,7 +297,7 @@
     first = 2 * layers * chunks
     own, other = handed_ref[first:], came_ref[first:]
     modes = jnp.where(odd, own, other)
-    step = jnp.where(odd, other, own)[:, 0:1]
+    step = jnp.where(odd, other, own)
     body = height_lines(modes, step, 0, row_total, row_total, chunks, column_total)
     heights_ref[chunks : (row_total + 1) * chunks] = body
     heights_ref[0:chunks] = body[0:chunks]
@@ -520,7 +522,7 @@
             out_shape=(jax.ShapeDtypeStruct(table_shape, f32), lines(1), lines(1)),
             in_specs=[hbm] * 2,
             scratch_shapes=[
-                pltpu.SMEM(step_index.shape, step_index.dtype),
+                pltpu.VMEM(step_index.shape, step_index.dtype),
                 pltpu.SemaphoreType.DMA((3,)),
             ],
             compiler_params=limit,

time: 25 us -> 24.9 us (level)
  no operation moved by 1% of the time
where the time goes in v24:
time: 24.9 us; the launch traced here: 24.5 us
  blocking collectives  17.4 us (70%)
  Pallas kernels  5.45 us (22%)
  starting transfers between devices  1.37 us (6%)
    all_gather x1, blocking collectives, gather_rows(): lax.all_gather(rows_sent, 'wide', axis_index_groups=cores, axis=0)  9.3 us
    all_to_all x1, blocking collectives, on_device(): lax.all_to_all(sent.reshape(wide_count, width, LANES), 'wide', split_axis...  8.13 us
    pallas_call x1, Pallas kernels, on_device(): pl.pallas_call(functools.partial(main_kernel, sizes), out_shape=(lines(wi...  1.77 us
    pallas_call x1, Pallas kernels, load_rows(): pl.pallas_call(row_kernel, out_shape=(jax.ShapeDtypeStruct(table_shape, f...  1.48 us
    ppermute x1, starting transfers between devices, on_device(): both_came = lax.ppermute(both, 'wide', swaps)  1.3 us
    pallas_call x1, Pallas kernels, on_device(): pl.pallas_call(functools.partial(load_kernel, sizes), out_shape=(lines(ro...  1.09 us
    pallas_call x1, Pallas kernels, on_device(): pl.pallas_call(functools.partial(last_kernel, sizes), out_shape=lines(row...  0.73 us
  transfers between devices with their start and end apart: 2, of which 1 were waited for; matrix products, arithmetic and copies ran while one was open for 0% of the time, Pallas kernels for 10%

profile of v24, /device:TPU:0, one launch (start us, length us, event | category | flops | bytes accessed | tf_op | source)
XLA Modules:
  0.0 24.5 jit_solution(944409876354469769)
XLA Ops:
  0.0 1.3 %collective-permute-start = (f32[64,128]{1,0:T(8,128)S(1)}, f32[64,128]{1,0:T(8,128)S(1)}, u32[]{:S(2)}, u32[]{:S(2)}) collective-permute-start(f32[64,128]{1,0:T(8,128)S(1)} %get-tuple-element.64), channel_id=1, source_target_pairs={{0,1},{1,0},{2,3},{3,2},{4,5},{5,4},{6,7},{7,6},{8,9},{9,8},{10,11... | collective-permute-start | bytes 98312 | tf_op jit(solution)/shard_map/ppermute | solution.py:513
  1.3 1.5 %conditional.4 = ((f32[8,128]{1,0:T(8,128)S(1)}, f32[32,128]{1,0:T(8,128)S(1)}, f32[32,128]{1,0:T(8,128)S(1)})) conditional(s32[]{:T(128)} %convert_element_type.2, (f32[256,128]{1,0:T(8,128)}, s32[1]{0:T(128)}) %tuple.51, f32[2,128]{1,0:T(2,128)S(1)} %get-tuple-element.60), branch_computations={%region_2.3_spmd, %region_3.4_spmd} | conditional | bytes 37928 | solution.py:531
  1.3 1.5 %branch_0_fun.1 = (f32[8,128]{1,0:T(8,128)S(1)}, f32[32,128]{1,0:T(8,128)S(1)}, f32[32,128]{1,0:T(8,128)S(1)}) custom-call(f32[256,128]{1,0:T(8,128)} %get-tuple-element.33.field_ref, s32[1]{0:T(128)} %get-tuple-element.89.step_ref), custom_call_target="tpu_custom_call" | custom-call | tf_op jit(solution)/shard_map/cond/branch_0_fun/pallas_call | solution.py:520
  2.8 0.0 collective-permute-done.both_ref
  2.8 9.4 %conditional.5 = (f32[32,128]{1,0:T(8,128)S(1)}, f32[32,128]{1,0:T(8,128)S(1)}) conditional(s32[]{:T(128)} %convert_element_type.2, (f32[64,128]{1,0:T(8,128)S(1)}, f32[32,128]{1,0:T(8,128)S(1)}, s32[]{:T(128)}) %tuple.38, () %tuple.39), branch_computations={%region_4.5_spmd, %region_5.6_spmd} | conditional | flops 8215 | bytes 327952 | solution.py:549
  2.9 9.3 %all-gather = f32[256,128]{1,0:T(8,128)S(1)} all-gather(f32[64,128]{1,0:T(8,128)S(1)} %pad_maximum_fusion), channel_id=2, replica_groups={{0,2,4,6},{1,3,5,7},{8,10,12,14},{9,11,13,15},{16,18,20,22},{17,19,21,2..., dimensions={0}, use_global_device_ids=true | all-gather | bytes 163840 | tf_op jit(solution)/shard_map/cond/branch_0_fun/all_gather | solution.py:538
  12.2 0.1 collective-permute-start.1
  12.3 1.1 %shard_map.69 = (f32[256,128]{1,0:T(8,128)S(1)}, f32[512,128]{1,0:T(8,128)S(1)}) custom-call(f32[256,128]{1,0:T(8,128)} %bitcast.33, f32[256,128]{1,0:T(8,128)} %bitcast.35), custom_call_target="tpu_custom_call" | custom-call | tf_op jit(solution)/shard_map/pallas_call | solution.py:553
  13.4 0.1 collective-permute-done.1.came_ref
  13.5 0.4 %shard_map.68.heights = f32[1056,128]{1,0:T(8,128)S(1)} custom-call(f32[72,128]{1,0:T(8,128)S(1)} %constant_dynamic-update-slice_fusion.handed_ref, f32[72,128]{1,0:T(8,128)S(1)} %collective-permute-done.1.came_ref), custom_call_target="tpu_custom_call" | custom-call | tf_op jit(solution)/shard_map/pallas_call | solution.py:568
  13.9 1.8 %shard_map.70 = (f32[256,128]{1,0:T(8,128)S(1)}, f32[256,128]{1,0:T(8,128)S(1)}, f32[256,128]{1,0:T(8,128)S(1)}, f32[256,128]{1,0:T(8,128)S(1)}, f32[256,128]{1,0:T(8,128)S(1)}, /*index=5*/f32[256,128]{1,0:T(8,128)S(1)}) custom-call(f32[1056,128]{1,0:T(8,128)S(1)} %shard_map.68.heights, f32[64,128]{1,0:T(8,128)S(1)} %collective-permute-done.both_ref, ...), custom_call_target="tpu_custom_call" | custom-call | tf_op jit(solution)/shard_map/pallas_call | solution.py:574
  15.7 8.1 %all_to_all.5 = f32[8,32,128]{2,1,0:T(8,128)S(1)} all-to-all(f32[8,32,128]{2,1,0:T(8,128)S(1)} %bitcast.30), channel_id=1, replica_groups=mesh['grp'=4,'wide'=8] {'wide'}, dimensions={0} | all-to-all | bytes 262144 | tf_op jit(solution)/shard_map/all_to_all | solution.py:586
  23.8 0.7 %shard_map.71 = f32[256,128]{1,0:T(8,128)} custom-call(f32[256,128]{1,0:T(8,128)S(1)} %bitcast.29, f32[256,128]{1,0:T(8,128)S(1)} %get-tuple-element.76.gain_ref, f32[256,128]{1,0:T(8,128)S(1)} %get-tuple-element.77.joint_ref, f32[256,128]{1,0:T(8,128)S(1)} %get-tuple-element.78.p_ref, f32[256,128]{1,0:T(8,128)S(1)} %get-tuple-element.79.u_ref, ...), custom_call_target="tpu_custom_call" | custom-call | tf_op jit(solution)/shard_map/pallas_call | solution.py:590
  (9 shorter events, 0.0 us)
Async XLA Ops:
  0.0 2.8 %collective-permute-start = (f32[64,128]{1,0:T(8,128)S(1)}, f32[64,128]{1,0:T(8,128)S(1)}, u32[]{:S(2)}, u32[]{:S(2)}) collective-permute-start(f32[64,128]{1,0:T(8,128)S(1)} %get-tuple-element.64), channel_id=1, source_target_pairs={{0,1},{1,0},{2,3},{3,2},{4,5},{5,4},{6,7},{7,6},{8,9},{9,8},{10,11... | collective-permute-start | bytes 98312 | tf_op jit(solution)/shard_map/ppermute | solution.py:513
  12.2 1.3 %collective-permute-start.1 = (f32[72,128]{1,0:T(8,128)S(1)}, f32[72,128]{1,0:T(8,128)S(1)}, u32[]{:S(2)}, u32[]{:S(2)}) collective-permute-start(f32[72,128]{1,0:T(8,128)S(1)} %constant_dynamic-update-slice_fusion.handed_ref), channel_id=1, source_target_pairs={{0,1},{1,0},{2,3},{3,2},{4,5},{5,4},{6,7},{7,6},{8,9},{9,8},{10,11... | collective-permute-start | bytes 110600 | tf_op jit(solution)/shard_map/ppermute | solution.py:551

commit v25 on v24

--- a/solution.py
+++ b/solution.py
@@ -534,14 +534,17 @@
     table, inner, outer, both_came = lax.optimization_barrier((table, inner, outer, both_came))
 
     def gather_rows(own, came):
-        rows_sent = jnp.concatenate([own, came[width:]], 0)
-        rows_all = lax.all_gather(rows_sent, "wide", axis_index_groups=cores, axis=0)
         chip = place // 2
+        to_next = jnp.arange(wide_count // 2)[:, None, None] == chip + 1
+        rows_sent = jnp.where(to_next, came[None, width:], own[None])
+        rows_all = lax.all_to_all(
+            rows_sent, "wide", split_axis=0, concat_axis=0, axis_index_groups=cores
+        )
         below = lax.dynamic_index_in_dim(rows_all, jnp.maximum(chip - 1, 0), 0, False)
         above = lax.dynamic_index_in_dim(
             rows_all, jnp.minimum(chip + 1, wide_count // 2 - 1), 0, False
         )
-        return below[width:], above[:width]
+        return below, above
 
     def no_rows(own, came):
         return jnp.zeros_like(own), jnp.zeros_like(own)

time: 24.9 us -> 25.6 us (1.028)
  blocking collectives: 17.4 us -> 7.92 us
  waiting for transfers between devices: 0.11 us -> 4.95 us
  starting transfers between devices: 1.37 us -> 5.92 us
  other arithmetic: 0.01 us -> 0.71 us
    all_gather x1 -> x0, blocking collectives: 9.3 us -> none  [gather_rows(): lax.all_gather(rows_sent, 'wide', axis_index_groups=cores, axis=0)]
    all_to_all x0 -> x1, waiting for transfers between devices: none -> 4.85 us  [gather_rows(): lax.all_to_all(rows_sent, 'wide', split_axis=0, concat_axis=0, axis_index...]
    all_to_all x0 -> x1, starting transfers between devices: none -> 4.55 us  [gather_rows(): lax.all_to_all(rows_sent, 'wide', split_axis=0, concat_axis=0, axis_index...]
    select_n x0 -> x1, other arithmetic: none -> 0.7 us  [gather_rows(): rows_sent = jnp.where(to_next, came[None, width:], own[None])]
  transfers between devices with their start and end apart: 2 -> 3, of which waited for: 1 -> 2; matrix products, arithmetic and copies ran while one was open for 0% -> 0% of each run, Pallas kernels for 10% -> 10%
where the time goes in v25:
time: 25.6 us; the launch traced here: 25.1 us
  blocking collectives  7.92 us (31%)
  starting transfers between devices  5.92 us (23%)
  Pallas kernels  5.45 us (21%)
  waiting for transfers between devices  4.95 us (19%)
  other arithmetic  0.71 us (3%)
    all_to_all x1, blocking collectives, on_device(): lax.all_to_all(sent.reshape(wide_count, width, LANES), 'wide', split_axis...  7.92 us
    all_to_all x1, waiting for transfers between devices, gather_rows(): lax.all_to_all(rows_sent, 'wide', split_axis=0, concat_axis=0, axis_index...  4.85 us
    all_to_all x1, starting transfers between devices, gather_rows(): lax.all_to_all(rows_sent, 'wide', split_axis=0, concat_axis=0, axis_index...  4.55 us
    pallas_call x1, Pallas kernels, on_device(): pl.pallas_call(functools.partial(main_kernel, sizes), out_shape=(lines(wi...  1.77 us
    pallas_call x1, Pallas kernels, load_rows(): pl.pallas_call(row_kernel, out_shape=(jax.ShapeDtypeStruct(table_shape, f...  1.48 us
    ppermute x1, starting transfers between devices, on_device(): both_came = lax.ppermute(both, 'wide', swaps)  1.3 us
    pallas_call x1, Pallas kernels, on_device(): pl.pallas_call(functools.partial(load_kernel, sizes), out_shape=(lines(ro...  1.09 us
    pallas_call x1, Pallas kernels, on_device(): pl.pallas_call(functools.partial(last_kernel, sizes), out_shape=lines(row...  0.73 us
  transfers between devices with their start and end apart: 3, of which 2 were waited for; matrix products, arithmetic and copies ran while one was open for 0% of the time, Pallas kernels for 10%

profile of v25, /device:TPU:0, one launch (start us, length us, event | category | flops | bytes accessed | tf_op | source)
XLA Modules:
  0.0 25.1 jit_solution(11162967729109592197)
XLA Ops:
  0.0 1.3 %collective-permute-start = (f32[64,128]{1,0:T(8,128)S(1)}, f32[64,128]{1,0:T(8,128)S(1)}, u32[]{:S(2)}, u32[]{:S(2)}) collective-permute-start(f32[64,128]{1,0:T(8,128)S(1)} %get-tuple-element.64), channel_id=1, source_target_pairs={{0,1},{1,0},{2,3},{3,2},{4,5},{5,4},{6,7},{7,6},{8,9},{9,8},{10,11... | collective-permute-start | bytes 98312 | tf_op jit(solution)/shard_map/ppermute | solution.py:513
  1.3 1.5 %conditional.4 = ((f32[8,128]{1,0:T(8,128)S(1)}, f32[32,128]{1,0:T(8,128)S(1)}, f32[32,128]{1,0:T(8,128)S(1)})) conditional(s32[]{:T(128)} %convert_element_type.2, (f32[256,128]{1,0:T(8,128)}, s32[1]{0:T(128)}) %tuple.51, f32[2,128]{1,0:T(2,128)S(1)} %get-tuple-element.60), branch_computations={%region_2.3_spmd, %region_3.4_spmd} | conditional | bytes 37928 | solution.py:531
  1.3 1.5 %branch_0_fun.1 = (f32[8,128]{1,0:T(8,128)S(1)}, f32[32,128]{1,0:T(8,128)S(1)}, f32[32,128]{1,0:T(8,128)S(1)}) custom-call(f32[256,128]{1,0:T(8,128)} %get-tuple-element.33.field_ref, s32[1]{0:T(128)} %get-tuple-element.89.step_ref), custom_call_target="tpu_custom_call" | custom-call | tf_op jit(solution)/shard_map/cond/branch_0_fun/pallas_call | solution.py:520
  2.8 0.0 collective-permute-done.both_ref
  2.8 10.2 %conditional.5 = (f32[32,128]{1,0:T(8,128)S(1)}, f32[32,128]{1,0:T(8,128)S(1)}) conditional(s32[]{:T(128)} %convert_element_type.2, (s32[]{:T(128)}, f32[64,128]{1,0:T(8,128)S(1)}, f32[32,128]{1,0:T(8,128)S(1)}) %tuple.38, () %tuple.39), branch_computations={%region_4.5_spmd, %region_5.6_spmd} | conditional | flops 16410 | bytes 393516 | solution.py:552
  2.9 0.7 %broadcast_select_fusion = f32[4,32,128]{2,1,0:T(8,128)} fusion(f32[32,128]{1,0:T(8,128)S(1)} %get-tuple-element.37, f32[32,128]{1,0:T(8,128)S(1)} %slice.2, pred[4]{0:T(512)(128)(4,1)S(1)} %iota_compare_fusion), kind=kLoop, calls=%fused_computation | loop fusion | flops 16384 | bytes 98308 | tf_op jit(solution)/shard_map/cond/branch_0_fun/jit(_where)/select_n | solution.py:539
  3.6 4.5 %all-to-all-start = ((f32[4,32,128]{2,1,0:T(8,128)}), f32[4,32,128]{2,1,0:T(8,128)S(1)}, u32[]{:S(2)}, u32[]{:S(2)}) async-start(f32[4,32,128]{2,1,0:T(8,128)} %broadcast_select_fusion), calls=%async_computation | async-start | bytes 131072 | tf_op jit(solution)/shard_map/cond/branch_0_fun/all_to_all | solution.py:540
  8.1 4.8 %all-to-all-done = f32[4,32,128]{2,1,0:T(8,128)S(1)} async-done(((f32[4,32,128]{2,1,0:T(8,128)}), f32[4,32,128]{2,1,0:T(8,128)S(1)}, u32[]{:S(2)}, u32[]{:S(2)}) %all-to-all-start) | async-done | bytes 65568 | tf_op jit(solution)/shard_map/cond/branch_0_fun/all_to_all | solution.py:540
  13.0 0.1 collective-permute-start.1
  13.1 1.1 %shard_map.69 = (f32[256,128]{1,0:T(8,128)S(1)}, f32[512,128]{1,0:T(8,128)S(1)}) custom-call(f32[256,128]{1,0:T(8,128)} %bitcast.32, f32[256,128]{1,0:T(8,128)} %bitcast.33), custom_call_target="tpu_custom_call" | custom-call | tf_op jit(solution)/shard_map/pallas_call | solution.py:556
  14.2 0.1 collective-permute-done.1.came_ref
  14.3 0.4 %shard_map.68.heights = f32[1056,128]{1,0:T(8,128)S(1)} custom-call(f32[72,128]{1,0:T(8,128)S(1)} %constant_dynamic-update-slice_fusion.handed_ref, f32[72,128]{1,0:T(8,128)S(1)} %collective-permute-done.1.came_ref), custom_call_target="tpu_custom_call" | custom-call | tf_op jit(solution)/shard_map/pallas_call | solution.py:571
  14.6 1.8 %shard_map.70 = (f32[256,128]{1,0:T(8,128)S(1)}, f32[256,128]{1,0:T(8,128)S(1)}, f32[256,128]{1,0:T(8,128)S(1)}, f32[256,128]{1,0:T(8,128)S(1)}, f32[256,128]{1,0:T(8,128)S(1)}, /*index=5*/f32[256,128]{1,0:T(8,128)S(1)}) custom-call(f32[1056,128]{1,0:T(8,128)S(1)} %shard_map.68.heights, f32[64,128]{1,0:T(8,128)S(1)} %collective-permute-done.both_ref, ...), custom_call_target="tpu_custom_call" | custom-call | tf_op jit(solution)/shard_map/pallas_call | solution.py:577
  16.4 7.9 %all_to_all.9 = f32[8,32,128]{2,1,0:T(8,128)S(1)} all-to-all(f32[8,32,128]{2,1,0:T(8,128)S(1)} %bitcast.29), channel_id=1, replica_groups=mesh['grp'=4,'wide'=8] {'wide'}, dimensions={0} | all-to-all | bytes 262144 | tf_op jit(solution)/shard_map/all_to_all | solution.py:589
  24.4 0.7 %shard_map.71 = f32[256,128]{1,0:T(8,128)} custom-call(f32[256,128]{1,0:T(8,128)S(1)} %bitcast.28, f32[256,128]{1,0:T(8,128)S(1)} %get-tuple-element.76.gain_ref, f32[256,128]{1,0:T(8,128)S(1)} %get-tuple-element.77.joint_ref, f32[256,128]{1,0:T(8,128)S(1)} %get-tuple-element.78.p_ref, f32[256,128]{1,0:T(8,128)S(1)} %get-tuple-element.79.u_ref, ...), custom_call_target="tpu_custom_call" | custom-call | tf_op jit(solution)/shard_map/pallas_call | solution.py:593
  (9 shorter events, 0.0 us)
Async XLA Ops:
  0.0 2.8 %collective-permute-start = (f32[64,128]{1,0:T(8,128)S(1)}, f32[64,128]{1,0:T(8,128)S(1)}, u32[]{:S(2)}, u32[]{:S(2)}) collective-permute-start(f32[64,128]{1,0:T(8,128)S(1)} %get-tuple-element.64), channel_id=1, source_target_pairs={{0,1},{1,0},{2,3},{3,2},{4,5},{5,4},{6,7},{7,6},{8,9},{9,8},{10,11... | collective-permute-start | bytes 98312 | tf_op jit(solution)/shard_map/ppermute | solution.py:513
  3.6 9.4 %all-to-all-start = ((f32[4,32,128]{2,1,0:T(8,128)}), f32[4,32,128]{2,1,0:T(8,128)S(1)}, u32[]{:S(2)}, u32[]{:S(2)}) async-start(f32[4,32,128]{2,1,0:T(8,128)} %broadcast_select_fusion), calls=%async_computation | async-start | bytes 131072 | tf_op jit(solution)/shard_map/cond/branch_0_fun/all_to_all | solution.py:540
  13.0 1.3 %collective-permute-start.1 = (f32[72,128]{1,0:T(8,128)S(1)}, f32[72,128]{1,0:T(8,128)S(1)}, u32[]{:S(2)}, u32[]{:S(2)}) collective-permute-start(f32[72,128]{1,0:T(8,128)S(1)} %constant_dynamic-update-slice_fusion.handed_ref), channel_id=1, source_target_pairs={{0,1},{1,0},{2,3},{3,2},{4,5},{5,4},{6,7},{7,6},{8,9},{9,8},{10,11... | collective-permute-start | bytes 110600 | tf_op jit(solution)/shard_map/ppermute | solution.py:554

commit v26 on v24

--- a/solution.py
+++ b/solution.py
@@ -254,8 +254,7 @@
         copy.start()
     for copy in copies:
         copy.wait()
-    step = step_in[...].astype(f32).reshape(1, 1)
-    table_ref[...] = jnp.broadcast_to(step, table_ref.shape)
+    table_ref[...] = jnp.full(table_ref.shape, step_in[0].astype(f32), f32)
 
 
 def load_kernel(sizes, field_ref, conduct_ref, field_out, turned_ref, conduct_in, sems):
@@ -306,9 +305,9 @@
     ]
 
 def main_kernel(
-    sizes, heights, both_ref, below_ref, came_ref, turned_ref,
+    sizes, handed_ref, both_ref, below_ref, came_ref, turned_ref,
     sent_ref, p_ref, u_ref, v_ref, gain_ref, joint_ref,
-    halo, solved,
+    heights, halo, solved,
 ):
     rows, layers, chunks, row_total, layer_total, column_total = sizes
     width = layers * chunks
@@ -319,6 +318,7 @@
         ((first_layer + k).astype(f32) + 0.5) * (1.0 / layer_total) for k in range(layers)
     ]
     half = 0.5 * weight
+    height_kernel(sizes, handed_ref, came_ref, heights)
     own_start = pl.multiple_of(me * (rows * chunks), 8)
 
     def face(low, high):
@@ -522,7 +522,7 @@
             out_shape=(jax.ShapeDtypeStruct(table_shape, f32), lines(1), lines(1)),
             in_specs=[hbm] * 2,
             scratch_shapes=[
-                pltpu.VMEM(step_index.shape, step_index.dtype),
+                pltpu.SMEM(step_index.shape, step_index.dtype),
                 pltpu.SemaphoreType.DMA((3,)),
             ],
             compiler_params=limit,
@@ -565,23 +565,18 @@
             for a in (field, conduct)
         )
     )
-    heights = pl.pallas_call(
-        functools.partial(height_kernel, sizes),
-        out_shape=jax.ShapeDtypeStruct(((row_total + 2) * chunks, LANES), f32),
-        compiler_params=limit,
-    )(handed, came)
-
     sent, p, u, v, gain, joint = pl.pallas_call(
         functools.partial(main_kernel, sizes),
         out_shape=(lines(wide_count),)
         + (lines(rows),) * 3
         + (lines(wide_count), lines(8)),
         scratch_shapes=[
+            pltpu.VMEM(((row_total + 2) * chunks, LANES), f32),
             pltpu.VMEM((2 * width, LANES), f32),
             pltpu.VMEM((rows * width, LANES), f32),
         ],
         compiler_params=limit,
-    )(heights, both_came, below, came, turned)
+    )(handed, both_came, below, came, turned)
 
     came = lax.all_to_all(
         sent.reshape(wide_count, width, LANES), "wide", split_axis=0, concat_axis=0

time: 24.9 us -> 24.6 us (0.988)
  Pallas kernels: 5.45 us -> 5.1 us
    pallas_call x1 -> x0, Pallas kernels: 0.38 us -> none  [on_device(): pl.pallas_call(functools.partial(height_kernel, sizes), out_shape=jax.Sha...]
where the time goes in v26:
time: 24.6 us; the launch traced here: 24.2 us
  blocking collectives  17.5 us (71%)
  Pallas kernels  5.1 us (21%)
  starting transfers between devices  1.37 us (6%)
    all_gather x1, blocking collectives, gather_rows(): lax.all_gather(rows_sent, 'wide', axis_index_groups=cores, axis=0)  9.3 us
    all_to_all x1, blocking collectives, on_device(): lax.all_to_all(sent.reshape(wide_count, width, LANES), 'wide', split_axis...  8.2 us
    pallas_call x1, Pallas kernels, on_device(): pl.pallas_call(functools.partial(main_kernel, sizes), out_shape=(lines(wi...  1.87 us
    pallas_call x1, Pallas kernels, load_rows(): pl.pallas_call(row_kernel, out_shape=(jax.ShapeDtypeStruct(table_shape, f...  1.41 us
    ppermute x1, starting transfers between devices, on_device(): both_came = lax.ppermute(both, 'wide', swaps)  1.3 us
    pallas_call x1, Pallas kernels, on_device(): pl.pallas_call(functools.partial(load_kernel, sizes), out_shape=(lines(ro...  1.09 us
    pallas_call x1, Pallas kernels, on_device(): pl.pallas_call(functools.partial(last_kernel, sizes), out_shape=lines(row...  0.74 us
  transfers between devices with their start and end apart: 2, of which 1 were waited for; matrix products, arithmetic and copies ran while one was open for 0% of the time, Pallas kernels for 10%

profile of v26, /device:TPU:0, one launch (start us, length us, event | category | flops | bytes accessed | tf_op | source)
XLA Modules:
  0.0 24.2 jit_solution(14796121134419492571)
XLA Ops:
  0.0 1.3 %collective-permute-start = (f32[64,128]{1,0:T(8,128)S(1)}, f32[64,128]{1,0:T(8,128)S(1)}, u32[]{:S(2)}, u32[]{:S(2)}) collective-permute-start(f32[64,128]{1,0:T(8,128)S(1)} %get-tuple-element.64), channel_id=1, source_target_pairs={{0,1},{1,0},{2,3},{3,2},{4,5},{5,4},{6,7},{7,6},{8,9},{9,8},{10,11... | collective-permute-start | bytes 98312 | tf_op jit(solution)/shard_map/ppermute | solution.py:513
  1.3 1.4 %conditional.4 = ((f32[8,128]{1,0:T(8,128)S(1)}, f32[32,128]{1,0:T(8,128)S(1)}, f32[32,128]{1,0:T(8,128)S(1)})) conditional(s32[]{:T(128)} %convert_element_type.2, (f32[256,128]{1,0:T(8,128)}, s32[1]{0:T(128)}) %tuple.51, f32[2,128]{1,0:T(2,128)S(1)} %get-tuple-element.60), branch_computations={%region_2.3_spmd, %region_3.4_spmd} | conditional | bytes 37928 | solution.py:531
  1.3 1.4 %branch_0_fun.1 = (f32[8,128]{1,0:T(8,128)S(1)}, f32[32,128]{1,0:T(8,128)S(1)}, f32[32,128]{1,0:T(8,128)S(1)}) custom-call(f32[256,128]{1,0:T(8,128)} %get-tuple-element.33.field_ref, s32[1]{0:T(128)} %get-tuple-element.89.step_ref), custom_call_target="tpu_custom_call" | custom-call | tf_op jit(solution)/shard_map/cond/branch_0_fun/pallas_call | solution.py:520
  2.7 0.0 collective-permute-done.both_ref
  2.7 9.4 %conditional.5 = (f32[32,128]{1,0:T(8,128)S(1)}, f32[32,128]{1,0:T(8,128)S(1)}) conditional(s32[]{:T(128)} %convert_element_type.2, (f32[64,128]{1,0:T(8,128)S(1)}, f32[32,128]{1,0:T(8,128)S(1)}, s32[]{:T(128)}) %tuple.38, () %tuple.39), branch_computations={%region_4.5_spmd, %region_5.6_spmd} | conditional | flops 8215 | bytes 327952 | solution.py:549
  2.8 9.3 %all-gather = f32[256,128]{1,0:T(8,128)S(1)} all-gather(f32[64,128]{1,0:T(8,128)S(1)} %pad_maximum_fusion), channel_id=2, replica_groups={{0,2,4,6},{1,3,5,7},{8,10,12,14},{9,11,13,15},{16,18,20,22},{17,19,21,2..., dimensions={0}, use_global_device_ids=true | all-gather | bytes 163840 | tf_op jit(solution)/shard_map/cond/branch_0_fun/all_gather | solution.py:538
  12.2 0.1 collective-permute-start.1
  12.2 1.1 %shard_map.68 = (f32[256,128]{1,0:T(8,128)S(1)}, f32[512,128]{1,0:T(8,128)S(1)}) custom-call(f32[256,128]{1,0:T(8,128)} %bitcast.33, f32[256,128]{1,0:T(8,128)} %bitcast.35), custom_call_target="tpu_custom_call" | custom-call | tf_op jit(solution)/shard_map/pallas_call | solution.py:553
  13.3 0.1 collective-permute-done.1.came_ref
  13.4 1.9 %shard_map.69 = (f32[256,128]{1,0:T(8,128)S(1)}, f32[256,128]{1,0:T(8,128)S(1)}, f32[256,128]{1,0:T(8,128)S(1)}, f32[256,128]{1,0:T(8,128)S(1)}, f32[256,128]{1,0:T(8,128)S(1)}, /*index=5*/f32[256,128]{1,0:T(8,128)S(1)}) custom-call(f32[72,128]{1,0:T(8,128)S(1)} %constant_dynamic-update-slice_fusion.handed_ref, f32[64,128]{1,0:T(8,128)S(1)} %collective-permute-done.both_ref, ...), custom_call_target="tpu_custom_call" | custom-call | tf_op jit(solution)/shard_map/pallas_call | solution.py:568
  15.3 8.2 %all_to_all.5 = f32[8,32,128]{2,1,0:T(8,128)S(1)} all-to-all(f32[8,32,128]{2,1,0:T(8,128)S(1)} %bitcast.30), channel_id=1, replica_groups=mesh['grp'=4,'wide'=8] {'wide'}, dimensions={0} | all-to-all | bytes 262144 | tf_op jit(solution)/shard_map/all_to_all | solution.py:581
  23.5 0.7 %shard_map.70 = f32[256,128]{1,0:T(8,128)} custom-call(f32[256,128]{1,0:T(8,128)S(1)} %bitcast.29, f32[256,128]{1,0:T(8,128)S(1)} %get-tuple-element.76.gain_ref, f32[256,128]{1,0:T(8,128)S(1)} %get-tuple-element.77.joint_ref, f32[256,128]{1,0:T(8,128)S(1)} %get-tuple-element.78.p_ref, f32[256,128]{1,0:T(8,128)S(1)} %get-tuple-element.79.u_ref, ...), custom_call_target="tpu_custom_call" | custom-call | tf_op jit(solution)/shard_map/pallas_call | solution.py:585
  (9 shorter events, 0.0 us)
Async XLA Ops:
  0.0 2.7 %collective-permute-start = (f32[64,128]{1,0:T(8,128)S(1)}, f32[64,128]{1,0:T(8,128)S(1)}, u32[]{:S(2)}, u32[]{:S(2)}) collective-permute-start(f32[64,128]{1,0:T(8,128)S(1)} %get-tuple-element.64), channel_id=1, source_target_pairs={{0,1},{1,0},{2,3},{3,2},{4,5},{5,4},{6,7},{7,6},{8,9},{9,8},{10,11... | collective-permute-start | bytes 98312 | tf_op jit(solution)/shard_map/ppermute | solution.py:513
  12.2 1.3 %collective-permute-start.1 = (f32[72,128]{1,0:T(8,128)S(1)}, f32[72,128]{1,0:T(8,128)S(1)}, u32[]{:S(2)}, u32[]{:S(2)}) collective-permute-start(f32[72,128]{1,0:T(8,128)S(1)} %constant_dynamic-update-slice_fusion.handed_ref), channel_id=1, source_target_pairs={{0,1},{1,0},{2,3},{3,2},{4,5},{5,4},{6,7},{7,6},{8,9},{9,8},{10,11... | collective-permute-start | bytes 110600 | tf_op jit(solution)/shard_map/ppermute | solution.py:551

commit v27 on v26

--- a/solution.py
+++ b/solution.py
@@ -321,15 +321,19 @@
     height_kernel(sizes, handed_ref, came_ref, heights)
     own_start = pl.multiple_of(me * (rows * chunks), 8)
 
+    def row_heights(places):
+        return [heights[pl.ds(place, chunks), :] for place in places]
+
     def face(low, high):
-        both = heights[pl.ds(low, chunks), :] + heights[pl.ds(high, chunks), :]
+        both = low + high
         return jnp.concatenate([weight + (half * z) * both for z in zeta], 0)
 
     def aligned(index):
         return pl.multiple_of(index, 8)
 
+    own_rows = row_heights([own_start + j * chunks for j in range(rows + 2)])
     inv, scaled, chain, u, v = block_factors(
-        [face(own_start + j * chunks, own_start + (j + 1) * chunks) for j in range(rows + 1)]
+        [face(own_rows[j], own_rows[j + 1]) for j in range(rows + 1)]
     )
     for j in range(rows):
         u_ref[j * width : (j + 1) * width] = u[j]
@@ -341,13 +345,13 @@
         b = jnp.where(upward, n, blocks - 1 - (n - me))
         start = b * (rows * chunks) + jnp.where(upward, 0, (rows + 1) * chunks)
         step = jnp.where(upward, chunks, -chunks)
-        places = [aligned(start + j * step) for j in range(rows + 2)]
-        first = face(places[0], places[1])
+        h = row_heights([aligned(start + j * step) for j in range(rows + 2)])
+        first = face(h[0], h[1])
         anew = (n == 0) | (n == me)
         left_link = jnp.where(n == me, link, left_link)
         rest = jnp.where(anew, 1.0 + first, rest)
         for j in range(rows):
-            after = face(places[j + 1], places[j + 2])
+            after = face(h[j + 1], h[j + 2])
             link = after * inverse(rest + after)
             through = through * link if j else link
             rest = 1.0 + rest * link

time: 24.6 us -> 24.6 us (level)
  no operation moved by 1% of the time
where the time goes in v27:
time: 24.6 us; the launch traced here: 24.2 us
  blocking collectives  17.5 us (71%)
  Pallas kernels  5.11 us (21%)
  starting transfers between devices  1.37 us (6%)
    all_gather x1, blocking collectives, gather_rows(): lax.all_gather(rows_sent, 'wide', axis_index_groups=cores, axis=0)  9.3 us
    all_to_all x1, blocking collectives, on_device(): lax.all_to_all(sent.reshape(wide_count, width, LANES), 'wide', split_axis...  8.2 us
    pallas_call x1, Pallas kernels, on_device(): pl.pallas_call(functools.partial(main_kernel, sizes), out_shape=(lines(wi...  1.88 us
    pallas_call x1, Pallas kernels, load_rows(): pl.pallas_call(row_kernel, out_shape=(jax.ShapeDtypeStruct(table_shape, f...  1.41 us
    ppermute x1, starting transfers between devices, on_device(): both_came = lax.ppermute(both, 'wide', swaps)  1.3 us
    pallas_call x1, Pallas kernels, on_device(): pl.pallas_call(functools.partial(load_kernel, sizes), out_shape=(lines(ro...  1.09 us
    pallas_call x1, Pallas kernels, on_device(): pl.pallas_call(functools.partial(last_kernel, sizes), out_shape=lines(row...  0.74 us
  transfers between devices with their start and end apart: 2, of which 1 were waited for; matrix products, arithmetic and copies ran while one was open for 0% of the time, Pallas kernels for 10%

profile of v27, /device:TPU:0, one launch (start us, length us, event | category | flops | bytes accessed | tf_op | source)
XLA Modules:
  0.0 24.2 jit_solution(6647150820913663258)
XLA Ops:
  0.0 1.3 %collective-permute-start = (f32[64,128]{1,0:T(8,128)S(1)}, f32[64,128]{1,0:T(8,128)S(1)}, u32[]{:S(2)}, u32[]{:S(2)}) collective-permute-start(f32[64,128]{1,0:T(8,128)S(1)} %get-tuple-element.64), channel_id=1, source_target_pairs={{0,1},{1,0},{2,3},{3,2},{4,5},{5,4},{6,7},{7,6},{8,9},{9,8},{10,11... | collective-permute-start | bytes 98312 | tf_op jit(solution)/shard_map/ppermute | solution.py:517
  1.3 1.4 %conditional.4 = ((f32[8,128]{1,0:T(8,128)S(1)}, f32[32,128]{1,0:T(8,128)S(1)}, f32[32,128]{1,0:T(8,128)S(1)})) conditional(s32[]{:T(128)} %convert_element_type.2, (f32[256,128]{1,0:T(8,128)}, s32[1]{0:T(128)}) %tuple.51, f32[2,128]{1,0:T(2,128)S(1)} %get-tuple-element.60), branch_computations={%region_2.3_spmd, %region_3.4_spmd} | conditional | bytes 37928 | solution.py:535
  1.3 1.4 %branch_0_fun.1 = (f32[8,128]{1,0:T(8,128)S(1)}, f32[32,128]{1,0:T(8,128)S(1)}, f32[32,128]{1,0:T(8,128)S(1)}) custom-call(f32[256,128]{1,0:T(8,128)} %get-tuple-element.33.field_ref, s32[1]{0:T(128)} %get-tuple-element.89.step_ref), custom_call_target="tpu_custom_call" | custom-call | tf_op jit(solution)/shard_map/cond/branch_0_fun/pallas_call | solution.py:524
  2.7 0.0 collective-permute-done.both_ref
  2.7 9.4 %conditional.5 = (f32[32,128]{1,0:T(8,128)S(1)}, f32[32,128]{1,0:T(8,128)S(1)}) conditional(s32[]{:T(128)} %convert_element_type.2, (f32[64,128]{1,0:T(8,128)S(1)}, f32[32,128]{1,0:T(8,128)S(1)}, s32[]{:T(128)}) %tuple.38, () %tuple.39), branch_computations={%region_4.5_spmd, %region_5.6_spmd} | conditional | flops 8215 | bytes 327952 | solution.py:553
  2.8 9.3 %all-gather = f32[256,128]{1,0:T(8,128)S(1)} all-gather(f32[64,128]{1,0:T(8,128)S(1)} %pad_maximum_fusion), channel_id=2, replica_groups={{0,2,4,6},{1,3,5,7},{8,10,12,14},{9,11,13,15},{16,18,20,22},{17,19,21,2..., dimensions={0}, use_global_device_ids=true | all-gather | bytes 163840 | tf_op jit(solution)/shard_map/cond/branch_0_fun/all_gather | solution.py:542
  12.2 0.1 collective-permute-start.1
  12.2 1.1 %shard_map.68 = (f32[256,128]{1,0:T(8,128)S(1)}, f32[512,128]{1,0:T(8,128)S(1)}) custom-call(f32[256,128]{1,0:T(8,128)} %bitcast.33, f32[256,128]{1,0:T(8,128)} %bitcast.35), custom_call_target="tpu_custom_call" | custom-call | tf_op jit(solution)/shard_map/pallas_call | solution.py:557
  13.3 0.1 collective-permute-done.1.came_ref
  13.4 1.9 %shard_map.69 = (f32[256,128]{1,0:T(8,128)S(1)}, f32[256,128]{1,0:T(8,128)S(1)}, f32[256,128]{1,0:T(8,128)S(1)}, f32[256,128]{1,0:T(8,128)S(1)}, f32[256,128]{1,0:T(8,128)S(1)}, /*index=5*/f32[256,128]{1,0:T(8,128)S(1)}) custom-call(f32[72,128]{1,0:T(8,128)S(1)} %constant_dynamic-update-slice_fusion.handed_ref, f32[64,128]{1,0:T(8,128)S(1)} %collective-permute-done.both_ref, ...), custom_call_target="tpu_custom_call" | custom-call | tf_op jit(solution)/shard_map/pallas_call | solution.py:572
  15.3 8.2 %all_to_all.5 = f32[8,32,128]{2,1,0:T(8,128)S(1)} all-to-all(f32[8,32,128]{2,1,0:T(8,128)S(1)} %bitcast.30), channel_id=1, replica_groups=mesh['grp'=4,'wide'=8] {'wide'}, dimensions={0} | all-to-all | bytes 262144 | tf_op jit(solution)/shard_map/all_to_all | solution.py:585
  23.5 0.7 %shard_map.70 = f32[256,128]{1,0:T(8,128)} custom-call(f32[256,128]{1,0:T(8,128)S(1)} %bitcast.29, f32[256,128]{1,0:T(8,128)S(1)} %get-tuple-element.76.gain_ref, f32[256,128]{1,0:T(8,128)S(1)} %get-tuple-element.77.joint_ref, f32[256,128]{1,0:T(8,128)S(1)} %get-tuple-element.78.p_ref, f32[256,128]{1,0:T(8,128)S(1)} %get-tuple-element.79.u_ref, ...), custom_call_target="tpu_custom_call" | custom-call | tf_op jit(solution)/shard_map/pallas_call | solution.py:589
  (9 shorter events, 0.0 us)
Async XLA Ops:
  0.0 2.7 %collective-permute-start = (f32[64,128]{1,0:T(8,128)S(1)}, f32[64,128]{1,0:T(8,128)S(1)}, u32[]{:S(2)}, u32[]{:S(2)}) collective-permute-start(f32[64,128]{1,0:T(8,128)S(1)} %get-tuple-element.64), channel_id=1, source_target_pairs={{0,1},{1,0},{2,3},{3,2},{4,5},{5,4},{6,7},{7,6},{8,9},{9,8},{10,11... | collective-permute-start | bytes 98312 | tf_op jit(solution)/shard_map/ppermute | solution.py:517
  12.2 1.3 %collective-permute-start.1 = (f32[72,128]{1,0:T(8,128)S(1)}, f32[72,128]{1,0:T(8,128)S(1)}, u32[]{:S(2)}, u32[]{:S(2)}) collective-permute-start(f32[72,128]{1,0:T(8,128)S(1)} %constant_dynamic-update-slice_fusion.handed_ref), channel_id=1, source_target_pairs={{0,1},{1,0},{2,3},{3,2},{4,5},{5,4},{6,7},{7,6},{8,9},{9,8},{10,11... | collective-permute-start | bytes 110600 | tf_op jit(solution)/shard_map/ppermute | solution.py:555

commit v28 on v26

--- a/solution.py
+++ b/solution.py
@@ -336,7 +336,7 @@
         v_ref[j * width : (j + 1) * width] = v[j]
 
     def one_block(n, carry):
-        rest, link, left_link = carry
+        passed, link, left_link = carry
         upward = n < me
         b = jnp.where(upward, n, blocks - 1 - (n - me))
         start = b * (rows * chunks) + jnp.where(upward, 0, (rows + 1) * chunks)
@@ -345,14 +345,15 @@
         first = face(places[0], places[1])
         anew = (n == 0) | (n == me)
         left_link = jnp.where(n == me, link, left_link)
-        rest = jnp.where(anew, 1.0 + first, rest)
+        passed = jnp.where(anew, first, passed)
         for j in range(rows):
             after = face(places[j + 1], places[j + 2])
-            link = after * inverse(rest + after)
+            one_inv = inverse(passed + (1.0 + after))
+            link = after * one_inv
             through = through * link if j else link
-            rest = 1.0 + rest * link
+            passed = ((1.0 + passed) * after) * one_inv
         gain_ref[pl.ds(aligned(b * width), width), :] = through * (first * inverse(after))
-        return rest, link, left_link
+        return passed, link, left_link
 
     gain_ref[pl.ds(aligned(me * width), width), :] = u[-1]
     nothing = 0.0 * u[0]

time: 24.6 us -> 24.6 us (level)
  no operation moved by 1% of the time
where the time goes in v28:
time: 24.6 us; the launch traced here: 24.3 us
  blocking collectives  17.5 us (71%)
  Pallas kernels  5.11 us (21%)
  starting transfers between devices  1.37 us (6%)
    all_gather x1, blocking collectives, gather_rows(): lax.all_gather(rows_sent, 'wide', axis_index_groups=cores, axis=0)  9.3 us
    all_to_all x1, blocking collectives, on_device(): lax.all_to_all(sent.reshape(wide_count, width, LANES), 'wide', split_axis...  8.2 us
    pallas_call x1, Pallas kernels, on_device(): pl.pallas_call(functools.partial(main_kernel, sizes), out_shape=(lines(wi...  1.88 us
    pallas_call x1, Pallas kernels, load_rows(): pl.pallas_call(row_kernel, out_shape=(jax.ShapeDtypeStruct(table_shape, f...  1.41 us
    ppermute x1, starting transfers between devices, on_device(): both_came = lax.ppermute(both, 'wide', swaps)  1.3 us
    pallas_call x1, Pallas kernels, on_device(): pl.pallas_call(functools.partial(load_kernel, sizes), out_shape=(lines(ro...  1.09 us
    pallas_call x1, Pallas kernels, on_device(): pl.pallas_call(functools.partial(last_kernel, sizes), out_shape=lines(row...  0.74 us
  transfers between devices with their start and end apart: 2, of which 1 were waited for; matrix products, arithmetic and copies ran while one was open for 0% of the time, Pallas kernels for 10%

profile of v28, /device:TPU:0, one launch (start us, length us, event | category | flops | bytes accessed | tf_op | source)
XLA Modules:
  0.0 24.3 jit_solution(449232329311868143)
XLA Ops:
  0.0 1.3 %collective-permute-start = (f32[64,128]{1,0:T(8,128)S(1)}, f32[64,128]{1,0:T(8,128)S(1)}, u32[]{:S(2)}, u32[]{:S(2)}) collective-permute-start(f32[64,128]{1,0:T(8,128)S(1)} %get-tuple-element.64), channel_id=1, source_target_pairs={{0,1},{1,0},{2,3},{3,2},{4,5},{5,4},{6,7},{7,6},{8,9},{9,8},{10,11... | collective-permute-start | bytes 98312 | tf_op jit(solution)/shard_map/ppermute | solution.py:514
  1.3 1.4 %conditional.4 = ((f32[8,128]{1,0:T(8,128)S(1)}, f32[32,128]{1,0:T(8,128)S(1)}, f32[32,128]{1,0:T(8,128)S(1)})) conditional(s32[]{:T(128)} %convert_element_type.2, (f32[256,128]{1,0:T(8,128)}, s32[1]{0:T(128)}) %tuple.51, f32[2,128]{1,0:T(2,128)S(1)} %get-tuple-element.60), branch_computations={%region_2.3_spmd, %region_3.4_spmd} | conditional | bytes 37928 | solution.py:532
  1.3 1.4 %branch_0_fun.1 = (f32[8,128]{1,0:T(8,128)S(1)}, f32[32,128]{1,0:T(8,128)S(1)}, f32[32,128]{1,0:T(8,128)S(1)}) custom-call(f32[256,128]{1,0:T(8,128)} %get-tuple-element.33.field_ref, s32[1]{0:T(128)} %get-tuple-element.89.step_ref), custom_call_target="tpu_custom_call" | custom-call | tf_op jit(solution)/shard_map/cond/branch_0_fun/pallas_call | solution.py:521
  2.7 0.0 collective-permute-done.both_ref
  2.7 9.4 %conditional.5 = (f32[32,128]{1,0:T(8,128)S(1)}, f32[32,128]{1,0:T(8,128)S(1)}) conditional(s32[]{:T(128)} %convert_element_type.2, (f32[64,128]{1,0:T(8,128)S(1)}, f32[32,128]{1,0:T(8,128)S(1)}, s32[]{:T(128)}) %tuple.38, () %tuple.39), branch_computations={%region_4.5_spmd, %region_5.6_spmd} | conditional | flops 8215 | bytes 327952 | solution.py:550
  2.8 9.3 %all-gather = f32[256,128]{1,0:T(8,128)S(1)} all-gather(f32[64,128]{1,0:T(8,128)S(1)} %pad_maximum_fusion), channel_id=2, replica_groups={{0,2,4,6},{1,3,5,7},{8,10,12,14},{9,11,13,15},{16,18,20,22},{17,19,21,2..., dimensions={0}, use_global_device_ids=true | all-gather | bytes 163840 | tf_op jit(solution)/shard_map/cond/branch_0_fun/all_gather | solution.py:539
  12.2 0.1 collective-permute-start.1
  12.2 1.1 %shard_map.68 = (f32[256,128]{1,0:T(8,128)S(1)}, f32[512,128]{1,0:T(8,128)S(1)}) custom-call(f32[256,128]{1,0:T(8,128)} %bitcast.33, f32[256,128]{1,0:T(8,128)} %bitcast.35), custom_call_target="tpu_custom_call" | custom-call | tf_op jit(solution)/shard_map/pallas_call | solution.py:554
  13.3 0.1 collective-permute-done.1.came_ref
  13.4 1.9 %shard_map.69 = (f32[256,128]{1,0:T(8,128)S(1)}, f32[256,128]{1,0:T(8,128)S(1)}, f32[256,128]{1,0:T(8,128)S(1)}, f32[256,128]{1,0:T(8,128)S(1)}, f32[256,128]{1,0:T(8,128)S(1)}, /*index=5*/f32[256,128]{1,0:T(8,128)S(1)}) custom-call(f32[72,128]{1,0:T(8,128)S(1)} %constant_dynamic-update-slice_fusion.handed_ref, f32[64,128]{1,0:T(8,128)S(1)} %collective-permute-done.both_ref, ...), custom_call_target="tpu_custom_call" | custom-call | tf_op jit(solution)/shard_map/pallas_call | solution.py:569
  15.3 8.2 %all_to_all.5 = f32[8,32,128]{2,1,0:T(8,128)S(1)} all-to-all(f32[8,32,128]{2,1,0:T(8,128)S(1)} %bitcast.30), channel_id=1, replica_groups=mesh['grp'=4,'wide'=8] {'wide'}, dimensions={0} | all-to-all | bytes 262144 | tf_op jit(solution)/shard_map/all_to_all | solution.py:582
  23.5 0.7 %shard_map.70 = f32[256,128]{1,0:T(8,128)} custom-call(f32[256,128]{1,0:T(8,128)S(1)} %bitcast.29, f32[256,128]{1,0:T(8,128)S(1)} %get-tuple-element.76.gain_ref, f32[256,128]{1,0:T(8,128)S(1)} %get-tuple-element.77.joint_ref, f32[256,128]{1,0:T(8,128)S(1)} %get-tuple-element.78.p_ref, f32[256,128]{1,0:T(8,128)S(1)} %get-tuple-element.79.u_ref, ...), custom_call_target="tpu_custom_call" | custom-call | tf_op jit(solution)/shard_map/pallas_call | solution.py:586
  (9 shorter events, 0.0 us)
Async XLA Ops:
  0.0 2.7 %collective-permute-start = (f32[64,128]{1,0:T(8,128)S(1)}, f32[64,128]{1,0:T(8,128)S(1)}, u32[]{:S(2)}, u32[]{:S(2)}) collective-permute-start(f32[64,128]{1,0:T(8,128)S(1)} %get-tuple-element.64), channel_id=1, source_target_pairs={{0,1},{1,0},{2,3},{3,2},{4,5},{5,4},{6,7},{7,6},{8,9},{9,8},{10,11... | collective-permute-start | bytes 98312 | tf_op jit(solution)/shard_map/ppermute | solution.py:514
  12.2 1.3 %collective-permute-start.1 = (f32[72,128]{1,0:T(8,128)S(1)}, f32[72,128]{1,0:T(8,128)S(1)}, u32[]{:S(2)}, u32[]{:S(2)}) collective-permute-start(f32[72,128]{1,0:T(8,128)S(1)} %constant_dynamic-update-slice_fusion.handed_ref), channel_id=1, source_target_pairs={{0,1},{1,0},{2,3},{3,2},{4,5},{5,4},{6,7},{7,6},{8,9},{9,8},{10,11... | collective-permute-start | bytes 110600 | tf_op jit(solution)/shard_map/ppermute | solution.py:552
